TPU v7x, 32 devices: a whole 2x2x4 slice. The times are simulated.
32 devices in a mesh: groups: 2 (over y), row: 16 (over z, x, core).
Axes of the slice: x: 2, y: 2, z: 4, core: 2. Of those that a mesh axis runs over, the one named last changes fastest.
Arguments:
- hidden: bfloat16 [4096, 5120], P(('groups', 'row')), parts along dimension 0, may hold values from -6 to 6
- kv_gain: float32 [5120], replicated, may hold values from 0.5 to 1.5
- kv_weight: bfloat16 [5120, 2048], P('row'), may hold values from -0.25 to 0.25
- query_states: bfloat16 [5120, 256], P('row', 'groups'), parts along dimension 1, may hold values from -6 to 6
- query_gain: float32 [2, 5120], replicated, may hold values from 0.5 to 1.5
- query_weight: bfloat16 [2, 16, 2560, 640], P(None, 'row'), may hold values from -0.078125 to 0.078125
- output_weight: bfloat16 [2, 16, 2560, 640], P(None, 'row'), may hold values from -0.078125 to 0.078125
- block_bounds: int32 [4, 2], P('groups'), parts along dimension 0, may hold values from 0 to 1984, as said below
Outputs:
- mixed: bfloat16 [5120, 256], P('row', 'groups'), parts along dimension 1
There are 2 independent parts, one for each index of `groups`. A program takes and returns all parts, laid end to end along the dimension named above; an argument that names none is the same for every part. Nothing has to cross between parts.
Inputs may be any that keep to these rules, and one draw needn't show every extreme that they name: `block_bounds`: row b is (lowest visible key position, first query position) of query block b; the first is at most the second, and block 0 starts 64 positions before the end of the prefix.
All inputs are finite; a program needn't handle non-finite values.
Results may differ from a plain program's by a relative error of at most 0.035.
Values may be sent and summed in bfloat16 or wider, within the bound.
No kernel may reach another device: no remote copies, remote signals or barrier semaphores. Data moves between devices by JAX's collectives and lax.ppermute only.
A program may use at most 128 MiB of HBM per device.

v0:
```python
import jax
import jax.numpy as jnp
from jax import lax
from jax.sharding import PartitionSpec as P

D = 5120
KVH = 8
HD = 128
QPK = 5
QBLK = 64
NQB = 2
SECTIONS = 2


CAP = 30.0
EPSILON = 1e-05


def swapped(value, axis, distance):
    mask = 2**distance
    pairs = [(source, source ^ mask) for source in range(lax.axis_size(axis))]
    return lax.ppermute(value, axis, pairs)


def halve_sum(first, second, bit_list, split_axis):
    device_index = lax.axis_index("row")
    for bit_number in reversed(bit_list):
        upper_half = device_index // 2**bit_number % 2
        first_low, first_high = jnp.split(first, 2, axis=split_axis)
        second_low, second_high = jnp.split(second, 2, axis=split_axis)
        kept_first = jnp.where(upper_half == 1, first_high, first_low)
        kept_second = jnp.where(upper_half == 1, second_high, second_low)
        sent_first = jnp.where(upper_half == 1, first_low, first_high)
        sent_second = jnp.where(upper_half == 1, second_low, second_high)
        got_first, got_second = (
            swapped(sent_first.astype(jnp.bfloat16), "row", bit_number).astype(sent_first.dtype),
            swapped(sent_second.astype(jnp.bfloat16), "row", bit_number).astype(sent_second.dtype),
        )
        first = kept_first + got_first
        second = kept_second + got_second
    return (first, second)


def halve_one(member, bit_list, split_axis):
    device_index = lax.axis_index("row")
    for bit_number in reversed(bit_list):
        upper_half = device_index // 2**bit_number % 2
        lower_piece, upper_piece = jnp.split(member, 2, axis=split_axis)
        kept = jnp.where(upper_half == 1, upper_piece, lower_piece)
        sent = jnp.where(upper_half == 1, lower_piece, upper_piece)
        member = kept + swapped(sent.astype(jnp.bfloat16), "row", bit_number).astype(sent.dtype)
    return member


def double_gather(gathered, bit_list, join_axis):
    device_index = lax.axis_index("row")
    for bit_number in bit_list:
        upper_half = device_index // 2**bit_number % 2
        partner = swapped(gathered, "row", bit_number)
        gathered = jnp.where(
            upper_half == 1,
            jnp.concatenate([partner, gathered], join_axis),
            jnp.concatenate([gathered, partner], join_axis),
        )
    return gathered


def attend_rows(queries, query_pos, query_floor, key_values, key_pos):
    row_count = queries.shape[0]
    head_width = key_values.shape[1] // 2
    head_count = queries.shape[1] // head_width
    key_part = key_values[:, :head_width]
    value_part = key_values[:, head_width:]
    grouped = queries.reshape(row_count, head_count, head_width)
    scores = jnp.einsum(
        "rhd,kd->rhk", grouped, key_part, preferred_element_type=jnp.float32
    ) * head_width ** (-0.5)
    capped = CAP * jnp.tanh(scores / CAP)
    visible = (key_pos[None, :] <= query_pos[:, None]) & (key_pos[None, :] >= query_floor[:, None])
    weights = jnp.where(visible[:, None, :], jnp.exp(capped), 0.0)
    totals = jnp.sum(weights, axis=2)
    weighted = jnp.einsum(
        "rhk,kd->rhd", weights.astype(jnp.bfloat16), value_part, preferred_element_type=jnp.float32
    )
    return (weighted.reshape(row_count, head_count * head_width), totals)


def on_device(
    hidden, kv_gain, kv_weight, query_states, query_gain, query_weight, output_weight, block_bounds
):
    lane_count = lax.axis_size("row")
    head_bits = KVH.bit_length() - 1
    total_bits = lane_count.bit_length() - 1
    tile_bits = list(range(head_bits))
    group_bits = list(range(head_bits, total_bits))
    tile_count = lane_count // KVH
    device_index = lax.axis_index("row")
    tile_index = device_index // KVH
    token_rows = hidden.shape[0]
    sub_rows = token_rows // tile_count
    pair_width = 2 * HD
    hidden_float = hidden.astype(jnp.float32)
    inverse = lax.rsqrt(jnp.mean(hidden_float * hidden_float, axis=1, keepdims=True) + EPSILON)
    normed = (hidden_float * inverse * kv_gain[None, :]).astype(jnp.bfloat16)
    grouped_rows = normed.reshape(tile_count, sub_rows, D)
    shard_rows = lax.all_gather(kv_weight, "row", axis=0, tiled=True)
    blocked = shard_rows.reshape(shard_rows.shape[0], KVH, pair_width)
    projected = jnp.einsum(
        "psd,dgc->pgsc", grouped_rows, blocked, preferred_element_type=jnp.float32
    )
    outgoing = projected.astype(jnp.bfloat16).reshape(lane_count, sub_rows, pair_width)
    arrived = lax.all_to_all(outgoing, "row", split_axis=0, concat_axis=0, tiled=True)
    key_values = arrived.reshape(lane_count * sub_rows, pair_width)
    source = jnp.arange(lane_count * sub_rows, dtype=jnp.int32)
    key_pos = source // sub_rows * token_rows + tile_index * sub_rows + source % sub_rows
    query_count = NQB * QBLK
    row_number = jnp.arange(query_count, dtype=jnp.int32)
    query_pos = (
        jnp.broadcast_to(block_bounds[:, 1:2], (NQB, QBLK)).reshape(query_count) + row_number % QBLK
    )
    query_floor = jnp.broadcast_to(block_bounds[:, 0:1], (NQB, QBLK)).reshape(query_count)
    rows_share = query_count // tile_count
    slice_depth = D // tile_count
    own_rows = query_states
    stream = double_gather(own_rows, tile_bits, 0)
    for section in range(SECTIONS):
        stream_float = stream.astype(jnp.float32)
        squares = jnp.sum(stream_float * stream_float, axis=0)
        gain_slice = lax.dynamic_slice_in_dim(
            query_gain[section], tile_index * slice_depth, slice_depth
        )
        scaled = (stream_float * gain_slice[:, None]).astype(jnp.bfloat16)
        partial_q = lax.dot_general(
            scaled,
            query_weight[section, 0],
            (((0,), (0,)), ((), ())),
            preferred_element_type=jnp.float32,
        )
        query_sum, square_sum = halve_sum(partial_q, squares, group_bits, 0)
        inverse_q = lax.rsqrt(square_sum / D + EPSILON)
        own_queries = (query_sum * inverse_q[:, None]).astype(jnp.bfloat16)
        all_queries = double_gather(own_queries, group_bits, 0)
        added_all, counted_all = attend_rows(
            all_queries, query_pos, query_floor, key_values, key_pos
        )
        accumulated, totals = halve_sum(added_all, counted_all, group_bits, 0)
        attended = (
            (accumulated.reshape(rows_share, QPK, HD) / totals[:, :, None])
            .reshape(rows_share, QPK * HD)
            .astype(jnp.bfloat16)
        )
        all_attended = double_gather(attended, group_bits, 0)
        update = lax.dot_general(
            output_weight[section, 0],
            all_attended,
            (((1,), (1,)), ((), ())),
            preferred_element_type=jnp.float32,
        )
        own_update = halve_one(update, tile_bits, 0)
        own_rows = (own_rows.astype(jnp.float32) + own_update).astype(jnp.bfloat16)
        if section + 1 < SECTIONS:
            stream = double_gather(own_rows, tile_bits, 0)
    return own_rows


def solution(mesh):
    in_specs = (
        P(("groups", "row"), None),
        P(),
        P("row", None),
        P("row", "groups"),
        P(),
        P(None, "row", None, None),
        P(None, "row", None, None),
        P("groups", None),
    )
    out_specs = P("row", "groups")
    return jax.shard_map(
        on_device, mesh=mesh, in_specs=in_specs, out_specs=out_specs, check_vma=False
    )
```

profile of v0, /device:TPU:0, one launch (start us, length us, event | category | flops | bytes accessed | tf_op | source)
XLA Modules:
  0.0 300.6 jit_solution(9287901784059346901)
XLA Ops:
  7.3 1.0 copy.35
  8.8 1.6 fusion.10
  11.0 2.6 collective-permute-start.1
  14.3 4.2 %collective-permute-done.1 = bf16[640,128]{0,1:T(8,128)(2,1)S(1)} collective-permute-done((bf16[640,128]{0,1:T(8,128)(2,1)S(1)}, bf16[640,128]{0,1:T(8,128)(2,1)S(1)}, u32[]{:S(2)}, u32[]{:S(2)}) %collective-permute-start.1) | collective-permute-done | bytes 163872 | tf_op jit(solution)/shard_map/ppermute | solution.py:22
  18.6 1.9 collective-permute-start.2
  20.5 15.3 %collective-permute-done.2 = bf16[1280,128]{0,1:T(8,128)(2,1)S(1)} collective-permute-done((bf16[1280,128]{0,1:T(8,128)(2,1)S(1)}, bf16[1280,128]{0,1:T(8,128)(2,1)S(1)}, u32[]{:S(2)}, u32[]{:S(2)}) %collective-permute-start.2) | collective-permute-done | bytes 327712 | tf_op jit(solution)/shard_map/ppermute | solution.py:22
  36.1 2.8 collective-permute-start.4
  38.9 2.7 fusion.4
  41.7 85.9 %all-gather.2.cloned.1.call-done = bf16[5120,2048]{1,0:T(8,128)(2,1)} async-done(((bf16[320,2048]{1,0:T(8,128)(2,1)}), bf16[5120,2048]{1,0:T(8,128)(2,1)}) %all-gather.2.cloned.1.call-update) | async-done | bytes 20971536 | tf_op jit(solution)/shard_map/all_gather | solution.py:106
  127.6 26.1 %copy.39 = bf16[5120,2048]{0,1:T(8,128)(2,1)} copy(bf16[5120,2048]{1,0:T(8,128)(2,1)} %all-gather.2.cloned.1.call-done) | data formatting | bytes 41943040 | tf_op jit(solution)/shard_map/all_gather | solution.py:106
  153.6 11.8 %convolution_convert_fusion = bf16[2,64,8,256]{3,1,2,0:T(8,128)(2,1)} fusion(bf16[2,64,5120,1]{2,1,3,0:T(8,128)(2,1)S(1)} %bitcast.77, bf16[5120,8,256,1]{0,2,1,3:T(8,128)(2,1)} %bitcast.76), kind=kOutput, calls=%fused_computation.35 | convolution fusion | flops 2684616704 | bytes 22806528 | tf_op jit(solution)/shard_map/psd,dgc->pgsc/dot_general | solution.py:108
  165.4 4.7 %all-to-all-start = ((bf16[16,64,256]{2,1,0:T(8,128)(2,1)}), bf16[16,64,256]{2,1,0:T(8,128)(2,1)S(1)}, u32[]{:S(2)}, u32[]{:S(2)}) async-start(bf16[16,64,256]{2,1,0:T(8,128)(2,1)} %bitcast.7), calls=%async_computation | async-start | bytes 1048576 | tf_op jit(solution)/shard_map/all_to_all | solution.py:112
  170.1 2.9 collective-permute-start.3
  173.1 15.8 %collective-permute-done.3 = bf16[64,640]{1,0:T(8,128)(2,1)S(1)} collective-permute-done((bf16[64,640]{1,0:T(8,128)(2,1)S(1)}, bf16[64,640]{1,0:T(8,128)(2,1)S(1)}, u32[]{:S(2)}, u32[]{:S(2)}) %collective-permute-start.3) | collective-permute-done | bytes 81952 | tf_op jit(solution)/shard_map/ppermute | solution.py:22
  189.4 5.3 %collective-permute-done.5 = bf16[64,640]{1,0:T(8,128)(2,1)S(1)} collective-permute-done((bf16[64,640]{1,0:T(8,128)(2,1)S(1)}, bf16[64,640]{1,0:T(8,128)(2,1)S(1)}, u32[]{:S(2)}, u32[]{:S(2)}) %collective-permute-start.5) | collective-permute-done | bytes 81952 | tf_op jit(solution)/shard_map/ppermute | solution.py:22
  194.9 1.1 fusion.13
  197.0 3.0 collective-permute-start.6
  199.9 1.5 collective-permute-done.7
  202.6 3.0 collective-permute-start.8
  205.6 3.0 %collective-permute-done.8 = bf16[64,640]{1,0:T(8,128)(2,1)S(1)} collective-permute-done((bf16[64,640]{1,0:T(8,128)(2,1)S(1)}, bf16[64,640]{1,0:T(8,128)(2,1)S(1)}, u32[]{:S(2)}, u32[]{:S(2)}) %collective-permute-start.8) | collective-permute-done | bytes 81952 | tf_op jit(solution)/shard_map/ppermute | solution.py:22
  208.6 3.1 %convolution_bitcast_fusion.1 = f32[2560,128]{0,1:T(8,128)S(1)} fusion(bf16[2,1,2560,640]{3,2,1,0:T(8,128)(2,1)} %param.14, bf16[64,640]{1,0:T(8,128)(2,1)S(1)} %fusion.34, bf16[64,640]{1,0:T(8,128)(2,1)S(1)} %collective-permute-done.8, pred[]{:T(512)S(6)} %eq.36), kind=kOutput, calls=%fused_computation.1 | convolution fusion | flops 420167680 | bytes 4751361 | tf_op jit(solution)/shard_map/dot_general | solution.py:153
  211.7 2.2 collective-permute-start.9
  213.9 5.3 %collective-permute-done.9 = bf16[1280,128]{0,1:T(8,128)(2,1)S(1)} collective-permute-done((bf16[1280,128]{0,1:T(8,128)(2,1)S(1)}, bf16[1280,128]{0,1:T(8,128)(2,1)S(1)}, u32[]{:S(2)}, u32[]{:S(2)}) %collective-permute-start.9) | collective-permute-done | bytes 327712 | tf_op jit(solution)/shard_map/ppermute | solution.py:22
  219.4 1.5 collective-permute-start.10
  220.9 3.9 %collective-permute-done.10 = bf16[640,128]{0,1:T(8,128)(2,1)S(1)} collective-permute-done((bf16[640,128]{0,1:T(8,128)(2,1)S(1)}, bf16[640,128]{0,1:T(8,128)(2,1)S(1)}, u32[]{:S(2)}, u32[]{:S(2)}) %collective-permute-start.10) | collective-permute-done | bytes 163872 | tf_op jit(solution)/shard_map/ppermute | solution.py:22
  225.0 1.3 collective-permute-done.11
  226.6 1.1 collective-permute-done.12
  227.9 1.5 collective-permute-start.13
  229.4 4.8 %collective-permute-done.13 = bf16[640,128]{0,1:T(8,128)(2,1)S(1)} collective-permute-done((bf16[640,128]{0,1:T(8,128)(2,1)S(1)}, bf16[640,128]{0,1:T(8,128)(2,1)S(1)}, u32[]{:S(2)}, u32[]{:S(2)}) %collective-permute-start.13) | collective-permute-done | bytes 163872 | tf_op jit(solution)/shard_map/ppermute | solution.py:22
  234.3 1.8 collective-permute-start.14
  236.2 7.2 %collective-permute-done.14 = bf16[1280,128]{0,1:T(8,128)(2,1)S(1)} collective-permute-done((bf16[1280,128]{0,1:T(8,128)(2,1)S(1)}, bf16[1280,128]{0,1:T(8,128)(2,1)S(1)}, u32[]{:S(2)}, u32[]{:S(2)}) %collective-permute-start.14) | collective-permute-done | bytes 327712 | tf_op jit(solution)/shard_map/ppermute | solution.py:22
  243.7 2.0 collective-permute-start.16
  245.7 2.6 fusion.1
  248.4 1.0 collective-permute-start.15
  249.5 6.1 %collective-permute-done.15 = bf16[64,640]{1,0:T(8,128)(2,1)S(1)} collective-permute-done((bf16[64,640]{1,0:T(8,128)(2,1)S(1)}, bf16[64,640]{1,0:T(8,128)(2,1)S(1)}, u32[]{:S(2)}, u32[]{:S(2)}) %collective-permute-start.15) | collective-permute-done | bytes 81952 | tf_op jit(solution)/shard_map/ppermute | solution.py:22
  255.8 5.2 %collective-permute-done.17 = bf16[64,640]{1,0:T(8,128)(2,1)S(1)} collective-permute-done((bf16[64,640]{1,0:T(8,128)(2,1)S(1)}, bf16[64,640]{1,0:T(8,128)(2,1)S(1)}, u32[]{:S(2)}, u32[]{:S(2)}) %collective-permute-start.17) | collective-permute-done | bytes 81952 | tf_op jit(solution)/shard_map/ppermute | solution.py:22
  261.3 1.1 fusion.15
  263.4 2.9 collective-permute-start.18
  266.3 1.5 collective-permute-done.19
  267.9 1.7 collective-permute-done.18
  269.9 2.0 collective-permute-start.20
  271.9 3.5 %collective-permute-done.20 = bf16[64,640]{1,0:T(8,128)(2,1)S(1)} collective-permute-done((bf16[64,640]{1,0:T(8,128)(2,1)S(1)}, bf16[64,640]{1,0:T(8,128)(2,1)S(1)}, u32[]{:S(2)}, u32[]{:S(2)}) %collective-permute-start.20) | collective-permute-done | bytes 81952 | tf_op jit(solution)/shard_map/ppermute | solution.py:22
  275.4 3.1 %convolution_bitcast_fusion = f32[2560,128]{0,1:T(8,128)S(1)} fusion(bf16[2,1,2560,640]{3,2,1,0:T(8,128)(2,1)} %param.14, bf16[64,640]{1,0:T(8,128)(2,1)S(1)} %fusion.33, bf16[64,640]{1,0:T(8,128)(2,1)S(1)} %collective-permute-done.20, pred[]{:T(512)S(6)} %eq.36), kind=kOutput, calls=%fused_computation | convolution fusion | flops 420167680 | bytes 4751361 | tf_op jit(solution)/shard_map/dot_general | solution.py:153
  278.6 2.3 collective-permute-start.21
  280.8 5.1 %collective-permute-done.21 = bf16[1280,128]{0,1:T(8,128)(2,1)S(1)} collective-permute-done((bf16[1280,128]{0,1:T(8,128)(2,1)S(1)}, bf16[1280,128]{0,1:T(8,128)(2,1)S(1)}, u32[]{:S(2)}, u32[]{:S(2)}) %collective-permute-start.21) | collective-permute-done | bytes 327712 | tf_op jit(solution)/shard_map/ppermute | solution.py:22
  286.0 1.5 collective-permute-start.22
  287.5 3.9 %collective-permute-done.22 = bf16[640,128]{0,1:T(8,128)(2,1)S(1)} collective-permute-done((bf16[640,128]{0,1:T(8,128)(2,1)S(1)}, bf16[640,128]{0,1:T(8,128)(2,1)S(1)}, u32[]{:S(2)}, u32[]{:S(2)}) %collective-permute-start.22) | collective-permute-done | bytes 163872 | tf_op jit(solution)/shard_map/ppermute | solution.py:22
  291.6 1.3 collective-permute-done.23
  (83 shorter events, 10.3 us)
Async XLA Ops:
  6.5 3.9 %copy-start = (bf16[128,5120]{1,0:T(8,128)(2,1)S(1)}, bf16[128,5120]{1,0:T(8,128)(2,1)}, u32[]{:S(2)}) copy-start(bf16[128,5120]{1,0:T(8,128)(2,1)} %param.8) | copy-start | bytes 3932164
  6.5 3.9 %copy-start.2 = (f32[5120]{0:T(1024)S(1)}, f32[5120]{0:T(1024)}, u32[]{:S(2)}) copy-start(f32[5120]{0:T(1024)} %param.9) | copy-start | bytes 61444
  6.5 7.1 %copy-start.1 = (f32[2,5120]{1,0:T(2,128)S(1)}, f32[2,5120]{1,0:T(2,128)}, u32[]{:S(2)}) copy-start(f32[2,5120]{1,0:T(2,128)} %param.12) | copy-start | bytes 122884
  6.5 121.0 %all-gather.2.cloned.1.call-start = ((), (), s32[]{:S(2)}) async-start(), calls=%async_computation.1 | async-start | bytes 22282240 | tf_op jit(solution)/shard_map/all_gather | solution.py:106
  7.3 6.5 %copy-start.3 = (s32[2,2]{1,0:T(2,128)S(1)}, s32[2,2]{1,0:T(2,128)}, u32[]{:S(2)}) copy-start(s32[2,2]{1,0:T(2,128)} %param.15) | copy-start | bytes 52
  8.3 2.6 collective-permute-start
  11.0 7.4 %collective-permute-start.1 = (bf16[640,128]{0,1:T(8,128)(2,1)S(1)}, bf16[640,128]{0,1:T(8,128)(2,1)S(1)}, u32[]{:S(2)}, u32[]{:S(2)}) collective-permute-start(bf16[640,128]{0,1:T(8,128)(2,1)S(1)} %maximum_select_fusion.6), channel_id=1, source_target_pairs={{0,2},{1,3},{2,0},{3,1},{4,6},{5,7},{6,4},{7,5},{8,10},{9,11},{10,... | collective-permute-start | bytes 491528 | tf_op jit(solution)/shard_map/ppermute | solution.py:22
  18.6 17.2 %collective-permute-start.2 = (bf16[1280,128]{0,1:T(8,128)(2,1)S(1)}, bf16[1280,128]{0,1:T(8,128)(2,1)S(1)}, u32[]{:S(2)}, u32[]{:S(2)}) collective-permute-start(bf16[1280,128]{0,1:T(8,128)(2,1)S(1)} %maximum_select_fusion.2), channel_id=1, source_target_pairs={{0,4},{1,5},{2,6},{3,7},{4,0},{5,1},{6,2},{7,3},{8,12},{9,13},{10,... | collective-permute-start | bytes 983048 | tf_op jit(solution)/shard_map/ppermute | solution.py:22
  36.1 136.9 %collective-permute-start.4 = (bf16[64]{0:T(256)(128)(2,1)S(1)}, bf16[64]{0:T(256)(128)(2,1)S(1)}, u32[]{:S(2)}, u32[]{:S(2)}) collective-permute-start(bf16[64]{0:T(256)(128)(2,1)S(1)} %fusion.64), channel_id=1, source_target_pairs={{0,8},{1,9},{2,10},{3,11},{4,12},{5,13},{6,14},{7,15},{8,0},{9,1},... | collective-permute-start | bytes 392 | tf_op jit(solution)/shard_map/ppermute | solution.py:22
  165.4 29.5 %all-to-all-start = ((bf16[16,64,256]{2,1,0:T(8,128)(2,1)}), bf16[16,64,256]{2,1,0:T(8,128)(2,1)S(1)}, u32[]{:S(2)}, u32[]{:S(2)}) async-start(bf16[16,64,256]{2,1,0:T(8,128)(2,1)} %bitcast.7), calls=%async_computation | async-start | bytes 1048576 | tf_op jit(solution)/shard_map/all_to_all | solution.py:112
  170.1 18.8 %collective-permute-start.3 = (bf16[64,640]{1,0:T(8,128)(2,1)S(1)}, bf16[64,640]{1,0:T(8,128)(2,1)S(1)}, u32[]{:S(2)}, u32[]{:S(2)}) collective-permute-start(bf16[64,640]{1,0:T(8,128)(2,1)S(1)} %select_convert_fusion.9), channel_id=1, source_target_pairs={{0,8},{1,9},{2,10},{3,11},{4,12},{5,13},{6,14},{7,15},{8,0},{9,1},... | collective-permute-start | bytes 245768 | tf_op jit(solution)/shard_map/ppermute | solution.py:22
  189.0 5.7 %collective-permute-start.5 = (bf16[64,640]{1,0:T(8,128)(2,1)S(1)}, bf16[64,640]{1,0:T(8,128)(2,1)S(1)}, u32[]{:S(2)}, u32[]{:S(2)}) collective-permute-start(bf16[64,640]{1,0:T(8,128)(2,1)S(1)} %multiply_convert_fusion.1), channel_id=1, source_target_pairs={{0,8},{1,9},{2,10},{3,11},{4,12},{5,13},{6,14},{7,15},{8,0},{9,1},... | collective-permute-start | bytes 245768 | tf_op jit(solution)/shard_map/ppermute | solution.py:22
  196.9 4.5 %collective-permute-start.7 = (bf16[64,5]{0,1:T(8,128)(2,1)S(1)}, bf16[64,5]{0,1:T(8,128)(2,1)S(1)}, u32[]{:S(2)}, u32[]{:S(2)}) collective-permute-start(bf16[64,5]{0,1:T(8,128)(2,1)S(1)} %select_convert_fusion.11), channel_id=1, source_target_pairs={{0,8},{1,9},{2,10},{3,11},{4,12},{5,13},{6,14},{7,15},{8,0},{9,1},... | collective-permute-start | bytes 1928 | tf_op jit(solution)/shard_map/ppermute | solution.py:22
  197.0 5.4 %collective-permute-start.6 = (bf16[64,640]{1,0:T(8,128)(2,1)S(1)}, bf16[64,640]{1,0:T(8,128)(2,1)S(1)}, u32[]{:S(2)}, u32[]{:S(2)}) collective-permute-start(bf16[64,640]{1,0:T(8,128)(2,1)S(1)} %copy_bitcast_fusion.1), channel_id=1, source_target_pairs={{0,8},{1,9},{2,10},{3,11},{4,12},{5,13},{6,14},{7,15},{8,0},{9,1},... | collective-permute-start | bytes 245768 | tf_op jit(solution)/shard_map/ppermute | solution.py:22
  202.6 6.0 %collective-permute-start.8 = (bf16[64,640]{1,0:T(8,128)(2,1)S(1)}, bf16[64,640]{1,0:T(8,128)(2,1)S(1)}, u32[]{:S(2)}, u32[]{:S(2)}) collective-permute-start(bf16[64,640]{1,0:T(8,128)(2,1)S(1)} %fusion.34), channel_id=1, source_target_pairs={{0,8},{1,9},{2,10},{3,11},{4,12},{5,13},{6,14},{7,15},{8,0},{9,1},... | collective-permute-start | bytes 245768 | tf_op jit(solution)/shard_map/ppermute | solution.py:22
  211.7 7.5 %collective-permute-start.9 = (bf16[1280,128]{0,1:T(8,128)(2,1)S(1)}, bf16[1280,128]{0,1:T(8,128)(2,1)S(1)}, u32[]{:S(2)}, u32[]{:S(2)}) collective-permute-start(bf16[1280,128]{0,1:T(8,128)(2,1)S(1)} %select_convert_fusion.1), channel_id=1, source_target_pairs={{0,4},{1,5},{2,6},{3,7},{4,0},{5,1},{6,2},{7,3},{8,12},{9,13},{10,... | collective-permute-start | bytes 983048 | tf_op jit(solution)/shard_map/ppermute | solution.py:22
  219.4 5.4 %collective-permute-start.10 = (bf16[640,128]{0,1:T(8,128)(2,1)S(1)}, bf16[640,128]{0,1:T(8,128)(2,1)S(1)}, u32[]{:S(2)}, u32[]{:S(2)}) collective-permute-start(bf16[640,128]{0,1:T(8,128)(2,1)S(1)} %select_convert_fusion.3), channel_id=1, source_target_pairs={{0,2},{1,3},{2,0},{3,1},{4,6},{5,7},{6,4},{7,5},{8,10},{9,11},{10,... | collective-permute-start | bytes 491528 | tf_op jit(solution)/shard_map/ppermute | solution.py:22
  224.9 1.4 collective-permute-start.11
  226.4 1.4 collective-permute-start.12
  227.9 6.3 %collective-permute-start.13 = (bf16[640,128]{0,1:T(8,128)(2,1)S(1)}, bf16[640,128]{0,1:T(8,128)(2,1)S(1)}, u32[]{:S(2)}, u32[]{:S(2)}) collective-permute-start(bf16[640,128]{0,1:T(8,128)(2,1)S(1)} %maximum_select_fusion.9), channel_id=1, source_target_pairs={{0,2},{1,3},{2,0},{3,1},{4,6},{5,7},{6,4},{7,5},{8,10},{9,11},{10,... | collective-permute-start | bytes 491528 | tf_op jit(solution)/shard_map/ppermute | solution.py:22
  234.3 9.0 %collective-permute-start.14 = (bf16[1280,128]{0,1:T(8,128)(2,1)S(1)}, bf16[1280,128]{0,1:T(8,128)(2,1)S(1)}, u32[]{:S(2)}, u32[]{:S(2)}) collective-permute-start(bf16[1280,128]{0,1:T(8,128)(2,1)S(1)} %maximum_select_fusion.3), channel_id=1, source_target_pairs={{0,4},{1,5},{2,6},{3,7},{4,0},{5,1},{6,2},{7,3},{8,12},{9,13},{10,... | collective-permute-start | bytes 983048 | tf_op jit(solution)/shard_map/ppermute | solution.py:22
  243.7 5.7 %collective-permute-start.16 = (bf16[64]{0:T(256)(128)(2,1)S(1)}, bf16[64]{0:T(256)(128)(2,1)S(1)}, u32[]{:S(2)}, u32[]{:S(2)}) collective-permute-start(bf16[64]{0:T(256)(128)(2,1)S(1)} %fusion.67), channel_id=1, source_target_pairs={{0,8},{1,9},{2,10},{3,11},{4,12},{5,13},{6,14},{7,15},{8,0},{9,1},... | collective-permute-start | bytes 392 | tf_op jit(solution)/shard_map/ppermute | solution.py:22
  248.4 7.2 %collective-permute-start.15 = (bf16[64,640]{1,0:T(8,128)(2,1)S(1)}, bf16[64,640]{1,0:T(8,128)(2,1)S(1)}, u32[]{:S(2)}, u32[]{:S(2)}) collective-permute-start(bf16[64,640]{1,0:T(8,128)(2,1)S(1)} %select_convert_fusion.7), channel_id=1, source_target_pairs={{0,8},{1,9},{2,10},{3,11},{4,12},{5,13},{6,14},{7,15},{8,0},{9,1},... | collective-permute-start | bytes 245768 | tf_op jit(solution)/shard_map/ppermute | solution.py:22
  255.6 5.4 %collective-permute-start.17 = (bf16[64,640]{1,0:T(8,128)(2,1)S(1)}, bf16[64,640]{1,0:T(8,128)(2,1)S(1)}, u32[]{:S(2)}, u32[]{:S(2)}) collective-permute-start(bf16[64,640]{1,0:T(8,128)(2,1)S(1)} %multiply_convert_fusion), channel_id=1, source_target_pairs={{0,8},{1,9},{2,10},{3,11},{4,12},{5,13},{6,14},{7,15},{8,0},{9,1},... | collective-permute-start | bytes 245768 | tf_op jit(solution)/shard_map/ppermute | solution.py:22
  263.3 4.5 %collective-permute-start.19 = (bf16[64,5]{0,1:T(8,128)(2,1)S(1)}, bf16[64,5]{0,1:T(8,128)(2,1)S(1)}, u32[]{:S(2)}, u32[]{:S(2)}) collective-permute-start(bf16[64,5]{0,1:T(8,128)(2,1)S(1)} %select_convert_fusion.10), channel_id=1, source_target_pairs={{0,8},{1,9},{2,10},{3,11},{4,12},{5,13},{6,14},{7,15},{8,0},{9,1},... | collective-permute-start | bytes 1928 | tf_op jit(solution)/shard_map/ppermute | solution.py:22
  263.4 6.3 %collective-permute-start.18 = (bf16[64,640]{1,0:T(8,128)(2,1)S(1)}, bf16[64,640]{1,0:T(8,128)(2,1)S(1)}, u32[]{:S(2)}, u32[]{:S(2)}) collective-permute-start(bf16[64,640]{1,0:T(8,128)(2,1)S(1)} %copy_bitcast_fusion), channel_id=1, source_target_pairs={{0,8},{1,9},{2,10},{3,11},{4,12},{5,13},{6,14},{7,15},{8,0},{9,1},... | collective-permute-start | bytes 245768 | tf_op jit(solution)/shard_map/ppermute | solution.py:22
  269.9 5.5 %collective-permute-start.20 = (bf16[64,640]{1,0:T(8,128)(2,1)S(1)}, bf16[64,640]{1,0:T(8,128)(2,1)S(1)}, u32[]{:S(2)}, u32[]{:S(2)}) collective-permute-start(bf16[64,640]{1,0:T(8,128)(2,1)S(1)} %fusion.33), channel_id=1, source_target_pairs={{0,8},{1,9},{2,10},{3,11},{4,12},{5,13},{6,14},{7,15},{8,0},{9,1},... | collective-permute-start | bytes 245768 | tf_op jit(solution)/shard_map/ppermute | solution.py:22
  278.6 7.3 %collective-permute-start.21 = (bf16[1280,128]{0,1:T(8,128)(2,1)S(1)}, bf16[1280,128]{0,1:T(8,128)(2,1)S(1)}, u32[]{:S(2)}, u32[]{:S(2)}) collective-permute-start(bf16[1280,128]{0,1:T(8,128)(2,1)S(1)} %select_convert_fusion), channel_id=1, source_target_pairs={{0,4},{1,5},{2,6},{3,7},{4,0},{5,1},{6,2},{7,3},{8,12},{9,13},{10,... | collective-permute-start | bytes 983048 | tf_op jit(solution)/shard_map/ppermute | solution.py:22
  286.0 5.4 %collective-permute-start.22 = (bf16[640,128]{0,1:T(8,128)(2,1)S(1)}, bf16[640,128]{0,1:T(8,128)(2,1)S(1)}, u32[]{:S(2)}, u32[]{:S(2)}) collective-permute-start(bf16[640,128]{0,1:T(8,128)(2,1)S(1)} %select_convert_fusion.2), channel_id=1, source_target_pairs={{0,2},{1,3},{2,0},{3,1},{4,6},{5,7},{6,4},{7,5},{8,10},{9,11},{10,... | collective-permute-start | bytes 491528 | tf_op jit(solution)/shard_map/ppermute | solution.py:22
  291.6 1.4 collective-permute-start.23
Sparse Core Ops, SparseCore 0:
  9.0 118.5 all-gather.1
where the time goes:
time: 302 us; the launch traced here: 301 us
  waiting for transfers between devices  184 us (61%)
  starting transfers between devices  40.6 us (13%)
  local copies, waits for them, and re-layouts  29.3 us (10%)
  matrix products  27.1 us (9%)
  between operations  13.9 us (5%)
  other arithmetic  5.42 us (2%)
    ppermute x24, waiting for transfers between devices, swapped(): return lax.ppermute(value, axis, pairs)  97.8 us
    all_gather x1, waiting for transfers between devices, on_device(): shard_rows = lax.all_gather(kv_weight, 'row', axis=0, tiled=True)  85.9 us
    ppermute x24, starting transfers between devices, swapped(): return lax.ppermute(value, axis, pairs)  35.9 us
    all_gather x1, local copies, waits for them, and re-layouts, on_device(): shard_rows = lax.all_gather(kv_weight, 'row', axis=0, tiled=True)  26.1 us
    dot_general x1, matrix products, on_device(): jnp.einsum('psd,dgc->pgsc', grouped_rows, blocked, preferred_element_type...  11.8 us
    dot_general x2, matrix products, on_device(): lax.dot_general(output_weight[section, 0], all_attended, (((1,), (1,)), (...  6.15 us
  transfers between devices with their start and end apart: 26, of which 22 were waited for; matrix products, arithmetic and copies ran while one was open for 16% of the time, Pallas kernels for 0%

commit v1 on v0

v1 whole, which is shorter than its diff:
```python
import jax
import jax.numpy as jnp
from jax import lax
from jax.sharding import PartitionSpec as P

KVH = 8
HD = 128
QPK = 5
QBLK = 64
CAP = 30.0
EPSILON = 1e-05
BF16 = jnp.bfloat16
F32 = jnp.float32

CHIPS = KVH // 2
ROUNDS = ((3,), (1,), (2,), (0,))


def swapped(value, mask, axis="row"):
    pairs = [(source, source ^ mask) for source in range(lax.axis_size(axis))]
    return lax.ppermute(value, axis, pairs)


def over_tiles(value, tile_count):
    values = [value]
    mask = 1
    while mask < tile_count:
        if len(values) == 1:
            values.append(swapped(values[0], mask * KVH))
        else:
            got = swapped(jnp.stack(values), mask * KVH)
            values.extend(got[place] for place in range(len(values)))
        mask *= 2
    return values


def natural(pieces, index):
    pieces = list(pieces)
    bit = 1
    while bit < len(pieces):
        upper = index // bit % 2 == 1
        pieces = [jnp.where(upper, pieces[j ^ bit], pieces[j]) for j in range(len(pieces))]
        bit *= 2
    return pieces


def key_values_of(hidden, kv_gain, kv_weight):
    lane_count = lax.axis_size("row")
    tile_count = lane_count // KVH
    me = lax.axis_index("row")
    tile, chip, core = me // KVH, me // 2 % CHIPS, me % 2
    rows, depth = hidden.shape
    unit = kv_weight.shape[0]
    pair = 2 * HD

    def head_columns(place, which_core):
        return lax.dynamic_slice_in_dim(kv_weight, ((chip ^ place) * 2 + which_core) * pair, pair, 1)

    order = [place for round_ in ROUNDS for place in round_]
    kept = {place: head_columns(place, core) for place in order}
    traded = swapped(jnp.stack([head_columns(place, 1 - core) for place in order]), 1)
    traded = {place: traded[number] for number, place in enumerate(order)}

    hidden_float = hidden.astype(F32)
    inverse = lax.rsqrt(jnp.mean(hidden_float * hidden_float, axis=1, keepdims=True) + EPSILON)
    normed = (hidden_float * inverse * kv_gain[None, :]).astype(BF16)

    def features(place):
        return jnp.concatenate(
            [
                lax.dynamic_slice_in_dim(
                    normed, ((tile ^ j) * KVH + (chip ^ place) * 2) * unit, 2 * unit, 1
                )
                for j in range(tile_count)
            ],
            axis=1,
        )

    share = lax.axis_size("groups") == 2
    part = lax.axis_index("groups")
    held = []
    for place in range(CHIPS):
        own = features(place)
        held.append(own if place == 0 else swapped(own, 2 * place))
    mine = jnp.concatenate(held, axis=0)
    tokens = jnp.concatenate([mine, swapped(mine, 1)], axis=0)

    total = None
    for round_ in ROUNDS:
        first = jnp.stack([kept[place] for place in round_])
        second = jnp.stack([traded[place] for place in round_])
        low, high = jnp.where(core == 0, first, second), jnp.where(core == 0, second, first)
        blocks = [(low, high)]
        if share:
            far = over_tiles(jnp.where(part == 0, low, high), tile_count)[1:]
            for value in far:
                other = swapped(value, 1, "groups")
                blocks.append((jnp.where(part == 0, value, other), jnp.where(part == 0, other, value)))
        else:
            far = over_tiles(jnp.stack([low, high]), tile_count)[1:]
            blocks.extend((value[0], value[1]) for value in far)
        for number, place in enumerate(round_):
            weight = jnp.concatenate([half[number] for block in blocks for half in block], axis=0)
            partial = lax.dot_general(
                tokens, weight, (((1,), (0,)), ((), ())), preferred_element_type=F32
            )
            if place:
                partial = swapped(partial.astype(BF16), 2 * place).astype(F32)
            pieces = partial.reshape(2, CHIPS, rows, pair)
            pieces = jnp.stack([pieces[:, j ^ place] for j in range(CHIPS)], axis=1)
            total = pieces if total is None else total + pieces
    key_values = total.astype(BF16).reshape(2 * CHIPS * rows, pair)
    sources = jnp.stack(
        [tile * KVH + (chip ^ j) * 2 + (core ^ e) for e in range(2) for j in range(CHIPS)]
    )
    key_pos = (sources[:, None] * rows + jnp.arange(rows, dtype=jnp.int32)[None, :]).reshape(-1)
    return key_values, key_pos


def gather_rows(own):
    me = lax.axis_index("row")
    chip, core = me // 2 % CHIPS, me % 2
    chips = [own] + [swapped(own, 2 * place) for place in range(1, CHIPS)]
    ours = jnp.stack(natural(chips, chip))
    theirs = swapped(ours, 1)
    low, high = jnp.where(core == 0, ours, theirs), jnp.where(core == 0, theirs, ours)
    return jnp.stack([low, high], axis=1).reshape(KVH * own.shape[0], own.shape[1])


def scatter_rows(update, rows):
    me = lax.axis_index("row")
    chip, core = me // 2 % CHIPS, me % 2
    split = update.reshape(CHIPS, 2, rows, update.shape[1])
    kept = jnp.where(core == 0, split[:, 0], split[:, 1])
    sent = jnp.where(core == 0, split[:, 1], split[:, 0])
    both = kept + swapped(sent.astype(BF16), 1).astype(F32)
    total = lax.dynamic_index_in_dim(both, chip, 0, keepdims=False)
    for place in range(1, CHIPS):
        piece = lax.dynamic_index_in_dim(both, chip ^ place, 0, keepdims=False)
        total = total + swapped(piece.astype(BF16), 2 * place).astype(F32)
    return total


def attend_rows(queries, query_pos, query_floor, key_values, key_pos):
    row_count = queries.shape[0]
    head_count = queries.shape[1] // HD
    key_part = key_values[:, :HD]
    value_part = key_values[:, HD:]
    grouped = queries.reshape(row_count, head_count, HD)
    scores = jnp.einsum("rhd,kd->rhk", grouped, key_part, preferred_element_type=F32) * HD ** (-0.5)
    capped = CAP * jnp.tanh(scores / CAP)
    visible = (key_pos[None, :] <= query_pos[:, None]) & (key_pos[None, :] >= query_floor[:, None])
    weights = jnp.where(visible[:, None, :], jnp.exp(capped), 0.0)
    totals = jnp.sum(weights, axis=2)
    weighted = jnp.einsum(
        "rhk,kd->rhd", weights.astype(BF16), value_part, preferred_element_type=F32
    )
    return weighted.reshape(row_count, head_count * HD), totals


def on_device(
    hidden, kv_gain, kv_weight, query_states, query_gain, query_weight, output_weight, block_bounds
):
    tile_count = lax.axis_size("row") // KVH
    tile = lax.axis_index("row") // KVH
    depth = hidden.shape[1]
    slice_depth = query_weight.shape[2]
    query_count = query_states.shape[1]
    row_number = jnp.arange(query_count, dtype=jnp.int32)
    query_pos = jnp.repeat(block_bounds[:, 1], QBLK) + row_number % QBLK
    query_floor = jnp.repeat(block_bounds[:, 0], QBLK)

    key_values, key_pos = key_values_of(hidden, kv_gain, kv_weight)
    own_rows = query_states
    for section in range(query_gain.shape[0]):
        stream = gather_rows(own_rows).astype(F32)
        squares = jnp.sum(stream * stream, axis=0)
        gain = lax.dynamic_slice_in_dim(query_gain[section], tile * slice_depth, slice_depth)
        scaled = (stream * gain[:, None]).astype(BF16)
        partial = lax.dot_general(
            scaled, query_weight[section, 0], (((0,), (0,)), ((), ())), preferred_element_type=F32
        )
        square_sum = sum(over_tiles(squares.astype(BF16), tile_count)[1:], squares)
        query_sum = sum(over_tiles(partial.astype(BF16), tile_count)[1:], partial)
        inverse = lax.rsqrt(square_sum / depth + EPSILON)
        queries = (query_sum * inverse[:, None]).astype(BF16)
        weighted, totals = attend_rows(queries, query_pos, query_floor, key_values, key_pos)
        total_sum = sum(over_tiles(totals.astype(BF16), tile_count)[1:], totals)
        weighted_sum = sum(over_tiles(weighted.astype(BF16), tile_count)[1:], weighted)
        attended = (
            (weighted_sum.reshape(query_count, QPK, HD) / total_sum[:, :, None])
            .reshape(query_count, QPK * HD)
            .astype(BF16)
        )
        update = lax.dot_general(
            output_weight[section, 0], attended, (((1,), (1,)), ((), ())), preferred_element_type=F32
        )
        own_rows = (
            own_rows.astype(F32) + scatter_rows(update, own_rows.shape[0])
        ).astype(BF16)
    return own_rows


def solution(mesh):
    in_specs = (
        P(("groups", "row"), None),
        P(),
        P("row", None),
        P("row", "groups"),
        P(),
        P(None, "row", None, None),
        P(None, "row", None, None),
        P("groups", None),
    )
    return jax.shard_map(
        on_device, mesh=mesh, in_specs=in_specs, out_specs=P("row", "groups"), check_vma=False
    )
```

time: 302 us -> 187 us (0.62)
  waiting for transfers between devices: 184 us -> 93.2 us
  local copies, waits for them, and re-layouts: 29.3 us -> 13.2 us
  between operations: 13.9 us -> 0.93 us
  matrix products: 27.1 us -> 16.3 us
  other arithmetic: 5.42 us -> 15.7 us
  starting transfers between devices: 40.6 us -> 47.1 us
    all_gather x1 -> x0, waiting for transfers between devices: 85.9 us -> none  [on_device(): shard_rows = lax.all_gather(kv_weight, 'row', axis=0, tiled=True)]
    all_gather x1 -> x0, local copies, waits for them, and re-layouts: 26.1 us -> none  [on_device(): shard_rows = lax.all_gather(kv_weight, 'row', axis=0, tiled=True)]
    ppermute x24 -> x40, starting transfers between devices: 35.9 us -> 47.1 us  [swapped(): return lax.ppermute(value, axis, pairs)]
    dot_general x7 -> x10, matrix products: 21.8 us -> 12.7 us  [the longest x4 5.31 us: key_values_of(): lax.dot_general(tokens, weight, (((1,), (0,)), ((), ())), preferred_eleme...]
    all_to_all x1 -> x0, starting transfers between devices: 4.68 us -> none  [on_device(): lax.all_to_all(outgoing, 'row', split_axis=0, concat_axis=0, tiled=True)]
    ppermute x24 -> x40, waiting for transfers between devices: 97.8 us -> 93.2 us  [swapped(): return lax.ppermute(value, axis, pairs)]
    concatenate x0 -> x4, other arithmetic: none -> 4.34 us  [the longest x3 3.15 us: features(): jnp.concatenate([lax.dynamic_slice_in_dim(normed, ((tile ^ j) * KVH + (ch...]
  transfers between devices with their start and end apart: 26 -> 40, of which waited for: 22 -> 25; matrix products, arithmetic and copies ran while one was open for 16% -> 18% of each run, Pallas kernels for 0% -> 0%
where the time goes in v1:
time: 187 us; the launch traced here: 186 us
  waiting for transfers between devices  93.2 us (50%)
  starting transfers between devices  47.1 us (25%)
  matrix products  16.3 us (9%)
  other arithmetic  15.7 us (8%)
  local copies, waits for them, and re-layouts  13.2 us (7%)
    ppermute x40, waiting for transfers between devices, swapped(): return lax.ppermute(value, axis, pairs)  93.2 us
    ppermute x40, starting transfers between devices, swapped(): return lax.ppermute(value, axis, pairs)  47.1 us
    dot_general x4, matrix products, key_values_of(): lax.dot_general(tokens, weight, (((1,), (0,)), ((), ())), preferred_eleme...  5.31 us
  transfers between devices with their start and end apart: 40, of which 25 were waited for; matrix products, arithmetic and copies ran while one was open for 18% of the time, Pallas kernels for 0%

profile of v1, /device:TPU:0, one launch (start us, length us, event | category | flops | bytes accessed | tf_op | source)
XLA Modules:
  0.0 186.4 jit_solution(4246237156133454854)
XLA Ops:
  0.0 4.0 %collective-permute-start = (bf16[320,128]{1,0:T(8,128)(2,1)}, bf16[320,128]{1,0:T(8,128)(2,1)}, u32[]{:S(2)}, u32[]{:S(2)}) collective-permute-start(bf16[320,128]{1,0:T(8,128)(2,1)} %param.11), channel_id=1, source_target_pairs={{0,6},{1,7},{2,4},{3,5},{4,2},{5,3},{6,0},{7,1},{8,14},{9,15},{10,... | collective-permute-start | bytes 245768 | tf_op jit(solution)/shard_map/ppermute | solution.py:21
  4.5 1.6 fusion.10
  6.2 1.7 fusion.12
  9.5 1.9 %collective-permute-start.6 = (bf16[128,1280]{1,0:T(8,128)(2,1)}, bf16[128,1280]{1,0:T(8,128)(2,1)S(1)}, u32[]{:S(2)}, u32[]{:S(2)}) collective-permute-start(bf16[128,1280]{1,0:T(8,128)(2,1)} %pad_maximum_fusion.5), channel_id=1, source_target_pairs={{0,2},{1,3},{2,0},{3,1},{4,6},{5,7},{6,4},{7,5},{8,10},{9,11},{10,... | collective-permute-start | bytes 983048 | tf_op jit(solution)/shard_map/ppermute | solution.py:21
  12.2 1.6 collective-permute-start.7
  13.8 1.5 fusion.99
  18.3 1.7 pad_maximum_fusion.7
  21.7 1.2 dynamic-slice_bitcast_fusion.3
  23.2 1.2 select_bitcast_fusion.19
  24.8 7.2 %collective-permute-done.8 = bf16[128,1280]{1,0:T(8,128)(2,1)S(1)} collective-permute-done((bf16[128,1280]{1,0:T(8,128)(2,1)S(1)}, bf16[128,1280]{1,0:T(8,128)(2,1)S(1)}, u32[]{:S(2)}, u32[]{:S(2)}) %collective-permute-start.8) | collective-permute-done | bytes 327712 | tf_op jit(solution)/shard_map/ppermute | solution.py:21
  32.0 1.2 pad_maximum_fusion
  36.0 2.7 %collective-permute-start.5 = (bf16[128]{0:T(256)(128)(2,1)S(1)}, bf16[128]{0:T(256)(128)(2,1)S(1)}, u32[]{:S(2)}, u32[]{:S(2)}) collective-permute-start(bf16[128]{0:T(256)(128)(2,1)S(1)} %convert_element_type.224), channel_id=1, source_target_pairs={{0,8},{1,9},{2,10},{3,11},{4,12},{5,13},{6,14},{7,15},{8,0},{9,1},... | collective-permute-start | bytes 776 | tf_op jit(solution)/shard_map/ppermute | solution.py:21
  39.8 1.2 fusion.83
  41.0 2.6 %collective-permute-start.17 = (bf16[1,320,256]{2,1,0:T(8,128)(2,1)S(1)}, bf16[1,320,256]{2,1,0:T(8,128)(2,1)S(1)}, u32[]{:S(2)}, u32[]{:S(2)}) collective-permute-start(bf16[1,320,256]{2,1,0:T(8,128)(2,1)S(1)} %get-tuple-element.9), channel_id=1, source_target_pairs={{0,8},{1,9},{2,10},{3,11},{4,12},{5,13},{6,14},{7,15},{8,0},{9,1},... | collective-permute-start | bytes 491528 | tf_op jit(solution)/shard_map/ppermute | solution.py:21
  44.0 2.6 %collective-permute-start.11 = (bf16[1,320,256]{2,1,0:T(8,128)(2,1)S(1)}, bf16[1,320,256]{2,1,0:T(8,128)(2,1)S(1)}, u32[]{:S(2)}, u32[]{:S(2)}) collective-permute-start(bf16[1,320,256]{2,1,0:T(8,128)(2,1)S(1)} %get-tuple-element.11), channel_id=1, source_target_pairs={{0,8},{1,9},{2,10},{3,11},{4,12},{5,13},{6,14},{7,15},{8,0},{9,1},... | collective-permute-start | bytes 491528 | tf_op jit(solution)/shard_map/ppermute | solution.py:21
  46.6 14.1 %collective-permute-done.4 = bf16[128,640]{1,0:T(8,128)(2,1)S(1)} collective-permute-done((bf16[128,640]{1,0:T(8,128)(2,1)S(1)}, bf16[128,640]{1,0:T(8,128)(2,1)S(1)}, u32[]{:S(2)}, u32[]{:S(2)}) %collective-permute-start.4) | collective-permute-done | bytes 163872 | tf_op jit(solution)/shard_map/ppermute | solution.py:21
  60.7 7.0 %collective-permute-done.17 = bf16[1,320,256]{2,1,0:T(8,128)(2,1)S(1)} collective-permute-done((bf16[1,320,256]{2,1,0:T(8,128)(2,1)S(1)}, bf16[1,320,256]{2,1,0:T(8,128)(2,1)S(1)}, u32[]{:S(2)}, u32[]{:S(2)}) %collective-permute-start.17) | collective-permute-done | bytes 163872 | tf_op jit(solution)/shard_map/ppermute | solution.py:21
  67.7 1.5 collective-permute-start.18
  69.5 1.7 collective-permute-done.14
  71.2 1.5 collective-permute-start.15
  72.7 2.0 %collective-permute-done.11 = bf16[1,320,256]{2,1,0:T(8,128)(2,1)S(1)} collective-permute-done((bf16[1,320,256]{2,1,0:T(8,128)(2,1)S(1)}, bf16[1,320,256]{2,1,0:T(8,128)(2,1)S(1)}, u32[]{:S(2)}, u32[]{:S(2)}) %collective-permute-start.11) | collective-permute-done | bytes 163872 | tf_op jit(solution)/shard_map/ppermute | solution.py:21
  74.7 1.5 collective-permute-start.12
  76.3 1.9 %collective-permute-done.20 = bf16[1,320,256]{2,1,0:T(8,128)(2,1)S(1)} collective-permute-done((bf16[1,320,256]{2,1,0:T(8,128)(2,1)S(1)}, bf16[1,320,256]{2,1,0:T(8,128)(2,1)S(1)}, u32[]{:S(2)}, u32[]{:S(2)}) %collective-permute-start.20) | collective-permute-done | bytes 163872 | tf_op jit(solution)/shard_map/ppermute | solution.py:21
  78.2 1.5 collective-permute-start.21
  80.9 2.5 %constant_dynamic-update-slice_fusion = bf16[1024,1280]{1,0:T(8,128)(2,1)} fusion(bf16[1024,1280]{1,0:T(8,128)(2,1)} %constant_dynamic-update-slice_fusion.1, bf16[512,1280]{1,0:T(8,128)(2,1)} %collective-permute-done.9), kind=kLoop, calls=%fused_computation.179 | loop fusion | bytes 2621440 | tf_op jit(solution)/shard_map/concatenate | solution.py:86
  83.3 2.7 %convolution_convert_fusion = bf16[1024,256]{1,0:T(8,128)(2,1)S(1)} fusion(bf16[1024,1280]{1,0:T(8,128)(2,1)} %constant_dynamic-update-slice_fusion, bf16[320,256]{1,0:T(8,128)(2,1)S(1)} %get-tuple-element.62, bf16[320,256]{1,0:T(8,128)(2,1)S(1)} %get-tuple-element.61, bf16[320,256]{1,0:T(8,128)(2,1)S(1)} %copy-done.3, bf16[320,256]{1,0:T(8,128)(2,1)S(1)} %copy-done.4), kind=kOutput, calls=%fused_computation.37 | convolution fusion | flops 673972224 | bytes 3801088 | tf_op jit(solution)/shard_map/dot_general | solution.py:104
  88.5 3.0 %collective-permute-start.13 = (bf16[1024,256]{1,0:T(8,128)(2,1)S(1)}, bf16[1024,256]{1,0:T(8,128)(2,1)S(1)}, u32[]{:S(2)}, u32[]{:S(2)}) collective-permute-start(bf16[1024,256]{1,0:T(8,128)(2,1)S(1)} %convolution_convert_fusion.2), channel_id=1, source_target_pairs={{0,6},{1,7},{2,4},{3,5},{4,2},{5,3},{6,0},{7,1},{8,14},{9,15},{10,... | collective-permute-start | bytes 1572872 | tf_op jit(solution)/shard_map/ppermute | solution.py:21
  91.5 19.8 %collective-permute-done.16 = bf16[1024,256]{1,0:T(8,128)(2,1)S(1)} collective-permute-done((bf16[1024,256]{1,0:T(8,128)(2,1)S(1)}, bf16[1024,256]{1,0:T(8,128)(2,1)S(1)}, u32[]{:S(2)}, u32[]{:S(2)}) %collective-permute-start.16) | collective-permute-done | bytes 524320 | tf_op jit(solution)/shard_map/ppermute | solution.py:21
  114.8 3.0 %collective-permute-start.22 = (bf16[128,640]{0,1:T(8,128)(2,1)S(1)}, bf16[128,640]{0,1:T(8,128)(2,1)S(1)}, u32[]{:S(2)}, u32[]{:S(2)}) collective-permute-start(bf16[128,640]{0,1:T(8,128)(2,1)S(1)} %bitcast_convert_fusion.1), channel_id=1, source_target_pairs={{0,8},{1,9},{2,10},{3,11},{4,12},{5,13},{6,14},{7,15},{8,0},{9,1},... | collective-permute-start | bytes 491528 | tf_op jit(solution)/shard_map/ppermute | solution.py:21
  118.6 4.3 %collective-permute-done.22 = bf16[128,640]{0,1:T(8,128)(2,1)S(1)} collective-permute-done((bf16[128,640]{0,1:T(8,128)(2,1)S(1)}, bf16[128,640]{0,1:T(8,128)(2,1)S(1)}, u32[]{:S(2)}, u32[]{:S(2)}) %collective-permute-start.22) | collective-permute-done | bytes 163872 | tf_op jit(solution)/shard_map/ppermute | solution.py:21
  123.0 1.2 convolution_bitcast_fusion.1
  124.9 1.4 collective-permute-done.24
  127.8 2.2 %collective-permute-start.27 = (bf16[320,128]{1,0:T(8,128)(2,1)S(1)}, bf16[320,128]{1,0:T(8,128)(2,1)S(1)}, u32[]{:S(2)}, u32[]{:S(2)}) collective-permute-start(bf16[320,128]{1,0:T(8,128)(2,1)S(1)} %get-tuple-element.39), channel_id=1, source_target_pairs={{0,6},{1,7},{2,4},{3,5},{4,2},{5,3},{6,0},{7,1},{8,14},{9,15},{10,... | collective-permute-start | bytes 245768 | tf_op jit(solution)/shard_map/ppermute | solution.py:21
  131.0 1.9 %collective-permute-done.26 = bf16[320,128]{1,0:T(8,128)(2,1)S(1)} collective-permute-done((bf16[320,128]{1,0:T(8,128)(2,1)S(1)}, bf16[320,128]{1,0:T(8,128)(2,1)S(1)}, u32[]{:S(2)}, u32[]{:S(2)}) %collective-permute-start.26) | collective-permute-done | bytes 81952 | tf_op jit(solution)/shard_map/ppermute | solution.py:21
  134.0 1.5 collective-permute-start.28
  135.5 1.3 collective-permute-start.29
  137.6 2.1 %collective-permute-done.28 = bf16[320,128]{1,0:T(8,128)(2,1)S(1)} collective-permute-done((bf16[320,128]{1,0:T(8,128)(2,1)S(1)}, bf16[320,128]{1,0:T(8,128)(2,1)S(1)}, u32[]{:S(2)}, u32[]{:S(2)}) %collective-permute-start.28) | collective-permute-done | bytes 81952 | tf_op jit(solution)/shard_map/ppermute | solution.py:21
  141.6 1.5 collective-permute-done.31
  143.6 3.1 %collective-permute-start.33 = (bf16[128]{0:T(256)(128)(2,1)S(1)}, bf16[128]{0:T(256)(128)(2,1)S(1)}, u32[]{:S(2)}, u32[]{:S(2)}) collective-permute-start(bf16[128]{0:T(256)(128)(2,1)S(1)} %convert_element_type.258), channel_id=1, source_target_pairs={{0,8},{1,9},{2,10},{3,11},{4,12},{5,13},{6,14},{7,15},{8,0},{9,1},... | collective-permute-start | bytes 776 | tf_op jit(solution)/shard_map/ppermute | solution.py:21
  146.7 2.8 %fusion.101 = (bf16[128,640]{1,0:T(8,128)(2,1)S(1)}, f32[128,640]{1,0:T(8,128)S(1)}) fusion(bf16[2560,128]{1,0:T(8,128)(2,1)S(1)} %bitcast.277, bf16[2,1,2560,640]{3,2,1,0:T(8,128)(2,1)} %param.13), kind=kOutput, calls=%fused_computation.219 | convolution fusion | flops 419512320 | bytes 4423680 | tf_op jit(solution)/shard_map/dot_general | solution.py:180
  149.6 10.3 %collective-permute-done.32 = bf16[128,640]{1,0:T(8,128)(2,1)S(1)} collective-permute-done((bf16[128,640]{1,0:T(8,128)(2,1)S(1)}, bf16[128,640]{1,0:T(8,128)(2,1)S(1)}, u32[]{:S(2)}, u32[]{:S(2)}) %collective-permute-start.32) | collective-permute-done | bytes 163872 | tf_op jit(solution)/shard_map/ppermute | solution.py:21
  162.3 3.0 %collective-permute-start.34 = (bf16[128,640]{0,1:T(8,128)(2,1)S(1)}, bf16[128,640]{0,1:T(8,128)(2,1)S(1)}, u32[]{:S(2)}, u32[]{:S(2)}) collective-permute-start(bf16[128,640]{0,1:T(8,128)(2,1)S(1)} %bitcast_convert_fusion), channel_id=1, source_target_pairs={{0,8},{1,9},{2,10},{3,11},{4,12},{5,13},{6,14},{7,15},{8,0},{9,1},... | collective-permute-start | bytes 491528 | tf_op jit(solution)/shard_map/ppermute | solution.py:21
  166.3 6.0 %collective-permute-done.34 = bf16[128,640]{0,1:T(8,128)(2,1)S(1)} collective-permute-done((bf16[128,640]{0,1:T(8,128)(2,1)S(1)}, bf16[128,640]{0,1:T(8,128)(2,1)S(1)}, u32[]{:S(2)}, u32[]{:S(2)}) %collective-permute-start.34) | collective-permute-done | bytes 163872 | tf_op jit(solution)/shard_map/ppermute | solution.py:21
  172.4 2.3 %convolution_bitcast_fusion = f32[2560,128]{0,1:T(8,128)} fusion(bf16[128,640]{0,1:T(8,128)(2,1)S(1)} %fusion.59, bf16[2,1,2560,640]{3,2,1,0:T(8,128)(2,1)S(1)} %bitcast.275), kind=kOutput, calls=%fused_computation | convolution fusion | flops 419430400 | bytes 4751360 | tf_op jit(solution)/shard_map/dot_general | solution.py:195
  174.6 1.7 copy.29
  176.6 1.6 collective-permute-done.36
  178.5 3.3 %collective-permute-start.39 = (bf16[320,128]{1,0:T(8,128)(2,1)S(1)}, bf16[320,128]{1,0:T(8,128)(2,1)S(1)}, u32[]{:S(2)}, u32[]{:S(2)}) collective-permute-start(bf16[320,128]{1,0:T(8,128)(2,1)S(1)} %get-tuple-element.32), channel_id=1, source_target_pairs={{0,6},{1,7},{2,4},{3,5},{4,2},{5,3},{6,0},{7,1},{8,14},{9,15},{10,... | collective-permute-start | bytes 245768 | tf_op jit(solution)/shard_map/ppermute | solution.py:21
  183.6 2.1 %collective-permute-done.39 = bf16[320,128]{1,0:T(8,128)(2,1)S(1)} collective-permute-done((bf16[320,128]{1,0:T(8,128)(2,1)S(1)}, bf16[320,128]{1,0:T(8,128)(2,1)S(1)}, u32[]{:S(2)}, u32[]{:S(2)}) %collective-permute-start.39) | collective-permute-done | bytes 81952 | tf_op jit(solution)/shard_map/ppermute | solution.py:21
  (156 shorter events, 34.5 us)
Async XLA Ops:
  0.0 23.0 %collective-permute-start = (bf16[320,128]{1,0:T(8,128)(2,1)}, bf16[320,128]{1,0:T(8,128)(2,1)}, u32[]{:S(2)}, u32[]{:S(2)}) collective-permute-start(bf16[320,128]{1,0:T(8,128)(2,1)} %param.11), channel_id=1, source_target_pairs={{0,6},{1,7},{2,4},{3,5},{4,2},{5,3},{6,0},{7,1},{8,14},{9,15},{10,... | collective-permute-start | bytes 245768 | tf_op jit(solution)/shard_map/ppermute | solution.py:21
  4.0 19.1 %collective-permute-start.1 = (bf16[320,128]{1,0:T(8,128)(2,1)}, bf16[320,128]{1,0:T(8,128)(2,1)}, u32[]{:S(2)}, u32[]{:S(2)}) collective-permute-start(bf16[320,128]{1,0:T(8,128)(2,1)} %param.11), channel_id=1, source_target_pairs={{0,4},{1,5},{2,6},{3,7},{4,0},{5,1},{6,2},{7,3},{8,12},{9,13},{10,... | collective-permute-start | bytes 245768 | tf_op jit(solution)/shard_map/ppermute | solution.py:21
  4.4 18.8 %collective-permute-start.2 = (bf16[320,128]{1,0:T(8,128)(2,1)}, bf16[320,128]{1,0:T(8,128)(2,1)}, u32[]{:S(2)}, u32[]{:S(2)}) collective-permute-start(bf16[320,128]{1,0:T(8,128)(2,1)} %param.11), channel_id=1, source_target_pairs={{0,2},{1,3},{2,0},{3,1},{4,6},{5,7},{6,4},{7,5},{8,10},{9,11},{10,... | collective-permute-start | bytes 245768 | tf_op jit(solution)/shard_map/ppermute | solution.py:21
  8.0 30.7 %slice-start = ((s8[6553600]{0:T(1024)(128)(4,1)}), s8[2359296]{0:T(1024)(128)(4,1)S(1)}, s32[]{:S(2)}) async-start(s8[6553600]{0:T(1024)(128)(4,1)} %bitcast.270), calls=%async_computation | async-start | bytes 4718592
  9.5 15.3 %collective-permute-start.6 = (bf16[128,1280]{1,0:T(8,128)(2,1)}, bf16[128,1280]{1,0:T(8,128)(2,1)S(1)}, u32[]{:S(2)}, u32[]{:S(2)}) collective-permute-start(bf16[128,1280]{1,0:T(8,128)(2,1)} %pad_maximum_fusion.5), channel_id=1, source_target_pairs={{0,2},{1,3},{2,0},{3,1},{4,6},{5,7},{6,4},{7,5},{8,10},{9,11},{10,... | collective-permute-start | bytes 983048 | tf_op jit(solution)/shard_map/ppermute | solution.py:21
  12.2 12.6 %collective-permute-start.7 = (bf16[128,1280]{1,0:T(8,128)(2,1)}, bf16[128,1280]{1,0:T(8,128)(2,1)S(1)}, u32[]{:S(2)}, u32[]{:S(2)}) collective-permute-start(bf16[128,1280]{1,0:T(8,128)(2,1)} %pad_maximum_fusion.6), channel_id=1, source_target_pairs={{0,4},{1,5},{2,6},{3,7},{4,0},{5,1},{6,2},{7,3},{8,12},{9,13},{10,... | collective-permute-start | bytes 983048 | tf_op jit(solution)/shard_map/ppermute | solution.py:21
  23.0 15.7 %slice-start.1 = ((s8[6553600]{0:T(1024)(128)(4,1)}), s8[4194304]{0:T(1024)(128)(4,1)S(1)}, s32[]{:S(2)}) async-start(s8[6553600]{0:T(1024)(128)(4,1)} %bitcast.270), calls=%async_computation.1 | async-start | bytes 8388608
  23.0 9.0 %collective-permute-start.8 = (bf16[128,1280]{1,0:T(8,128)(2,1)S(1)}, bf16[128,1280]{1,0:T(8,128)(2,1)S(1)}, u32[]{:S(2)}, u32[]{:S(2)}) collective-permute-start(bf16[128,1280]{1,0:T(8,128)(2,1)S(1)} %copy-done.1), channel_id=1, source_target_pairs={{0,6},{1,7},{2,4},{3,5},{4,2},{5,3},{6,0},{7,1},{8,14},{9,15},{10,... | collective-permute-start | bytes 983048 | tf_op jit(solution)/shard_map/ppermute | solution.py:21
  23.1 16.7 %collective-permute-start.10 = (bf16[4,320,256]{2,1,0:T(8,128)(2,1)S(1)}, bf16[4,320,256]{2,1,0:T(8,128)(2,1)S(1)}, u32[]{:S(2)}, u32[]{:S(2)}) collective-permute-start(bf16[4,320,256]{2,1,0:T(8,128)(2,1)S(1)} %pad_maximum_fusion.2), channel_id=1, source_target_pairs={{0,1},{1,0},{2,3},{3,2},{4,5},{5,4},{6,7},{7,6},{8,9},{9,8},{10,11... | collective-permute-start | bytes 1966088 | tf_op jit(solution)/shard_map/ppermute | solution.py:21
  24.4 11.1 %collective-permute-start.3 = (bf16[4,320,128]{2,1,0:T(8,128)(2,1)S(1)}, bf16[4,320,128]{2,1,0:T(8,128)(2,1)S(1)}, u32[]{:S(2)}, u32[]{:S(2)}) collective-permute-start(bf16[4,320,128]{2,1,0:T(8,128)(2,1)S(1)} %pad_maximum_fusion.4), channel_id=1, source_target_pairs={{0,1},{1,0},{2,3},{3,2},{4,5},{5,4},{6,7},{7,6},{8,9},{9,8},{10,11... | collective-permute-start | bytes 983048 | tf_op jit(solution)/shard_map/ppermute | solution.py:21
  33.2 47.6 %collective-permute-start.9 = (bf16[512,1280]{1,0:T(8,128)(2,1)}, bf16[512,1280]{1,0:T(8,128)(2,1)}, u32[]{:S(2)}, u32[]{:S(2)}) collective-permute-start(bf16[512,1280]{1,0:T(8,128)(2,1)} %pad_maximum_fusion), channel_id=1, source_target_pairs={{0,1},{1,0},{2,3},{3,2},{4,5},{5,4},{6,7},{7,6},{8,9},{9,8},{10,11... | collective-permute-start | bytes 3932168 | tf_op jit(solution)/shard_map/ppermute | solution.py:21
  36.0 7.6 %collective-permute-start.5 = (bf16[128]{0:T(256)(128)(2,1)S(1)}, bf16[128]{0:T(256)(128)(2,1)S(1)}, u32[]{:S(2)}, u32[]{:S(2)}) collective-permute-start(bf16[128]{0:T(256)(128)(2,1)S(1)} %convert_element_type.224), channel_id=1, source_target_pairs={{0,8},{1,9},{2,10},{3,11},{4,12},{5,13},{6,14},{7,15},{8,0},{9,1},... | collective-permute-start | bytes 776 | tf_op jit(solution)/shard_map/ppermute | solution.py:21
  39.4 21.3 %collective-permute-start.4 = (bf16[128,640]{1,0:T(8,128)(2,1)S(1)}, bf16[128,640]{1,0:T(8,128)(2,1)S(1)}, u32[]{:S(2)}, u32[]{:S(2)}) collective-permute-start(bf16[128,640]{1,0:T(8,128)(2,1)S(1)} %get-tuple-element.73), channel_id=1, source_target_pairs={{0,8},{1,9},{2,10},{3,11},{4,12},{5,13},{6,14},{7,15},{8,0},{9,1},... | collective-permute-start | bytes 491528 | tf_op jit(solution)/shard_map/ppermute | solution.py:21
  41.0 26.7 %collective-permute-start.17 = (bf16[1,320,256]{2,1,0:T(8,128)(2,1)S(1)}, bf16[1,320,256]{2,1,0:T(8,128)(2,1)S(1)}, u32[]{:S(2)}, u32[]{:S(2)}) collective-permute-start(bf16[1,320,256]{2,1,0:T(8,128)(2,1)S(1)} %get-tuple-element.9), channel_id=1, source_target_pairs={{0,8},{1,9},{2,10},{3,11},{4,12},{5,13},{6,14},{7,15},{8,0},{9,1},... | collective-permute-start | bytes 491528 | tf_op jit(solution)/shard_map/ppermute | solution.py:21
  43.6 27.7 %collective-permute-start.14 = (bf16[1,320,256]{2,1,0:T(8,128)(2,1)S(1)}, bf16[1,320,256]{2,1,0:T(8,128)(2,1)S(1)}, u32[]{:S(2)}, u32[]{:S(2)}) collective-permute-start(bf16[1,320,256]{2,1,0:T(8,128)(2,1)S(1)} %get-tuple-element.10), channel_id=1, source_target_pairs={{0,8},{1,9},{2,10},{3,11},{4,12},{5,13},{6,14},{7,15},{8,0},{9,1},... | collective-permute-start | bytes 491528 | tf_op jit(solution)/shard_map/ppermute | solution.py:21
  44.0 30.8 %collective-permute-start.11 = (bf16[1,320,256]{2,1,0:T(8,128)(2,1)S(1)}, bf16[1,320,256]{2,1,0:T(8,128)(2,1)S(1)}, u32[]{:S(2)}, u32[]{:S(2)}) collective-permute-start(bf16[1,320,256]{2,1,0:T(8,128)(2,1)S(1)} %get-tuple-element.11), channel_id=1, source_target_pairs={{0,8},{1,9},{2,10},{3,11},{4,12},{5,13},{6,14},{7,15},{8,0},{9,1},... | collective-permute-start | bytes 491528 | tf_op jit(solution)/shard_map/ppermute | solution.py:21
  60.7 17.5 %collective-permute-start.20 = (bf16[1,320,256]{2,1,0:T(8,128)(2,1)S(1)}, bf16[1,320,256]{2,1,0:T(8,128)(2,1)S(1)}, u32[]{:S(2)}, u32[]{:S(2)}) collective-permute-start(bf16[1,320,256]{2,1,0:T(8,128)(2,1)S(1)} %get-tuple-element.8), channel_id=1, source_target_pairs={{0,8},{1,9},{2,10},{3,11},{4,12},{5,13},{6,14},{7,15},{8,0},{9,1},... | collective-permute-start | bytes 491528 | tf_op jit(solution)/shard_map/ppermute | solution.py:21
  67.7 12.0 %collective-permute-start.18 = (bf16[1,320,256]{2,1,0:T(8,128)(2,1)S(1)}, bf16[1,320,256]{2,1,0:T(8,128)(2,1)S(1)}, u32[]{:S(2)}, u32[]{:S(2)}) collective-permute-start(bf16[1,320,256]{2,1,0:T(8,128)(2,1)S(1)} %collective-permute-done.17), channel_id=1, source_target_pairs={{0,16},{16,0},{1,17},{17,1},{2,18},{18,2},{3,19},{19,3},{4,20},{20... | collective-permute-start | bytes 491528 | tf_op jit(solution)/shard_map/ppermute | solution.py:21
  69.3 14.0 %copy-start.3 = (bf16[320,256]{1,0:T(8,128)(2,1)S(1)}, bf16[320,256]{1,0:T(8,128)(2,1)}, u32[]{:S(2)}) copy-start(bf16[320,256]{1,0:T(8,128)(2,1)} %get-tuple-element.14) | copy-start | bytes 491524
  69.5 13.8 %copy-start.4 = (bf16[320,256]{1,0:T(8,128)(2,1)S(1)}, bf16[320,256]{1,0:T(8,128)(2,1)}, u32[]{:S(2)}) copy-start(bf16[320,256]{1,0:T(8,128)(2,1)} %get-tuple-element.16) | copy-start | bytes 491524
  71.2 8.5 %collective-permute-start.15 = (bf16[1,320,256]{2,1,0:T(8,128)(2,1)S(1)}, bf16[1,320,256]{2,1,0:T(8,128)(2,1)S(1)}, u32[]{:S(2)}, u32[]{:S(2)}) collective-permute-start(bf16[1,320,256]{2,1,0:T(8,128)(2,1)S(1)} %collective-permute-done.14), channel_id=1, source_target_pairs={{0,16},{16,0},{1,17},{17,1},{2,18},{18,2},{3,19},{19,3},{4,20},{20... | collective-permute-start | bytes 491528 | tf_op jit(solution)/shard_map/ppermute | solution.py:21
  74.7 6.1 %collective-permute-start.12 = (bf16[1,320,256]{2,1,0:T(8,128)(2,1)S(1)}, bf16[1,320,256]{2,1,0:T(8,128)(2,1)S(1)}, u32[]{:S(2)}, u32[]{:S(2)}) collective-permute-start(bf16[1,320,256]{2,1,0:T(8,128)(2,1)S(1)} %collective-permute-done.11), channel_id=1, source_target_pairs={{0,16},{16,0},{1,17},{17,1},{2,18},{18,2},{3,19},{19,3},{4,20},{20... | collective-permute-start | bytes 491528 | tf_op jit(solution)/shard_map/ppermute | solution.py:21
  78.2 13.3 %collective-permute-start.21 = (bf16[1,320,256]{2,1,0:T(8,128)(2,1)S(1)}, bf16[1,320,256]{2,1,0:T(8,128)(2,1)S(1)}, u32[]{:S(2)}, u32[]{:S(2)}) collective-permute-start(bf16[1,320,256]{2,1,0:T(8,128)(2,1)S(1)} %collective-permute-done.20), channel_id=1, source_target_pairs={{0,16},{16,0},{1,17},{17,1},{2,18},{18,2},{3,19},{19,3},{4,20},{20... | collective-permute-start | bytes 491528 | tf_op jit(solution)/shard_map/ppermute | solution.py:21
  86.1 25.3 %collective-permute-start.19 = (bf16[1024,256]{1,0:T(8,128)(2,1)S(1)}, bf16[1024,256]{1,0:T(8,128)(2,1)S(1)}, u32[]{:S(2)}, u32[]{:S(2)}) collective-permute-start(bf16[1024,256]{1,0:T(8,128)(2,1)S(1)} %convolution_convert_fusion), channel_id=1, source_target_pairs={{0,4},{1,5},{2,6},{3,7},{4,0},{5,1},{6,2},{7,3},{8,12},{9,13},{10,... | collective-permute-start | bytes 1572872 | tf_op jit(solution)/shard_map/ppermute | solution.py:21
  87.0 24.3 %collective-permute-start.16 = (bf16[1024,256]{1,0:T(8,128)(2,1)S(1)}, bf16[1024,256]{1,0:T(8,128)(2,1)S(1)}, u32[]{:S(2)}, u32[]{:S(2)}) collective-permute-start(bf16[1024,256]{1,0:T(8,128)(2,1)S(1)} %convolution_convert_fusion.1), channel_id=1, source_target_pairs={{0,2},{1,3},{2,0},{3,1},{4,6},{5,7},{6,4},{7,5},{8,10},{9,11},{10,... | collective-permute-start | bytes 1572872 | tf_op jit(solution)/shard_map/ppermute | solution.py:21
  88.5 23.0 %collective-permute-start.13 = (bf16[1024,256]{1,0:T(8,128)(2,1)S(1)}, bf16[1024,256]{1,0:T(8,128)(2,1)S(1)}, u32[]{:S(2)}, u32[]{:S(2)}) collective-permute-start(bf16[1024,256]{1,0:T(8,128)(2,1)S(1)} %convolution_convert_fusion.2), channel_id=1, source_target_pairs={{0,6},{1,7},{2,4},{3,5},{4,2},{5,3},{6,0},{7,1},{8,14},{9,15},{10,... | collective-permute-start | bytes 1572872 | tf_op jit(solution)/shard_map/ppermute | solution.py:21
  113.9 4.8 %collective-permute-start.23 = (bf16[128,5]{0,1:T(8,128)(2,1)S(1)}, bf16[128,5]{0,1:T(8,128)(2,1)S(1)}, u32[]{:S(2)}, u32[]{:S(2)}) collective-permute-start(bf16[128,5]{0,1:T(8,128)(2,1)S(1)} %convert_element_type.236), channel_id=1, source_target_pairs={{0,8},{1,9},{2,10},{3,11},{4,12},{5,13},{6,14},{7,15},{8,0},{9,1},... | collective-permute-start | bytes 3848 | tf_op jit(solution)/shard_map/ppermute | solution.py:21
  114.8 8.1 %collective-permute-start.22 = (bf16[128,640]{0,1:T(8,128)(2,1)S(1)}, bf16[128,640]{0,1:T(8,128)(2,1)S(1)}, u32[]{:S(2)}, u32[]{:S(2)}) collective-permute-start(bf16[128,640]{0,1:T(8,128)(2,1)S(1)} %bitcast_convert_fusion.1), channel_id=1, source_target_pairs={{0,8},{1,9},{2,10},{3,11},{4,12},{5,13},{6,14},{7,15},{8,0},{9,1},... | collective-permute-start | bytes 491528 | tf_op jit(solution)/shard_map/ppermute | solution.py:21
  124.6 16.9 %copy-start.6 = (f32[1,5120]{1,0:T(1,128)S(1)}, f32[1,5120]{1,0:T(1,128)}, u32[]{:S(2)}) copy-start(f32[1,5120]{1,0:T(1,128)} %get-tuple-element.72) | copy-start | bytes 61444
  124.6 1.7 collective-permute-start.24
  126.5 4.6 %collective-permute-start.25 = (bf16[320,128]{1,0:T(8,128)(2,1)S(1)}, bf16[320,128]{1,0:T(8,128)(2,1)S(1)}, u32[]{:S(2)}, u32[]{:S(2)}) collective-permute-start(bf16[320,128]{1,0:T(8,128)(2,1)S(1)} %get-tuple-element.38), channel_id=1, source_target_pairs={{0,2},{1,3},{2,0},{3,1},{4,6},{5,7},{6,4},{7,5},{8,10},{9,11},{10,... | collective-permute-start | bytes 245768 | tf_op jit(solution)/shard_map/ppermute | solution.py:21
  127.6 5.3 %collective-permute-start.26 = (bf16[320,128]{1,0:T(8,128)(2,1)S(1)}, bf16[320,128]{1,0:T(8,128)(2,1)S(1)}, u32[]{:S(2)}, u32[]{:S(2)}) collective-permute-start(bf16[320,128]{1,0:T(8,128)(2,1)S(1)} %get-tuple-element.40), channel_id=1, source_target_pairs={{0,4},{1,5},{2,6},{3,7},{4,0},{5,1},{6,2},{7,3},{8,12},{9,13},{10,... | collective-permute-start | bytes 245768 | tf_op jit(solution)/shard_map/ppermute | solution.py:21
  127.8 6.1 %collective-permute-start.27 = (bf16[320,128]{1,0:T(8,128)(2,1)S(1)}, bf16[320,128]{1,0:T(8,128)(2,1)S(1)}, u32[]{:S(2)}, u32[]{:S(2)}) collective-permute-start(bf16[320,128]{1,0:T(8,128)(2,1)S(1)} %get-tuple-element.39), channel_id=1, source_target_pairs={{0,6},{1,7},{2,4},{3,5},{4,2},{5,3},{6,0},{7,1},{8,14},{9,15},{10,... | collective-permute-start | bytes 245768 | tf_op jit(solution)/shard_map/ppermute | solution.py:21
  134.0 5.6 %collective-permute-start.28 = (bf16[320,128]{1,0:T(8,128)(2,1)S(1)}, bf16[320,128]{1,0:T(8,128)(2,1)S(1)}, u32[]{:S(2)}, u32[]{:S(2)}) collective-permute-start(bf16[320,128]{1,0:T(8,128)(2,1)S(1)} %fusion.70), channel_id=1, source_target_pairs={{0,6},{1,7},{2,4},{3,5},{4,2},{5,3},{6,0},{7,1},{8,14},{9,15},{10,... | collective-permute-start | bytes 245768 | tf_op jit(solution)/shard_map/ppermute | solution.py:21
  135.5 4.6 %collective-permute-start.29 = (bf16[320,128]{1,0:T(8,128)(2,1)S(1)}, bf16[320,128]{1,0:T(8,128)(2,1)S(1)}, u32[]{:S(2)}, u32[]{:S(2)}) collective-permute-start(bf16[320,128]{1,0:T(8,128)(2,1)S(1)} %fusion.70), channel_id=1, source_target_pairs={{0,4},{1,5},{2,6},{3,7},{4,0},{5,1},{6,2},{7,3},{8,12},{9,13},{10,... | collective-permute-start | bytes 245768 | tf_op jit(solution)/shard_map/ppermute | solution.py:21
  136.8 4.4 %collective-permute-start.30 = (bf16[320,128]{1,0:T(8,128)(2,1)S(1)}, bf16[320,128]{1,0:T(8,128)(2,1)S(1)}, u32[]{:S(2)}, u32[]{:S(2)}) collective-permute-start(bf16[320,128]{1,0:T(8,128)(2,1)S(1)} %fusion.70), channel_id=1, source_target_pairs={{0,2},{1,3},{2,0},{3,1},{4,6},{5,7},{6,4},{7,5},{8,10},{9,11},{10,... | collective-permute-start | bytes 245768 | tf_op jit(solution)/shard_map/ppermute | solution.py:21
  141.4 1.7 collective-permute-start.31
  143.6 6.1 %collective-permute-start.33 = (bf16[128]{0:T(256)(128)(2,1)S(1)}, bf16[128]{0:T(256)(128)(2,1)S(1)}, u32[]{:S(2)}, u32[]{:S(2)}) collective-permute-start(bf16[128]{0:T(256)(128)(2,1)S(1)} %convert_element_type.258), channel_id=1, source_target_pairs={{0,8},{1,9},{2,10},{3,11},{4,12},{5,13},{6,14},{7,15},{8,0},{9,1},... | collective-permute-start | bytes 776 | tf_op jit(solution)/shard_map/ppermute | solution.py:21
  146.7 13.5 %copy-start.10 = (bf16[1024,256]{1,0:T(8,128)(2,1)S(1)}, bf16[1024,256]{1,0:T(8,128)(2,1)}, u32[]{:S(2)}) copy-start(bf16[1024,256]{1,0:T(8,128)(2,1)} %copy-done.9) | copy-start | bytes 1572868
  146.7 25.6 %slice-start.4 = ((s8[6553600]{0:T(1024)(128)(4,1)}), s8[2359296]{0:T(1024)(128)(4,1)S(1)}, s32[]{:S(2)}) async-start(s8[6553600]{0:T(1024)(128)(4,1)} %bitcast.274), calls=%async_computation.4 | async-start | bytes 4718592
  149.5 10.4 %collective-permute-start.32 = (bf16[128,640]{1,0:T(8,128)(2,1)S(1)}, bf16[128,640]{1,0:T(8,128)(2,1)S(1)}, u32[]{:S(2)}, u32[]{:S(2)}) collective-permute-start(bf16[128,640]{1,0:T(8,128)(2,1)S(1)} %get-tuple-element.77), channel_id=1, source_target_pairs={{0,8},{1,9},{2,10},{3,11},{4,12},{5,13},{6,14},{7,15},{8,0},{9,1},... | collective-permute-start | bytes 491528 | tf_op jit(solution)/shard_map/ppermute | solution.py:21
  160.2 12.1 %slice-start.5 = ((s8[6553600]{0:T(1024)(128)(4,1)}), s8[4194304]{0:T(1024)(128)(4,1)S(1)}, s32[]{:S(2)}) async-start(s8[6553600]{0:T(1024)(128)(4,1)} %bitcast.274), calls=%async_computation.5 | async-start | bytes 8388608
  161.4 4.9 %collective-permute-start.35 = (bf16[128,5]{0,1:T(8,128)(2,1)S(1)}, bf16[128,5]{0,1:T(8,128)(2,1)S(1)}, u32[]{:S(2)}, u32[]{:S(2)}) collective-permute-start(bf16[128,5]{0,1:T(8,128)(2,1)S(1)} %convert_element_type.264), channel_id=1, source_target_pairs={{0,8},{1,9},{2,10},{3,11},{4,12},{5,13},{6,14},{7,15},{8,0},{9,1},... | collective-permute-start | bytes 3848 | tf_op jit(solution)/shard_map/ppermute | solution.py:21
  162.3 9.9 %collective-permute-start.34 = (bf16[128,640]{0,1:T(8,128)(2,1)S(1)}, bf16[128,640]{0,1:T(8,128)(2,1)S(1)}, u32[]{:S(2)}, u32[]{:S(2)}) collective-permute-start(bf16[128,640]{0,1:T(8,128)(2,1)S(1)} %bitcast_convert_fusion), channel_id=1, source_target_pairs={{0,8},{1,9},{2,10},{3,11},{4,12},{5,13},{6,14},{7,15},{8,0},{9,1},... | collective-permute-start | bytes 491528 | tf_op jit(solution)/shard_map/ppermute | solution.py:21
  176.4 1.7 collective-permute-start.36
  178.3 4.6 %collective-permute-start.37 = (bf16[320,128]{1,0:T(8,128)(2,1)S(1)}, bf16[320,128]{1,0:T(8,128)(2,1)S(1)}, u32[]{:S(2)}, u32[]{:S(2)}) collective-permute-start(bf16[320,128]{1,0:T(8,128)(2,1)S(1)} %get-tuple-element.31), channel_id=1, source_target_pairs={{0,2},{1,3},{2,0},{3,1},{4,6},{5,7},{6,4},{7,5},{8,10},{9,11},{10,... | collective-permute-start | bytes 245768 | tf_op jit(solution)/shard_map/ppermute | solution.py:21
  178.5 5.1 %collective-permute-start.38 = (bf16[320,128]{1,0:T(8,128)(2,1)S(1)}, bf16[320,128]{1,0:T(8,128)(2,1)S(1)}, u32[]{:S(2)}, u32[]{:S(2)}) collective-permute-start(bf16[320,128]{1,0:T(8,128)(2,1)S(1)} %get-tuple-element.33), channel_id=1, source_target_pairs={{0,4},{1,5},{2,6},{3,7},{4,0},{5,1},{6,2},{7,3},{8,12},{9,13},{10,... | collective-permute-start | bytes 245768 | tf_op jit(solution)/shard_map/ppermute | solution.py:21
  178.5 7.3 %collective-permute-start.39 = (bf16[320,128]{1,0:T(8,128)(2,1)S(1)}, bf16[320,128]{1,0:T(8,128)(2,1)S(1)}, u32[]{:S(2)}, u32[]{:S(2)}) collective-permute-start(bf16[320,128]{1,0:T(8,128)(2,1)S(1)} %get-tuple-element.32), channel_id=1, source_target_pairs={{0,6},{1,7},{2,4},{3,5},{4,2},{5,3},{6,0},{7,1},{8,14},{9,15},{10,... | collective-permute-start | bytes 245768 | tf_op jit(solution)/shard_map/ppermute | solution.py:21
  (9 other events, 55.9 us)

commit v2 on v1

--- a/solution.py
+++ b/solution.py
@@ -1,6 +1,10 @@
+import functools
+
 import jax
 import jax.numpy as jnp
 from jax import lax
+from jax.experimental import pallas as pl
+from jax.experimental.pallas import tpu as pltpu
 from jax.sharding import PartitionSpec as P
 
 KVH = 8
@@ -44,63 +48,149 @@
     return pieces
 
 
+def arrange_kernel(pair, heads_ref, weight_ref, *refs):
+    out_refs, sems = refs[:-1], refs[-1]
+    copies = []
+    for out_ref in out_refs:
+        for place in range(out_ref.shape[0]):
+            column = pl.multiple_of(heads_ref[len(copies)] * pair, pair)
+            copies.append(
+                pltpu.make_async_copy(
+                    weight_ref.at[:, pl.ds(column, pair)], out_ref.at[place], sems.at[len(copies)]
+                )
+            )
+    for copy in copies:
+        copy.start()
+    for copy in copies:
+        copy.wait()
+
+
+def arranged(weight, groups, pair):
+    unit = weight.shape[0]
+    heads = [head for group in groups for head in group]
+    if unit % 16:
+        columns = [lax.dynamic_slice_in_dim(weight, head * pair, pair, 1) for head in heads]
+        results = []
+        for group in groups:
+            results.append(jnp.stack(columns[: len(group)]))
+            columns = columns[len(group) :]
+        return results
+    return pl.pallas_call(
+        functools.partial(arrange_kernel, pair),
+        out_shape=[jax.ShapeDtypeStruct((len(group), unit, pair), weight.dtype) for group in groups],
+        in_specs=[
+            pl.BlockSpec(memory_space=pltpu.SMEM),
+            pl.BlockSpec(memory_space=pl.ANY),
+        ],
+        out_specs=[pl.BlockSpec(memory_space=pl.ANY)] * len(groups),
+        scratch_shapes=[pltpu.SemaphoreType.DMA((len(heads),))],
+        name="arrange_weight",
+    )(jnp.stack(heads).astype(jnp.int32), weight)
+
+
+def norm_kernel(width, starts_ref, hidden_ref, gain_ref, *refs):
+    out_refs, normed = refs[:-1], refs[-1]
+    hidden = hidden_ref[...].astype(F32)
+    inverse = lax.rsqrt(jnp.mean(hidden * hidden, axis=1, keepdims=True) + EPSILON)
+    normed[...] = (hidden * inverse * gain_ref[...]).astype(BF16)
+    number = 0
+    for out_ref in out_refs:
+        for place in range(out_ref.shape[1] // width):
+            start = pl.multiple_of(starts_ref[number] * width, 128)
+            out_ref[:, place * width : (place + 1) * width] = normed[:, pl.ds(start, width)]
+            number += 1
+
+
+def normed_features(hidden, gain, groups, width):
+    rows, depth = hidden.shape
+    if width % 128 or rows % 16:
+        hidden_float = hidden.astype(F32)
+        inverse = lax.rsqrt(jnp.mean(hidden_float * hidden_float, axis=1, keepdims=True) + EPSILON)
+        normed = (hidden_float * inverse * gain[None, :]).astype(BF16)
+        return [
+            jnp.concatenate(
+                [lax.dynamic_slice_in_dim(normed, block * width, width, 1) for block in group], axis=1
+            )
+            for group in groups
+        ]
+    blocks = [block for group in groups for block in group]
+    vmem = pl.BlockSpec(memory_space=pltpu.VMEM)
+    return pl.pallas_call(
+        functools.partial(norm_kernel, width),
+        out_shape=[jax.ShapeDtypeStruct((rows, len(group) * width), BF16) for group in groups],
+        in_specs=[pl.BlockSpec(memory_space=pltpu.SMEM), vmem, vmem],
+        out_specs=[vmem] * len(groups),
+        scratch_shapes=[pltpu.VMEM((rows, depth), BF16)],
+        compiler_params=pltpu.CompilerParams(vmem_limit_bytes=32 * 1024 * 1024),
+        name="norm_hidden",
+    )(jnp.stack(blocks).astype(jnp.int32), hidden, gain[None, :])
+
+
 def key_values_of(hidden, kv_gain, kv_weight):
     lane_count = lax.axis_size("row")
     tile_count = lane_count // KVH
     me = lax.axis_index("row")
     tile, chip, core = me // KVH, me // 2 % CHIPS, me % 2
-    rows, depth = hidden.shape
+    rows = hidden.shape[0]
     unit = kv_weight.shape[0]
     pair = 2 * HD
-
-    def head_columns(place, which_core):
-        return lax.dynamic_slice_in_dim(kv_weight, ((chip ^ place) * 2 + which_core) * pair, pair, 1)
+    share = lax.axis_size("groups") == 2
+    part = lax.axis_index("groups") if share else 0
 
     order = [place for round_ in ROUNDS for place in round_]
-    kept = {place: head_columns(place, core) for place in order}
-    traded = swapped(jnp.stack([head_columns(place, 1 - core) for place in order]), 1)
-    traded = {place: traded[number] for number, place in enumerate(order)}
-
-    hidden_float = hidden.astype(F32)
-    inverse = lax.rsqrt(jnp.mean(hidden_float * hidden_float, axis=1, keepdims=True) + EPSILON)
-    normed = (hidden_float * inverse * kv_gain[None, :]).astype(BF16)
-
-    def features(place):
-        return jnp.concatenate(
-            [
-                lax.dynamic_slice_in_dim(
-                    normed, ((tile ^ j) * KVH + (chip ^ place) * 2) * unit, 2 * unit, 1
-                )
-                for j in range(tile_count)
-            ],
-            axis=1,
-        )
-
-    share = lax.axis_size("groups") == 2
-    part = lax.axis_index("groups")
-    held = []
-    for place in range(CHIPS):
-        own = features(place)
-        held.append(own if place == 0 else swapped(own, 2 * place))
+    heads = {place: (chip ^ place) * 2 + core for place in order}
+    others = {place: (chip ^ place) * 2 + 1 - core for place in order}
+    sent = [[heads[place] ^ part for place in round_] for round_ in ROUNDS]
+    pieces = arranged(
+        kv_weight, sent + [[others[p] for p in order], [heads[p] for p in order]], pair
+    )
+    sent, traded, kept = pieces[: len(ROUNDS)], pieces[-2], pieces[-1]
+
+    def to_tile(value, j, flip):
+        if not share:
+            return swapped(value, j * KVH)
+        pairs = [
+            (g * lane_count + d, g * lane_count + (d ^ (j * KVH) ^ (g if flip else 0)))
+            for g in range(2)
+            for d in range(lane_count)
+        ]
+        return lax.ppermute(value, ("groups", "row"), pairs)
+
+    far = [[to_tile(value, j, True) for j in range(1, tile_count)] for value in sent]
+    traded = swapped(traded, 1)
+
+    width = 2 * unit
+    features = normed_features(
+        hidden,
+        kv_gain,
+        [
+            [(tile ^ j) * CHIPS + (chip ^ place) for j in range(tile_count)]
+            for place in range(CHIPS)
+        ],
+        width,
+    )
+    held = [features[0]] + [swapped(features[p], 2 * p) for p in range(1, CHIPS)]
     mine = jnp.concatenate(held, axis=0)
     tokens = jnp.concatenate([mine, swapped(mine, 1)], axis=0)
 
     total = None
-    for round_ in ROUNDS:
-        first = jnp.stack([kept[place] for place in round_])
-        second = jnp.stack([traded[place] for place in round_])
-        low, high = jnp.where(core == 0, first, second), jnp.where(core == 0, second, first)
-        blocks = [(low, high)]
-        if share:
-            far = over_tiles(jnp.where(part == 0, low, high), tile_count)[1:]
-            for value in far:
+    place_in_order = 0
+    for number, round_ in enumerate(ROUNDS):
+        span = slice(place_in_order, place_in_order + len(round_))
+        place_in_order += len(round_)
+        blocks = [(kept[span], traded[span])]
+        for j, value in enumerate(far[number], 1):
+            if share:
                 other = swapped(value, 1, "groups")
                 blocks.append((jnp.where(part == 0, value, other), jnp.where(part == 0, other, value)))
-        else:
-            far = over_tiles(jnp.stack([low, high]), tile_count)[1:]
-            blocks.extend((value[0], value[1]) for value in far)
-        for number, place in enumerate(round_):
-            weight = jnp.concatenate([half[number] for block in blocks for half in block], axis=0)
+            else:
+                blocks.append((value, to_tile(traded[span], j, False)))
+        blocks = [
+            (jnp.where(core == 0, own, other), jnp.where(core == 0, other, own))
+            for own, other in blocks
+        ]
+        for inner, place in enumerate(round_):
+            weight = jnp.concatenate([half[inner] for block in blocks for half in block], axis=0)
             partial = lax.dot_general(
                 tokens, weight, (((1,), (0,)), ((), ())), preferred_element_type=F32
             )

time: 187 us -> 233 us (1.25)
  Pallas kernels: 0 us -> 62.8 us
  other arithmetic: 15.7 us -> 3.49 us
  waiting for transfers between devices: 93.2 us -> 86 us
  matrix products: 16.3 us -> 19.8 us
    pallas_call x0 -> x2, Pallas kernels: none -> 62.8 us  [the longest x1 61.4 us: arranged(): pl.pallas_call(functools.partial(arrange_kernel, pair), out_shape=[jax.Sh...]
    ppermute x40 -> x36, waiting for transfers between devices: 93.2 us -> 67 us  [swapped(): return lax.ppermute(value, axis, pairs)]
    ppermute x0 -> x4, waiting for transfers between devices: none -> 19 us  [to_tile(): return lax.ppermute(value, ('groups', 'row'), pairs)]
    ppermute x0 -> x4, starting transfers between devices: none -> 6.35 us  [to_tile(): return lax.ppermute(value, ('groups', 'row'), pairs)]
    ppermute x40 -> x36, starting transfers between devices: 47.1 us -> 42.5 us  [swapped(): return lax.ppermute(value, axis, pairs)]
    concatenate x3 -> x0, other arithmetic: 3.15 us -> none  [features(): jnp.concatenate([lax.dynamic_slice_in_dim(normed, ((tile ^ j) * KVH + (ch...]
    unnamed x37 -> x30, local copies, waits for them, and re-layouts: 2.36 us -> 5.17 us
    concatenate x1, local copies, waits for them, and re-layouts: 2.47 us -> 0.09 us  [key_values_of(): tokens = jnp.concatenate([mine, swapped(mine, 1)], axis=0)]
  transfers between devices with their start and end apart: 40 -> 40, of which waited for: 25 -> 26; matrix products, arithmetic and copies ran while one was open for 18% -> 8% of each run, Pallas kernels for 0% -> 27%
where the time goes in v2:
time: 233 us
  waiting for transfers between devices  86 us (37%)
  Pallas kernels  62.8 us (27%)
  starting transfers between devices  48.9 us (21%)
  matrix products  19.8 us (8%)
  local copies, waits for them, and re-layouts  11.2 us (5%)
  other arithmetic  3.49 us (1%)
    ppermute x36, waiting for transfers between devices, swapped(): return lax.ppermute(value, axis, pairs)  67 us
    pallas_call x1, Pallas kernels, arranged(): pl.pallas_call(functools.partial(arrange_kernel, pair), out_shape=[jax.Sh...  61.4 us
    ppermute x36, starting transfers between devices, swapped(): return lax.ppermute(value, axis, pairs)  42.5 us
    ppermute x4, waiting for transfers between devices, to_tile(): return lax.ppermute(value, ('groups', 'row'), pairs)  19 us
    ppermute x4, starting transfers between devices, to_tile(): return lax.ppermute(value, ('groups', 'row'), pairs)  6.35 us
    dot_general x4, matrix products, key_values_of(): lax.dot_general(tokens, weight, (((1,), (0,)), ((), ())), preferred_eleme...  5.81 us
    dot_general x2, matrix products, on_device(): lax.dot_general(scaled, query_weight[section, 0], (((0,), (0,)), ((), ())...  5.46 us
    unnamed x30, local copies, waits for them, and re-layouts  5.17 us
  transfers between devices with their start and end apart: 40, of which 26 were waited for; matrix products, arithmetic and copies ran while one was open for 8% of the time, Pallas kernels for 27%

profile of v2, /device:TPU:0, one launch (start us, length us, event | category | flops | bytes accessed | tf_op | source)
XLA Modules:
  0.0 232.9 jit_solution(8343192164442552160)
XLA Ops:
  0.0 4.0 %collective-permute-start = (bf16[320,128]{1,0:T(8,128)(2,1)}, bf16[320,128]{1,0:T(8,128)(2,1)S(1)}, u32[]{:S(2)}, u32[]{:S(2)}) collective-permute-start(bf16[320,128]{1,0:T(8,128)(2,1)} %param.11), channel_id=1, source_target_pairs={{0,6},{1,7},{2,4},{3,5},{4,2},{5,3},{6,0},{7,1},{8,14},{9,15},{10,... | collective-permute-start | bytes 245768 | tf_op jit(solution)/shard_map/ppermute | solution.py:25
  4.7 1.3 copy-done
  6.7 1.4 norm_hidden.1
  8.1 1.9 collective-permute-start.6
  10.0 1.6 collective-permute-start.7
  15.7 61.4 %arrange_weight.1 = (bf16[1,320,256]{2,1,0:T(8,128)(2,1)}, bf16[1,320,256]{2,1,0:T(8,128)(2,1)}, bf16[1,320,256]{2,1,0:T(8,128)(2,1)}, bf16[1,320,256]{2,1,0:T(8...) custom-call(s32[12]{0:T(128)} %stack.191.heads_ref, bf16[320,2048]{1,0:T(8,128)(2,1)} %weight_ref.1), custom_call_target="tpu_custom_call" | custom-call | tf_op jit(solution)/shard_map/arrange_weight/pallas_call | solution.py:78
  77.3 2.9 %collective-permute-start.17 = (bf16[1,320,256]{2,1,0:T(8,128)(2,1)}, bf16[1,320,256]{2,1,0:T(8,128)(2,1)S(1)}, u32[]{:S(2)}, u32[]{:S(2)}) collective-permute-start(bf16[1,320,256]{2,1,0:T(8,128)(2,1)} %get-tuple-element.23), channel_id=1, source_target_pairs={{0,8},{1,9},{2,10},{3,11},{4,12},{5,13},{6,14},{7,15},{8,0},{9,1},... | collective-permute-start | bytes 491528 | tf_op jit(solution)/shard_map/ppermute | solution.py:157
  81.2 7.5 %collective-permute-done.17 = bf16[1,320,256]{2,1,0:T(8,128)(2,1)S(1)} collective-permute-done((bf16[1,320,256]{2,1,0:T(8,128)(2,1)}, bf16[1,320,256]{2,1,0:T(8,128)(2,1)S(1)}, u32[]{:S(2)}, u32[]{:S(2)}) %collective-permute-start.17) | collective-permute-done | bytes 163872 | tf_op jit(solution)/shard_map/ppermute | solution.py:157
  88.8 3.3 %collective-permute-start.11 = (bf16[1,320,256]{2,1,0:T(8,128)(2,1)}, bf16[1,320,256]{2,1,0:T(8,128)(2,1)S(1)}, u32[]{:S(2)}, u32[]{:S(2)}) collective-permute-start(bf16[1,320,256]{2,1,0:T(8,128)(2,1)} %get-tuple-element.21), channel_id=1, source_target_pairs={{0,8},{1,9},{2,10},{3,11},{4,12},{5,13},{6,14},{7,15},{8,0},{9,1},... | collective-permute-start | bytes 491528 | tf_op jit(solution)/shard_map/ppermute | solution.py:157
  92.1 4.1 %collective-permute-done.20 = bf16[1,320,256]{2,1,0:T(8,128)(2,1)S(1)} collective-permute-done((bf16[1,320,256]{2,1,0:T(8,128)(2,1)}, bf16[1,320,256]{2,1,0:T(8,128)(2,1)S(1)}, u32[]{:S(2)}, u32[]{:S(2)}) %collective-permute-start.20) | collective-permute-done | bytes 163872 | tf_op jit(solution)/shard_map/ppermute | solution.py:157
  96.2 2.7 %collective-permute-start.18 = (bf16[1,320,256]{2,1,0:T(8,128)(2,1)S(1)}, bf16[1,320,256]{2,1,0:T(8,128)(2,1)S(1)}, u32[]{:S(2)}, u32[]{:S(2)}) collective-permute-start(bf16[1,320,256]{2,1,0:T(8,128)(2,1)S(1)} %collective-permute-done.17), channel_id=1, source_target_pairs={{0,16},{16,0},{1,17},{17,1},{2,18},{18,2},{3,19},{19,3},{4,20},{20... | collective-permute-start | bytes 491528 | tf_op jit(solution)/shard_map/ppermute | solution.py:25
  99.7 6.7 %collective-permute-done.14 = bf16[1,320,256]{2,1,0:T(8,128)(2,1)S(1)} collective-permute-done((bf16[1,320,256]{2,1,0:T(8,128)(2,1)}, bf16[1,320,256]{2,1,0:T(8,128)(2,1)S(1)}, u32[]{:S(2)}, u32[]{:S(2)}) %collective-permute-start.14) | collective-permute-done | bytes 163872 | tf_op jit(solution)/shard_map/ppermute | solution.py:157
  106.4 4.9 %collective-permute-start.12 = (bf16[1,320,256]{2,1,0:T(8,128)(2,1)S(1)}, bf16[1,320,256]{2,1,0:T(8,128)(2,1)S(1)}, u32[]{:S(2)}, u32[]{:S(2)}) collective-permute-start(bf16[1,320,256]{2,1,0:T(8,128)(2,1)S(1)} %collective-permute-done.11), channel_id=1, source_target_pairs={{0,16},{16,0},{1,17},{17,1},{2,18},{18,2},{3,19},{19,3},{4,20},{20... | collective-permute-start | bytes 491528 | tf_op jit(solution)/shard_map/ppermute | solution.py:25
  111.5 4.8 %collective-permute-done.12 = bf16[1,320,256]{2,1,0:T(8,128)(2,1)S(1)} collective-permute-done((bf16[1,320,256]{2,1,0:T(8,128)(2,1)S(1)}, bf16[1,320,256]{2,1,0:T(8,128)(2,1)S(1)}, u32[]{:S(2)}, u32[]{:S(2)}) %collective-permute-start.12) | collective-permute-done | bytes 163872 | tf_op jit(solution)/shard_map/ppermute | solution.py:25
  116.3 3.0 %collective-permute-done.15 = bf16[1,320,256]{2,1,0:T(8,128)(2,1)S(1)} collective-permute-done((bf16[1,320,256]{2,1,0:T(8,128)(2,1)S(1)}, bf16[1,320,256]{2,1,0:T(8,128)(2,1)S(1)}, u32[]{:S(2)}, u32[]{:S(2)}) %collective-permute-start.15) | collective-permute-done | bytes 163872 | tf_op jit(solution)/shard_map/ppermute | solution.py:25
  120.0 2.7 %fusion.89 = (bf16[128,640]{1,0:T(8,128)(2,1)S(1)}, f32[128,640]{1,0:T(8,128)S(1)}) fusion(bf16[2560,128]{1,0:T(8,128)(2,1)S(1)} %bitcast.244, bf16[2,1,2560,640]{3,2,1,0:T(8,128)(2,1)} %param.13), kind=kOutput, calls=%fused_computation.192 | convolution fusion | flops 419512320 | bytes 4423680 | tf_op jit(solution)/shard_map/dot_general | solution.py:270
  122.6 3.0 %collective-permute-start.4 = (bf16[128,640]{1,0:T(8,128)(2,1)S(1)}, bf16[128,640]{1,0:T(8,128)(2,1)S(1)}, u32[]{:S(2)}, u32[]{:S(2)}) collective-permute-start(bf16[128,640]{1,0:T(8,128)(2,1)S(1)} %get-tuple-element.77), channel_id=1, source_target_pairs={{0,8},{1,9},{2,10},{3,11},{4,12},{5,13},{6,14},{7,15},{8,0},{9,1},... | collective-permute-start | bytes 491528 | tf_op jit(solution)/shard_map/ppermute | solution.py:25
  125.8 1.6 convolution_convert_fusion
  127.5 2.0 collective-permute-start.19
  129.5 1.7 convolution_convert_fusion.1
  131.2 1.4 collective-permute-start.16
  132.5 1.7 convolution_convert_fusion.2
  134.6 8.2 %collective-permute-done.16 = bf16[1024,256]{1,0:T(8,128)(2,1)S(1)} collective-permute-done((bf16[1024,256]{1,0:T(8,128)(2,1)}, bf16[1024,256]{1,0:T(8,128)(2,1)S(1)}, u32[]{:S(2)}, u32[]{:S(2)}) %collective-permute-start.16) | collective-permute-done | bytes 524320 | tf_op jit(solution)/shard_map/ppermute | solution.py:25
  144.0 11.1 %collective-permute-done.13 = bf16[1024,256]{1,0:T(8,128)(2,1)S(1)} collective-permute-done((bf16[1024,256]{1,0:T(8,128)(2,1)}, bf16[1024,256]{1,0:T(8,128)(2,1)S(1)}, u32[]{:S(2)}, u32[]{:S(2)}) %collective-permute-start.13) | collective-permute-done | bytes 524320 | tf_op jit(solution)/shard_map/ppermute | solution.py:25
  155.5 1.5 copy-done.6
  157.9 1.1 fusion.10
  160.0 3.0 %collective-permute-start.22 = (bf16[128,640]{0,1:T(8,128)(2,1)S(1)}, bf16[128,640]{0,1:T(8,128)(2,1)S(1)}, u32[]{:S(2)}, u32[]{:S(2)}) collective-permute-start(bf16[128,640]{0,1:T(8,128)(2,1)S(1)} %bitcast_convert_fusion.1), channel_id=1, source_target_pairs={{0,8},{1,9},{2,10},{3,11},{4,12},{5,13},{6,14},{7,15},{8,0},{9,1},... | collective-permute-start | bytes 491528 | tf_op jit(solution)/shard_map/ppermute | solution.py:25
  163.6 5.1 %collective-permute-done.22 = bf16[128,640]{0,1:T(8,128)(2,1)S(1)} collective-permute-done((bf16[128,640]{0,1:T(8,128)(2,1)S(1)}, bf16[128,640]{0,1:T(8,128)(2,1)S(1)}, u32[]{:S(2)}, u32[]{:S(2)}) %collective-permute-start.22) | collective-permute-done | bytes 163872 | tf_op jit(solution)/shard_map/ppermute | solution.py:25
  168.7 1.2 convolution_bitcast_fusion.1
  170.5 1.6 collective-permute-done.24
  173.0 2.8 %collective-permute-start.27 = (bf16[320,128]{1,0:T(8,128)(2,1)S(1)}, bf16[320,128]{1,0:T(8,128)(2,1)S(1)}, u32[]{:S(2)}, u32[]{:S(2)}) collective-permute-start(bf16[320,128]{1,0:T(8,128)(2,1)S(1)} %get-tuple-element.43), channel_id=1, source_target_pairs={{0,6},{1,7},{2,4},{3,5},{4,2},{5,3},{6,0},{7,1},{8,14},{9,15},{10,... | collective-permute-start | bytes 245768 | tf_op jit(solution)/shard_map/ppermute | solution.py:25
  176.8 1.3 collective-permute-done.26
  178.1 1.6 collective-permute-done.27
  179.9 1.5 collective-permute-start.28
  182.2 1.3 collective-permute-start.30
  183.5 1.9 collective-permute-done.28
  186.9 1.5 collective-permute-done.31
  188.9 2.6 %collective-permute-start.33 = (bf16[128]{0:T(256)(128)(2,1)S(1)}, bf16[128]{0:T(256)(128)(2,1)S(1)}, u32[]{:S(2)}, u32[]{:S(2)}) collective-permute-start(bf16[128]{0:T(256)(128)(2,1)S(1)} %convert_element_type.250), channel_id=1, source_target_pairs={{0,8},{1,9},{2,10},{3,11},{4,12},{5,13},{6,14},{7,15},{8,0},{9,1},... | collective-permute-start | bytes 776 | tf_op jit(solution)/shard_map/ppermute | solution.py:25
  191.6 2.8 %fusion.90 = (bf16[128,640]{1,0:T(8,128)(2,1)S(1)}, f32[128,640]{1,0:T(8,128)S(1)}) fusion(bf16[2560,128]{1,0:T(8,128)(2,1)S(1)} %bitcast.245, bf16[2,1,2560,640]{3,2,1,0:T(8,128)(2,1)} %param.13), kind=kOutput, calls=%fused_computation.193 | convolution fusion | flops 419512320 | bytes 4423680 | tf_op jit(solution)/shard_map/dot_general | solution.py:270
  194.8 10.0 %collective-permute-done.32 = bf16[128,640]{1,0:T(8,128)(2,1)S(1)} collective-permute-done((bf16[128,640]{1,0:T(8,128)(2,1)S(1)}, bf16[128,640]{1,0:T(8,128)(2,1)S(1)}, u32[]{:S(2)}, u32[]{:S(2)}) %collective-permute-start.32) | collective-permute-done | bytes 163872 | tf_op jit(solution)/shard_map/ppermute | solution.py:25
  205.1 2.2 fusion.12
  208.3 3.0 %collective-permute-start.34 = (bf16[128,640]{0,1:T(8,128)(2,1)S(1)}, bf16[128,640]{0,1:T(8,128)(2,1)S(1)}, u32[]{:S(2)}, u32[]{:S(2)}) collective-permute-start(bf16[128,640]{0,1:T(8,128)(2,1)S(1)} %bitcast_convert_fusion), channel_id=1, source_target_pairs={{0,8},{1,9},{2,10},{3,11},{4,12},{5,13},{6,14},{7,15},{8,0},{9,1},... | collective-permute-start | bytes 491528 | tf_op jit(solution)/shard_map/ppermute | solution.py:25
  211.9 6.8 %collective-permute-done.34 = bf16[128,640]{0,1:T(8,128)(2,1)S(1)} collective-permute-done((bf16[128,640]{0,1:T(8,128)(2,1)S(1)}, bf16[128,640]{0,1:T(8,128)(2,1)S(1)}, u32[]{:S(2)}, u32[]{:S(2)}) %collective-permute-start.34) | collective-permute-done | bytes 163872 | tf_op jit(solution)/shard_map/ppermute | solution.py:25
  218.8 2.3 convolution_bitcast_fusion
  221.1 1.7 copy.29
  223.0 1.6 collective-permute-done.36
  225.0 3.3 %collective-permute-start.39 = (bf16[320,128]{1,0:T(8,128)(2,1)S(1)}, bf16[320,128]{1,0:T(8,128)(2,1)S(1)}, u32[]{:S(2)}, u32[]{:S(2)}) collective-permute-start(bf16[320,128]{1,0:T(8,128)(2,1)S(1)} %get-tuple-element.36), channel_id=1, source_target_pairs={{0,6},{1,7},{2,4},{3,5},{4,2},{5,3},{6,0},{7,1},{8,14},{9,15},{10,... | collective-permute-start | bytes 245768 | tf_op jit(solution)/shard_map/ppermute | solution.py:25
  230.1 2.1 collective-permute-done.39
  (140 shorter events, 23.5 us)
Async XLA Ops:
  0.0 80.3 %copy-start.3 = (bf16[320,128]{1,0:T(8,128)(2,1)S(1)}, bf16[320,128]{1,0:T(8,128)(2,1)}, u32[]{:S(2)}) copy-start(bf16[320,128]{1,0:T(8,128)(2,1)} %param.11) | copy-start | bytes 245764
  0.0 77.1 %collective-permute-start = (bf16[320,128]{1,0:T(8,128)(2,1)}, bf16[320,128]{1,0:T(8,128)(2,1)S(1)}, u32[]{:S(2)}, u32[]{:S(2)}) collective-permute-start(bf16[320,128]{1,0:T(8,128)(2,1)} %param.11), channel_id=1, source_target_pairs={{0,6},{1,7},{2,4},{3,5},{4,2},{5,3},{6,0},{7,1},{8,14},{9,15},{10,... | collective-permute-start | bytes 245768 | tf_op jit(solution)/shard_map/ppermute | solution.py:25
  4.0 73.3 %collective-permute-start.1 = (bf16[320,128]{1,0:T(8,128)(2,1)}, bf16[320,128]{1,0:T(8,128)(2,1)S(1)}, u32[]{:S(2)}, u32[]{:S(2)}) collective-permute-start(bf16[320,128]{1,0:T(8,128)(2,1)} %param.11), channel_id=1, source_target_pairs={{0,4},{1,5},{2,6},{3,7},{4,0},{5,1},{6,2},{7,3},{8,12},{9,13},{10,... | collective-permute-start | bytes 245768 | tf_op jit(solution)/shard_map/ppermute | solution.py:25
  4.4 75.8 %collective-permute-start.2 = (bf16[320,128]{1,0:T(8,128)(2,1)}, bf16[320,128]{1,0:T(8,128)(2,1)S(1)}, u32[]{:S(2)}, u32[]{:S(2)}) collective-permute-start(bf16[320,128]{1,0:T(8,128)(2,1)} %param.11), channel_id=1, source_target_pairs={{0,2},{1,3},{2,0},{3,1},{4,6},{5,7},{6,4},{7,5},{8,10},{9,11},{10,... | collective-permute-start | bytes 245768 | tf_op jit(solution)/shard_map/ppermute | solution.py:25
  8.1 72.3 %collective-permute-start.6 = (bf16[128,1280]{1,0:T(8,128)(2,1)S(1)}, bf16[128,1280]{1,0:T(8,128)(2,1)S(1)}, u32[]{:S(2)}, u32[]{:S(2)}) collective-permute-start(bf16[128,1280]{1,0:T(8,128)(2,1)S(1)} %get-tuple-element.16), channel_id=1, source_target_pairs={{0,2},{1,3},{2,0},{3,1},{4,6},{5,7},{6,4},{7,5},{8,10},{9,11},{10,... | collective-permute-start | bytes 983048 | tf_op jit(solution)/shard_map/ppermute | solution.py:25
  10.0 86.2 %collective-permute-start.7 = (bf16[128,1280]{1,0:T(8,128)(2,1)S(1)}, bf16[128,1280]{1,0:T(8,128)(2,1)S(1)}, u32[]{:S(2)}, u32[]{:S(2)}) collective-permute-start(bf16[128,1280]{1,0:T(8,128)(2,1)S(1)} %get-tuple-element.17), channel_id=1, source_target_pairs={{0,4},{1,5},{2,6},{3,7},{4,0},{5,1},{6,2},{7,3},{8,12},{9,13},{10,... | collective-permute-start | bytes 983048 | tf_op jit(solution)/shard_map/ppermute | solution.py:25
  77.1 21.7 %collective-permute-start.8 = (bf16[128,1280]{1,0:T(8,128)(2,1)S(1)}, bf16[128,1280]{1,0:T(8,128)(2,1)S(1)}, u32[]{:S(2)}, u32[]{:S(2)}) collective-permute-start(bf16[128,1280]{1,0:T(8,128)(2,1)S(1)} %get-tuple-element.18), channel_id=1, source_target_pairs={{0,6},{1,7},{2,4},{3,5},{4,2},{5,3},{6,0},{7,1},{8,14},{9,15},{10,... | collective-permute-start | bytes 983048 | tf_op jit(solution)/shard_map/ppermute | solution.py:25
  77.3 11.5 %collective-permute-start.17 = (bf16[1,320,256]{2,1,0:T(8,128)(2,1)}, bf16[1,320,256]{2,1,0:T(8,128)(2,1)S(1)}, u32[]{:S(2)}, u32[]{:S(2)}) collective-permute-start(bf16[1,320,256]{2,1,0:T(8,128)(2,1)} %get-tuple-element.23), channel_id=1, source_target_pairs={{0,8},{1,9},{2,10},{3,11},{4,12},{5,13},{6,14},{7,15},{8,0},{9,1},... | collective-permute-start | bytes 491528 | tf_op jit(solution)/shard_map/ppermute | solution.py:157
  80.2 16.0 %collective-permute-start.20 = (bf16[1,320,256]{2,1,0:T(8,128)(2,1)}, bf16[1,320,256]{2,1,0:T(8,128)(2,1)S(1)}, u32[]{:S(2)}, u32[]{:S(2)}) collective-permute-start(bf16[1,320,256]{2,1,0:T(8,128)(2,1)} %get-tuple-element.24), channel_id=1, source_target_pairs={{0,8},{1,9},{2,10},{3,11},{4,12},{5,13},{6,14},{7,15},{8,0},{9,1},... | collective-permute-start | bytes 491528 | tf_op jit(solution)/shard_map/ppermute | solution.py:157
  80.4 45.2 %collective-permute-start.10 = (bf16[4,320,256]{2,1,0:T(8,128)(2,1)}, bf16[4,320,256]{2,1,0:T(8,128)(2,1)S(1)}, u32[]{:S(2)}, u32[]{:S(2)}) collective-permute-start(bf16[4,320,256]{2,1,0:T(8,128)(2,1)} %get-tuple-element.20), channel_id=1, source_target_pairs={{0,1},{1,0},{2,3},{3,2},{4,5},{5,4},{6,7},{7,6},{8,9},{9,8},{10,11... | collective-permute-start | bytes 1966088 | tf_op jit(solution)/shard_map/ppermute | solution.py:25
  81.2 17.8 %copy-start.4 = (bf16[1024,1280]{1,0:T(8,128)(2,1)S(1)}, bf16[1024,1280]{1,0:T(8,128)(2,1)}, u32[]{:S(2)}) copy-start(bf16[1024,1280]{1,0:T(8,128)(2,1)} %constant_dynamic-update-slice_fusion.3) | copy-start | bytes 7864324
  88.8 10.9 %collective-permute-start.11 = (bf16[1,320,256]{2,1,0:T(8,128)(2,1)}, bf16[1,320,256]{2,1,0:T(8,128)(2,1)S(1)}, u32[]{:S(2)}, u32[]{:S(2)}) collective-permute-start(bf16[1,320,256]{2,1,0:T(8,128)(2,1)} %get-tuple-element.21), channel_id=1, source_target_pairs={{0,8},{1,9},{2,10},{3,11},{4,12},{5,13},{6,14},{7,15},{8,0},{9,1},... | collective-permute-start | bytes 491528 | tf_op jit(solution)/shard_map/ppermute | solution.py:157
  96.2 10.2 %collective-permute-start.14 = (bf16[1,320,256]{2,1,0:T(8,128)(2,1)}, bf16[1,320,256]{2,1,0:T(8,128)(2,1)S(1)}, u32[]{:S(2)}, u32[]{:S(2)}) collective-permute-start(bf16[1,320,256]{2,1,0:T(8,128)(2,1)} %get-tuple-element.22), channel_id=1, source_target_pairs={{0,8},{1,9},{2,10},{3,11},{4,12},{5,13},{6,14},{7,15},{8,0},{9,1},... | collective-permute-start | bytes 491528 | tf_op jit(solution)/shard_map/ppermute | solution.py:157
  96.2 15.1 %collective-permute-start.18 = (bf16[1,320,256]{2,1,0:T(8,128)(2,1)S(1)}, bf16[1,320,256]{2,1,0:T(8,128)(2,1)S(1)}, u32[]{:S(2)}, u32[]{:S(2)}) collective-permute-start(bf16[1,320,256]{2,1,0:T(8,128)(2,1)S(1)} %collective-permute-done.17), channel_id=1, source_target_pairs={{0,16},{16,0},{1,17},{17,1},{2,18},{18,2},{3,19},{19,3},{4,20},{20... | collective-permute-start | bytes 491528 | tf_op jit(solution)/shard_map/ppermute | solution.py:25
  98.9 12.5 %collective-permute-start.21 = (bf16[1,320,256]{2,1,0:T(8,128)(2,1)S(1)}, bf16[1,320,256]{2,1,0:T(8,128)(2,1)S(1)}, u32[]{:S(2)}, u32[]{:S(2)}) collective-permute-start(bf16[1,320,256]{2,1,0:T(8,128)(2,1)S(1)} %collective-permute-done.20), channel_id=1, source_target_pairs={{0,16},{16,0},{1,17},{17,1},{2,18},{18,2},{3,19},{19,3},{4,20},{20... | collective-permute-start | bytes 491528 | tf_op jit(solution)/shard_map/ppermute | solution.py:25
  99.7 19.7 %collective-permute-start.3 = (bf16[4,320,128]{2,1,0:T(8,128)(2,1)S(1)}, bf16[4,320,128]{2,1,0:T(8,128)(2,1)S(1)}, u32[]{:S(2)}, u32[]{:S(2)}) collective-permute-start(bf16[4,320,128]{2,1,0:T(8,128)(2,1)S(1)} %pad_maximum_fusion.3), channel_id=1, source_target_pairs={{0,1},{1,0},{2,3},{3,2},{4,5},{5,4},{6,7},{7,6},{8,9},{9,8},{10,11... | collective-permute-start | bytes 983048 | tf_op jit(solution)/shard_map/ppermute | solution.py:25
  106.4 9.9 %collective-permute-start.12 = (bf16[1,320,256]{2,1,0:T(8,128)(2,1)S(1)}, bf16[1,320,256]{2,1,0:T(8,128)(2,1)S(1)}, u32[]{:S(2)}, u32[]{:S(2)}) collective-permute-start(bf16[1,320,256]{2,1,0:T(8,128)(2,1)S(1)} %collective-permute-done.11), channel_id=1, source_target_pairs={{0,16},{16,0},{1,17},{17,1},{2,18},{18,2},{3,19},{19,3},{4,20},{20... | collective-permute-start | bytes 491528 | tf_op jit(solution)/shard_map/ppermute | solution.py:25
  111.3 8.0 %collective-permute-start.15 = (bf16[1,320,256]{2,1,0:T(8,128)(2,1)S(1)}, bf16[1,320,256]{2,1,0:T(8,128)(2,1)S(1)}, u32[]{:S(2)}, u32[]{:S(2)}) collective-permute-start(bf16[1,320,256]{2,1,0:T(8,128)(2,1)S(1)} %collective-permute-done.14), channel_id=1, source_target_pairs={{0,16},{16,0},{1,17},{17,1},{2,18},{18,2},{3,19},{19,3},{4,20},{20... | collective-permute-start | bytes 491528 | tf_op jit(solution)/shard_map/ppermute | solution.py:25
  111.3 14.4 %collective-permute-start.9 = (bf16[512,1280]{1,0:T(8,128)(2,1)S(1)}, bf16[512,1280]{1,0:T(8,128)(2,1)S(1)}, u32[]{:S(2)}, u32[]{:S(2)}) collective-permute-start(bf16[512,1280]{1,0:T(8,128)(2,1)S(1)} %pad_maximum_fusion), channel_id=1, source_target_pairs={{0,1},{1,0},{2,3},{3,2},{4,5},{5,4},{6,7},{7,6},{8,9},{9,8},{10,11... | collective-permute-start | bytes 3932168 | tf_op jit(solution)/shard_map/ppermute | solution.py:25
  119.4 6.2 %copy-start.2 = (bf16[4,320,256]{2,1,0:T(8,128)(2,1)S(1)}, bf16[4,320,256]{2,1,0:T(8,128)(2,1)}, u32[]{:S(2)}) copy-start(bf16[4,320,256]{2,1,0:T(8,128)(2,1)} %get-tuple-element.19) | copy-start | bytes 1966084
  119.9 5.7 %collective-permute-start.5 = (bf16[128]{0:T(256)(128)(2,1)S(1)}, bf16[128]{0:T(256)(128)(2,1)S(1)}, u32[]{:S(2)}, u32[]{:S(2)}) collective-permute-start(bf16[128]{0:T(256)(128)(2,1)S(1)} %convert_element_type.218), channel_id=1, source_target_pairs={{0,8},{1,9},{2,10},{3,11},{4,12},{5,13},{6,14},{7,15},{8,0},{9,1},... | collective-permute-start | bytes 776 | tf_op jit(solution)/shard_map/ppermute | solution.py:25
  122.6 11.7 %collective-permute-start.4 = (bf16[128,640]{1,0:T(8,128)(2,1)S(1)}, bf16[128,640]{1,0:T(8,128)(2,1)S(1)}, u32[]{:S(2)}, u32[]{:S(2)}) collective-permute-start(bf16[128,640]{1,0:T(8,128)(2,1)S(1)} %get-tuple-element.77), channel_id=1, source_target_pairs={{0,8},{1,9},{2,10},{3,11},{4,12},{5,13},{6,14},{7,15},{8,0},{9,1},... | collective-permute-start | bytes 491528 | tf_op jit(solution)/shard_map/ppermute | solution.py:25
  125.8 8.4 %copy-start.5 = (bf16[1024,1280]{1,0:T(8,128)(2,1)}, bf16[1024,1280]{1,0:T(8,128)(2,1)S(1)}, u32[]{:S(2)}) copy-start(bf16[1024,1280]{1,0:T(8,128)(2,1)S(1)} %constant_dynamic-update-slice_fusion) | copy-start | bytes 7864324
  127.5 16.4 %collective-permute-start.19 = (bf16[1024,256]{1,0:T(8,128)(2,1)}, bf16[1024,256]{1,0:T(8,128)(2,1)S(1)}, u32[]{:S(2)}, u32[]{:S(2)}) collective-permute-start(bf16[1024,256]{1,0:T(8,128)(2,1)} %convolution_convert_fusion), channel_id=1, source_target_pairs={{0,4},{1,5},{2,6},{3,7},{4,0},{5,1},{6,2},{7,3},{8,12},{9,13},{10,... | collective-permute-start | bytes 1572872 | tf_op jit(solution)/shard_map/ppermute | solution.py:25
  131.2 11.6 %collective-permute-start.16 = (bf16[1024,256]{1,0:T(8,128)(2,1)}, bf16[1024,256]{1,0:T(8,128)(2,1)S(1)}, u32[]{:S(2)}, u32[]{:S(2)}) collective-permute-start(bf16[1024,256]{1,0:T(8,128)(2,1)} %convolution_convert_fusion.1), channel_id=1, source_target_pairs={{0,2},{1,3},{2,0},{3,1},{4,6},{5,7},{6,4},{7,5},{8,10},{9,11},{10,... | collective-permute-start | bytes 1572872 | tf_op jit(solution)/shard_map/ppermute | solution.py:25
  134.2 20.9 %collective-permute-start.13 = (bf16[1024,256]{1,0:T(8,128)(2,1)}, bf16[1024,256]{1,0:T(8,128)(2,1)S(1)}, u32[]{:S(2)}, u32[]{:S(2)}) collective-permute-start(bf16[1024,256]{1,0:T(8,128)(2,1)} %convolution_convert_fusion.2), channel_id=1, source_target_pairs={{0,6},{1,7},{2,4},{3,5},{4,2},{5,3},{6,0},{7,1},{8,14},{9,15},{10,... | collective-permute-start | bytes 1572872 | tf_op jit(solution)/shard_map/ppermute | solution.py:25
  157.0 11.7 %slice-start = ((s8[6553600]{0:T(1024)(128)(4,1)}), s8[4194304]{0:T(1024)(128)(4,1)S(1)}, s32[]{:S(2)}) async-start(s8[6553600]{0:T(1024)(128)(4,1)} %bitcast.240), calls=%async_computation | async-start | bytes 8388608
  157.9 10.8 %slice-start.1 = ((s8[6553600]{0:T(1024)(128)(4,1)}), s8[2359296]{0:T(1024)(128)(4,1)S(1)}, s32[]{:S(2)}) async-start(s8[6553600]{0:T(1024)(128)(4,1)} %bitcast.240), calls=%async_computation.1 | async-start | bytes 4718592
  159.0 4.6 %collective-permute-start.23 = (bf16[128,5]{0,1:T(8,128)(2,1)S(1)}, bf16[128,5]{0,1:T(8,128)(2,1)S(1)}, u32[]{:S(2)}, u32[]{:S(2)}) collective-permute-start(bf16[128,5]{0,1:T(8,128)(2,1)S(1)} %convert_element_type.228), channel_id=1, source_target_pairs={{0,8},{1,9},{2,10},{3,11},{4,12},{5,13},{6,14},{7,15},{8,0},{9,1},... | collective-permute-start | bytes 3848 | tf_op jit(solution)/shard_map/ppermute | solution.py:25
  160.0 8.7 %collective-permute-start.22 = (bf16[128,640]{0,1:T(8,128)(2,1)S(1)}, bf16[128,640]{0,1:T(8,128)(2,1)S(1)}, u32[]{:S(2)}, u32[]{:S(2)}) collective-permute-start(bf16[128,640]{0,1:T(8,128)(2,1)S(1)} %bitcast_convert_fusion.1), channel_id=1, source_target_pairs={{0,8},{1,9},{2,10},{3,11},{4,12},{5,13},{6,14},{7,15},{8,0},{9,1},... | collective-permute-start | bytes 491528 | tf_op jit(solution)/shard_map/ppermute | solution.py:25
  170.4 1.7 collective-permute-start.24
  172.2 4.6 %collective-permute-start.25 = (bf16[320,128]{1,0:T(8,128)(2,1)S(1)}, bf16[320,128]{1,0:T(8,128)(2,1)S(1)}, u32[]{:S(2)}, u32[]{:S(2)}) collective-permute-start(bf16[320,128]{1,0:T(8,128)(2,1)S(1)} %get-tuple-element.42), channel_id=1, source_target_pairs={{0,2},{1,3},{2,0},{3,1},{4,6},{5,7},{6,4},{7,5},{8,10},{9,11},{10,... | collective-permute-start | bytes 245768 | tf_op jit(solution)/shard_map/ppermute | solution.py:25
  173.0 5.1 %collective-permute-start.26 = (bf16[320,128]{1,0:T(8,128)(2,1)S(1)}, bf16[320,128]{1,0:T(8,128)(2,1)S(1)}, u32[]{:S(2)}, u32[]{:S(2)}) collective-permute-start(bf16[320,128]{1,0:T(8,128)(2,1)S(1)} %get-tuple-element.44), channel_id=1, source_target_pairs={{0,4},{1,5},{2,6},{3,7},{4,0},{5,1},{6,2},{7,3},{8,12},{9,13},{10,... | collective-permute-start | bytes 245768 | tf_op jit(solution)/shard_map/ppermute | solution.py:25
  173.0 6.7 %collective-permute-start.27 = (bf16[320,128]{1,0:T(8,128)(2,1)S(1)}, bf16[320,128]{1,0:T(8,128)(2,1)S(1)}, u32[]{:S(2)}, u32[]{:S(2)}) collective-permute-start(bf16[320,128]{1,0:T(8,128)(2,1)S(1)} %get-tuple-element.43), channel_id=1, source_target_pairs={{0,6},{1,7},{2,4},{3,5},{4,2},{5,3},{6,0},{7,1},{8,14},{9,15},{10,... | collective-permute-start | bytes 245768 | tf_op jit(solution)/shard_map/ppermute | solution.py:25
  179.9 5.4 %collective-permute-start.28 = (bf16[320,128]{1,0:T(8,128)(2,1)S(1)}, bf16[320,128]{1,0:T(8,128)(2,1)S(1)}, u32[]{:S(2)}, u32[]{:S(2)}) collective-permute-start(bf16[320,128]{1,0:T(8,128)(2,1)S(1)} %fusion.67), channel_id=1, source_target_pairs={{0,6},{1,7},{2,4},{3,5},{4,2},{5,3},{6,0},{7,1},{8,14},{9,15},{10,... | collective-permute-start | bytes 245768 | tf_op jit(solution)/shard_map/ppermute | solution.py:25
  181.4 4.4 %collective-permute-start.29 = (bf16[320,128]{1,0:T(8,128)(2,1)S(1)}, bf16[320,128]{1,0:T(8,128)(2,1)S(1)}, u32[]{:S(2)}, u32[]{:S(2)}) collective-permute-start(bf16[320,128]{1,0:T(8,128)(2,1)S(1)} %fusion.67), channel_id=1, source_target_pairs={{0,4},{1,5},{2,6},{3,7},{4,0},{5,1},{6,2},{7,3},{8,12},{9,13},{10,... | collective-permute-start | bytes 245768 | tf_op jit(solution)/shard_map/ppermute | solution.py:25
  182.2 4.4 %collective-permute-start.30 = (bf16[320,128]{1,0:T(8,128)(2,1)S(1)}, bf16[320,128]{1,0:T(8,128)(2,1)S(1)}, u32[]{:S(2)}, u32[]{:S(2)}) collective-permute-start(bf16[320,128]{1,0:T(8,128)(2,1)S(1)} %fusion.67), channel_id=1, source_target_pairs={{0,2},{1,3},{2,0},{3,1},{4,6},{5,7},{6,4},{7,5},{8,10},{9,11},{10,... | collective-permute-start | bytes 245768 | tf_op jit(solution)/shard_map/ppermute | solution.py:25
  186.7 1.7 collective-permute-start.31
  188.9 5.9 %collective-permute-start.33 = (bf16[128]{0:T(256)(128)(2,1)S(1)}, bf16[128]{0:T(256)(128)(2,1)S(1)}, u32[]{:S(2)}, u32[]{:S(2)}) collective-permute-start(bf16[128]{0:T(256)(128)(2,1)S(1)} %convert_element_type.250), channel_id=1, source_target_pairs={{0,8},{1,9},{2,10},{3,11},{4,12},{5,13},{6,14},{7,15},{8,0},{9,1},... | collective-permute-start | bytes 776 | tf_op jit(solution)/shard_map/ppermute | solution.py:25
  191.6 27.2 %slice-start.2 = ((s8[6553600]{0:T(1024)(128)(4,1)}), s8[2359296]{0:T(1024)(128)(4,1)S(1)}, s32[]{:S(2)}) async-start(s8[6553600]{0:T(1024)(128)(4,1)} %bitcast.242), calls=%async_computation.2 | async-start | bytes 4718592
  194.4 10.4 %collective-permute-start.32 = (bf16[128,640]{1,0:T(8,128)(2,1)S(1)}, bf16[128,640]{1,0:T(8,128)(2,1)S(1)}, u32[]{:S(2)}, u32[]{:S(2)}) collective-permute-start(bf16[128,640]{1,0:T(8,128)(2,1)S(1)} %get-tuple-element.81), channel_id=1, source_target_pairs={{0,8},{1,9},{2,10},{3,11},{4,12},{5,13},{6,14},{7,15},{8,0},{9,1},... | collective-permute-start | bytes 491528 | tf_op jit(solution)/shard_map/ppermute | solution.py:25
  205.1 13.7 %slice-start.3 = ((s8[6553600]{0:T(1024)(128)(4,1)}), s8[4194304]{0:T(1024)(128)(4,1)S(1)}, s32[]{:S(2)}) async-start(s8[6553600]{0:T(1024)(128)(4,1)} %bitcast.242), calls=%async_computation.3 | async-start | bytes 8388608
  207.3 4.6 %collective-permute-start.35 = (bf16[128,5]{0,1:T(8,128)(2,1)S(1)}, bf16[128,5]{0,1:T(8,128)(2,1)S(1)}, u32[]{:S(2)}, u32[]{:S(2)}) collective-permute-start(bf16[128,5]{0,1:T(8,128)(2,1)S(1)} %convert_element_type.256), channel_id=1, source_target_pairs={{0,8},{1,9},{2,10},{3,11},{4,12},{5,13},{6,14},{7,15},{8,0},{9,1},... | collective-permute-start | bytes 3848 | tf_op jit(solution)/shard_map/ppermute | solution.py:25
  208.3 10.4 %collective-permute-start.34 = (bf16[128,640]{0,1:T(8,128)(2,1)S(1)}, bf16[128,640]{0,1:T(8,128)(2,1)S(1)}, u32[]{:S(2)}, u32[]{:S(2)}) collective-permute-start(bf16[128,640]{0,1:T(8,128)(2,1)S(1)} %bitcast_convert_fusion), channel_id=1, source_target_pairs={{0,8},{1,9},{2,10},{3,11},{4,12},{5,13},{6,14},{7,15},{8,0},{9,1},... | collective-permute-start | bytes 491528 | tf_op jit(solution)/shard_map/ppermute | solution.py:25
  222.9 1.7 collective-permute-start.36
  224.7 4.6 %collective-permute-start.37 = (bf16[320,128]{1,0:T(8,128)(2,1)S(1)}, bf16[320,128]{1,0:T(8,128)(2,1)S(1)}, u32[]{:S(2)}, u32[]{:S(2)}) collective-permute-start(bf16[320,128]{1,0:T(8,128)(2,1)S(1)} %get-tuple-element.35), channel_id=1, source_target_pairs={{0,2},{1,3},{2,0},{3,1},{4,6},{5,7},{6,4},{7,5},{8,10},{9,11},{10,... | collective-permute-start | bytes 245768 | tf_op jit(solution)/shard_map/ppermute | solution.py:25
  225.0 5.1 %collective-permute-start.38 = (bf16[320,128]{1,0:T(8,128)(2,1)S(1)}, bf16[320,128]{1,0:T(8,128)(2,1)S(1)}, u32[]{:S(2)}, u32[]{:S(2)}) collective-permute-start(bf16[320,128]{1,0:T(8,128)(2,1)S(1)} %get-tuple-element.37), channel_id=1, source_target_pairs={{0,4},{1,5},{2,6},{3,7},{4,0},{5,1},{6,2},{7,3},{8,12},{9,13},{10,... | collective-permute-start | bytes 245768 | tf_op jit(solution)/shard_map/ppermute | solution.py:25
  225.0 7.3 %collective-permute-start.39 = (bf16[320,128]{1,0:T(8,128)(2,1)S(1)}, bf16[320,128]{1,0:T(8,128)(2,1)S(1)}, u32[]{:S(2)}, u32[]{:S(2)}) collective-permute-start(bf16[320,128]{1,0:T(8,128)(2,1)S(1)} %get-tuple-element.36), channel_id=1, source_target_pairs={{0,6},{1,7},{2,4},{3,5},{4,2},{5,3},{6,0},{7,1},{8,14},{9,15},{10,... | collective-permute-start | bytes 245768 | tf_op jit(solution)/shard_map/ppermute | solution.py:25
  (5 other events, 8.2 us)

commit v3 on v2

--- a/solution.py
+++ b/solution.py
@@ -48,21 +48,13 @@
     return pieces
 
 
-def arrange_kernel(pair, heads_ref, weight_ref, *refs):
-    out_refs, sems = refs[:-1], refs[-1]
-    copies = []
+def arrange_kernel(pair, heads_ref, weight_ref, *out_refs):
+    number = 0
     for out_ref in out_refs:
         for place in range(out_ref.shape[0]):
-            column = pl.multiple_of(heads_ref[len(copies)] * pair, pair)
-            copies.append(
-                pltpu.make_async_copy(
-                    weight_ref.at[:, pl.ds(column, pair)], out_ref.at[place], sems.at[len(copies)]
-                )
-            )
-    for copy in copies:
-        copy.start()
-    for copy in copies:
-        copy.wait()
+            column = pl.multiple_of(heads_ref[number] * pair, pair)
+            out_ref[place] = weight_ref[:, pl.ds(column, pair)]
+            number += 1
 
 
 def arranged(weight, groups, pair):
@@ -75,21 +67,20 @@
             results.append(jnp.stack(columns[: len(group)]))
             columns = columns[len(group) :]
         return results
+    vmem = pl.BlockSpec(memory_space=pltpu.VMEM)
     return pl.pallas_call(
         functools.partial(arrange_kernel, pair),
         out_shape=[jax.ShapeDtypeStruct((len(group), unit, pair), weight.dtype) for group in groups],
-        in_specs=[
-            pl.BlockSpec(memory_space=pltpu.SMEM),
-            pl.BlockSpec(memory_space=pl.ANY),
-        ],
-        out_specs=[pl.BlockSpec(memory_space=pl.ANY)] * len(groups),
-        scratch_shapes=[pltpu.SemaphoreType.DMA((len(heads),))],
+        in_specs=[pl.BlockSpec(memory_space=pltpu.SMEM), vmem],
+        out_specs=[vmem] * len(groups),
+        compiler_params=pltpu.CompilerParams(vmem_limit_bytes=16 * 1024 * 1024),
         name="arrange_weight",
     )(jnp.stack(heads).astype(jnp.int32), weight)
 
 
-def norm_kernel(width, starts_ref, hidden_ref, gain_ref, *refs):
+def norm_kernel(width, starts_ref, hidden_ref, gain_ref, extra_ref, *refs):
     out_refs, normed = refs[:-1], refs[-1]
+    rows = hidden_ref.shape[0]
     hidden = hidden_ref[...].astype(F32)
     inverse = lax.rsqrt(jnp.mean(hidden * hidden, axis=1, keepdims=True) + EPSILON)
     normed[...] = (hidden * inverse * gain_ref[...]).astype(BF16)
@@ -97,19 +88,30 @@
     for out_ref in out_refs:
         for place in range(out_ref.shape[1] // width):
             start = pl.multiple_of(starts_ref[number] * width, 128)
-            out_ref[:, place * width : (place + 1) * width] = normed[:, pl.ds(start, width)]
+            out_ref[:rows, place * width : (place + 1) * width] = normed[:, pl.ds(start, width)]
             number += 1
-
-
-def normed_features(hidden, gain, groups, width):
+        out_ref[rows:, :] = extra_ref[...]
+
+
+def normed_features(hidden, gain, groups, width, extra):
     rows, depth = hidden.shape
-    if width % 128 or rows % 16:
+    if width % 128 or rows % 16 or extra.shape[0] % 16:
         hidden_float = hidden.astype(F32)
         inverse = lax.rsqrt(jnp.mean(hidden_float * hidden_float, axis=1, keepdims=True) + EPSILON)
         normed = (hidden_float * inverse * gain[None, :]).astype(BF16)
         return [
             jnp.concatenate(
-                [lax.dynamic_slice_in_dim(normed, block * width, width, 1) for block in group], axis=1
+                [
+                    jnp.concatenate(
+                        [
+                            lax.dynamic_slice_in_dim(normed, block * width, width, 1)
+                            for block in group
+                        ],
+                        axis=1,
+                    ),
+                    extra,
+                ],
+                axis=0,
             )
             for group in groups
         ]
@@ -117,16 +119,24 @@
     vmem = pl.BlockSpec(memory_space=pltpu.VMEM)
     return pl.pallas_call(
         functools.partial(norm_kernel, width),
-        out_shape=[jax.ShapeDtypeStruct((rows, len(group) * width), BF16) for group in groups],
-        in_specs=[pl.BlockSpec(memory_space=pltpu.SMEM), vmem, vmem],
+        out_shape=[
+            jax.ShapeDtypeStruct((rows + extra.shape[0], len(group) * width), BF16)
+            for group in groups
+        ],
+        in_specs=[pl.BlockSpec(memory_space=pltpu.SMEM), vmem, vmem, vmem],
         out_specs=[vmem] * len(groups),
         scratch_shapes=[pltpu.VMEM((rows, depth), BF16)],
         compiler_params=pltpu.CompilerParams(vmem_limit_bytes=32 * 1024 * 1024),
         name="norm_hidden",
-    )(jnp.stack(blocks).astype(jnp.int32), hidden, gain[None, :])
-
-
-def key_values_of(hidden, kv_gain, kv_weight):
+    )(jnp.stack(blocks).astype(jnp.int32), hidden, gain[None, :], extra)
+
+
+def in_order(ours, theirs, core):
+    low, high = jnp.where(core == 0, ours, theirs), jnp.where(core == 0, theirs, ours)
+    return jnp.stack([low, high], axis=1).reshape(-1, ours.shape[-1])
+
+
+def key_values_of(hidden, kv_gain, kv_weight, query_states):
     lane_count = lax.axis_size("row")
     tile_count = lane_count // KVH
     me = lax.axis_index("row")
@@ -168,10 +178,18 @@
             for place in range(CHIPS)
         ],
         width,
+        query_states.reshape(-1, tile_count * width),
     )
     held = [features[0]] + [swapped(features[p], 2 * p) for p in range(1, CHIPS)]
-    mine = jnp.concatenate(held, axis=0)
-    tokens = jnp.concatenate([mine, swapped(mine, 1)], axis=0)
+    mine = jnp.stack(held)
+    mine, far[0] = lax.optimization_barrier((mine, far[0]))
+    theirs = swapped(mine, 1)
+    tokens = jnp.concatenate([held[p][:rows] for p in range(CHIPS)] + [theirs[p, :rows] for p in range(CHIPS)])
+    ours, theirs = (
+        jnp.stack(natural([value[p, rows:].reshape(query_states.shape) for p in range(CHIPS)], chip))
+        for value in (mine, theirs)
+    )
+    stream = in_order(ours, theirs, core)
 
     total = None
     place_in_order = 0
@@ -204,7 +222,7 @@
         [tile * KVH + (chip ^ j) * 2 + (core ^ e) for e in range(2) for j in range(CHIPS)]
     )
     key_pos = (sources[:, None] * rows + jnp.arange(rows, dtype=jnp.int32)[None, :]).reshape(-1)
-    return key_values, key_pos
+    return key_values, key_pos, stream
 
 
 def gather_rows(own):
@@ -212,9 +230,7 @@
     chip, core = me // 2 % CHIPS, me % 2
     chips = [own] + [swapped(own, 2 * place) for place in range(1, CHIPS)]
     ours = jnp.stack(natural(chips, chip))
-    theirs = swapped(ours, 1)
-    low, high = jnp.where(core == 0, ours, theirs), jnp.where(core == 0, theirs, ours)
-    return jnp.stack([low, high], axis=1).reshape(KVH * own.shape[0], own.shape[1])
+    return in_order(ours, swapped(ours, 1), core)
 
 
 def scatter_rows(update, rows):
@@ -260,10 +276,12 @@
     query_pos = jnp.repeat(block_bounds[:, 1], QBLK) + row_number % QBLK
     query_floor = jnp.repeat(block_bounds[:, 0], QBLK)
 
-    key_values, key_pos = key_values_of(hidden, kv_gain, kv_weight)
+    key_values, key_pos, stream = key_values_of(hidden, kv_gain, kv_weight, query_states)
     own_rows = query_states
     for section in range(query_gain.shape[0]):
-        stream = gather_rows(own_rows).astype(F32)
+        if section:
+            stream = gather_rows(own_rows)
+        stream = stream.astype(F32)
         squares = jnp.sum(stream * stream, axis=0)
         gain = lax.dynamic_slice_in_dim(query_gain[section], tile * slice_depth, slice_depth)
         scaled = (stream * gain[:, None]).astype(BF16)

time: 233 us -> 184 us (0.79)
  Pallas kernels: 62.8 us -> 2.89 us
  other arithmetic: 3.49 us -> 14.1 us
  local copies, waits for them, and re-layouts: 11.2 us -> 16.3 us
  starting transfers between devices: 48.9 us -> 45.4 us
    pallas_call x1, Pallas kernels: 61.4 us -> 1.49 us  [arranged(): pl.pallas_call(functools.partial(arrange_kernel, pair), out_shape=[jax.Sh...]
    ppermute x36 -> x32, waiting for transfers between devices: 67 us -> 60.5 us  [swapped(): return lax.ppermute(value, axis, pairs)]
    ppermute x36 -> x32, starting transfers between devices: 42.5 us -> 36.4 us  [swapped(): return lax.ppermute(value, axis, pairs)]
    squeeze x3, other arithmetic: 0.21 us -> 5.86 us  [key_values_of(): half[inner]]
    ppermute x4, waiting for transfers between devices: 19 us -> 24 us  [to_tile(): return lax.ppermute(value, ('groups', 'row'), pairs)]
    unnamed x30 -> x65, local copies, waits for them, and re-layouts: 5.17 us -> 9.24 us
    ppermute x4, starting transfers between devices: 6.35 us -> 9.03 us  [to_tile(): return lax.ppermute(value, ('groups', 'row'), pairs)]
    another operation x2, other arithmetic: 0.14 us -> 2.69 us  [the longest x1 2.62 us: key_values_of(): mine = jnp.stack(held)]
  transfers between devices with their start and end apart: 40 -> 36, of which waited for: 26 -> 22; matrix products, arithmetic and copies ran while one was open for 8% -> 14% of each run, Pallas kernels for 27% -> 1%
where the time goes in v3:
time: 184 us; the launch traced here: 183 us
  waiting for transfers between devices  84.5 us (46%)
  starting transfers between devices  45.4 us (25%)
  matrix products  18.9 us (10%)
  local copies, waits for them, and re-layouts  16.3 us (9%)
  other arithmetic  14.1 us (8%)
  Pallas kernels  2.89 us (2%)
    ppermute x32, waiting for transfers between devices, swapped(): return lax.ppermute(value, axis, pairs)  60.5 us
    ppermute x32, starting transfers between devices, swapped(): return lax.ppermute(value, axis, pairs)  36.4 us
    ppermute x4, waiting for transfers between devices, to_tile(): return lax.ppermute(value, ('groups', 'row'), pairs)  24 us
    unnamed x65, local copies, waits for them, and re-layouts  9.24 us
    ppermute x4, starting transfers between devices, to_tile(): return lax.ppermute(value, ('groups', 'row'), pairs)  9.03 us
    squeeze x3, other arithmetic, key_values_of(): half[inner]  5.86 us
    dot_general x4, matrix products, key_values_of(): lax.dot_general(tokens, weight, (((1,), (0,)), ((), ())), preferred_eleme...  5.82 us
    dot_general x2, matrix products, on_device(): lax.dot_general(scaled, query_weight[section, 0], (((0,), (0,)), ((), ())...  5.69 us
  transfers between devices with their start and end apart: 36, of which 22 were waited for; matrix products, arithmetic and copies ran while one was open for 14% of the time, Pallas kernels for 1%

profile of v3, /device:TPU:0, one launch (start us, length us, event | category | flops | bytes accessed | tf_op | source)
XLA Modules:
  0.0 183.1 jit_solution(17588226617158624790)
XLA Ops:
  3.2 1.4 norm_hidden.1
  4.6 4.0 %collective-permute-start.2 = (bf16[160,1280]{1,0:T(8,128)(2,1)S(1)}, bf16[160,1280]{1,0:T(8,128)(2,1)}, u32[]{:S(2)}, u32[]{:S(2)}) collective-permute-start(bf16[160,1280]{1,0:T(8,128)(2,1)S(1)} %get-tuple-element.20), channel_id=1, source_target_pairs={{0,6},{1,7},{2,4},{3,5},{4,2},{5,3},{6,0},{7,1},{8,14},{9,15},{10,... | collective-permute-start | bytes 1228808 | tf_op jit(solution)/shard_map/ppermute | solution.py:25
  10.7 1.5 arrange_weight.1
  12.1 2.9 %collective-permute-start.16 = (bf16[1,320,256]{2,1,0:T(8,128)(2,1)}, bf16[1,320,256]{2,1,0:T(8,128)(2,1)}, u32[]{:S(2)}, u32[]{:S(2)}) collective-permute-start(bf16[1,320,256]{2,1,0:T(8,128)(2,1)} %get-tuple-element.28), channel_id=1, source_target_pairs={{0,8},{1,9},{2,10},{3,11},{4,12},{5,13},{6,14},{7,15},{8,0},{9,1},... | collective-permute-start | bytes 491528 | tf_op jit(solution)/shard_map/ppermute | solution.py:167
  17.2 13.7 %collective-permute-done.16 = bf16[1,320,256]{2,1,0:T(8,128)(2,1)} collective-permute-done((bf16[1,320,256]{2,1,0:T(8,128)(2,1)}, bf16[1,320,256]{2,1,0:T(8,128)(2,1)}, u32[]{:S(2)}, u32[]{:S(2)}) %collective-permute-start.16) | collective-permute-done | bytes 163872 | tf_op jit(solution)/shard_map/ppermute | solution.py:167
  30.9 1.5 collective-permute-start.17
  33.2 1.5 collective-permute-start.14
  35.5 2.4 %collective-permute-done.17 = bf16[1,320,256]{2,1,0:T(8,128)(2,1)S(1)} collective-permute-done((bf16[1,320,256]{2,1,0:T(8,128)(2,1)}, bf16[1,320,256]{2,1,0:T(8,128)(2,1)S(1)}, u32[]{:S(2)}, u32[]{:S(2)}) %collective-permute-start.17) | collective-permute-done | bytes 163872 | tf_op jit(solution)/shard_map/ppermute | solution.py:25
  37.9 3.6 %collective-permute-start.3 = (bf16[1,320,256]{2,1,0:T(8,128)(2,1)S(1)}, bf16[1,320,256]{2,1,0:T(8,128)(2,1)}, u32[]{:S(2)}, u32[]{:S(2)}) collective-permute-start(bf16[1,320,256]{2,1,0:T(8,128)(2,1)S(1)} %get-tuple-element.21), channel_id=1, source_target_pairs={{0,8},{1,9},{2,10},{3,11},{4,12},{5,13},{6,14},{7,15},{8,0},{9,1},... | collective-permute-start | bytes 491528 | tf_op jit(solution)/shard_map/ppermute | solution.py:167
  41.6 2.4 %collective-permute-start.10 = (bf16[1,320,256]{2,1,0:T(8,128)(2,1)S(1)}, bf16[1,320,256]{2,1,0:T(8,128)(2,1)}, u32[]{:S(2)}, u32[]{:S(2)}) collective-permute-start(bf16[1,320,256]{2,1,0:T(8,128)(2,1)S(1)} %get-tuple-element.26), channel_id=1, source_target_pairs={{0,8},{1,9},{2,10},{3,11},{4,12},{5,13},{6,14},{7,15},{8,0},{9,1},... | collective-permute-start | bytes 491528 | tf_op jit(solution)/shard_map/ppermute | solution.py:167
  44.0 1.9 %select_bitcast_fusion.3 = (bf16[320,256]{1,0:T(8,128)(2,1)}, bf16[320,256]{1,0:T(8,128)(2,1)}, bf16[320,256]{1,0:T(8,128)(2,1)}, bf16[320,256]{1,0:T(8,128)(2,1)}) fusion(pred[]{:T(512)S(6)} %eq.25, bf16[1,320,256]{2,1,0:T(8,128)(2,1)} %collective-permute-done.16, bf16[1,320,256]{2,1,0:T(8,128)(2,1)S(1)} %collective-permute-done.17, pred[]{:T(512)S(6)} %eq.28, ...), kind=kLoop, calls=%fused_computation.130 | loop fusion | flops 655360 | bytes 1310722 | tf_op jit(solution)/shard_map/squeeze | solution.py:211
  45.9 9.5 %collective-permute-done.10 = bf16[1,320,256]{2,1,0:T(8,128)(2,1)} collective-permute-done((bf16[1,320,256]{2,1,0:T(8,128)(2,1)S(1)}, bf16[1,320,256]{2,1,0:T(8,128)(2,1)}, u32[]{:S(2)}, u32[]{:S(2)}) %collective-permute-start.10) | collective-permute-done | bytes 163872 | tf_op jit(solution)/shard_map/ppermute | solution.py:167
  55.4 1.6 collective-permute-start.11
  56.9 2.6 %pad_maximum_fusion = bf16[4,160,1280]{2,1,0:T(8,128)(2,1)} fusion(bf16[1,160,1280]{2,1,0:T(8,128)(2,1)} %bitcast.22, bf16[1,160,1280]{2,1,0:T(8,128)(2,1)} %bitcast.21, bf16[1,160,1280]{2,1,0:T(8,128)(2,1)} %bitcast.20, bf16[1,160,1280]{2,1,0:T(8,128)(2,1)S(1)} %bitcast.255), kind=kLoop, calls=%fused_computation.18 | loop fusion | flops 2457600 | bytes 3276800 | tf_op jit(solution)/shard_map/stack | solution.py:184
  63.3 1.4 broadcast_select_fusion.26
  66.8 2.0 %select_bitcast_fusion.11 = (bf16[320,256]{1,0:T(8,128)(2,1)}, bf16[320,256]{1,0:T(8,128)(2,1)}, bf16[320,256]{1,0:T(8,128)(2,1)}, bf16[320,256]{1,0:T(8,128)(2,1)}) fusion(pred[]{:T(512)S(6)} %eq.25, bf16[1,320,256]{2,1,0:T(8,128)(2,1)} %collective-permute-done.10, bf16[1,320,256]{2,1,0:T(8,128)(2,1)} %collective-permute-done.11, pred[]{:T(512)S(6)} %eq.28, ...), kind=kLoop, calls=%fused_computation.138 | loop fusion | flops 655360 | bytes 1310722 | tf_op jit(solution)/shard_map/squeeze | solution.py:211
  68.8 2.0 %select_bitcast_fusion.5 = (bf16[320,256]{1,0:T(8,128)(2,1)S(1)}, bf16[320,256]{1,0:T(8,128)(2,1)}, bf16[320,256]{1,0:T(8,128)(2,1)S(1)}, bf16[320,256]{1,0:T(8,...) fusion(pred[]{:T(512)S(6)} %eq.25, ...), kind=kLoop, calls=%fused_computation.132 | loop fusion | flops 655360 | bytes 2621441 | tf_op jit(solution)/shard_map/squeeze | solution.py:211
  72.0 2.9 %fusion.98 = (bf16[128,640]{1,0:T(8,128)(2,1)S(1)}, f32[128,640]{1,0:T(8,128)S(1)}) fusion(bf16[2560,128]{1,0:T(8,128)(2,1)S(1)} %bitcast.266, bf16[2,1,2560,640]{3,2,1,0:T(8,128)(2,1)} %param.13), kind=kOutput, calls=%fused_computation.217 | convolution fusion | flops 419512320 | bytes 4423680 | tf_op jit(solution)/shard_map/dot_general | solution.py:288
  75.0 2.9 %collective-permute-start.6 = (bf16[128]{0:T(256)(128)(2,1)S(1)}, bf16[128]{0:T(256)(128)(2,1)S(1)}, u32[]{:S(2)}, u32[]{:S(2)}) collective-permute-start(bf16[128]{0:T(256)(128)(2,1)S(1)} %convert_element_type.218), channel_id=1, source_target_pairs={{0,8},{1,9},{2,10},{3,11},{4,12},{5,13},{6,14},{7,15},{8,0},{9,1},... | collective-permute-start | bytes 776 | tf_op jit(solution)/shard_map/ppermute | solution.py:25
  78.1 1.6 convolution_convert_fusion.2
  79.7 1.7 convolution_convert_fusion.1
  81.4 1.5 collective-permute-start.12
  82.9 1.7 convolution_convert_fusion
  84.5 2.0 %collective-permute-start.15 = (bf16[1024,256]{1,0:T(8,128)(2,1)}, bf16[1024,256]{1,0:T(8,128)(2,1)S(1)}, u32[]{:S(2)}, u32[]{:S(2)}) collective-permute-start(bf16[1024,256]{1,0:T(8,128)(2,1)} %convolution_convert_fusion), channel_id=1, source_target_pairs={{0,4},{1,5},{2,6},{3,7},{4,0},{5,1},{6,2},{7,3},{8,12},{9,13},{10,... | collective-permute-start | bytes 1572872 | tf_op jit(solution)/shard_map/ppermute | solution.py:25
  86.8 9.6 %collective-permute-done.9 = bf16[1024,256]{1,0:T(8,128)(2,1)S(1)} collective-permute-done((bf16[1024,256]{1,0:T(8,128)(2,1)}, bf16[1024,256]{1,0:T(8,128)(2,1)S(1)}, u32[]{:S(2)}, u32[]{:S(2)}) %collective-permute-start.9) | collective-permute-done | bytes 524320 | tf_op jit(solution)/shard_map/ppermute | solution.py:25
  96.6 9.5 %collective-permute-done.12 = bf16[1024,256]{1,0:T(8,128)(2,1)S(1)} collective-permute-done((bf16[1024,256]{1,0:T(8,128)(2,1)}, bf16[1024,256]{1,0:T(8,128)(2,1)S(1)}, u32[]{:S(2)}, u32[]{:S(2)}) %collective-permute-start.12) | collective-permute-done | bytes 524320 | tf_op jit(solution)/shard_map/ppermute | solution.py:25
  106.1 1.5 collective-permute-done.15
  112.7 3.0 %collective-permute-start.18 = (bf16[128,640]{0,1:T(8,128)(2,1)S(1)}, bf16[128,640]{0,1:T(8,128)(2,1)S(1)}, u32[]{:S(2)}, u32[]{:S(2)}) collective-permute-start(bf16[128,640]{0,1:T(8,128)(2,1)S(1)} %bitcast_convert_fusion.1), channel_id=1, source_target_pairs={{0,8},{1,9},{2,10},{3,11},{4,12},{5,13},{6,14},{7,15},{8,0},{9,1},... | collective-permute-start | bytes 491528 | tf_op jit(solution)/shard_map/ppermute | solution.py:25
  115.6 1.5 collective-permute-done.19
  117.1 6.2 %collective-permute-done.18 = bf16[128,640]{0,1:T(8,128)(2,1)S(1)} collective-permute-done((bf16[128,640]{0,1:T(8,128)(2,1)S(1)}, bf16[128,640]{0,1:T(8,128)(2,1)S(1)}, u32[]{:S(2)}, u32[]{:S(2)}) %collective-permute-start.18) | collective-permute-done | bytes 163872 | tf_op jit(solution)/shard_map/ppermute | solution.py:25
  125.3 1.6 collective-permute-done.20
  127.1 2.0 %collective-permute-start.22 = (bf16[320,128]{1,0:T(8,128)(2,1)S(1)}, bf16[320,128]{1,0:T(8,128)(2,1)S(1)}, u32[]{:S(2)}, u32[]{:S(2)}) collective-permute-start(bf16[320,128]{1,0:T(8,128)(2,1)S(1)} %get-tuple-element.56), channel_id=1, source_target_pairs={{0,4},{1,5},{2,6},{3,7},{4,0},{5,1},{6,2},{7,3},{8,12},{9,13},{10,... | collective-permute-start | bytes 245768 | tf_op jit(solution)/shard_map/ppermute | solution.py:25
  129.1 1.5 collective-permute-start.21
  130.6 2.7 %collective-permute-done.23 = bf16[320,128]{1,0:T(8,128)(2,1)S(1)} collective-permute-done((bf16[320,128]{1,0:T(8,128)(2,1)S(1)}, bf16[320,128]{1,0:T(8,128)(2,1)S(1)}, u32[]{:S(2)}, u32[]{:S(2)}) %collective-permute-start.23) | collective-permute-done | bytes 81952 | tf_op jit(solution)/shard_map/ppermute | solution.py:25
  134.7 2.0 %collective-permute-start.25 = (bf16[320,128]{1,0:T(8,128)(2,1)S(1)}, bf16[320,128]{1,0:T(8,128)(2,1)S(1)}, u32[]{:S(2)}, u32[]{:S(2)}) collective-permute-start(bf16[320,128]{1,0:T(8,128)(2,1)S(1)} %fusion.76), channel_id=1, source_target_pairs={{0,4},{1,5},{2,6},{3,7},{4,0},{5,1},{6,2},{7,3},{8,12},{9,13},{10,... | collective-permute-start | bytes 245768 | tf_op jit(solution)/shard_map/ppermute | solution.py:25
  137.9 2.2 %collective-permute-done.24 = bf16[320,128]{1,0:T(8,128)(2,1)S(1)} collective-permute-done((bf16[320,128]{1,0:T(8,128)(2,1)S(1)}, bf16[320,128]{1,0:T(8,128)(2,1)S(1)}, u32[]{:S(2)}, u32[]{:S(2)}) %collective-permute-start.24) | collective-permute-done | bytes 81952 | tf_op jit(solution)/shard_map/ppermute | solution.py:25
  141.3 1.5 collective-permute-done.27
  143.8 2.8 %fusion.99 = (bf16[128,640]{1,0:T(8,128)(2,1)S(1)}, f32[128,640]{1,0:T(8,128)S(1)}) fusion(bf16[2560,128]{1,0:T(8,128)(2,1)S(1)} %bitcast.265, bf16[2,1,2560,640]{3,2,1,0:T(8,128)(2,1)} %param.13), kind=kOutput, calls=%fused_computation.218 | convolution fusion | flops 419512320 | bytes 4423680 | tf_op jit(solution)/shard_map/dot_general | solution.py:288
  146.6 2.7 %collective-permute-start.28 = (bf16[128,640]{1,0:T(8,128)(2,1)S(1)}, bf16[128,640]{1,0:T(8,128)(2,1)S(1)}, u32[]{:S(2)}, u32[]{:S(2)}) collective-permute-start(bf16[128,640]{1,0:T(8,128)(2,1)S(1)} %get-tuple-element.89), channel_id=1, source_target_pairs={{0,8},{1,9},{2,10},{3,11},{4,12},{5,13},{6,14},{7,15},{8,0},{9,1},... | collective-permute-start | bytes 491528 | tf_op jit(solution)/shard_map/ppermute | solution.py:25
  149.3 7.8 %collective-permute-done.28 = bf16[128,640]{1,0:T(8,128)(2,1)S(1)} collective-permute-done((bf16[128,640]{1,0:T(8,128)(2,1)S(1)}, bf16[128,640]{1,0:T(8,128)(2,1)S(1)}, u32[]{:S(2)}, u32[]{:S(2)}) %collective-permute-start.28) | collective-permute-done | bytes 163872 | tf_op jit(solution)/shard_map/ppermute | solution.py:25
  159.4 3.0 %collective-permute-start.30 = (bf16[128,640]{0,1:T(8,128)(2,1)S(1)}, bf16[128,640]{0,1:T(8,128)(2,1)S(1)}, u32[]{:S(2)}, u32[]{:S(2)}) collective-permute-start(bf16[128,640]{0,1:T(8,128)(2,1)S(1)} %bitcast_convert_fusion), channel_id=1, source_target_pairs={{0,8},{1,9},{2,10},{3,11},{4,12},{5,13},{6,14},{7,15},{8,0},{9,1},... | collective-permute-start | bytes 491528 | tf_op jit(solution)/shard_map/ppermute | solution.py:25
  162.4 1.7 collective-permute-done.31
  164.1 5.0 %collective-permute-done.30 = bf16[128,640]{0,1:T(8,128)(2,1)S(1)} collective-permute-done((bf16[128,640]{0,1:T(8,128)(2,1)S(1)}, bf16[128,640]{0,1:T(8,128)(2,1)S(1)}, u32[]{:S(2)}, u32[]{:S(2)}) %collective-permute-start.30) | collective-permute-done | bytes 163872 | tf_op jit(solution)/shard_map/ppermute | solution.py:25
  169.1 2.3 %convolution_bitcast_fusion = f32[2560,128]{0,1:T(8,128)} fusion(bf16[128,640]{0,1:T(8,128)(2,1)S(1)} %fusion.65, bf16[2,1,2560,640]{3,2,1,0:T(8,128)(2,1)S(1)} %bitcast.264), kind=kOutput, calls=%fused_computation | convolution fusion | flops 419430400 | bytes 4751360 | tf_op jit(solution)/shard_map/dot_general | solution.py:303
  171.4 1.7 copy.38
  173.3 1.6 collective-permute-done.32
  175.1 2.7 %collective-permute-start.34 = (bf16[320,128]{1,0:T(8,128)(2,1)S(1)}, bf16[320,128]{1,0:T(8,128)(2,1)S(1)}, u32[]{:S(2)}, u32[]{:S(2)}) collective-permute-start(bf16[320,128]{1,0:T(8,128)(2,1)S(1)} %get-tuple-element.49), channel_id=1, source_target_pairs={{0,4},{1,5},{2,6},{3,7},{4,0},{5,1},{6,2},{7,3},{8,12},{9,13},{10,... | collective-permute-start | bytes 245768 | tf_op jit(solution)/shard_map/ppermute | solution.py:25
  178.6 2.7 %collective-permute-done.35 = bf16[320,128]{1,0:T(8,128)(2,1)S(1)} collective-permute-done((bf16[320,128]{1,0:T(8,128)(2,1)S(1)}, bf16[320,128]{1,0:T(8,128)(2,1)S(1)}, u32[]{:S(2)}, u32[]{:S(2)}) %collective-permute-start.35) | collective-permute-done | bytes 81952 | tf_op jit(solution)/shard_map/ppermute | solution.py:25
  (176 shorter events, 33.3 us)
Async XLA Ops:
  0.0 15.3 %copy-start.21 = (s32[2,2]{1,0:T(2,128)S(1)}, s32[2,2]{1,0:T(2,128)}, u32[]{:S(2)}) copy-start(s32[2,2]{1,0:T(2,128)} %param.15) | copy-start | bytes 52
  0.0 16.3 %copy-start.20 = (f32[2,5120]{1,0:T(2,128)S(1)}, f32[2,5120]{1,0:T(2,128)}, u32[]{:S(2)}) copy-start(f32[2,5120]{1,0:T(2,128)} %param.12) | copy-start | bytes 122884
  4.6 50.8 %collective-permute-start.2 = (bf16[160,1280]{1,0:T(8,128)(2,1)S(1)}, bf16[160,1280]{1,0:T(8,128)(2,1)}, u32[]{:S(2)}, u32[]{:S(2)}) collective-permute-start(bf16[160,1280]{1,0:T(8,128)(2,1)S(1)} %get-tuple-element.20), channel_id=1, source_target_pairs={{0,6},{1,7},{2,4},{3,5},{4,2},{5,3},{6,0},{7,1},{8,14},{9,15},{10,... | collective-permute-start | bytes 1228808 | tf_op jit(solution)/shard_map/ppermute | solution.py:25
  8.6 48.3 %collective-permute-start.1 = (bf16[160,1280]{1,0:T(8,128)(2,1)S(1)}, bf16[160,1280]{1,0:T(8,128)(2,1)}, u32[]{:S(2)}, u32[]{:S(2)}) collective-permute-start(bf16[160,1280]{1,0:T(8,128)(2,1)S(1)} %get-tuple-element.19), channel_id=1, source_target_pairs={{0,4},{1,5},{2,6},{3,7},{4,0},{5,1},{6,2},{7,3},{8,12},{9,13},{10,... | collective-permute-start | bytes 1228808 | tf_op jit(solution)/shard_map/ppermute | solution.py:25
  9.0 47.9 %collective-permute-start = (bf16[160,1280]{1,0:T(8,128)(2,1)S(1)}, bf16[160,1280]{1,0:T(8,128)(2,1)}, u32[]{:S(2)}, u32[]{:S(2)}) collective-permute-start(bf16[160,1280]{1,0:T(8,128)(2,1)S(1)} %get-tuple-element.18), channel_id=1, source_target_pairs={{0,2},{1,3},{2,0},{3,1},{4,6},{5,7},{6,4},{7,5},{8,10},{9,11},{10,... | collective-permute-start | bytes 1228808 | tf_op jit(solution)/shard_map/ppermute | solution.py:25
  12.1 18.8 %collective-permute-start.16 = (bf16[1,320,256]{2,1,0:T(8,128)(2,1)}, bf16[1,320,256]{2,1,0:T(8,128)(2,1)}, u32[]{:S(2)}, u32[]{:S(2)}) collective-permute-start(bf16[1,320,256]{2,1,0:T(8,128)(2,1)} %get-tuple-element.28), channel_id=1, source_target_pairs={{0,8},{1,9},{2,10},{3,11},{4,12},{5,13},{6,14},{7,15},{8,0},{9,1},... | collective-permute-start | bytes 491528 | tf_op jit(solution)/shard_map/ppermute | solution.py:167
  15.1 18.1 %collective-permute-start.13 = (bf16[1,320,256]{2,1,0:T(8,128)(2,1)S(1)}, bf16[1,320,256]{2,1,0:T(8,128)(2,1)}, u32[]{:S(2)}, u32[]{:S(2)}) collective-permute-start(bf16[1,320,256]{2,1,0:T(8,128)(2,1)S(1)} %get-tuple-element.27), channel_id=1, source_target_pairs={{0,8},{1,9},{2,10},{3,11},{4,12},{5,13},{6,14},{7,15},{8,0},{9,1},... | collective-permute-start | bytes 491528 | tf_op jit(solution)/shard_map/ppermute | solution.py:167
  30.9 7.0 %collective-permute-start.17 = (bf16[1,320,256]{2,1,0:T(8,128)(2,1)}, bf16[1,320,256]{2,1,0:T(8,128)(2,1)S(1)}, u32[]{:S(2)}, u32[]{:S(2)}) collective-permute-start(bf16[1,320,256]{2,1,0:T(8,128)(2,1)} %collective-permute-done.16), channel_id=1, source_target_pairs={{0,16},{16,0},{1,17},{17,1},{2,18},{18,2},{3,19},{19,3},{4,20},{20... | collective-permute-start | bytes 491528 | tf_op jit(solution)/shard_map/ppermute | solution.py:25
  33.2 8.4 %collective-permute-start.14 = (bf16[1,320,256]{2,1,0:T(8,128)(2,1)}, bf16[1,320,256]{2,1,0:T(8,128)(2,1)S(1)}, u32[]{:S(2)}, u32[]{:S(2)}) collective-permute-start(bf16[1,320,256]{2,1,0:T(8,128)(2,1)} %collective-permute-done.13), channel_id=1, source_target_pairs={{0,16},{16,0},{1,17},{17,1},{2,18},{18,2},{3,19},{19,3},{4,20},{20... | collective-permute-start | bytes 491528 | tf_op jit(solution)/shard_map/ppermute | solution.py:25
  37.9 21.6 %collective-permute-start.3 = (bf16[1,320,256]{2,1,0:T(8,128)(2,1)S(1)}, bf16[1,320,256]{2,1,0:T(8,128)(2,1)}, u32[]{:S(2)}, u32[]{:S(2)}) collective-permute-start(bf16[1,320,256]{2,1,0:T(8,128)(2,1)S(1)} %get-tuple-element.21), channel_id=1, source_target_pairs={{0,8},{1,9},{2,10},{3,11},{4,12},{5,13},{6,14},{7,15},{8,0},{9,1},... | collective-permute-start | bytes 491528 | tf_op jit(solution)/shard_map/ppermute | solution.py:167
  41.6 13.8 %collective-permute-start.10 = (bf16[1,320,256]{2,1,0:T(8,128)(2,1)S(1)}, bf16[1,320,256]{2,1,0:T(8,128)(2,1)}, u32[]{:S(2)}, u32[]{:S(2)}) collective-permute-start(bf16[1,320,256]{2,1,0:T(8,128)(2,1)S(1)} %get-tuple-element.26), channel_id=1, source_target_pairs={{0,8},{1,9},{2,10},{3,11},{4,12},{5,13},{6,14},{7,15},{8,0},{9,1},... | collective-permute-start | bytes 491528 | tf_op jit(solution)/shard_map/ppermute | solution.py:167
  55.4 13.5 %collective-permute-start.7 = (bf16[4,320,256]{2,1,0:T(8,128)(2,1)S(1)}, bf16[4,320,256]{2,1,0:T(8,128)(2,1)}, u32[]{:S(2)}, u32[]{:S(2)}) collective-permute-start(bf16[4,320,256]{2,1,0:T(8,128)(2,1)S(1)} %get-tuple-element.24), channel_id=1, source_target_pairs={{0,1},{1,0},{2,3},{3,2},{4,5},{5,4},{6,7},{7,6},{8,9},{9,8},{10,11... | collective-permute-start | bytes 1966088 | tf_op jit(solution)/shard_map/ppermute | solution.py:25
  55.4 11.4 %collective-permute-start.11 = (bf16[1,320,256]{2,1,0:T(8,128)(2,1)}, bf16[1,320,256]{2,1,0:T(8,128)(2,1)}, u32[]{:S(2)}, u32[]{:S(2)}) collective-permute-start(bf16[1,320,256]{2,1,0:T(8,128)(2,1)} %collective-permute-done.10), channel_id=1, source_target_pairs={{0,16},{16,0},{1,17},{17,1},{2,18},{18,2},{3,19},{19,3},{4,20},{20... | collective-permute-start | bytes 491528 | tf_op jit(solution)/shard_map/ppermute | solution.py:25
  59.6 11.2 %collective-permute-start.4 = (bf16[4,160,1280]{2,1,0:T(8,128)(2,1)}, bf16[4,160,1280]{2,1,0:T(8,128)(2,1)S(1)}, u32[]{:S(2)}, u32[]{:S(2)}) collective-permute-start(bf16[4,160,1280]{2,1,0:T(8,128)(2,1)} %pad_maximum_fusion), channel_id=1, source_target_pairs={{0,1},{1,0},{2,3},{3,2},{4,5},{5,4},{6,7},{7,6},{8,9},{9,8},{10,11... | collective-permute-start | bytes 4915208 | tf_op jit(solution)/shard_map/ppermute | solution.py:25
  59.8 7.0 %collective-permute-start.8 = (bf16[1,320,256]{2,1,0:T(8,128)(2,1)}, bf16[1,320,256]{2,1,0:T(8,128)(2,1)}, u32[]{:S(2)}, u32[]{:S(2)}) collective-permute-start(bf16[1,320,256]{2,1,0:T(8,128)(2,1)} %collective-permute-done.3), channel_id=1, source_target_pairs={{0,16},{16,0},{1,17},{17,1},{2,18},{18,2},{3,19},{19,3},{4,20},{20... | collective-permute-start | bytes 491528 | tf_op jit(solution)/shard_map/ppermute | solution.py:25
  71.5 6.4 %copy-start.17 = (bf16[1024,1280]{1,0:T(8,128)(2,1)S(1)}, bf16[1024,1280]{1,0:T(8,128)(2,1)}, u32[]{:S(2)}) copy-start(bf16[1024,1280]{1,0:T(8,128)(2,1)} %copy-done.16) | copy-start | bytes 7864324
  71.9 6.1 %copy-start.5 = (bf16[320,256]{1,0:T(8,128)(2,1)S(1)}, bf16[320,256]{1,0:T(8,128)(2,1)}, u32[]{:S(2)}) copy-start(bf16[320,256]{1,0:T(8,128)(2,1)} %get-tuple-element.40) | copy-start | bytes 491524
  71.9 6.1 %copy-start.6 = (bf16[320,256]{1,0:T(8,128)(2,1)S(1)}, bf16[320,256]{1,0:T(8,128)(2,1)}, u32[]{:S(2)}) copy-start(bf16[320,256]{1,0:T(8,128)(2,1)} %get-tuple-element.46) | copy-start | bytes 491524
  71.9 6.1 %copy-start.13 = (bf16[320,256]{1,0:T(8,128)(2,1)S(1)}, bf16[320,256]{1,0:T(8,128)(2,1)}, u32[]{:S(2)}) copy-start(bf16[320,256]{1,0:T(8,128)(2,1)} %get-tuple-element.95) | copy-start | bytes 491524
  74.9 11.7 %collective-permute-start.5 = (bf16[128,640]{1,0:T(8,128)(2,1)S(1)}, bf16[128,640]{1,0:T(8,128)(2,1)S(1)}, u32[]{:S(2)}, u32[]{:S(2)}) collective-permute-start(bf16[128,640]{1,0:T(8,128)(2,1)S(1)} %get-tuple-element.85), channel_id=1, source_target_pairs={{0,8},{1,9},{2,10},{3,11},{4,12},{5,13},{6,14},{7,15},{8,0},{9,1},... | collective-permute-start | bytes 491528 | tf_op jit(solution)/shard_map/ppermute | solution.py:25
  75.0 11.6 %collective-permute-start.6 = (bf16[128]{0:T(256)(128)(2,1)S(1)}, bf16[128]{0:T(256)(128)(2,1)S(1)}, u32[]{:S(2)}, u32[]{:S(2)}) collective-permute-start(bf16[128]{0:T(256)(128)(2,1)S(1)} %convert_element_type.218), channel_id=1, source_target_pairs={{0,8},{1,9},{2,10},{3,11},{4,12},{5,13},{6,14},{7,15},{8,0},{9,1},... | collective-permute-start | bytes 776 | tf_op jit(solution)/shard_map/ppermute | solution.py:25
  78.0 6.6 %copy-start.18 = (bf16[1024,1280]{1,0:T(8,128)(2,1)}, bf16[1024,1280]{1,0:T(8,128)(2,1)S(1)}, u32[]{:S(2)}) copy-start(bf16[1024,1280]{1,0:T(8,128)(2,1)S(1)} %fusion.61) | copy-start | bytes 7864324
  79.7 16.8 %collective-permute-start.9 = (bf16[1024,256]{1,0:T(8,128)(2,1)}, bf16[1024,256]{1,0:T(8,128)(2,1)S(1)}, u32[]{:S(2)}, u32[]{:S(2)}) collective-permute-start(bf16[1024,256]{1,0:T(8,128)(2,1)} %convolution_convert_fusion.2), channel_id=1, source_target_pairs={{0,6},{1,7},{2,4},{3,5},{4,2},{5,3},{6,0},{7,1},{8,14},{9,15},{10,... | collective-permute-start | bytes 1572872 | tf_op jit(solution)/shard_map/ppermute | solution.py:25
  81.4 24.6 %collective-permute-start.12 = (bf16[1024,256]{1,0:T(8,128)(2,1)}, bf16[1024,256]{1,0:T(8,128)(2,1)S(1)}, u32[]{:S(2)}, u32[]{:S(2)}) collective-permute-start(bf16[1024,256]{1,0:T(8,128)(2,1)} %convolution_convert_fusion.1), channel_id=1, source_target_pairs={{0,2},{1,3},{2,0},{3,1},{4,6},{5,7},{6,4},{7,5},{8,10},{9,11},{10,... | collective-permute-start | bytes 1572872 | tf_op jit(solution)/shard_map/ppermute | solution.py:25
  84.5 23.1 %collective-permute-start.15 = (bf16[1024,256]{1,0:T(8,128)(2,1)}, bf16[1024,256]{1,0:T(8,128)(2,1)S(1)}, u32[]{:S(2)}, u32[]{:S(2)}) collective-permute-start(bf16[1024,256]{1,0:T(8,128)(2,1)} %convolution_convert_fusion), channel_id=1, source_target_pairs={{0,4},{1,5},{2,6},{3,7},{4,0},{5,1},{6,2},{7,3},{8,12},{9,13},{10,... | collective-permute-start | bytes 1572872 | tf_op jit(solution)/shard_map/ppermute | solution.py:25
  109.7 13.8 %slice-start = ((s8[6553600]{0:T(1024)(128)(4,1)}), s8[4194304]{0:T(1024)(128)(4,1)S(1)}, s32[]{:S(2)}) async-start(s8[6553600]{0:T(1024)(128)(4,1)} %bitcast.261), calls=%async_computation | async-start | bytes 8388608
  110.6 13.0 %slice-start.1 = ((s8[6553600]{0:T(1024)(128)(4,1)}), s8[2359296]{0:T(1024)(128)(4,1)S(1)}, s32[]{:S(2)}) async-start(s8[6553600]{0:T(1024)(128)(4,1)} %bitcast.261), calls=%async_computation.1 | async-start | bytes 4718592
  112.5 4.6 %collective-permute-start.19 = (bf16[128,5]{0,1:T(8,128)(2,1)S(1)}, bf16[128,5]{0,1:T(8,128)(2,1)S(1)}, u32[]{:S(2)}, u32[]{:S(2)}) collective-permute-start(bf16[128,5]{0,1:T(8,128)(2,1)S(1)} %convert_element_type.228), channel_id=1, source_target_pairs={{0,8},{1,9},{2,10},{3,11},{4,12},{5,13},{6,14},{7,15},{8,0},{9,1},... | collective-permute-start | bytes 3848 | tf_op jit(solution)/shard_map/ppermute | solution.py:25
  112.7 10.6 %collective-permute-start.18 = (bf16[128,640]{0,1:T(8,128)(2,1)S(1)}, bf16[128,640]{0,1:T(8,128)(2,1)S(1)}, u32[]{:S(2)}, u32[]{:S(2)}) collective-permute-start(bf16[128,640]{0,1:T(8,128)(2,1)S(1)} %bitcast_convert_fusion.1), channel_id=1, source_target_pairs={{0,8},{1,9},{2,10},{3,11},{4,12},{5,13},{6,14},{7,15},{8,0},{9,1},... | collective-permute-start | bytes 491528 | tf_op jit(solution)/shard_map/ppermute | solution.py:25
  124.7 9.5 %copy-start.3 = (bf16[320,128]{1,0:T(8,128)(2,1)S(1)}, bf16[320,128]{1,0:T(8,128)(2,1)}, u32[]{:S(2)}) copy-start(bf16[320,128]{1,0:T(8,128)(2,1)} %param.11) | copy-start | bytes 245764
  125.2 1.7 collective-permute-start.20
  127.0 6.3 %collective-permute-start.23 = (bf16[320,128]{1,0:T(8,128)(2,1)S(1)}, bf16[320,128]{1,0:T(8,128)(2,1)S(1)}, u32[]{:S(2)}, u32[]{:S(2)}) collective-permute-start(bf16[320,128]{1,0:T(8,128)(2,1)S(1)} %get-tuple-element.55), channel_id=1, source_target_pairs={{0,6},{1,7},{2,4},{3,5},{4,2},{5,3},{6,0},{7,1},{8,14},{9,15},{10,... | collective-permute-start | bytes 245768 | tf_op jit(solution)/shard_map/ppermute | solution.py:25
  127.1 6.2 %collective-permute-start.22 = (bf16[320,128]{1,0:T(8,128)(2,1)S(1)}, bf16[320,128]{1,0:T(8,128)(2,1)S(1)}, u32[]{:S(2)}, u32[]{:S(2)}) collective-permute-start(bf16[320,128]{1,0:T(8,128)(2,1)S(1)} %get-tuple-element.56), channel_id=1, source_target_pairs={{0,4},{1,5},{2,6},{3,7},{4,0},{5,1},{6,2},{7,3},{8,12},{9,13},{10,... | collective-permute-start | bytes 245768 | tf_op jit(solution)/shard_map/ppermute | solution.py:25
  129.1 5.1 %collective-permute-start.21 = (bf16[320,128]{1,0:T(8,128)(2,1)S(1)}, bf16[320,128]{1,0:T(8,128)(2,1)S(1)}, u32[]{:S(2)}, u32[]{:S(2)}) collective-permute-start(bf16[320,128]{1,0:T(8,128)(2,1)S(1)} %get-tuple-element.54), channel_id=1, source_target_pairs={{0,2},{1,3},{2,0},{3,1},{4,6},{5,7},{6,4},{7,5},{8,10},{9,11},{10,... | collective-permute-start | bytes 245768 | tf_op jit(solution)/shard_map/ppermute | solution.py:25
  134.3 5.8 %collective-permute-start.24 = (bf16[320,128]{1,0:T(8,128)(2,1)S(1)}, bf16[320,128]{1,0:T(8,128)(2,1)S(1)}, u32[]{:S(2)}, u32[]{:S(2)}) collective-permute-start(bf16[320,128]{1,0:T(8,128)(2,1)S(1)} %fusion.76), channel_id=1, source_target_pairs={{0,6},{1,7},{2,4},{3,5},{4,2},{5,3},{6,0},{7,1},{8,14},{9,15},{10,... | collective-permute-start | bytes 245768 | tf_op jit(solution)/shard_map/ppermute | solution.py:25
  134.7 5.4 %collective-permute-start.25 = (bf16[320,128]{1,0:T(8,128)(2,1)S(1)}, bf16[320,128]{1,0:T(8,128)(2,1)S(1)}, u32[]{:S(2)}, u32[]{:S(2)}) collective-permute-start(bf16[320,128]{1,0:T(8,128)(2,1)S(1)} %fusion.76), channel_id=1, source_target_pairs={{0,4},{1,5},{2,6},{3,7},{4,0},{5,1},{6,2},{7,3},{8,12},{9,13},{10,... | collective-permute-start | bytes 245768 | tf_op jit(solution)/shard_map/ppermute | solution.py:25
  136.6 4.4 %collective-permute-start.26 = (bf16[320,128]{1,0:T(8,128)(2,1)S(1)}, bf16[320,128]{1,0:T(8,128)(2,1)S(1)}, u32[]{:S(2)}, u32[]{:S(2)}) collective-permute-start(bf16[320,128]{1,0:T(8,128)(2,1)S(1)} %fusion.76), channel_id=1, source_target_pairs={{0,2},{1,3},{2,0},{3,1},{4,6},{5,7},{6,4},{7,5},{8,10},{9,11},{10,... | collective-permute-start | bytes 245768 | tf_op jit(solution)/shard_map/ppermute | solution.py:25
  141.2 1.7 collective-permute-start.27
  143.4 5.9 %collective-permute-start.29 = (bf16[128]{0:T(256)(128)(2,1)S(1)}, bf16[128]{0:T(256)(128)(2,1)S(1)}, u32[]{:S(2)}, u32[]{:S(2)}) collective-permute-start(bf16[128]{0:T(256)(128)(2,1)S(1)} %convert_element_type.250), channel_id=1, source_target_pairs={{0,8},{1,9},{2,10},{3,11},{4,12},{5,13},{6,14},{7,15},{8,0},{9,1},... | collective-permute-start | bytes 776 | tf_op jit(solution)/shard_map/ppermute | solution.py:25
  143.8 25.3 %slice-start.2 = ((s8[6553600]{0:T(1024)(128)(4,1)}), s8[2359296]{0:T(1024)(128)(4,1)S(1)}, s32[]{:S(2)}) async-start(s8[6553600]{0:T(1024)(128)(4,1)} %bitcast.263), calls=%async_computation.2 | async-start | bytes 4718592
  146.6 10.4 %collective-permute-start.28 = (bf16[128,640]{1,0:T(8,128)(2,1)S(1)}, bf16[128,640]{1,0:T(8,128)(2,1)S(1)}, u32[]{:S(2)}, u32[]{:S(2)}) collective-permute-start(bf16[128,640]{1,0:T(8,128)(2,1)S(1)} %get-tuple-element.89), channel_id=1, source_target_pairs={{0,8},{1,9},{2,10},{3,11},{4,12},{5,13},{6,14},{7,15},{8,0},{9,1},... | collective-permute-start | bytes 491528 | tf_op jit(solution)/shard_map/ppermute | solution.py:25
  157.3 11.8 %slice-start.3 = ((s8[6553600]{0:T(1024)(128)(4,1)}), s8[4194304]{0:T(1024)(128)(4,1)S(1)}, s32[]{:S(2)}) async-start(s8[6553600]{0:T(1024)(128)(4,1)} %bitcast.263), calls=%async_computation.3 | async-start | bytes 8388608
  159.3 4.8 %collective-permute-start.31 = (bf16[128,5]{0,1:T(8,128)(2,1)S(1)}, bf16[128,5]{0,1:T(8,128)(2,1)S(1)}, u32[]{:S(2)}, u32[]{:S(2)}) collective-permute-start(bf16[128,5]{0,1:T(8,128)(2,1)S(1)} %convert_element_type.256), channel_id=1, source_target_pairs={{0,8},{1,9},{2,10},{3,11},{4,12},{5,13},{6,14},{7,15},{8,0},{9,1},... | collective-permute-start | bytes 3848 | tf_op jit(solution)/shard_map/ppermute | solution.py:25
  159.4 9.6 %collective-permute-start.30 = (bf16[128,640]{0,1:T(8,128)(2,1)S(1)}, bf16[128,640]{0,1:T(8,128)(2,1)S(1)}, u32[]{:S(2)}, u32[]{:S(2)}) collective-permute-start(bf16[128,640]{0,1:T(8,128)(2,1)S(1)} %bitcast_convert_fusion), channel_id=1, source_target_pairs={{0,8},{1,9},{2,10},{3,11},{4,12},{5,13},{6,14},{7,15},{8,0},{9,1},... | collective-permute-start | bytes 491528 | tf_op jit(solution)/shard_map/ppermute | solution.py:25
  173.2 1.7 collective-permute-start.32
  175.1 6.3 %collective-permute-start.35 = (bf16[320,128]{1,0:T(8,128)(2,1)S(1)}, bf16[320,128]{1,0:T(8,128)(2,1)S(1)}, u32[]{:S(2)}, u32[]{:S(2)}) collective-permute-start(bf16[320,128]{1,0:T(8,128)(2,1)S(1)} %get-tuple-element.48), channel_id=1, source_target_pairs={{0,6},{1,7},{2,4},{3,5},{4,2},{5,3},{6,0},{7,1},{8,14},{9,15},{10,... | collective-permute-start | bytes 245768 | tf_op jit(solution)/shard_map/ppermute | solution.py:25
  175.1 6.9 %collective-permute-start.34 = (bf16[320,128]{1,0:T(8,128)(2,1)S(1)}, bf16[320,128]{1,0:T(8,128)(2,1)S(1)}, u32[]{:S(2)}, u32[]{:S(2)}) collective-permute-start(bf16[320,128]{1,0:T(8,128)(2,1)S(1)} %get-tuple-element.49), channel_id=1, source_target_pairs={{0,4},{1,5},{2,6},{3,7},{4,0},{5,1},{6,2},{7,3},{8,12},{9,13},{10,... | collective-permute-start | bytes 245768 | tf_op jit(solution)/shard_map/ppermute | solution.py:25
  177.8 4.6 %collective-permute-start.33 = (bf16[320,128]{1,0:T(8,128)(2,1)S(1)}, bf16[320,128]{1,0:T(8,128)(2,1)S(1)}, u32[]{:S(2)}, u32[]{:S(2)}) collective-permute-start(bf16[320,128]{1,0:T(8,128)(2,1)S(1)} %get-tuple-element.47), channel_id=1, source_target_pairs={{0,2},{1,3},{2,0},{3,1},{4,6},{5,7},{6,4},{7,5},{8,10},{9,11},{10,... | collective-permute-start | bytes 245768 | tf_op jit(solution)/shard_map/ppermute | solution.py:25
  (14 other events, 26.9 us)

commit v4 on v3

--- a/solution.py
+++ b/solution.py
@@ -17,7 +17,7 @@
 F32 = jnp.float32
 
 CHIPS = KVH // 2
-ROUNDS = ((3,), (1,), (2,), (0,))
+ROUNDS = ((1, 2), (3, 0))
 
 
 def swapped(value, mask, axis="row"):
@@ -131,6 +131,55 @@
     )(jnp.stack(blocks).astype(jnp.int32), hidden, gain[None, :], extra)
 
 
+def project_kernel(rows, first_ref, mine_ref, theirs_ref, *refs):
+    out_ref, weight = refs[-2:]
+    blocks = refs[:-2]
+    unit = blocks[0].shape[1]
+    for head in range(out_ref.shape[0]):
+        for tile in range(len(blocks) // 2):
+            base = 2 * unit * tile
+            first = pl.multiple_of(base + first_ref[tile] * unit, unit)
+            second = pl.multiple_of(base + (1 - first_ref[tile]) * unit, unit)
+            weight[pl.ds(first, unit), :] = blocks[2 * tile][head]
+            weight[pl.ds(second, unit), :] = blocks[2 * tile + 1][head]
+        for half, tokens_ref in enumerate((mine_ref, theirs_ref)):
+            tokens = tokens_ref[:, :rows, :].reshape(-1, tokens_ref.shape[2])
+            result = jnp.dot(tokens, weight[...], preferred_element_type=F32)
+            out_ref[head, half] = result.astype(BF16).reshape(out_ref.shape[2:])
+
+
+def projected(mine, theirs, blocks, rows):
+    heads, unit, pair = blocks[0][0].shape
+    depth = mine.shape[2]
+    shape = (heads, 2, CHIPS, rows, pair)
+    if unit % 16 or rows % 16:
+        ordered = [
+            jnp.where(first == 0, a, b) for one, two, first in blocks for a, b in ((one, two), (two, one))
+        ]
+        weight = jnp.concatenate(ordered, axis=1)
+        tokens = jnp.stack([mine[:, :rows], theirs[:, :rows]])
+        result = jnp.einsum("epsd,hdc->hepsc", tokens, weight, preferred_element_type=F32)
+        return list(result.astype(BF16))
+    vmem = pl.BlockSpec(memory_space=pltpu.VMEM)
+    pieces = [piece for one, two, _ in blocks for piece in (one, two)]
+    return list(
+        pl.pallas_call(
+            functools.partial(project_kernel, rows),
+            out_shape=jax.ShapeDtypeStruct(shape, BF16),
+            in_specs=[pl.BlockSpec(memory_space=pltpu.SMEM)] + [vmem] * (2 + len(pieces)),
+            out_specs=vmem,
+            scratch_shapes=[pltpu.VMEM((depth, pair), BF16)],
+            compiler_params=pltpu.CompilerParams(vmem_limit_bytes=40 * 1024 * 1024),
+            cost_estimate=pl.CostEstimate(
+                flops=2 * heads * 2 * CHIPS * rows * depth * pair,
+                bytes_accessed=4 * CHIPS * rows * depth,
+                transcendentals=0,
+            ),
+            name="project",
+        )(jnp.stack([first for _, _, first in blocks]).astype(jnp.int32), mine, theirs, *pieces)
+    )
+
+
 def in_order(ours, theirs, core):
     low, high = jnp.where(core == 0, ours, theirs), jnp.where(core == 0, theirs, ours)
     return jnp.stack([low, high], axis=1).reshape(-1, ours.shape[-1])
@@ -184,38 +233,28 @@
     mine = jnp.stack(held)
     mine, far[0] = lax.optimization_barrier((mine, far[0]))
     theirs = swapped(mine, 1)
-    tokens = jnp.concatenate([held[p][:rows] for p in range(CHIPS)] + [theirs[p, :rows] for p in range(CHIPS)])
-    ours, theirs = (
+    ours, others = (
         jnp.stack(natural([value[p, rows:].reshape(query_states.shape) for p in range(CHIPS)], chip))
         for value in (mine, theirs)
     )
-    stream = in_order(ours, theirs, core)
+    stream = in_order(ours, others, core)
 
     total = None
-    place_in_order = 0
+    done = 0
     for number, round_ in enumerate(ROUNDS):
-        span = slice(place_in_order, place_in_order + len(round_))
-        place_in_order += len(round_)
-        blocks = [(kept[span], traded[span])]
+        span = slice(done, done + len(round_))
+        done += len(round_)
+        blocks = [(kept[span], traded[span], core)]
         for j, value in enumerate(far[number], 1):
             if share:
-                other = swapped(value, 1, "groups")
-                blocks.append((jnp.where(part == 0, value, other), jnp.where(part == 0, other, value)))
+                blocks.append((value, swapped(value, 1, "groups"), core ^ part))
             else:
-                blocks.append((value, to_tile(traded[span], j, False)))
-        blocks = [
-            (jnp.where(core == 0, own, other), jnp.where(core == 0, other, own))
-            for own, other in blocks
-        ]
-        for inner, place in enumerate(round_):
-            weight = jnp.concatenate([half[inner] for block in blocks for half in block], axis=0)
-            partial = lax.dot_general(
-                tokens, weight, (((1,), (0,)), ((), ())), preferred_element_type=F32
-            )
+                blocks.append((value, to_tile(traded[span], j, False), core))
+        partials = projected(mine, theirs, blocks, rows)
+        for partial, place in zip(partials, round_):
             if place:
-                partial = swapped(partial.astype(BF16), 2 * place).astype(F32)
-            pieces = partial.reshape(2, CHIPS, rows, pair)
-            pieces = jnp.stack([pieces[:, j ^ place] for j in range(CHIPS)], axis=1)
+                partial = swapped(partial, 2 * place)
+            pieces = jnp.stack([partial[:, j ^ place] for j in range(CHIPS)], axis=1).astype(F32)
             total = pieces if total is None else total + pieces
     key_values = total.astype(BF16).reshape(2 * CHIPS * rows, pair)
     sources = jnp.stack(

time: 184 us -> 165 us (0.90)
  waiting for transfers between devices: 84.5 us -> 73.2 us
  other arithmetic: 14.1 us -> 6.72 us
  local copies, waits for them, and re-layouts: 16.3 us -> 23.1 us
  matrix products: 18.9 us -> 12.7 us
  starting transfers between devices: 45.4 us -> 39.5 us
  Pallas kernels: 2.89 us -> 8.54 us
    ppermute x4 -> x2, waiting for transfers between devices: 24 us -> 1.71 us  [to_tile(): return lax.ppermute(value, ('groups', 'row'), pairs)]
    ppermute x32 -> x30, waiting for transfers between devices: 60.5 us -> 71.5 us  [swapped(): return lax.ppermute(value, axis, pairs)]
    squeeze x3 -> x0, other arithmetic: 5.86 us -> none  [key_values_of(): half[inner]]
    dot_general x4 -> x0, matrix products: 5.82 us -> none  [key_values_of(): lax.dot_general(tokens, weight, (((1,), (0,)), ((), ())), preferred_eleme...]
    pallas_call x0 -> x2, Pallas kernels: none -> 5.34 us  [projected(): pl.pallas_call(functools.partial(project_kernel, rows), out_shape=jax.Sha...]
    ppermute x32 -> x30, starting transfers between devices: 36.4 us -> 33.4 us  [swapped(): return lax.ppermute(value, axis, pairs)]
    slice x3 -> x5, local copies, waits for them, and re-layouts: 0.27 us -> 3.21 us  [the longest x2 2 us: key_values_of(): blocks = [(kept[span], traded[span], core)]]
    ppermute x4 -> x2, starting transfers between devices: 9.03 us -> 6.09 us  [to_tile(): return lax.ppermute(value, ('groups', 'row'), pairs)]
  transfers between devices with their start and end apart: 36 -> 32, of which waited for: 22 -> 25; matrix products, arithmetic and copies ran while one was open for 14% -> 15% of each run, Pallas kernels for 1% -> 4%
where the time goes in v4:
time: 165 us; the launch traced here: 164 us
  waiting for transfers between devices  73.2 us (44%)
  starting transfers between devices  39.5 us (24%)
  local copies, waits for them, and re-layouts  23.1 us (14%)
  matrix products  12.7 us (8%)
  Pallas kernels  8.54 us (5%)
  other arithmetic  6.72 us (4%)
    ppermute x30, waiting for transfers between devices, swapped(): return lax.ppermute(value, axis, pairs)  71.5 us
    ppermute x30, starting transfers between devices, swapped(): return lax.ppermute(value, axis, pairs)  33.4 us
    unnamed x38, local copies, waits for them, and re-layouts  9.39 us
    ppermute x2, starting transfers between devices, to_tile(): return lax.ppermute(value, ('groups', 'row'), pairs)  6.09 us
    pallas_call x2, Pallas kernels, projected(): pl.pallas_call(functools.partial(project_kernel, rows), out_shape=jax.Sha...  5.34 us
    dot_general x2, matrix products, on_device(): lax.dot_general(scaled, query_weight[section, 0], (((0,), (0,)), ((), ())...  5.31 us
    another operation x9, local copies, waits for them, and re-layouts, key_values_of(): jnp.stack(natural([value[p, rows:].reshape(query_states.shape) for p in r...  3.77 us
    dot_general x2, matrix products, on_device(): lax.dot_general(output_weight[section, 0], attended, (((1,), (1,)), ((),...  3.52 us
  transfers between devices with their start and end apart: 32, of which 25 were waited for; matrix products, arithmetic and copies ran while one was open for 15% of the time, Pallas kernels for 4%

profile of v4, /device:TPU:0, one launch (start us, length us, event | category | flops | bytes accessed | tf_op | source)
XLA Modules:
  0.0 164.4 jit_solution(3050661395737268643)
XLA Ops:
  1.1 1.3 copy-done.2
  3.2 1.4 norm_hidden.1
  4.6 3.0 %collective-permute-start = (bf16[160,1280]{1,0:T(8,128)(2,1)S(1)}, bf16[160,1280]{1,0:T(8,128)(2,1)S(1)}, u32[]{:S(2)}, u32[]{:S(2)}) collective-permute-start(bf16[160,1280]{1,0:T(8,128)(2,1)S(1)} %get-tuple-element.16), channel_id=1, source_target_pairs={{0,2},{1,3},{2,0},{3,1},{4,6},{5,7},{6,4},{7,5},{8,10},{9,11},{10,... | collective-permute-start | bytes 1228808 | tf_op jit(solution)/shard_map/ppermute | solution.py:25
  7.6 1.6 collective-permute-start.1
  9.3 1.3 copy-done.3
  10.6 1.8 %arrange_weight.1 = (bf16[2,320,256]{2,1,0:T(8,128)(2,1)S(1)}, bf16[2,320,256]{2,1,0:T(8,128)(2,1)}, bf16[4,320,256]{2,1,0:T(8,128)(2,1)}, bf16[4,320,256]{2,1,0:T(8,128)(2,1)S(1)}) custom-call(s32[12]{0:T(128)S(1)} %stack.226.heads_ref, bf16[320,2048]{1,0:T(8,128)(2,1)S(1)} %copy-done.3), custom_call_target="tpu_custom_call" | custom-call | tf_op jit(solution)/shard_map/arrange_weight/pallas_call | solution.py:71
  13.2 3.0 %collective-permute-start.3 = (bf16[2,320,256]{2,1,0:T(8,128)(2,1)S(1)}, bf16[2,320,256]{2,1,0:T(8,128)(2,1)}, u32[]{:S(2)}, u32[]{:S(2)}) collective-permute-start(bf16[2,320,256]{2,1,0:T(8,128)(2,1)S(1)} %get-tuple-element.19), channel_id=1, source_target_pairs={{0,8},{1,9},{2,10},{3,11},{4,12},{5,13},{6,14},{7,15},{8,0},{9,1},... | collective-permute-start | bytes 983048 | tf_op jit(solution)/shard_map/ppermute | solution.py:216
  17.1 3.1 %collective-permute-start.11 = (bf16[2,320,256]{2,1,0:T(8,128)(2,1)}, bf16[2,320,256]{2,1,0:T(8,128)(2,1)}, u32[]{:S(2)}, u32[]{:S(2)}) collective-permute-start(bf16[2,320,256]{2,1,0:T(8,128)(2,1)} %get-tuple-element.24), channel_id=1, source_target_pairs={{0,8},{1,9},{2,10},{3,11},{4,12},{5,13},{6,14},{7,15},{8,0},{9,1},... | collective-permute-start | bytes 983048 | tf_op jit(solution)/shard_map/ppermute | solution.py:216
  20.2 13.1 %collective-permute-done.1 = bf16[160,1280]{1,0:T(8,128)(2,1)S(1)} collective-permute-done((bf16[160,1280]{1,0:T(8,128)(2,1)S(1)}, bf16[160,1280]{1,0:T(8,128)(2,1)S(1)}, u32[]{:S(2)}, u32[]{:S(2)}) %collective-permute-start.1) | collective-permute-done | bytes 409632 | tf_op jit(solution)/shard_map/ppermute | solution.py:25
  33.3 6.2 %collective-permute-done.2 = bf16[160,1280]{1,0:T(8,128)(2,1)} collective-permute-done((bf16[160,1280]{1,0:T(8,128)(2,1)S(1)}, bf16[160,1280]{1,0:T(8,128)(2,1)}, u32[]{:S(2)}, u32[]{:S(2)}) %collective-permute-start.2) | collective-permute-done | bytes 409632 | tf_op jit(solution)/shard_map/ppermute | solution.py:25
  39.5 1.2 pad_maximum_fusion.mine_ref
  42.6 1.7 %collective-permute-done.11.refs_2_ = bf16[2,320,256]{2,1,0:T(8,128)(2,1)} collective-permute-done((bf16[2,320,256]{2,1,0:T(8,128)(2,1)}, bf16[2,320,256]{2,1,0:T(8,128)(2,1)}, u32[]{:S(2)}, u32[]{:S(2)}) %collective-permute-start.11) | collective-permute-done | bytes 327712 | tf_op jit(solution)/shard_map/ppermute | solution.py:216
  44.3 2.7 %collective-permute-start.12 = (bf16[2,320,256]{2,1,0:T(8,128)(2,1)}, bf16[2,320,256]{2,1,0:T(8,128)(2,1)}, u32[]{:S(2)}, u32[]{:S(2)}) collective-permute-start(bf16[2,320,256]{2,1,0:T(8,128)(2,1)} %collective-permute-done.11.refs_2_), channel_id=1, source_target_pairs={{0,16},{16,0},{1,17},{17,1},{2,18},{18,2},{3,19},{19,3},{4,20},{20... | collective-permute-start | bytes 983048 | tf_op jit(solution)/shard_map/ppermute | solution.py:25
  47.7 1.6 stack.227
  50.4 1.5 constant_dynamic-update-slice_fusion.3
  51.9 1.5 constant_dynamic-update-slice_fusion.2
  56.8 2.7 %project.3 = bf16[2,2,4,128,256]{4,3,2,1,0:T(8,128)(2,1)S(1)} custom-call(s32[2]{0:T(128)S(1)} %pad_add_fusion.first_ref, bf16[4,160,1280]{2,1,0:T(8,128)(2,1)S(1)} %pad_maximum_fusion.mine_ref, bf16[4,160,1280]{2,1,0:T(8,128)(2,1)S(1)} %collective-permute-done.4.theirs_ref, bf16[2,320,256]{2,1,0:T(8,128)(2,1)S(1)} %copy-done.1, ...), custom_call_target="tpu_custom_call" | custom-call | flops 1342177280 | bytes 2621440 | tf_op jit(solution)/shard_map/project/pallas_call | solution.py:166
  62.3 2.6 %project.2 = bf16[2,2,4,128,256]{4,3,2,1,0:T(8,128)(2,1)S(1)} custom-call(s32[2]{0:T(128)S(1)} %pad_add_fusion.first_ref, bf16[4,160,1280]{2,1,0:T(8,128)(2,1)S(1)} %pad_maximum_fusion.mine_ref, bf16[4,160,1280]{2,1,0:T(8,128)(2,1)S(1)} %collective-permute-done.4.theirs_ref, bf16[2,320,256]{2,1,0:T(8,128)(2,1)S(1)} %copy-done, ...), custom_call_target="tpu_custom_call" | custom-call | flops 1342177280 | bytes 2621440 | tf_op jit(solution)/shard_map/project/pallas_call | solution.py:166
  66.1 1.2 collective-permute-start.10
  70.5 2.6 %collective-permute-start.6 = (bf16[128]{0:T(256)(128)(2,1)S(1)}, bf16[128]{0:T(256)(128)(2,1)S(1)}, u32[]{:S(2)}, u32[]{:S(2)}) collective-permute-start(bf16[128]{0:T(256)(128)(2,1)S(1)} %convert_element_type.228), channel_id=1, source_target_pairs={{0,8},{1,9},{2,10},{3,11},{4,12},{5,13},{6,14},{7,15},{8,0},{9,1},... | collective-permute-start | bytes 776 | tf_op jit(solution)/shard_map/ppermute | solution.py:25
  73.1 2.7 %fusion.64 = (bf16[128,640]{1,0:T(8,128)(2,1)S(1)}, f32[128,640]{1,0:T(8,128)S(1)}) fusion(bf16[2560,128]{1,0:T(8,128)(2,1)S(1)} %bitcast.219, bf16[2,1,2560,640]{3,2,1,0:T(8,128)(2,1)} %param.13), kind=kOutput, calls=%fused_computation.152 | convolution fusion | flops 419512320 | bytes 4423680 | tf_op jit(solution)/shard_map/dot_general | solution.py:327
  76.2 9.4 %collective-permute-done.6 = bf16[128]{0:T(256)(128)(2,1)S(1)} collective-permute-done((bf16[128]{0:T(256)(128)(2,1)S(1)}, bf16[128]{0:T(256)(128)(2,1)S(1)}, u32[]{:S(2)}, u32[]{:S(2)}) %collective-permute-start.6) | collective-permute-done | bytes 288 | tf_op jit(solution)/shard_map/ppermute | solution.py:25
  85.6 1.6 %collective-permute-done.5 = bf16[128,640]{1,0:T(8,128)(2,1)S(1)} collective-permute-done((bf16[128,640]{1,0:T(8,128)(2,1)S(1)}, bf16[128,640]{1,0:T(8,128)(2,1)S(1)}, u32[]{:S(2)}, u32[]{:S(2)}) %collective-permute-start.5) | collective-permute-done | bytes 163872 | tf_op jit(solution)/shard_map/ppermute | solution.py:25
  87.5 1.1 fusion.60
  91.7 2.8 %collective-permute-start.15 = (bf16[128,5]{0,1:T(8,128)(2,1)S(1)}, bf16[128,5]{0,1:T(8,128)(2,1)S(1)}, u32[]{:S(2)}, u32[]{:S(2)}) collective-permute-start(bf16[128,5]{0,1:T(8,128)(2,1)S(1)} %convert_element_type.240), channel_id=1, source_target_pairs={{0,8},{1,9},{2,10},{3,11},{4,12},{5,13},{6,14},{7,15},{8,0},{9,1},... | collective-permute-start | bytes 3848 | tf_op jit(solution)/shard_map/ppermute | solution.py:25
  96.4 6.4 %collective-permute-done.14 = bf16[128,640]{0,1:T(8,128)(2,1)S(1)} collective-permute-done((bf16[128,640]{0,1:T(8,128)(2,1)S(1)}, bf16[128,640]{0,1:T(8,128)(2,1)S(1)}, u32[]{:S(2)}, u32[]{:S(2)}) %collective-permute-start.14) | collective-permute-done | bytes 163872 | tf_op jit(solution)/shard_map/ppermute | solution.py:25
  102.9 1.2 convolution_bitcast_fusion.1
  104.7 1.6 collective-permute-done.16
  107.1 2.9 %collective-permute-start.19 = (bf16[320,128]{1,0:T(8,128)(2,1)S(1)}, bf16[320,128]{1,0:T(8,128)(2,1)S(1)}, u32[]{:S(2)}, u32[]{:S(2)}) collective-permute-start(bf16[320,128]{1,0:T(8,128)(2,1)S(1)} %get-tuple-element.47), channel_id=1, source_target_pairs={{0,6},{1,7},{2,4},{3,5},{4,2},{5,3},{6,0},{7,1},{8,14},{9,15},{10,... | collective-permute-start | bytes 245768 | tf_op jit(solution)/shard_map/ppermute | solution.py:25
  111.0 1.2 collective-permute-done.18
  112.2 1.8 %collective-permute-done.19 = bf16[320,128]{1,0:T(8,128)(2,1)S(1)} collective-permute-done((bf16[320,128]{1,0:T(8,128)(2,1)S(1)}, bf16[320,128]{1,0:T(8,128)(2,1)S(1)}, u32[]{:S(2)}, u32[]{:S(2)}) %collective-permute-start.19) | collective-permute-done | bytes 81952 | tf_op jit(solution)/shard_map/ppermute | solution.py:25
  114.0 1.5 collective-permute-start.20
  116.1 1.4 collective-permute-start.22
  117.5 1.9 %collective-permute-done.20 = bf16[320,128]{1,0:T(8,128)(2,1)S(1)} collective-permute-done((bf16[320,128]{1,0:T(8,128)(2,1)S(1)}, bf16[320,128]{1,0:T(8,128)(2,1)S(1)}, u32[]{:S(2)}, u32[]{:S(2)}) %collective-permute-start.20) | collective-permute-done | bytes 81952 | tf_op jit(solution)/shard_map/ppermute | solution.py:25
  120.8 1.5 collective-permute-done.23
  122.8 1.6 collective-permute-start.25
  124.5 2.7 %fusion.65 = (bf16[128,640]{1,0:T(8,128)(2,1)S(1)}, f32[128,640]{1,0:T(8,128)S(1)}) fusion(bf16[2560,128]{1,0:T(8,128)(2,1)S(1)} %bitcast.220, bf16[2,1,2560,640]{3,2,1,0:T(8,128)(2,1)} %param.13), kind=kOutput, calls=%fused_computation.153 | convolution fusion | flops 419512320 | bytes 4423680 | tf_op jit(solution)/shard_map/dot_general | solution.py:327
  127.1 1.5 collective-permute-start.24
  128.6 9.0 %collective-permute-done.24 = bf16[128,640]{1,0:T(8,128)(2,1)S(1)} collective-permute-done((bf16[128,640]{1,0:T(8,128)(2,1)S(1)}, bf16[128,640]{1,0:T(8,128)(2,1)S(1)}, u32[]{:S(2)}, u32[]{:S(2)}) %collective-permute-start.24) | collective-permute-done | bytes 163872 | tf_op jit(solution)/shard_map/ppermute | solution.py:25
  139.9 3.0 %collective-permute-start.26 = (bf16[128,640]{0,1:T(8,128)(2,1)S(1)}, bf16[128,640]{0,1:T(8,128)(2,1)S(1)}, u32[]{:S(2)}, u32[]{:S(2)}) collective-permute-start(bf16[128,640]{0,1:T(8,128)(2,1)S(1)} %bitcast_convert_fusion), channel_id=1, source_target_pairs={{0,8},{1,9},{2,10},{3,11},{4,12},{5,13},{6,14},{7,15},{8,0},{9,1},... | collective-permute-start | bytes 491528 | tf_op jit(solution)/shard_map/ppermute | solution.py:25
  143.5 6.2 %collective-permute-done.26 = bf16[128,640]{0,1:T(8,128)(2,1)S(1)} collective-permute-done((bf16[128,640]{0,1:T(8,128)(2,1)S(1)}, bf16[128,640]{0,1:T(8,128)(2,1)S(1)}, u32[]{:S(2)}, u32[]{:S(2)}) %collective-permute-start.26) | collective-permute-done | bytes 163872 | tf_op jit(solution)/shard_map/ppermute | solution.py:25
  149.8 2.3 %convolution_bitcast_fusion = f32[2560,128]{0,1:T(8,128)} fusion(bf16[128,640]{0,1:T(8,128)(2,1)S(1)} %fusion.32, bf16[2,1,2560,640]{3,2,1,0:T(8,128)(2,1)S(1)} %bitcast.218), kind=kOutput, calls=%fused_computation | convolution fusion | flops 419430400 | bytes 4751360 | tf_op jit(solution)/shard_map/dot_general | solution.py:342
  152.1 1.7 %copy.38 = f32[2560,128]{1,0:T(8,128)S(1)} copy(f32[2560,128]{0,1:T(8,128)} %convolution_bitcast_fusion) | data formatting | bytes 2621440 | tf_op jit(solution)/shard_map/dot_general | solution.py:342
  154.0 1.6 collective-permute-done.28
  155.8 2.2 %collective-permute-start.29 = (bf16[320,128]{1,0:T(8,128)(2,1)S(1)}, bf16[320,128]{1,0:T(8,128)(2,1)S(1)}, u32[]{:S(2)}, u32[]{:S(2)}) collective-permute-start(bf16[320,128]{1,0:T(8,128)(2,1)S(1)} %get-tuple-element.39), channel_id=1, source_target_pairs={{0,2},{1,3},{2,0},{3,1},{4,6},{5,7},{6,4},{7,5},{8,10},{9,11},{10,... | collective-permute-start | bytes 245768 | tf_op jit(solution)/shard_map/ppermute | solution.py:25
  157.9 1.5 collective-permute-start.31
  159.5 1.2 collective-permute-done.29
  160.7 2.3 %collective-permute-done.30 = bf16[320,128]{1,0:T(8,128)(2,1)S(1)} collective-permute-done((bf16[320,128]{1,0:T(8,128)(2,1)S(1)}, bf16[320,128]{1,0:T(8,128)(2,1)S(1)}, u32[]{:S(2)}, u32[]{:S(2)}) %collective-permute-start.30) | collective-permute-done | bytes 81952 | tf_op jit(solution)/shard_map/ppermute | solution.py:25
  (141 shorter events, 32.8 us)
Async XLA Ops:
  0.0 16.2 %copy-start.10 = (f32[2,5120]{1,0:T(2,128)S(1)}, f32[2,5120]{1,0:T(2,128)}, u32[]{:S(2)}) copy-start(f32[2,5120]{1,0:T(2,128)} %param.12) | copy-start | bytes 122884
  0.0 16.3 %copy-start.11 = (s32[2,2]{1,0:T(2,128)S(1)}, s32[2,2]{1,0:T(2,128)}, u32[]{:S(2)}) copy-start(s32[2,2]{1,0:T(2,128)} %param.15) | copy-start | bytes 52
  1.1 1.3 copy-start.2
  2.4 0.7 copy-start.6
  4.6 12.5 %collective-permute-start = (bf16[160,1280]{1,0:T(8,128)(2,1)S(1)}, bf16[160,1280]{1,0:T(8,128)(2,1)S(1)}, u32[]{:S(2)}, u32[]{:S(2)}) collective-permute-start(bf16[160,1280]{1,0:T(8,128)(2,1)S(1)} %get-tuple-element.16), channel_id=1, source_target_pairs={{0,2},{1,3},{2,0},{3,1},{4,6},{5,7},{6,4},{7,5},{8,10},{9,11},{10,... | collective-permute-start | bytes 1228808 | tf_op jit(solution)/shard_map/ppermute | solution.py:25
  7.6 25.7 %collective-permute-start.1 = (bf16[160,1280]{1,0:T(8,128)(2,1)S(1)}, bf16[160,1280]{1,0:T(8,128)(2,1)S(1)}, u32[]{:S(2)}, u32[]{:S(2)}) collective-permute-start(bf16[160,1280]{1,0:T(8,128)(2,1)S(1)} %get-tuple-element.17), channel_id=1, source_target_pairs={{0,4},{1,5},{2,6},{3,7},{4,0},{5,1},{6,2},{7,3},{8,12},{9,13},{10,... | collective-permute-start | bytes 1228808 | tf_op jit(solution)/shard_map/ppermute | solution.py:25
  9.2 30.3 %collective-permute-start.2 = (bf16[160,1280]{1,0:T(8,128)(2,1)S(1)}, bf16[160,1280]{1,0:T(8,128)(2,1)}, u32[]{:S(2)}, u32[]{:S(2)}) collective-permute-start(bf16[160,1280]{1,0:T(8,128)(2,1)S(1)} %get-tuple-element.18), channel_id=1, source_target_pairs={{0,6},{1,7},{2,4},{3,5},{4,2},{5,3},{6,0},{7,1},{8,14},{9,15},{10,... | collective-permute-start | bytes 1228808 | tf_op jit(solution)/shard_map/ppermute | solution.py:25
  9.2 1.3 copy-start.3
  12.4 0.8 copy-start.4
  13.2 27.5 %collective-permute-start.3 = (bf16[2,320,256]{2,1,0:T(8,128)(2,1)S(1)}, bf16[2,320,256]{2,1,0:T(8,128)(2,1)}, u32[]{:S(2)}, u32[]{:S(2)}) collective-permute-start(bf16[2,320,256]{2,1,0:T(8,128)(2,1)S(1)} %get-tuple-element.19), channel_id=1, source_target_pairs={{0,8},{1,9},{2,10},{3,11},{4,12},{5,13},{6,14},{7,15},{8,0},{9,1},... | collective-permute-start | bytes 983048 | tf_op jit(solution)/shard_map/ppermute | solution.py:216
  16.2 37.8 %collective-permute-start.7 = (bf16[4,320,256]{2,1,0:T(8,128)(2,1)}, bf16[4,320,256]{2,1,0:T(8,128)(2,1)}, u32[]{:S(2)}, u32[]{:S(2)}) collective-permute-start(bf16[4,320,256]{2,1,0:T(8,128)(2,1)} %get-tuple-element.22), channel_id=1, source_target_pairs={{0,1},{1,0},{2,3},{3,2},{4,5},{5,4},{6,7},{7,6},{8,9},{9,8},{10,11... | collective-permute-start | bytes 1966088 | tf_op jit(solution)/shard_map/ppermute | solution.py:25
  17.1 24.6 %copy-start.5 = (bf16[4,320,256]{2,1,0:T(8,128)(2,1)S(1)}, bf16[4,320,256]{2,1,0:T(8,128)(2,1)}, u32[]{:S(2)}) copy-start(bf16[4,320,256]{2,1,0:T(8,128)(2,1)} %copy-done.4) | copy-start | bytes 1966084
  17.1 27.2 %collective-permute-start.11 = (bf16[2,320,256]{2,1,0:T(8,128)(2,1)}, bf16[2,320,256]{2,1,0:T(8,128)(2,1)}, u32[]{:S(2)}, u32[]{:S(2)}) collective-permute-start(bf16[2,320,256]{2,1,0:T(8,128)(2,1)} %get-tuple-element.24), channel_id=1, source_target_pairs={{0,8},{1,9},{2,10},{3,11},{4,12},{5,13},{6,14},{7,15},{8,0},{9,1},... | collective-permute-start | bytes 983048 | tf_op jit(solution)/shard_map/ppermute | solution.py:216
  40.7 15.1 %collective-permute-start.4 = (bf16[4,160,1280]{2,1,0:T(8,128)(2,1)S(1)}, bf16[4,160,1280]{2,1,0:T(8,128)(2,1)S(1)}, u32[]{:S(2)}, u32[]{:S(2)}) collective-permute-start(bf16[4,160,1280]{2,1,0:T(8,128)(2,1)S(1)} %pad_maximum_fusion.mine_ref), channel_id=1, source_target_pairs={{0,1},{1,0},{2,3},{3,2},{4,5},{5,4},{6,7},{7,6},{8,9},{9,8},{10,11... | collective-permute-start | bytes 4915208 | tf_op jit(solution)/shard_map/ppermute | solution.py:25
  44.3 11.5 %collective-permute-start.12 = (bf16[2,320,256]{2,1,0:T(8,128)(2,1)}, bf16[2,320,256]{2,1,0:T(8,128)(2,1)}, u32[]{:S(2)}, u32[]{:S(2)}) collective-permute-start(bf16[2,320,256]{2,1,0:T(8,128)(2,1)} %collective-permute-done.11.refs_2_), channel_id=1, source_target_pairs={{0,16},{16,0},{1,17},{17,1},{2,18},{18,2},{3,19},{19,3},{4,20},{20... | collective-permute-start | bytes 983048 | tf_op jit(solution)/shard_map/ppermute | solution.py:25
  47.0 15.3 %collective-permute-start.8 = (bf16[2,320,256]{2,1,0:T(8,128)(2,1)}, bf16[2,320,256]{2,1,0:T(8,128)(2,1)}, u32[]{:S(2)}, u32[]{:S(2)}) collective-permute-start(bf16[2,320,256]{2,1,0:T(8,128)(2,1)} %collective-permute-done.3.refs_2_), channel_id=1, source_target_pairs={{0,16},{16,0},{1,17},{17,1},{2,18},{18,2},{3,19},{19,3},{4,20},{20... | collective-permute-start | bytes 983048 | tf_op jit(solution)/shard_map/ppermute | solution.py:25
  55.8 1.0 copy-start.1
  56.8 5.5 %copy-start = (bf16[2,320,256]{2,1,0:T(8,128)(2,1)S(1)}, bf16[2,320,256]{2,1,0:T(8,128)(2,1)}, u32[]{:S(2)}) copy-start(bf16[2,320,256]{2,1,0:T(8,128)(2,1)} %get-tuple-element.52.refs_0_) | copy-start | bytes 983044
  60.6 27.0 %collective-permute-start.13 = (bf16[2,4,128,256]{3,2,1,0:T(8,128)(2,1)}, bf16[2,4,128,256]{3,2,1,0:T(8,128)(2,1)}, u32[]{:S(2)}, u32[]{:S(2)}) collective-permute-start(bf16[2,4,128,256]{3,2,1,0:T(8,128)(2,1)} %get-tuple-element.36), channel_id=1, source_target_pairs={{0,6},{1,7},{2,4},{3,5},{4,2},{5,3},{6,0},{7,1},{8,14},{9,15},{10,... | collective-permute-start | bytes 1572872 | tf_op jit(solution)/shard_map/ppermute | solution.py:25
  66.1 23.4 %collective-permute-start.10 = (bf16[2,4,128,256]{3,2,1,0:T(8,128)(2,1)}, bf16[2,4,128,256]{3,2,1,0:T(8,128)(2,1)S(1)}, u32[]{:S(2)}, u32[]{:S(2)}) collective-permute-start(bf16[2,4,128,256]{3,2,1,0:T(8,128)(2,1)} %get-tuple-element.37), channel_id=1, source_target_pairs={{0,4},{1,5},{2,6},{3,7},{4,0},{5,1},{6,2},{7,3},{8,12},{9,13},{10,... | collective-permute-start | bytes 1572872 | tf_op jit(solution)/shard_map/ppermute | solution.py:25
  67.3 22.3 %collective-permute-start.9 = (bf16[2,4,128,256]{3,2,1,0:T(8,128)(2,1)}, bf16[2,4,128,256]{3,2,1,0:T(8,128)(2,1)S(1)}, u32[]{:S(2)}, u32[]{:S(2)}) collective-permute-start(bf16[2,4,128,256]{3,2,1,0:T(8,128)(2,1)} %get-tuple-element.38), channel_id=1, source_target_pairs={{0,2},{1,3},{2,0},{3,1},{4,6},{5,7},{6,4},{7,5},{8,10},{9,11},{10,... | collective-permute-start | bytes 1572872 | tf_op jit(solution)/shard_map/ppermute | solution.py:25
  70.5 15.1 %collective-permute-start.6 = (bf16[128]{0:T(256)(128)(2,1)S(1)}, bf16[128]{0:T(256)(128)(2,1)S(1)}, u32[]{:S(2)}, u32[]{:S(2)}) collective-permute-start(bf16[128]{0:T(256)(128)(2,1)S(1)} %convert_element_type.228), channel_id=1, source_target_pairs={{0,8},{1,9},{2,10},{3,11},{4,12},{5,13},{6,14},{7,15},{8,0},{9,1},... | collective-permute-start | bytes 776 | tf_op jit(solution)/shard_map/ppermute | solution.py:25
  75.8 11.5 %collective-permute-start.5 = (bf16[128,640]{1,0:T(8,128)(2,1)S(1)}, bf16[128,640]{1,0:T(8,128)(2,1)S(1)}, u32[]{:S(2)}, u32[]{:S(2)}) collective-permute-start(bf16[128,640]{1,0:T(8,128)(2,1)S(1)} %get-tuple-element.73), channel_id=1, source_target_pairs={{0,8},{1,9},{2,10},{3,11},{4,12},{5,13},{6,14},{7,15},{8,0},{9,1},... | collective-permute-start | bytes 491528 | tf_op jit(solution)/shard_map/ppermute | solution.py:25
  88.7 1.2 copy-start.7
  89.6 0.9 copy-start.9
  89.9 13.0 %slice-start = ((s8[6553600]{0:T(1024)(128)(4,1)}), s8[4194304]{0:T(1024)(128)(4,1)S(1)}, s32[]{:S(2)}) async-start(s8[6553600]{0:T(1024)(128)(4,1)} %bitcast.215), calls=%async_computation | async-start | bytes 8388608
  90.5 12.4 %slice-start.1 = ((s8[6553600]{0:T(1024)(128)(4,1)}), s8[2359296]{0:T(1024)(128)(4,1)S(1)}, s32[]{:S(2)}) async-start(s8[6553600]{0:T(1024)(128)(4,1)} %bitcast.215), calls=%async_computation.1 | async-start | bytes 4718592
  91.7 4.8 %collective-permute-start.15 = (bf16[128,5]{0,1:T(8,128)(2,1)S(1)}, bf16[128,5]{0,1:T(8,128)(2,1)S(1)}, u32[]{:S(2)}, u32[]{:S(2)}) collective-permute-start(bf16[128,5]{0,1:T(8,128)(2,1)S(1)} %convert_element_type.240), channel_id=1, source_target_pairs={{0,8},{1,9},{2,10},{3,11},{4,12},{5,13},{6,14},{7,15},{8,0},{9,1},... | collective-permute-start | bytes 3848 | tf_op jit(solution)/shard_map/ppermute | solution.py:25
  95.3 7.5 %collective-permute-start.14 = (bf16[128,640]{0,1:T(8,128)(2,1)S(1)}, bf16[128,640]{0,1:T(8,128)(2,1)S(1)}, u32[]{:S(2)}, u32[]{:S(2)}) collective-permute-start(bf16[128,640]{0,1:T(8,128)(2,1)S(1)} %bitcast_convert_fusion.1), channel_id=1, source_target_pairs={{0,8},{1,9},{2,10},{3,11},{4,12},{5,13},{6,14},{7,15},{8,0},{9,1},... | collective-permute-start | bytes 491528 | tf_op jit(solution)/shard_map/ppermute | solution.py:25
  104.1 9.8 %copy-start.8 = (bf16[320,128]{1,0:T(8,128)(2,1)S(1)}, bf16[320,128]{1,0:T(8,128)(2,1)}, u32[]{:S(2)}) copy-start(bf16[320,128]{1,0:T(8,128)(2,1)} %param.11) | copy-start | bytes 245764
  104.6 1.7 %collective-permute-start.16 = (bf16[4,320,128]{2,1,0:T(8,128)(2,1)S(1)}, bf16[4,320,128]{2,1,0:T(8,128)(2,1)S(1)}, u32[]{:S(2)}, u32[]{:S(2)}) collective-permute-start(bf16[4,320,128]{2,1,0:T(8,128)(2,1)S(1)} %fusion.31), channel_id=1, source_target_pairs={{0,1},{1,0},{2,3},{3,2},{4,5},{5,4},{6,7},{7,6},{8,9},{9,8},{10,11... | collective-permute-start | bytes 983048 | tf_op jit(solution)/shard_map/ppermute | solution.py:25
  106.4 4.6 %collective-permute-start.17 = (bf16[320,128]{1,0:T(8,128)(2,1)S(1)}, bf16[320,128]{1,0:T(8,128)(2,1)S(1)}, u32[]{:S(2)}, u32[]{:S(2)}) collective-permute-start(bf16[320,128]{1,0:T(8,128)(2,1)S(1)} %get-tuple-element.46), channel_id=1, source_target_pairs={{0,2},{1,3},{2,0},{3,1},{4,6},{5,7},{6,4},{7,5},{8,10},{9,11},{10,... | collective-permute-start | bytes 245768 | tf_op jit(solution)/shard_map/ppermute | solution.py:25
  107.1 5.1 %collective-permute-start.18 = (bf16[320,128]{1,0:T(8,128)(2,1)S(1)}, bf16[320,128]{1,0:T(8,128)(2,1)S(1)}, u32[]{:S(2)}, u32[]{:S(2)}) collective-permute-start(bf16[320,128]{1,0:T(8,128)(2,1)S(1)} %get-tuple-element.48), channel_id=1, source_target_pairs={{0,4},{1,5},{2,6},{3,7},{4,0},{5,1},{6,2},{7,3},{8,12},{9,13},{10,... | collective-permute-start | bytes 245768 | tf_op jit(solution)/shard_map/ppermute | solution.py:25
  107.1 6.9 %collective-permute-start.19 = (bf16[320,128]{1,0:T(8,128)(2,1)S(1)}, bf16[320,128]{1,0:T(8,128)(2,1)S(1)}, u32[]{:S(2)}, u32[]{:S(2)}) collective-permute-start(bf16[320,128]{1,0:T(8,128)(2,1)S(1)} %get-tuple-element.47), channel_id=1, source_target_pairs={{0,6},{1,7},{2,4},{3,5},{4,2},{5,3},{6,0},{7,1},{8,14},{9,15},{10,... | collective-permute-start | bytes 245768 | tf_op jit(solution)/shard_map/ppermute | solution.py:25
  114.0 5.4 %collective-permute-start.20 = (bf16[320,128]{1,0:T(8,128)(2,1)S(1)}, bf16[320,128]{1,0:T(8,128)(2,1)S(1)}, u32[]{:S(2)}, u32[]{:S(2)}) collective-permute-start(bf16[320,128]{1,0:T(8,128)(2,1)S(1)} %fusion.43), channel_id=1, source_target_pairs={{0,6},{1,7},{2,4},{3,5},{4,2},{5,3},{6,0},{7,1},{8,14},{9,15},{10,... | collective-permute-start | bytes 245768 | tf_op jit(solution)/shard_map/ppermute | solution.py:25
  115.5 4.4 %collective-permute-start.21 = (bf16[320,128]{1,0:T(8,128)(2,1)S(1)}, bf16[320,128]{1,0:T(8,128)(2,1)S(1)}, u32[]{:S(2)}, u32[]{:S(2)}) collective-permute-start(bf16[320,128]{1,0:T(8,128)(2,1)S(1)} %fusion.43), channel_id=1, source_target_pairs={{0,4},{1,5},{2,6},{3,7},{4,0},{5,1},{6,2},{7,3},{8,12},{9,13},{10,... | collective-permute-start | bytes 245768 | tf_op jit(solution)/shard_map/ppermute | solution.py:25
  116.1 4.4 %collective-permute-start.22 = (bf16[320,128]{1,0:T(8,128)(2,1)S(1)}, bf16[320,128]{1,0:T(8,128)(2,1)S(1)}, u32[]{:S(2)}, u32[]{:S(2)}) collective-permute-start(bf16[320,128]{1,0:T(8,128)(2,1)S(1)} %fusion.43), channel_id=1, source_target_pairs={{0,2},{1,3},{2,0},{3,1},{4,6},{5,7},{6,4},{7,5},{8,10},{9,11},{10,... | collective-permute-start | bytes 245768 | tf_op jit(solution)/shard_map/ppermute | solution.py:25
  120.6 1.7 %collective-permute-start.23 = (bf16[4,320,128]{2,1,0:T(8,128)(2,1)S(1)}, bf16[4,320,128]{2,1,0:T(8,128)(2,1)S(1)}, u32[]{:S(2)}, u32[]{:S(2)}) collective-permute-start(bf16[4,320,128]{2,1,0:T(8,128)(2,1)S(1)} %pad_maximum_fusion.3), channel_id=1, source_target_pairs={{0,1},{1,0},{2,3},{3,2},{4,5},{5,4},{6,7},{7,6},{8,9},{9,8},{10,11... | collective-permute-start | bytes 983048 | tf_op jit(solution)/shard_map/ppermute | solution.py:25
  122.8 5.8 %collective-permute-start.25 = (bf16[128]{0:T(256)(128)(2,1)S(1)}, bf16[128]{0:T(256)(128)(2,1)S(1)}, u32[]{:S(2)}, u32[]{:S(2)}) collective-permute-start(bf16[128]{0:T(256)(128)(2,1)S(1)} %convert_element_type.262), channel_id=1, source_target_pairs={{0,8},{1,9},{2,10},{3,11},{4,12},{5,13},{6,14},{7,15},{8,0},{9,1},... | collective-permute-start | bytes 776 | tf_op jit(solution)/shard_map/ppermute | solution.py:25
  127.1 10.4 %collective-permute-start.24 = (bf16[128,640]{1,0:T(8,128)(2,1)S(1)}, bf16[128,640]{1,0:T(8,128)(2,1)S(1)}, u32[]{:S(2)}, u32[]{:S(2)}) collective-permute-start(bf16[128,640]{1,0:T(8,128)(2,1)S(1)} %get-tuple-element.77), channel_id=1, source_target_pairs={{0,8},{1,9},{2,10},{3,11},{4,12},{5,13},{6,14},{7,15},{8,0},{9,1},... | collective-permute-start | bytes 491528 | tf_op jit(solution)/shard_map/ppermute | solution.py:25
  137.6 12.2 %slice-start.2 = ((s8[6553600]{0:T(1024)(128)(4,1)}), s8[2359296]{0:T(1024)(128)(4,1)S(1)}, s32[]{:S(2)}) async-start(s8[6553600]{0:T(1024)(128)(4,1)} %bitcast.217), calls=%async_computation.2 | async-start | bytes 4718592
  137.9 11.9 %slice-start.3 = ((s8[6553600]{0:T(1024)(128)(4,1)}), s8[4194304]{0:T(1024)(128)(4,1)S(1)}, s32[]{:S(2)}) async-start(s8[6553600]{0:T(1024)(128)(4,1)} %bitcast.217), calls=%async_computation.3 | async-start | bytes 8388608
  139.0 4.6 %collective-permute-start.27 = (bf16[128,5]{0,1:T(8,128)(2,1)S(1)}, bf16[128,5]{0,1:T(8,128)(2,1)S(1)}, u32[]{:S(2)}, u32[]{:S(2)}) collective-permute-start(bf16[128,5]{0,1:T(8,128)(2,1)S(1)} %convert_element_type.268), channel_id=1, source_target_pairs={{0,8},{1,9},{2,10},{3,11},{4,12},{5,13},{6,14},{7,15},{8,0},{9,1},... | collective-permute-start | bytes 3848 | tf_op jit(solution)/shard_map/ppermute | solution.py:25
  139.9 9.8 %collective-permute-start.26 = (bf16[128,640]{0,1:T(8,128)(2,1)S(1)}, bf16[128,640]{0,1:T(8,128)(2,1)S(1)}, u32[]{:S(2)}, u32[]{:S(2)}) collective-permute-start(bf16[128,640]{0,1:T(8,128)(2,1)S(1)} %bitcast_convert_fusion), channel_id=1, source_target_pairs={{0,8},{1,9},{2,10},{3,11},{4,12},{5,13},{6,14},{7,15},{8,0},{9,1},... | collective-permute-start | bytes 491528 | tf_op jit(solution)/shard_map/ppermute | solution.py:25
  153.9 1.7 %collective-permute-start.28 = (bf16[4,320,128]{2,1,0:T(8,128)(2,1)S(1)}, bf16[4,320,128]{2,1,0:T(8,128)(2,1)S(1)}, u32[]{:S(2)}, u32[]{:S(2)}) collective-permute-start(bf16[4,320,128]{2,1,0:T(8,128)(2,1)S(1)} %fusion.30), channel_id=1, source_target_pairs={{0,1},{1,0},{2,3},{3,2},{4,5},{5,4},{6,7},{7,6},{8,9},{9,8},{10,11... | collective-permute-start | bytes 983048 | tf_op jit(solution)/shard_map/ppermute | solution.py:25
  155.8 4.9 %collective-permute-start.29 = (bf16[320,128]{1,0:T(8,128)(2,1)S(1)}, bf16[320,128]{1,0:T(8,128)(2,1)S(1)}, u32[]{:S(2)}, u32[]{:S(2)}) collective-permute-start(bf16[320,128]{1,0:T(8,128)(2,1)S(1)} %get-tuple-element.39), channel_id=1, source_target_pairs={{0,2},{1,3},{2,0},{3,1},{4,6},{5,7},{6,4},{7,5},{8,10},{9,11},{10,... | collective-permute-start | bytes 245768 | tf_op jit(solution)/shard_map/ppermute | solution.py:25
  157.9 5.1 %collective-permute-start.30 = (bf16[320,128]{1,0:T(8,128)(2,1)S(1)}, bf16[320,128]{1,0:T(8,128)(2,1)S(1)}, u32[]{:S(2)}, u32[]{:S(2)}) collective-permute-start(bf16[320,128]{1,0:T(8,128)(2,1)S(1)} %get-tuple-element.41), channel_id=1, source_target_pairs={{0,4},{1,5},{2,6},{3,7},{4,0},{5,1},{6,2},{7,3},{8,12},{9,13},{10,... | collective-permute-start | bytes 245768 | tf_op jit(solution)/shard_map/ppermute | solution.py:25
  157.9 5.8 %collective-permute-start.31 = (bf16[320,128]{1,0:T(8,128)(2,1)S(1)}, bf16[320,128]{1,0:T(8,128)(2,1)S(1)}, u32[]{:S(2)}, u32[]{:S(2)}) collective-permute-start(bf16[320,128]{1,0:T(8,128)(2,1)S(1)} %get-tuple-element.40), channel_id=1, source_target_pairs={{0,6},{1,7},{2,4},{3,5},{4,2},{5,3},{6,0},{7,1},{8,14},{9,15},{10,... | collective-permute-start | bytes 245768 | tf_op jit(solution)/shard_map/ppermute | solution.py:25

commit v5 on v1

v5 whole, which is shorter than its diff:
```python
import functools

import jax
import jax.numpy as jnp
from jax import lax
from jax.experimental import pallas as pl
from jax.experimental.pallas import tpu as pltpu
from jax.sharding import PartitionSpec as P

KVH = 8
HD = 128
QPK = 5
QBLK = 64
CAP = 30.0
EPSILON = 1e-05
BF16 = jnp.bfloat16
F32 = jnp.float32

CHIPS = KVH // 2
ROUNDS = ((1, 2), (3, 0))
PROJECT_COST = 8


def swapped(value, mask, axis="row"):
    pairs = [(source, source ^ mask) for source in range(lax.axis_size(axis))]
    return lax.ppermute(value, axis, pairs)


def over_tiles(value, tile_count):
    values = [value]
    mask = 1
    while mask < tile_count:
        if len(values) == 1:
            values.append(swapped(values[0], mask * KVH))
        else:
            got = swapped(jnp.stack(values), mask * KVH)
            values.extend(got[place] for place in range(len(values)))
        mask *= 2
    return values


def natural(pieces, index):
    pieces = list(pieces)
    bit = 1
    while bit < len(pieces):
        upper = index // bit % 2 == 1
        pieces = [jnp.where(upper, pieces[j ^ bit], pieces[j]) for j in range(len(pieces))]
        bit *= 2
    return pieces


def prepare_kernel(
    pair, counts, width, heads_ref, starts_ref, weight_any, hidden_any, gain_any, extra_any, *refs
):
    weight_ref, hidden_ref, gain_ref, extra_ref, normed, sems = refs[-6:]
    head_refs, out_refs = refs[: len(counts)], refs[len(counts) : -6]
    rows = hidden_ref.shape[0]
    lanes = extra_ref.shape[1]
    more = out_refs[0].shape[0] - rows
    copies = [
        pltpu.make_async_copy(source, target, sems.at[number])
        for number, (source, target) in enumerate(
            (
                (weight_any, weight_ref),
                (hidden_any, hidden_ref),
                (gain_any, gain_ref),
                (extra_any, extra_ref),
            )
        )
    ]
    for copy in copies:
        copy.start()
    copies[0].wait()
    number = 0
    for head_ref in head_refs:
        for place in range(head_ref.shape[0]):
            column = pl.multiple_of(heads_ref[number] * pair, pair)
            head_ref[place] = weight_ref[:, pl.ds(column, pair)]
            number += 1
    for copy in copies[1:]:
        copy.wait()
    hidden = hidden_ref[...].astype(F32)
    inverse = lax.rsqrt(jnp.mean(hidden * hidden, axis=1, keepdims=True) + EPSILON)
    normed[...] = (hidden * inverse * gain_ref[...]).astype(BF16)
    number = 0
    for out_ref in out_refs:
        for place in range(out_ref.shape[1] // width):
            start = pl.multiple_of(starts_ref[number] * width, 128)
            out_ref[:rows, place * width : (place + 1) * width] = normed[:, pl.ds(start, width)]
            number += 1
        for block in range(out_ref.shape[1] // lanes):
            out_ref[rows:, block * lanes : (block + 1) * lanes] = extra_ref[
                block * more : (block + 1) * more, :
            ]


def in_kernels(unit, rows):
    return unit % 64 == 0 and rows % 16 == 0


def prepared(weight, head_groups, pair, hidden, gain, groups, width, extra, kernels):
    rows, depth = hidden.shape
    total_width = len(groups[0]) * width
    more = extra.size // total_width
    if not kernels:
        columns = [
            jnp.stack([lax.dynamic_slice_in_dim(weight, head * pair, pair, 1) for head in group])
            for group in head_groups
        ]
        hidden_float = hidden.astype(F32)
        inverse = lax.rsqrt(jnp.mean(hidden_float * hidden_float, axis=1, keepdims=True) + EPSILON)
        normed = (hidden_float * inverse * gain[None, :]).astype(BF16)
        results = []
        for group in groups:
            blocks = [lax.dynamic_slice_in_dim(normed, block * width, width, 1) for block in group]
            rest = extra.reshape(more, total_width)
            results.append(jnp.concatenate([jnp.concatenate(blocks, axis=1), rest], axis=0))
        return columns, results
    counts = [len(group) for group in head_groups]
    vmem = pl.BlockSpec(memory_space=pltpu.VMEM)
    smem = pl.BlockSpec(memory_space=pltpu.SMEM)
    results = pl.pallas_call(
        functools.partial(prepare_kernel, pair, counts, width),
        out_shape=[jax.ShapeDtypeStruct((count, weight.shape[0], pair), BF16) for count in counts]
        + [jax.ShapeDtypeStruct((rows + more, total_width), BF16) for group in groups],
        in_specs=[smem, smem] + [pl.BlockSpec(memory_space=pltpu.HBM)] * 4,
        out_specs=[vmem] * (len(counts) + len(groups)),
        scratch_shapes=[
            pltpu.VMEM(weight.shape, BF16),
            pltpu.VMEM((rows, depth), BF16),
            pltpu.VMEM((1, depth), F32),
            pltpu.VMEM(extra.shape, BF16),
            pltpu.VMEM((rows, depth), BF16),
            pltpu.SemaphoreType.DMA((4,)),
        ],
        compiler_params=pltpu.CompilerParams(vmem_limit_bytes=60 * 1024 * 1024),
        name="prepare",
    )(
        jnp.stack([head for group in head_groups for head in group]).astype(jnp.int32),
        jnp.stack([block for group in groups for block in group]).astype(jnp.int32),
        weight,
        hidden,
        gain[None, :],
        extra,
    )
    return results[: len(counts)], results[len(counts) :]


def project_kernel(rows, heads, pair, start, first_ref, heads_ref, weight_any, traded_ref, *refs):
    token_refs, refs = refs[: 2 * CHIPS], refs[2 * CHIPS :]
    own, weight, sem = refs[-3:]
    out_refs = refs[-3 - heads : -3]
    blocks = refs[: -3 - heads]
    unit = own.shape[0]
    get_own = pltpu.make_async_copy(weight_any, own, sem)
    get_own.start()

    def put(head, tile, second, value):
        which = 1 - first_ref[tile] if second else first_ref[tile]
        base = pl.multiple_of(2 * unit * tile + which * unit, unit)
        weight[pl.ds(base, unit), head * pair : (head + 1) * pair] = value

    for head in range(heads):
        put(head, 0, 1, traded_ref[start + head])
        for number, block_ref in enumerate(blocks):
            put(head, 1 + number // 2, number % 2, block_ref[head])
    get_own.wait()
    for head in range(heads):
        column = pl.multiple_of(heads_ref[head] * pair, pair)
        put(head, 0, 0, own[:, pl.ds(column, pair)])
    for number, token_ref in enumerate(token_refs):
        span = slice(number * rows, (number + 1) * rows)
        result = jnp.dot(token_ref[:rows, :], weight[...], preferred_element_type=F32).astype(BF16)
        for head, out_ref in enumerate(out_refs):
            out_ref[span, :] = result[:, head * pair : (head + 1) * pair]


def projected(tokens, heads, pair, kv_weight, traded, start, firsts, blocks, rows, kernels):
    unit, depth = kv_weight.shape[0], tokens[0].shape[1]
    count = len(tokens) * rows
    firsts = jnp.stack(firsts).astype(jnp.int32)
    if not kernels:
        kept = jnp.stack([lax.dynamic_slice_in_dim(kv_weight, h * pair, pair, 1) for h in heads])
        pieces = [kept, traded[start : start + len(heads)]] + blocks
        ordered = []
        for tile in range(len(pieces) // 2):
            one, two = pieces[2 * tile : 2 * tile + 2]
            first = firsts[tile] == 0
            ordered += [jnp.where(first, one, two), jnp.where(first, two, one)]
        weight = jnp.concatenate(ordered, axis=1)
        tokens = jnp.concatenate([piece[:rows] for piece in tokens])
        result = jnp.einsum("td,hdc->htc", tokens, weight, preferred_element_type=F32)
        return list(result.astype(BF16))
    vmem = pl.BlockSpec(memory_space=pltpu.VMEM)
    smem = pl.BlockSpec(memory_space=pltpu.SMEM)
    return list(
        pl.pallas_call(
            functools.partial(project_kernel, rows, len(heads), pair, start),
            out_shape=[jax.ShapeDtypeStruct((count, pair), BF16)] * len(heads),
            in_specs=[smem, smem, pl.BlockSpec(memory_space=pltpu.HBM), vmem]
            + [vmem] * (len(tokens) + len(blocks)),
            out_specs=[vmem] * len(heads),
            scratch_shapes=[
                pltpu.VMEM(kv_weight.shape, BF16),
                pltpu.VMEM((depth, len(heads) * pair), BF16),
                pltpu.SemaphoreType.DMA,
            ],
            compiler_params=pltpu.CompilerParams(vmem_limit_bytes=20 * 1024 * 1024),
            cost_estimate=pl.CostEstimate(
                flops=PROJECT_COST * 2 * len(heads) * count * depth * pair,
                bytes_accessed=2 * count * depth,
                transcendentals=0,
            ),
            name="project",
        )(firsts, jnp.stack(heads).astype(jnp.int32), kv_weight, traded, *tokens, *blocks)
    )


def query_kernel(lanes, place_ref, gain_ref, weight_ref, *refs):
    piece_refs, refs = refs[:-7], refs[-7:]
    sent_ref, kept_ref, squares_sent_ref, squares_ref, stream, parts, sems = refs
    unit = stream.shape[0] // KVH
    more = parts.shape[1]
    blocks = parts.shape[2] // lanes
    sources = [
        piece_ref.at[place] if len(piece_ref.shape) == 3 else piece_ref
        for piece_ref in piece_refs
        for place in range(CHIPS if len(piece_ref.shape) == 3 else 1)
    ]
    bases = [
        pl.multiple_of(
            ((place_ref[0] ^ number % CHIPS) * 2 + (place_ref[1] ^ number // CHIPS)) * unit, unit
        )
        for number in range(KVH)
    ]
    packed = sources[0].shape[1] != lanes
    copies = []
    for number, source in enumerate(sources):
        if packed:
            source, target = source.at[source.shape[0] - more :], parts.at[number]
        else:
            target = stream.at[pl.ds(bases[number], unit)]
        copies.append(pltpu.make_async_copy(source, target, sems.at[number]))
        copies[-1].start()
    for number, copy in enumerate(copies):
        copy.wait()
        for block in range(blocks if packed else 0):
            stream[pl.ds(pl.multiple_of(bases[number] + block * more, more), more), :] = parts[
                number, :, block * lanes : (block + 1) * lanes
            ]
    rows = stream[...].astype(F32).T
    squares = jnp.sum(rows * rows, axis=1, keepdims=True)
    scaled = (rows * gain_ref[...]).astype(BF16)
    partial = jnp.dot(scaled, weight_ref[...], preferred_element_type=F32)
    kept_ref[...] = partial
    sent_ref[...] = partial.astype(BF16)
    spread = jnp.broadcast_to(squares, (lanes, lanes))
    squares_ref[...] = spread
    across = spread.T[:8]
    high = across.astype(BF16)
    squares_sent_ref[:8] = high
    squares_sent_ref[8:] = (across - high.astype(F32)).astype(BF16)


def spread_back(pair_ref, lanes):
    across = pair_ref[:8].astype(F32) + pair_ref[8:].astype(F32)
    return jnp.concatenate([across, jnp.zeros((lanes - 8, lanes), F32)], axis=0).T


def attend_kernel(depth, others, query_pos_ref, query_floor_ref, key_pos_ref, kv_ref, *refs):
    kept_ref, squares_ref = refs[:2]
    far = refs[2 : 2 + 2 * others]
    sent_ref, out_ref, totals_sent_ref, totals_ref = refs[2 + 2 * others :]
    lanes = kept_ref.shape[0]
    queries = kept_ref[...]
    squares = squares_ref[:, :1]
    for other in range(others):
        queries = queries + far[2 * other][...].astype(F32)
        squares = squares + spread_back(far[2 * other + 1], lanes)[:, :1]
    queries = (queries * lax.rsqrt(squares / depth + EPSILON)).astype(BF16)
    visible = (key_pos_ref[...] <= query_pos_ref[...]) & (key_pos_ref[...] >= query_floor_ref[...])
    keys, values = kv_ref[:, :HD], kv_ref[:, HD:]
    lane = lax.broadcasted_iota(jnp.int32, (lanes, lanes), 1)
    totals = jnp.zeros((lanes, lanes), F32)
    for head in range(queries.shape[1] // HD):
        span = slice(head * HD, (head + 1) * HD)
        scores = lax.dot_general(
            queries[:, span], keys, (((1,), (1,)), ((), ())), preferred_element_type=F32
        ) * HD ** (-0.5)
        weights = jnp.where(visible, jnp.exp(CAP * jnp.tanh(scores / CAP)), 0.0)
        totals = jnp.where(lane == head, jnp.sum(weights, axis=1, keepdims=True), totals)
        weighted = jnp.dot(weights.astype(BF16), values, preferred_element_type=F32)
        out_ref[:, span] = weighted
        sent_ref[:, span] = weighted.astype(BF16)
    totals_ref[...] = totals
    across = totals.T[:8]
    high = across.astype(BF16)
    totals_sent_ref[:8] = high
    totals_sent_ref[8:] = (across - high.astype(F32)).astype(BF16)


def update_kernel(others, place_ref, weight_ref, kept_ref, totals_ref, *refs):
    far, (own_ref, sent_ref) = refs[: 2 * others], refs[2 * others :]
    lanes = kept_ref.shape[0]
    unit = own_ref.shape[1]
    weighted = kept_ref[...]
    totals = totals_ref[...]
    for other in range(others):
        weighted = weighted + far[2 * other][...].astype(F32)
        totals = totals + spread_back(far[2 * other + 1], lanes)
    attended = jnp.concatenate(
        [
            (weighted[:, head * HD : (head + 1) * HD] / totals[:, head : head + 1]).astype(BF16)
            for head in range(weighted.shape[1] // HD)
        ],
        axis=1,
    )
    for core, out_ref in enumerate((own_ref, sent_ref)):
        for chip in range(CHIPS):
            base = ((place_ref[0] ^ chip) * 2 + (place_ref[1] ^ core)) * unit
            update = lax.dot_general(
                weight_ref[pl.ds(pl.multiple_of(base, unit), unit), :],
                attended,
                (((1,), (1,)), ((), ())),
                preferred_element_type=F32,
            )
            out_ref[chip] = update.astype(out_ref.dtype)


def call(kernel, name, out_shape, scalars, arrays, scratch=(), flops=0, loose=()):
    vmem = pl.BlockSpec(memory_space=pltpu.VMEM)
    smem = pl.BlockSpec(memory_space=pltpu.SMEM)
    return pl.pallas_call(
        kernel,
        out_shape=out_shape,
        in_specs=[smem] * len(scalars)
        + [vmem] * len(arrays)
        + [pl.BlockSpec(memory_space=pl.ANY)] * len(loose),
        out_specs=[vmem] * len(out_shape),
        scratch_shapes=list(scratch),
        compiler_params=pltpu.CompilerParams(vmem_limit_bytes=20 * 1024 * 1024),
        cost_estimate=pl.CostEstimate(
            flops=flops, bytes_accessed=sum(2 * a.size for a in arrays), transcendentals=0
        ),
        name=name,
    )(*scalars, *arrays, *loose)


def in_order(ours, theirs, core):
    low, high = jnp.where(core == 0, ours, theirs), jnp.where(core == 0, theirs, ours)
    return jnp.stack([low, high], axis=1).reshape(-1, ours.shape[-1])


def key_values_of(hidden, kv_gain, kv_weight, query_states, meanwhile):
    lane_count = lax.axis_size("row")
    tile_count = lane_count // KVH
    me = lax.axis_index("row")
    tile, chip, core = me // KVH, me // 2 % CHIPS, me % 2
    rows = hidden.shape[0]
    unit = kv_weight.shape[0]
    pair = 2 * HD
    share = lax.axis_size("groups") == 2
    part = lax.axis_index("groups") if share else 0

    order = [place for round_ in ROUNDS for place in round_]
    heads = {place: (chip ^ place) * 2 + core for place in order}
    others = {place: (chip ^ place) * 2 + 1 - core for place in order}
    sent = [[heads[place] ^ part for place in round_] for round_ in ROUNDS]
    kernels = in_kernels(unit, rows)
    width = 2 * unit
    pieces, features = prepared(
        kv_weight,
        sent + [[others[p] for p in order]],
        pair,
        hidden,
        kv_gain,
        [
            [(tile ^ j) * CHIPS + (chip ^ place) for j in range(tile_count)]
            for place in range(CHIPS)
        ],
        width,
        query_states,
        kernels,
    )
    sent, traded = pieces[:-1], pieces[-1]

    def to_tile(value, j, flip):
        if not share:
            return swapped(value, j * KVH)
        pairs = [
            (g * lane_count + d, g * lane_count + (d ^ (j * KVH) ^ (g if flip else 0)))
            for g in range(2)
            for d in range(lane_count)
        ]
        return lax.ppermute(value, ("groups", "row"), pairs)

    far = [[to_tile(value, j, True) for j in range(1, tile_count)] for value in sent]
    held = [features[0]] + [swapped(features[p], 2 * p) for p in range(1, CHIPS)]

    traded, held[1] = lax.optimization_barrier((traded, held[1]))
    traded = swapped(traded, 1)

    def shared(number):
        blocks = []
        for j, value in enumerate(far[number], 1):
            other = swapped(value, 1, "groups") if share else to_tile(traded[number], j, False)
            blocks += [value, other]
        return blocks

    firsts = [core] + [core ^ part] * (tile_count - 1)
    blocks = shared(0)
    held[2], held[3], blocks, far = lax.optimization_barrier((held[2], held[3], blocks, far))
    tokens = held + [swapped(piece, 1) for piece in held]
    total = None
    done = 0
    for number, round_ in enumerate(ROUNDS):
        if number:
            blocks = shared(number)
        here = [heads[place] for place in round_]
        partials = projected(
            tokens, here, pair, kv_weight, traded, done, firsts, blocks, rows, kernels
        )
        done += len(round_)
        if number == 0:
            partials, tokens = lax.optimization_barrier((partials, tokens))
            results = meanwhile(tokens)
        for partial, place in zip(partials, round_):
            if place:
                partial = swapped(partial, 2 * place)
            pieces = partial.reshape(2, CHIPS, rows, pair).astype(F32)
            pieces = jnp.stack([pieces[:, j ^ place] for j in range(CHIPS)], axis=1)
            total = pieces if total is None else total + pieces
    key_values = total.astype(BF16).reshape(2 * CHIPS * rows, pair)
    sources = jnp.stack(
        [tile * KVH + (chip ^ j) * 2 + (core ^ e) for e in range(2) for j in range(CHIPS)]
    )
    key_pos = (sources[:, None] * rows + jnp.arange(rows, dtype=jnp.int32)[None, :]).reshape(-1)
    return key_values, key_pos, results


def gather_rows(own):
    ours = [own] + [swapped(own, 2 * place) for place in range(1, CHIPS)]
    theirs = swapped(jnp.stack(ours), 1)
    return ours + [theirs]


def scatter_rows(kept, sent):
    both = kept + swapped(sent, 1).astype(F32)
    total = both[0]
    for place in range(1, CHIPS):
        total = total + swapped(both[place].astype(BF16), 2 * place).astype(F32)
    return total


def attend_rows(queries, query_pos, query_floor, key_values, key_pos):
    row_count = queries.shape[0]
    head_count = queries.shape[1] // HD
    key_part = key_values[:, :HD]
    value_part = key_values[:, HD:]
    grouped = queries.reshape(row_count, head_count, HD)
    scores = jnp.einsum("rhd,kd->rhk", grouped, key_part, preferred_element_type=F32) * HD ** (-0.5)
    capped = CAP * jnp.tanh(scores / CAP)
    visible = (key_pos[None, :] <= query_pos[:, None]) & (key_pos[None, :] >= query_floor[:, None])
    weights = jnp.where(visible[:, None, :], jnp.exp(capped), 0.0)
    totals = jnp.sum(weights, axis=2)
    weighted = jnp.einsum(
        "rhk,kd->rhd", weights.astype(BF16), value_part, preferred_element_type=F32
    )
    return weighted.reshape(row_count, head_count * HD), totals


def on_device(
    hidden, kv_gain, kv_weight, query_states, query_gain, query_weight, output_weight, block_bounds
):
    tile_count = lax.axis_size("row") // KVH
    tile = lax.axis_index("row") // KVH
    depth = hidden.shape[1]
    slice_depth = query_weight.shape[2]
    query_count = query_states.shape[1]
    row_number = jnp.arange(query_count, dtype=jnp.int32)
    query_pos = jnp.repeat(block_bounds[:, 1], QBLK) + row_number % QBLK
    query_floor = jnp.repeat(block_bounds[:, 0], QBLK)

    me = lax.axis_index("row")
    chip, core = me // 2 % CHIPS, me % 2
    place_now = jnp.stack([chip, core]).astype(jnp.int32)
    unit, rows = query_states.shape[0], hidden.shape[0]
    kernels = in_kernels(unit, rows)
    width = query_weight.shape[3]
    own_rows = query_states
    small = jax.ShapeDtypeStruct((16, query_count), BF16)
    spread = jax.ShapeDtypeStruct((query_count, query_count), F32)
    wide = [jax.ShapeDtypeStruct((query_count, width), kind) for kind in (BF16, F32)]
    flops = 2 * query_count * slice_depth * width

    def query_parts(section, pieces):
        gain = lax.dynamic_slice_in_dim(query_gain[section], tile * slice_depth, slice_depth)
        if not kernels:
            pieces = [
                part
                for piece in pieces
                for part in (piece if piece.ndim == 3 else [piece[-(own_rows.size // piece.shape[1]) :]])
            ]
            pieces = [piece.reshape(own_rows.shape) for piece in pieces]
            ours, theirs = (
                jnp.stack(natural(half, chip)) for half in (pieces[:CHIPS], pieces[CHIPS:])
            )
            stream = in_order(ours, theirs, core).astype(F32)
            scaled = (stream * gain[:, None]).astype(BF16)
            partial = lax.dot_general(
                scaled, query_weight[section, 0], (((0,), (0,)), ((), ())), preferred_element_type=F32
            )
            squares = jnp.sum(stream * stream, axis=0)
            return partial.astype(BF16), partial, squares.astype(BF16), squares
        return call(
            functools.partial(query_kernel, query_count),
            "query",
            wide + [small, spread],
            [place_now],
            [gain[None, :], query_weight[section, 0]],
            [
                pltpu.VMEM((slice_depth, query_count), BF16),
                pltpu.VMEM((KVH, own_rows.size // (2 * unit * tile_count), 2 * unit * tile_count), BF16),
                pltpu.SemaphoreType.DMA((KVH,)),
            ],
            flops,
            pieces,
        )

    key_values, key_pos, parts = key_values_of(
        hidden, kv_gain, kv_weight, query_states, functools.partial(query_parts, 0)
    )
    positions = [query_pos[:, None], query_floor[:, None], key_pos[None, :]]
    for section in range(query_gain.shape[0]):
        if section:
            parts = query_parts(section, gather_rows(own_rows))
        sent, partial, squares_sent, squares = parts
        if kernels:
            far = zip(over_tiles(sent, tile_count)[1:], over_tiles(squares_sent, tile_count)[1:])
            sent, weighted, totals_sent, totals = call(
                functools.partial(attend_kernel, depth, tile_count - 1),
                "attend",
                wide + [small, spread],
                [],
                positions + [key_values, partial, squares] + [value for pair in far for value in pair],
                (),
                flops // 2,
            )
            far = zip(over_tiles(sent, tile_count)[1:], over_tiles(totals_sent, tile_count)[1:])
            shape = (CHIPS, unit, query_count)
            kept, sent = call(
                functools.partial(update_kernel, tile_count - 1),
                "update",
                [jax.ShapeDtypeStruct(shape, F32), jax.ShapeDtypeStruct(shape, BF16)],
                [place_now],
                [output_weight[section, 0], weighted, totals]
                + [value for pair in far for value in pair],
                (),
                flops,
            )
        else:
            square_sum = sum(over_tiles(squares_sent, tile_count)[1:], squares)
            query_sum = sum(over_tiles(sent, tile_count)[1:], partial)
            inverse = lax.rsqrt(square_sum / depth + EPSILON)
            queries = (query_sum * inverse[:, None]).astype(BF16)
            weighted, totals = attend_rows(queries, query_pos, query_floor, key_values, key_pos)
            total_sum = sum(over_tiles(totals.astype(BF16), tile_count)[1:], totals)
            weighted_sum = sum(over_tiles(weighted.astype(BF16), tile_count)[1:], weighted)
            attended = (
                (weighted_sum.reshape(query_count, QPK, HD) / total_sum[:, :, None])
                .reshape(query_count, QPK * HD)
                .astype(BF16)
            )
            update = lax.dot_general(
                output_weight[section, 0],
                attended,
                (((1,), (1,)), ((), ())),
                preferred_element_type=F32,
            )
            split = update.reshape(CHIPS, 2, unit, query_count)
            kept = jnp.where(core == 0, split[:, 0], split[:, 1])
            sent = jnp.where(core == 0, split[:, 1], split[:, 0]).astype(BF16)
            kept, sent = (jnp.stack(natural(value, chip)) for value in (kept, sent))
        own_rows = (own_rows.astype(F32) + scatter_rows(kept, sent)).astype(BF16)
    return own_rows


def solution(mesh):
    in_specs = (
        P(("groups", "row"), None),
        P(),
        P("row", None),
        P("row", "groups"),
        P(),
        P(None, "row", None, None),
        P(None, "row", None, None),
        P("groups", None),
    )
    return jax.shard_map(
        on_device, mesh=mesh, in_specs=in_specs, out_specs=P("row", "groups"), check_vma=False
    )
```

time: 187 us -> 154 us (0.82)
  Pallas kernels: 0 us -> 24 us
  waiting for transfers between devices: 93.2 us -> 75.9 us
  matrix products: 16.3 us -> 0 us
  other arithmetic: 15.7 us -> 1.69 us
  starting transfers between devices: 47.1 us -> 39.7 us
    ppermute x40 -> x33, waiting for transfers between devices: 93.2 us -> 59.4 us  [swapped(): return lax.ppermute(value, axis, pairs)]
    pallas_call x0 -> x9, Pallas kernels: none -> 24 us  [the longest x6 12.7 us: call(): pl.pallas_call(kernel, out_shape=out_shape, in_specs=[smem] * len(scalars...]
    ppermute x0 -> x2, waiting for transfers between devices: none -> 16.4 us  [to_tile(): return lax.ppermute(value, ('groups', 'row'), pairs)]
    dot_general x12 -> x0, matrix products: 16.3 us -> none  [the longest x4 5.31 us: key_values_of(): lax.dot_general(tokens, weight, (((1,), (0,)), ((), ())), preferred_eleme...]
    ppermute x40 -> x33, starting transfers between devices: 47.1 us -> 35.5 us  [swapped(): return lax.ppermute(value, axis, pairs)]
    squeeze x0 -> x2, local copies, waits for them, and re-layouts: none -> 5.71 us  [the longest x1 5.15 us: query_parts(): query_weight[section, 0]]
    concatenate x4 -> x0, other arithmetic: 4.34 us -> none  [the longest x3 3.15 us: features(): jnp.concatenate([lax.dynamic_slice_in_dim(normed, ((tile ^ j) * KVH + (ch...]
    ppermute x0 -> x2, starting transfers between devices: none -> 4.18 us  [to_tile(): return lax.ppermute(value, ('groups', 'row'), pairs)]
  transfers between devices with their start and end apart: 40 -> 35, of which waited for: 25 -> 22; matrix products, arithmetic and copies ran while one was open for 18% -> 6% of each run, Pallas kernels for 0% -> 6%
where the time goes in v5:
time: 154 us; the launch traced here: 153 us
  waiting for transfers between devices  75.9 us (49%)
  starting transfers between devices  39.7 us (26%)
  Pallas kernels  24 us (16%)
  local copies, waits for them, and re-layouts  11.9 us (8%)
  other arithmetic  1.69 us (1%)
    ppermute x33, waiting for transfers between devices, swapped(): return lax.ppermute(value, axis, pairs)  59.4 us
    ppermute x33, starting transfers between devices, swapped(): return lax.ppermute(value, axis, pairs)  35.5 us
    ppermute x2, waiting for transfers between devices, to_tile(): return lax.ppermute(value, ('groups', 'row'), pairs)  16.4 us
    pallas_call x6, Pallas kernels, call(): pl.pallas_call(kernel, out_shape=out_shape, in_specs=[smem] * len(scalars...  12.7 us
    pallas_call x2, Pallas kernels, projected(): pl.pallas_call(functools.partial(project_kernel, rows, len(heads), pair,...  6.45 us
    squeeze x1, local copies, waits for them, and re-layouts, query_parts(): query_weight[section, 0]  5.15 us
    pallas_call x1, Pallas kernels, prepared(): pl.pallas_call(functools.partial(prepare_kernel, pair, counts, width), ou...  4.79 us
    ppermute x2, starting transfers between devices, to_tile(): return lax.ppermute(value, ('groups', 'row'), pairs)  4.18 us
  transfers between devices with their start and end apart: 35, of which 22 were waited for; matrix products, arithmetic and copies ran while one was open for 6% of the time, Pallas kernels for 6%

profile of v5, /device:TPU:0, one launch (start us, length us, event | category | flops | bytes accessed | tf_op | source)
XLA Modules:
  0.0 153.4 jit_solution(17223437364032009593)
XLA Ops:
  1.2 4.8 %prepare.1 = (bf16[2,320,256]{2,1,0:T(8,128)(2,1)}, bf16[2,320,256]{2,1,0:T(8,128)(2,1)}, bf16[4,320,256]{2,1,0:T(8,128)(2,1)}, bf16[160,1280]{1,0:T(8,128)(2,1)...) custom-call(s32[8]{0:T(128)} %stack.170.heads_ref, s32[8]{0:T(128)} %stack.179.starts_ref, ...), custom_call_target="tpu_custom_call" | custom-call | tf_op jit(solution)/shard_map/prepare/pallas_call | solution.py:122
  6.0 4.1 %collective-permute-start.4 = (bf16[2,320,256]{2,1,0:T(8,128)(2,1)}, bf16[2,320,256]{2,1,0:T(8,128)(2,1)}, u32[]{:S(2)}, u32[]{:S(2)}) collective-permute-start(bf16[2,320,256]{2,1,0:T(8,128)(2,1)} %get-tuple-element.60), channel_id=1, source_target_pairs={{0,8},{1,9},{2,10},{3,11},{4,12},{5,13},{6,14},{7,15},{8,0},{9,1},... | collective-permute-start | bytes 983048 | tf_op jit(solution)/shard_map/ppermute | solution.py:395
  10.2 1.7 %collective-permute-start = (bf16[160,1280]{1,0:T(8,128)(2,1)}, bf16[160,1280]{1,0:T(8,128)(2,1)}, u32[]{:S(2)}, u32[]{:S(2)}) collective-permute-start(bf16[160,1280]{1,0:T(8,128)(2,1)} %get-tuple-element.54), channel_id=1, source_target_pairs={{0,2},{1,3},{2,0},{3,1},{4,6},{5,7},{6,4},{7,5},{8,10},{9,11},{10,... | collective-permute-start | bytes 1228808 | tf_op jit(solution)/shard_map/ppermute | solution.py:26
  12.0 1.6 %collective-permute-start.2 = (bf16[160,1280]{1,0:T(8,128)(2,1)}, bf16[160,1280]{1,0:T(8,128)(2,1)}, u32[]{:S(2)}, u32[]{:S(2)}) collective-permute-start(bf16[160,1280]{1,0:T(8,128)(2,1)} %get-tuple-element.58), channel_id=1, source_target_pairs={{0,4},{1,5},{2,6},{3,7},{4,0},{5,1},{6,2},{7,3},{8,12},{9,13},{10,... | collective-permute-start | bytes 1228808 | tf_op jit(solution)/shard_map/ppermute | solution.py:26
  13.7 1.0 slice_reduce_fusion
  16.0 5.1 %slice_bitcast_fusion.2 = (bf16[2560,640]{1,0:T(8,128)(2,1)S(1)}, bf16[2560,640]{1,0:T(8,128)(2,1)}) fusion(bf16[2,1,2560,640]{3,2,1,0:T(8,128)(2,1)} %param.13), kind=kLoop, calls=%fused_computation.2 | loop fusion | bytes 13107200 | tf_op jit(solution)/shard_map/squeeze | solution.py:520
  21.4 11.7 %collective-permute-done.4.refs_8_ = bf16[2,320,256]{2,1,0:T(8,128)(2,1)} collective-permute-done((bf16[2,320,256]{2,1,0:T(8,128)(2,1)}, bf16[2,320,256]{2,1,0:T(8,128)(2,1)}, u32[]{:S(2)}, u32[]{:S(2)}) %collective-permute-start.4) | collective-permute-done | bytes 327712 | tf_op jit(solution)/shard_map/ppermute | solution.py:395
  33.1 1.1 collective-permute-start.5
  34.6 4.7 %collective-permute-done.6.refs_8_ = bf16[2,320,256]{2,1,0:T(8,128)(2,1)} collective-permute-done((bf16[2,320,256]{2,1,0:T(8,128)(2,1)}, bf16[2,320,256]{2,1,0:T(8,128)(2,1)}, u32[]{:S(2)}, u32[]{:S(2)}) %collective-permute-start.6) | collective-permute-done | bytes 327712 | tf_op jit(solution)/shard_map/ppermute | solution.py:395
  39.8 4.5 %collective-permute-done.3.refs_3_ = bf16[160,1280]{1,0:T(8,128)(2,1)} collective-permute-done((bf16[160,1280]{1,0:T(8,128)(2,1)}, bf16[160,1280]{1,0:T(8,128)(2,1)}, u32[]{:S(2)}, u32[]{:S(2)}) %collective-permute-start.3) | collective-permute-done | bytes 409632 | tf_op jit(solution)/shard_map/ppermute | solution.py:26
  44.9 2.1 %collective-permute-start.13 = (bf16[2,320,256]{2,1,0:T(8,128)(2,1)}, bf16[2,320,256]{2,1,0:T(8,128)(2,1)S(1)}, u32[]{:S(2)}, u32[]{:S(2)}) collective-permute-start(bf16[2,320,256]{2,1,0:T(8,128)(2,1)} %collective-permute-done.6.refs_8_), channel_id=1, source_target_pairs={{0,16},{16,0},{1,17},{17,1},{2,18},{18,2},{3,19},{19,3},{4,20},{20... | collective-permute-start | bytes 983048 | tf_op jit(solution)/shard_map/ppermute | solution.py:26
  47.1 1.3 copy-done.1
  48.4 1.0 copy-done.2
  49.4 3.3 %project.2 = (bf16[1024,256]{1,0:T(8,128)(2,1)S(1)}, bf16[1024,256]{1,0:T(8,128)(2,1)S(1)}) custom-call(s32[2]{0:T(128)S(1)} %pad_add_fusion.1.first_ref, s32[2]{0:T(128)S(1)} %pad_add_fusion.2.heads_ref, bf16[320,2048]{1,0:T(8,128)(2,1)S(1)} %copy-done.1, bf16[4,320,256]{2,1,0:T(8,128)(2,1)S(1)} %collective-permute-done.1.traded_ref, ...), custom_call_target="tpu_custom_call" | custom-call | flops 10737418240 | bytes 2621440 | tf_op jit(solution)/shard_map/project/pallas_call | solution.py:197
  52.8 1.6 %collective-permute-start.11 = (bf16[1024,256]{1,0:T(8,128)(2,1)S(1)}, bf16[1024,256]{1,0:T(8,128)(2,1)S(1)}, u32[]{:S(2)}, u32[]{:S(2)}) collective-permute-start(bf16[1024,256]{1,0:T(8,128)(2,1)S(1)} %get-tuple-element.68), channel_id=1, source_target_pairs={{0,2},{1,3},{2,0},{3,1},{4,6},{5,7},{6,4},{7,5},{8,10},{9,11},{10,... | collective-permute-start | bytes 1572872 | tf_op jit(solution)/shard_map/ppermute | solution.py:26
  55.2 3.1 %project.3 = (bf16[1024,256]{1,0:T(8,128)(2,1)S(1)}, bf16[1024,256]{1,0:T(8,128)(2,1)S(1)}) custom-call(s32[2]{0:T(128)S(1)} %pad_add_fusion.1.first_ref, s32[2]{0:T(128)S(1)} %pad_add_fusion.3.heads_ref, bf16[320,2048]{1,0:T(8,128)(2,1)S(1)} %copy-done.1, bf16[4,320,256]{2,1,0:T(8,128)(2,1)S(1)} %collective-permute-done.1.traded_ref, ...), custom_call_target="tpu_custom_call" | custom-call | flops 10737418240 | bytes 2621440 | tf_op jit(solution)/shard_map/project/pallas_call | solution.py:197
  58.3 1.2 collective-permute-start.14
  59.5 2.9 %query.2 = (bf16[128,640]{1,0:T(8,128)(2,1)S(1)}, f32[128,640]{1,0:T(8,128)S(1)}, bf16[16,128]{1,0:T(8,128)(2,1)S(1)}, f32[128,128]{1,0:T(8,128)S(1)}) custom-call(s32[2]{0:T(128)S(1)} %pad_add_fusion.place_ref, f32[1,2560]{1,0:T(1,128)S(1)} %constant_dynamic-slice_fusion.1.gain_ref, bf16[2560,640]{1,0:T(8,128)(2,1)S(1)} %get-tuple-element.107.weight_ref, ...), custom_call_target="tpu_custom_call" | custom-call | flops 419430400 | bytes 3281920 | tf_op jit(solution)/shard_map/query/pallas_call | solution.py:333
  62.4 4.7 %collective-permute-start.16 = (bf16[16,128]{1,0:T(8,128)(2,1)S(1)}, bf16[16,128]{1,0:T(8,128)(2,1)S(1)}, u32[]{:S(2)}, u32[]{:S(2)}) collective-permute-start(bf16[16,128]{1,0:T(8,128)(2,1)S(1)} %get-tuple-element.84), channel_id=1, source_target_pairs={{0,8},{1,9},{2,10},{3,11},{4,12},{5,13},{6,14},{7,15},{8,0},{9,1},... | collective-permute-start | bytes 12296 | tf_op jit(solution)/shard_map/ppermute | solution.py:26
  67.3 2.0 %collective-permute-done.12 = bf16[1024,256]{1,0:T(8,128)(2,1)S(1)} collective-permute-done((bf16[1024,256]{1,0:T(8,128)(2,1)S(1)}, bf16[1024,256]{1,0:T(8,128)(2,1)S(1)}, u32[]{:S(2)}, u32[]{:S(2)}) %collective-permute-start.12) | collective-permute-done | bytes 524320 | tf_op jit(solution)/shard_map/ppermute | solution.py:26
  69.3 13.3 %collective-permute-done.14 = bf16[1024,256]{1,0:T(8,128)(2,1)S(1)} collective-permute-done((bf16[1024,256]{1,0:T(8,128)(2,1)S(1)}, bf16[1024,256]{1,0:T(8,128)(2,1)S(1)}, u32[]{:S(2)}, u32[]{:S(2)}) %collective-permute-start.14) | collective-permute-done | bytes 524320 | tf_op jit(solution)/shard_map/ppermute | solution.py:26
  83.1 1.9 %attend.2 = (bf16[128,640]{1,0:T(8,128)(2,1)S(1)}, f32[128,640]{1,0:T(8,128)S(1)}, bf16[16,128]{1,0:T(8,128)(2,1)S(1)}, f32[128,128]{1,0:T(8,128)S(1)}) custom-call(s32[128,1]{1,0:T(8,128)S(1)} %fusion.12.query_pos_ref, s32[128,1]{1,0:T(8,128)S(1)} %broadcast_in_dim_reshape.5.query_floor_ref, s32[1,1024]{1,0:T(1,128)S(1)} %bitcast.95, ...), custom_call_target="tpu_custom_call" | custom-call | flops 209715200 | bytes 891392 | tf_op jit(solution)/shard_map/attend/pallas_call | solution.py:333
  85.0 2.8 %collective-permute-start.18 = (bf16[16,128]{1,0:T(8,128)(2,1)S(1)}, bf16[16,128]{1,0:T(8,128)(2,1)S(1)}, u32[]{:S(2)}, u32[]{:S(2)}) collective-permute-start(bf16[16,128]{1,0:T(8,128)(2,1)S(1)} %get-tuple-element.88), channel_id=1, source_target_pairs={{0,8},{1,9},{2,10},{3,11},{4,12},{5,13},{6,14},{7,15},{8,0},{9,1},... | collective-permute-start | bytes 12296 | tf_op jit(solution)/shard_map/ppermute | solution.py:26
  88.5 1.0 collective-permute-done.18.refs_1_
  89.5 7.6 %collective-permute-done.17.refs_0_ = bf16[128,640]{1,0:T(8,128)(2,1)S(1)} collective-permute-done((bf16[128,640]{1,0:T(8,128)(2,1)S(1)}, bf16[128,640]{1,0:T(8,128)(2,1)S(1)}, u32[]{:S(2)}, u32[]{:S(2)}) %collective-permute-start.17) | collective-permute-done | bytes 163872 | tf_op jit(solution)/shard_map/ppermute | solution.py:26
  97.1 1.8 %update.2 = (f32[4,320,128]{2,1,0:T(8,128)S(1)}, bf16[4,320,128]{2,1,0:T(8,128)(2,1)S(1)}) custom-call(s32[2]{0:T(128)S(1)} %pad_add_fusion.place_ref, bf16[2560,640]{1,0:T(8,128)(2,1)S(1)} %get-tuple-element.109.weight_ref, f32[128,640]{1,0:T(8,128)S(1)} %get-tuple-element.85.kept_ref, f32[128,128]{1,0:T(8,128)S(1)} %get-tuple-element.86.totals_ref, ...), custom_call_target="tpu_custom_call" | custom-call | flops 419430400 | bytes 3641344 | tf_op jit(solution)/shard_map/update/pallas_call | solution.py:333
  99.0 1.6 %collective-permute-done.19 = bf16[4,320,128]{2,1,0:T(8,128)(2,1)S(1)} collective-permute-done((bf16[4,320,128]{2,1,0:T(8,128)(2,1)S(1)}, bf16[4,320,128]{2,1,0:T(8,128)(2,1)S(1)}, u32[]{:S(2)}, u32[]{:S(2)}) %collective-permute-start.19) | collective-permute-done | bytes 327712 | tf_op jit(solution)/shard_map/ppermute | solution.py:26
  100.7 0.9 collective-permute-start.20
  101.7 2.6 %collective-permute-start.21 = (bf16[320,128]{1,0:T(8,128)(2,1)S(1)}, bf16[320,128]{1,0:T(8,128)(2,1)S(1)}, u32[]{:S(2)}, u32[]{:S(2)}) collective-permute-start(bf16[320,128]{1,0:T(8,128)(2,1)S(1)} %get-tuple-element.126), channel_id=1, source_target_pairs={{0,4},{1,5},{2,6},{3,7},{4,0},{5,1},{6,2},{7,3},{8,12},{9,13},{10,... | collective-permute-start | bytes 245768 | tf_op jit(solution)/shard_map/ppermute | solution.py:26
  104.3 1.9 %collective-permute-done.20 = bf16[320,128]{1,0:T(8,128)(2,1)S(1)} collective-permute-done((bf16[320,128]{1,0:T(8,128)(2,1)S(1)}, bf16[320,128]{1,0:T(8,128)(2,1)S(1)}, u32[]{:S(2)}, u32[]{:S(2)}) %collective-permute-start.20) | collective-permute-done | bytes 81952 | tf_op jit(solution)/shard_map/ppermute | solution.py:26
  106.2 1.5 collective-permute-done.22
  109.2 1.5 collective-permute-start.24
  110.7 1.2 collective-permute-start.23
  111.8 1.9 %collective-permute-done.25.refs_3_ = bf16[320,128]{1,0:T(8,128)(2,1)S(1)} collective-permute-done((bf16[320,128]{1,0:T(8,128)(2,1)S(1)}, bf16[320,128]{1,0:T(8,128)(2,1)S(1)}, u32[]{:S(2)}, u32[]{:S(2)}) %collective-permute-start.25) | collective-permute-done | bytes 81952 | tf_op jit(solution)/shard_map/ppermute | solution.py:26
  114.0 1.1 collective-permute-done.23.refs_1_
  115.3 1.6 %collective-permute-done.26.refs_4_ = bf16[4,320,128]{2,1,0:T(8,128)(2,1)S(1)} collective-permute-done((bf16[4,320,128]{2,1,0:T(8,128)(2,1)S(1)}, bf16[4,320,128]{2,1,0:T(8,128)(2,1)S(1)}, u32[]{:S(2)}, u32[]{:S(2)}) %collective-permute-start.26) | collective-permute-done | bytes 327712 | tf_op jit(solution)/shard_map/ppermute | solution.py:26
  116.9 2.5 %query.3 = (bf16[128,640]{1,0:T(8,128)(2,1)S(1)}, f32[128,640]{1,0:T(8,128)S(1)}, bf16[16,128]{1,0:T(8,128)(2,1)S(1)}, f32[128,128]{1,0:T(8,128)S(1)}) custom-call(s32[2]{0:T(128)S(1)} %pad_add_fusion.place_ref, f32[1,2560]{1,0:T(1,128)S(1)} %constant_dynamic-slice_fusion.gain_ref, bf16[2560,640]{1,0:T(8,128)(2,1)S(1)} %copy-done, ...), custom_call_target="tpu_custom_call" | custom-call | flops 419430400 | bytes 3281920 | tf_op jit(solution)/shard_map/query/pallas_call | solution.py:333
  119.9 2.5 %collective-permute-start.28 = (bf16[16,128]{1,0:T(8,128)(2,1)S(1)}, bf16[16,128]{1,0:T(8,128)(2,1)S(1)}, u32[]{:S(2)}, u32[]{:S(2)}) collective-permute-start(bf16[16,128]{1,0:T(8,128)(2,1)S(1)} %get-tuple-element.94), channel_id=1, source_target_pairs={{0,8},{1,9},{2,10},{3,11},{4,12},{5,13},{6,14},{7,15},{8,0},{9,1},... | collective-permute-start | bytes 12296 | tf_op jit(solution)/shard_map/ppermute | solution.py:26
  122.3 7.8 %collective-permute-done.28.refs_3_ = bf16[16,128]{1,0:T(8,128)(2,1)S(1)} collective-permute-done((bf16[16,128]{1,0:T(8,128)(2,1)S(1)}, bf16[16,128]{1,0:T(8,128)(2,1)S(1)}, u32[]{:S(2)}, u32[]{:S(2)}) %collective-permute-start.28) | collective-permute-done | bytes 4128 | tf_op jit(solution)/shard_map/ppermute | solution.py:26
  130.2 1.9 %attend.3 = (bf16[128,640]{1,0:T(8,128)(2,1)S(1)}, f32[128,640]{1,0:T(8,128)S(1)}, bf16[16,128]{1,0:T(8,128)(2,1)S(1)}, f32[128,128]{1,0:T(8,128)S(1)}) custom-call(s32[128,1]{1,0:T(8,128)S(1)} %fusion.12.query_pos_ref, s32[128,1]{1,0:T(8,128)S(1)} %broadcast_in_dim_reshape.5.query_floor_ref, s32[1,1024]{1,0:T(1,128)S(1)} %bitcast.96, ...), custom_call_target="tpu_custom_call" | custom-call | flops 209715200 | bytes 891392 | tf_op jit(solution)/shard_map/attend/pallas_call | solution.py:333
  132.1 2.9 %collective-permute-start.30 = (bf16[16,128]{1,0:T(8,128)(2,1)S(1)}, bf16[16,128]{1,0:T(8,128)(2,1)S(1)}, u32[]{:S(2)}, u32[]{:S(2)}) collective-permute-start(bf16[16,128]{1,0:T(8,128)(2,1)S(1)} %get-tuple-element.98), channel_id=1, source_target_pairs={{0,8},{1,9},{2,10},{3,11},{4,12},{5,13},{6,14},{7,15},{8,0},{9,1},... | collective-permute-start | bytes 12296 | tf_op jit(solution)/shard_map/ppermute | solution.py:26
  135.1 6.6 %collective-permute-done.30.refs_1_ = bf16[16,128]{1,0:T(8,128)(2,1)S(1)} collective-permute-done((bf16[16,128]{1,0:T(8,128)(2,1)S(1)}, bf16[16,128]{1,0:T(8,128)(2,1)S(1)}, u32[]{:S(2)}, u32[]{:S(2)}) %collective-permute-start.30) | collective-permute-done | bytes 4128 | tf_op jit(solution)/shard_map/ppermute | solution.py:26
  141.6 1.8 %update.3 = (f32[4,320,128]{2,1,0:T(8,128)S(1)}, bf16[4,320,128]{2,1,0:T(8,128)(2,1)S(1)}) custom-call(s32[2]{0:T(128)S(1)} %pad_add_fusion.place_ref, bf16[2560,640]{1,0:T(8,128)(2,1)S(1)} %get-tuple-element.110.weight_ref, f32[128,640]{1,0:T(8,128)S(1)} %get-tuple-element.95.kept_ref, f32[128,128]{1,0:T(8,128)S(1)} %get-tuple-element.96.totals_ref, ...), custom_call_target="tpu_custom_call" | custom-call | flops 419430400 | bytes 3641344 | tf_op jit(solution)/shard_map/update/pallas_call | solution.py:333
  143.5 1.6 %collective-permute-done.31 = bf16[4,320,128]{2,1,0:T(8,128)(2,1)S(1)} collective-permute-done((bf16[4,320,128]{2,1,0:T(8,128)(2,1)S(1)}, bf16[4,320,128]{2,1,0:T(8,128)(2,1)S(1)}, u32[]{:S(2)}, u32[]{:S(2)}) %collective-permute-start.31) | collective-permute-done | bytes 327712 | tf_op jit(solution)/shard_map/ppermute | solution.py:26
  145.2 1.1 collective-permute-start.32
  146.4 2.4 %collective-permute-start.33 = (bf16[320,128]{1,0:T(8,128)(2,1)S(1)}, bf16[320,128]{1,0:T(8,128)(2,1)S(1)}, u32[]{:S(2)}, u32[]{:S(2)}) collective-permute-start(bf16[320,128]{1,0:T(8,128)(2,1)S(1)} %get-tuple-element.123), channel_id=1, source_target_pairs={{0,4},{1,5},{2,6},{3,7},{4,0},{5,1},{6,2},{7,3},{8,12},{9,13},{10,... | collective-permute-start | bytes 245768 | tf_op jit(solution)/shard_map/ppermute | solution.py:26
  148.8 1.9 %collective-permute-done.32 = bf16[320,128]{1,0:T(8,128)(2,1)S(1)} collective-permute-done((bf16[320,128]{1,0:T(8,128)(2,1)S(1)}, bf16[320,128]{1,0:T(8,128)(2,1)S(1)}, u32[]{:S(2)}, u32[]{:S(2)}) %collective-permute-start.32) | collective-permute-done | bytes 81952 | tf_op jit(solution)/shard_map/ppermute | solution.py:26
  150.7 1.6 %collective-permute-done.34 = bf16[320,128]{1,0:T(8,128)(2,1)S(1)} collective-permute-done((bf16[320,128]{1,0:T(8,128)(2,1)S(1)}, bf16[320,128]{1,0:T(8,128)(2,1)S(1)}, u32[]{:S(2)}, u32[]{:S(2)}) %collective-permute-start.34) | collective-permute-done | bytes 81952 | tf_op jit(solution)/shard_map/ppermute | solution.py:26
  (78 shorter events, 10.9 us)
Async XLA Ops:
  6.0 27.1 %collective-permute-start.4 = (bf16[2,320,256]{2,1,0:T(8,128)(2,1)}, bf16[2,320,256]{2,1,0:T(8,128)(2,1)}, u32[]{:S(2)}, u32[]{:S(2)}) collective-permute-start(bf16[2,320,256]{2,1,0:T(8,128)(2,1)} %get-tuple-element.60), channel_id=1, source_target_pairs={{0,8},{1,9},{2,10},{3,11},{4,12},{5,13},{6,14},{7,15},{8,0},{9,1},... | collective-permute-start | bytes 983048 | tf_op jit(solution)/shard_map/ppermute | solution.py:395
  10.1 29.2 %collective-permute-start.6 = (bf16[2,320,256]{2,1,0:T(8,128)(2,1)}, bf16[2,320,256]{2,1,0:T(8,128)(2,1)}, u32[]{:S(2)}, u32[]{:S(2)}) collective-permute-start(bf16[2,320,256]{2,1,0:T(8,128)(2,1)} %get-tuple-element.61), channel_id=1, source_target_pairs={{0,8},{1,9},{2,10},{3,11},{4,12},{5,13},{6,14},{7,15},{8,0},{9,1},... | collective-permute-start | bytes 983048 | tf_op jit(solution)/shard_map/ppermute | solution.py:395
  10.2 24.1 %collective-permute-start = (bf16[160,1280]{1,0:T(8,128)(2,1)}, bf16[160,1280]{1,0:T(8,128)(2,1)}, u32[]{:S(2)}, u32[]{:S(2)}) collective-permute-start(bf16[160,1280]{1,0:T(8,128)(2,1)} %get-tuple-element.54), channel_id=1, source_target_pairs={{0,2},{1,3},{2,0},{3,1},{4,6},{5,7},{6,4},{7,5},{8,10},{9,11},{10,... | collective-permute-start | bytes 1228808 | tf_op jit(solution)/shard_map/ppermute | solution.py:26
  12.0 27.4 %collective-permute-start.2 = (bf16[160,1280]{1,0:T(8,128)(2,1)}, bf16[160,1280]{1,0:T(8,128)(2,1)}, u32[]{:S(2)}, u32[]{:S(2)}) collective-permute-start(bf16[160,1280]{1,0:T(8,128)(2,1)} %get-tuple-element.58), channel_id=1, source_target_pairs={{0,4},{1,5},{2,6},{3,7},{4,0},{5,1},{6,2},{7,3},{8,12},{9,13},{10,... | collective-permute-start | bytes 1228808 | tf_op jit(solution)/shard_map/ppermute | solution.py:26
  13.5 30.8 %collective-permute-start.3 = (bf16[160,1280]{1,0:T(8,128)(2,1)}, bf16[160,1280]{1,0:T(8,128)(2,1)}, u32[]{:S(2)}, u32[]{:S(2)}) collective-permute-start(bf16[160,1280]{1,0:T(8,128)(2,1)} %get-tuple-element.59), channel_id=1, source_target_pairs={{0,6},{1,7},{2,4},{3,5},{4,2},{5,3},{6,0},{7,1},{8,14},{9,15},{10,... | collective-permute-start | bytes 1228808 | tf_op jit(solution)/shard_map/ppermute | solution.py:26
  33.1 11.2 %collective-permute-start.5 = (bf16[2,320,256]{2,1,0:T(8,128)(2,1)}, bf16[2,320,256]{2,1,0:T(8,128)(2,1)S(1)}, u32[]{:S(2)}, u32[]{:S(2)}) collective-permute-start(bf16[2,320,256]{2,1,0:T(8,128)(2,1)} %collective-permute-done.4.refs_8_), channel_id=1, source_target_pairs={{0,16},{16,0},{1,17},{17,1},{2,18},{18,2},{3,19},{19,3},{4,20},{20... | collective-permute-start | bytes 983048 | tf_op jit(solution)/shard_map/ppermute | solution.py:26
  34.3 12.8 %collective-permute-start.1 = (bf16[4,320,256]{2,1,0:T(8,128)(2,1)}, bf16[4,320,256]{2,1,0:T(8,128)(2,1)S(1)}, u32[]{:S(2)}, u32[]{:S(2)}) collective-permute-start(bf16[4,320,256]{2,1,0:T(8,128)(2,1)} %get-tuple-element.55), channel_id=1, source_target_pairs={{0,1},{1,0},{2,3},{3,2},{4,5},{5,4},{6,7},{7,6},{8,9},{9,8},{10,11... | collective-permute-start | bytes 1966088 | tf_op jit(solution)/shard_map/ppermute | solution.py:26
  39.3 5.6 %collective-permute-start.7 = (bf16[160,1280]{1,0:T(8,128)(2,1)}, bf16[160,1280]{1,0:T(8,128)(2,1)S(1)}, u32[]{:S(2)}, u32[]{:S(2)}) collective-permute-start(bf16[160,1280]{1,0:T(8,128)(2,1)} %get-tuple-element.70.refs_0_), channel_id=1, source_target_pairs={{0,1},{1,0},{2,3},{3,2},{4,5},{5,4},{6,7},{7,6},{8,9},{9,8},{10,11... | collective-permute-start | bytes 1228808 | tf_op jit(solution)/shard_map/ppermute | solution.py:26
  39.3 7.7 %collective-permute-start.8 = (bf16[160,1280]{1,0:T(8,128)(2,1)}, bf16[160,1280]{1,0:T(8,128)(2,1)S(1)}, u32[]{:S(2)}, u32[]{:S(2)}) collective-permute-start(bf16[160,1280]{1,0:T(8,128)(2,1)} %collective-permute-done.refs_1_), channel_id=1, source_target_pairs={{0,1},{1,0},{2,3},{3,2},{4,5},{5,4},{6,7},{7,6},{8,9},{9,8},{10,11... | collective-permute-start | bytes 1228808 | tf_op jit(solution)/shard_map/ppermute | solution.py:26
  44.4 2.7 %collective-permute-start.9 = (bf16[160,1280]{1,0:T(8,128)(2,1)}, bf16[160,1280]{1,0:T(8,128)(2,1)S(1)}, u32[]{:S(2)}, u32[]{:S(2)}) collective-permute-start(bf16[160,1280]{1,0:T(8,128)(2,1)} %collective-permute-done.2.refs_2_), channel_id=1, source_target_pairs={{0,1},{1,0},{2,3},{3,2},{4,5},{5,4},{6,7},{7,6},{8,9},{9,8},{10,11... | collective-permute-start | bytes 1228808 | tf_op jit(solution)/shard_map/ppermute | solution.py:26
  44.4 2.7 %collective-permute-start.10 = (bf16[160,1280]{1,0:T(8,128)(2,1)}, bf16[160,1280]{1,0:T(8,128)(2,1)S(1)}, u32[]{:S(2)}, u32[]{:S(2)}) collective-permute-start(bf16[160,1280]{1,0:T(8,128)(2,1)} %collective-permute-done.3.refs_3_), channel_id=1, source_target_pairs={{0,1},{1,0},{2,3},{3,2},{4,5},{5,4},{6,7},{7,6},{8,9},{9,8},{10,11... | collective-permute-start | bytes 1228808 | tf_op jit(solution)/shard_map/ppermute | solution.py:26
  44.9 10.2 %collective-permute-start.13 = (bf16[2,320,256]{2,1,0:T(8,128)(2,1)}, bf16[2,320,256]{2,1,0:T(8,128)(2,1)S(1)}, u32[]{:S(2)}, u32[]{:S(2)}) collective-permute-start(bf16[2,320,256]{2,1,0:T(8,128)(2,1)} %collective-permute-done.6.refs_8_), channel_id=1, source_target_pairs={{0,16},{16,0},{1,17},{17,1},{2,18},{18,2},{3,19},{19,3},{4,20},{20... | collective-permute-start | bytes 983048 | tf_op jit(solution)/shard_map/ppermute | solution.py:26
  47.1 1.3 copy-start.1
  48.4 1.0 copy-start.2
  49.4 5.8 %copy-start.3 = (bf16[160,1280]{1,0:T(8,128)(2,1)S(1)}, bf16[160,1280]{1,0:T(8,128)(2,1)}, u32[]{:S(2)}) copy-start(bf16[160,1280]{1,0:T(8,128)(2,1)} %get-tuple-element.70.refs_0_) | copy-start | bytes 1228804
  52.8 14.5 %collective-permute-start.11 = (bf16[1024,256]{1,0:T(8,128)(2,1)S(1)}, bf16[1024,256]{1,0:T(8,128)(2,1)S(1)}, u32[]{:S(2)}, u32[]{:S(2)}) collective-permute-start(bf16[1024,256]{1,0:T(8,128)(2,1)S(1)} %get-tuple-element.68), channel_id=1, source_target_pairs={{0,2},{1,3},{2,0},{3,1},{4,6},{5,7},{6,4},{7,5},{8,10},{9,11},{10,... | collective-permute-start | bytes 1572872 | tf_op jit(solution)/shard_map/ppermute | solution.py:26
  54.3 14.9 %collective-permute-start.12 = (bf16[1024,256]{1,0:T(8,128)(2,1)S(1)}, bf16[1024,256]{1,0:T(8,128)(2,1)S(1)}, u32[]{:S(2)}, u32[]{:S(2)}) collective-permute-start(bf16[1024,256]{1,0:T(8,128)(2,1)S(1)} %get-tuple-element.69), channel_id=1, source_target_pairs={{0,4},{1,5},{2,6},{3,7},{4,0},{5,1},{6,2},{7,3},{8,12},{9,13},{10,... | collective-permute-start | bytes 1572872 | tf_op jit(solution)/shard_map/ppermute | solution.py:26
  58.3 24.3 %collective-permute-start.14 = (bf16[1024,256]{1,0:T(8,128)(2,1)S(1)}, bf16[1024,256]{1,0:T(8,128)(2,1)S(1)}, u32[]{:S(2)}, u32[]{:S(2)}) collective-permute-start(bf16[1024,256]{1,0:T(8,128)(2,1)S(1)} %get-tuple-element.79), channel_id=1, source_target_pairs={{0,6},{1,7},{2,4},{3,5},{4,2},{5,3},{6,0},{7,1},{8,14},{9,15},{10,... | collective-permute-start | bytes 1572872 | tf_op jit(solution)/shard_map/ppermute | solution.py:26
  59.5 28.5 %slice-start = ((s8[6553600]{0:T(1024)(128)(4,1)}), s8[4194304]{0:T(1024)(128)(4,1)S(1)}, s32[]{:S(2)}) async-start(s8[6553600]{0:T(1024)(128)(4,1)} %bitcast.97), calls=%async_computation | async-start | bytes 8388608
  62.4 20.6 %collective-permute-start.16 = (bf16[16,128]{1,0:T(8,128)(2,1)S(1)}, bf16[16,128]{1,0:T(8,128)(2,1)S(1)}, u32[]{:S(2)}, u32[]{:S(2)}) collective-permute-start(bf16[16,128]{1,0:T(8,128)(2,1)S(1)} %get-tuple-element.84), channel_id=1, source_target_pairs={{0,8},{1,9},{2,10},{3,11},{4,12},{5,13},{6,14},{7,15},{8,0},{9,1},... | collective-permute-start | bytes 12296 | tf_op jit(solution)/shard_map/ppermute | solution.py:26
  67.1 15.9 %collective-permute-start.15 = (bf16[128,640]{1,0:T(8,128)(2,1)S(1)}, bf16[128,640]{1,0:T(8,128)(2,1)S(1)}, u32[]{:S(2)}, u32[]{:S(2)}) collective-permute-start(bf16[128,640]{1,0:T(8,128)(2,1)S(1)} %get-tuple-element.83), channel_id=1, source_target_pairs={{0,8},{1,9},{2,10},{3,11},{4,12},{5,13},{6,14},{7,15},{8,0},{9,1},... | collective-permute-start | bytes 491528 | tf_op jit(solution)/shard_map/ppermute | solution.py:26
  69.2 18.7 %slice-start.1 = ((s8[6553600]{0:T(1024)(128)(4,1)}), s8[2359296]{0:T(1024)(128)(4,1)S(1)}, s32[]{:S(2)}) async-start(s8[6553600]{0:T(1024)(128)(4,1)} %bitcast.97), calls=%async_computation.1 | async-start | bytes 4718592
  85.0 4.6 %collective-permute-start.18 = (bf16[16,128]{1,0:T(8,128)(2,1)S(1)}, bf16[16,128]{1,0:T(8,128)(2,1)S(1)}, u32[]{:S(2)}, u32[]{:S(2)}) collective-permute-start(bf16[16,128]{1,0:T(8,128)(2,1)S(1)} %get-tuple-element.88), channel_id=1, source_target_pairs={{0,8},{1,9},{2,10},{3,11},{4,12},{5,13},{6,14},{7,15},{8,0},{9,1},... | collective-permute-start | bytes 12296 | tf_op jit(solution)/shard_map/ppermute | solution.py:26
  87.7 9.4 %collective-permute-start.17 = (bf16[128,640]{1,0:T(8,128)(2,1)S(1)}, bf16[128,640]{1,0:T(8,128)(2,1)S(1)}, u32[]{:S(2)}, u32[]{:S(2)}) collective-permute-start(bf16[128,640]{1,0:T(8,128)(2,1)S(1)} %get-tuple-element.87), channel_id=1, source_target_pairs={{0,8},{1,9},{2,10},{3,11},{4,12},{5,13},{6,14},{7,15},{8,0},{9,1},... | collective-permute-start | bytes 491528 | tf_op jit(solution)/shard_map/ppermute | solution.py:26
  88.5 19.7 %copy-start.4 = (bf16[320,128]{1,0:T(8,128)(2,1)S(1)}, bf16[320,128]{1,0:T(8,128)(2,1)}, u32[]{:S(2)}) copy-start(bf16[320,128]{1,0:T(8,128)(2,1)} %extra_any.1) | copy-start | bytes 245764
  97.1 19.7 %copy-start = (bf16[2560,640]{1,0:T(8,128)(2,1)S(1)}, bf16[2560,640]{1,0:T(8,128)(2,1)}, u32[]{:S(2)}) copy-start(bf16[2560,640]{1,0:T(8,128)(2,1)} %get-tuple-element.108.weight_ref) | copy-start | bytes 9830404
  98.9 1.7 %collective-permute-start.19 = (bf16[4,320,128]{2,1,0:T(8,128)(2,1)S(1)}, bf16[4,320,128]{2,1,0:T(8,128)(2,1)S(1)}, u32[]{:S(2)}, u32[]{:S(2)}) collective-permute-start(bf16[4,320,128]{2,1,0:T(8,128)(2,1)S(1)} %get-tuple-element.90), channel_id=1, source_target_pairs={{0,1},{1,0},{2,3},{3,2},{4,5},{5,4},{6,7},{7,6},{8,9},{9,8},{10,11... | collective-permute-start | bytes 983048 | tf_op jit(solution)/shard_map/ppermute | solution.py:26
  100.7 5.5 %collective-permute-start.20 = (bf16[320,128]{1,0:T(8,128)(2,1)S(1)}, bf16[320,128]{1,0:T(8,128)(2,1)S(1)}, u32[]{:S(2)}, u32[]{:S(2)}) collective-permute-start(bf16[320,128]{1,0:T(8,128)(2,1)S(1)} %get-tuple-element.124), channel_id=1, source_target_pairs={{0,2},{1,3},{2,0},{3,1},{4,6},{5,7},{6,4},{7,5},{8,10},{9,11},{10,... | collective-permute-start | bytes 245768 | tf_op jit(solution)/shard_map/ppermute | solution.py:26
  101.7 6.0 %collective-permute-start.22 = (bf16[320,128]{1,0:T(8,128)(2,1)S(1)}, bf16[320,128]{1,0:T(8,128)(2,1)S(1)}, u32[]{:S(2)}, u32[]{:S(2)}) collective-permute-start(bf16[320,128]{1,0:T(8,128)(2,1)S(1)} %get-tuple-element.125), channel_id=1, source_target_pairs={{0,6},{1,7},{2,4},{3,5},{4,2},{5,3},{6,0},{7,1},{8,14},{9,15},{10,... | collective-permute-start | bytes 245768 | tf_op jit(solution)/shard_map/ppermute | solution.py:26
  101.7 6.6 %collective-permute-start.21 = (bf16[320,128]{1,0:T(8,128)(2,1)S(1)}, bf16[320,128]{1,0:T(8,128)(2,1)S(1)}, u32[]{:S(2)}, u32[]{:S(2)}) collective-permute-start(bf16[320,128]{1,0:T(8,128)(2,1)S(1)} %get-tuple-element.126), channel_id=1, source_target_pairs={{0,4},{1,5},{2,6},{3,7},{4,0},{5,1},{6,2},{7,3},{8,12},{9,13},{10,... | collective-permute-start | bytes 245768 | tf_op jit(solution)/shard_map/ppermute | solution.py:26
  108.3 5.4 %collective-permute-start.25 = (bf16[320,128]{1,0:T(8,128)(2,1)S(1)}, bf16[320,128]{1,0:T(8,128)(2,1)S(1)}, u32[]{:S(2)}, u32[]{:S(2)}) collective-permute-start(bf16[320,128]{1,0:T(8,128)(2,1)S(1)} %fusion.11.refs_0_), channel_id=1, source_target_pairs={{0,6},{1,7},{2,4},{3,5},{4,2},{5,3},{6,0},{7,1},{8,14},{9,15},{10,... | collective-permute-start | bytes 245768 | tf_op jit(solution)/shard_map/ppermute | solution.py:26
  109.2 4.8 %collective-permute-start.24 = (bf16[320,128]{1,0:T(8,128)(2,1)S(1)}, bf16[320,128]{1,0:T(8,128)(2,1)S(1)}, u32[]{:S(2)}, u32[]{:S(2)}) collective-permute-start(bf16[320,128]{1,0:T(8,128)(2,1)S(1)} %fusion.11.refs_0_), channel_id=1, source_target_pairs={{0,4},{1,5},{2,6},{3,7},{4,0},{5,1},{6,2},{7,3},{8,12},{9,13},{10,... | collective-permute-start | bytes 245768 | tf_op jit(solution)/shard_map/ppermute | solution.py:26
  110.7 4.4 %collective-permute-start.23 = (bf16[320,128]{1,0:T(8,128)(2,1)S(1)}, bf16[320,128]{1,0:T(8,128)(2,1)S(1)}, u32[]{:S(2)}, u32[]{:S(2)}) collective-permute-start(bf16[320,128]{1,0:T(8,128)(2,1)S(1)} %fusion.11.refs_0_), channel_id=1, source_target_pairs={{0,2},{1,3},{2,0},{3,1},{4,6},{5,7},{6,4},{7,5},{8,10},{9,11},{10,... | collective-permute-start | bytes 245768 | tf_op jit(solution)/shard_map/ppermute | solution.py:26
  115.2 1.7 %collective-permute-start.26 = (bf16[4,320,128]{2,1,0:T(8,128)(2,1)S(1)}, bf16[4,320,128]{2,1,0:T(8,128)(2,1)S(1)}, u32[]{:S(2)}, u32[]{:S(2)}) collective-permute-start(bf16[4,320,128]{2,1,0:T(8,128)(2,1)S(1)} %pad_maximum_fusion), channel_id=1, source_target_pairs={{0,1},{1,0},{2,3},{3,2},{4,5},{5,4},{6,7},{7,6},{8,9},{9,8},{10,11... | collective-permute-start | bytes 983048 | tf_op jit(solution)/shard_map/ppermute | solution.py:26
  119.4 10.8 %collective-permute-start.27 = (bf16[128,640]{1,0:T(8,128)(2,1)S(1)}, bf16[128,640]{1,0:T(8,128)(2,1)S(1)}, u32[]{:S(2)}, u32[]{:S(2)}) collective-permute-start(bf16[128,640]{1,0:T(8,128)(2,1)S(1)} %get-tuple-element.93), channel_id=1, source_target_pairs={{0,8},{1,9},{2,10},{3,11},{4,12},{5,13},{6,14},{7,15},{8,0},{9,1},... | collective-permute-start | bytes 491528 | tf_op jit(solution)/shard_map/ppermute | solution.py:26
  119.9 10.3 %collective-permute-start.28 = (bf16[16,128]{1,0:T(8,128)(2,1)S(1)}, bf16[16,128]{1,0:T(8,128)(2,1)S(1)}, u32[]{:S(2)}, u32[]{:S(2)}) collective-permute-start(bf16[16,128]{1,0:T(8,128)(2,1)S(1)} %get-tuple-element.94), channel_id=1, source_target_pairs={{0,8},{1,9},{2,10},{3,11},{4,12},{5,13},{6,14},{7,15},{8,0},{9,1},... | collective-permute-start | bytes 12296 | tf_op jit(solution)/shard_map/ppermute | solution.py:26
  132.1 9.5 %collective-permute-start.29 = (bf16[128,640]{1,0:T(8,128)(2,1)S(1)}, bf16[128,640]{1,0:T(8,128)(2,1)S(1)}, u32[]{:S(2)}, u32[]{:S(2)}) collective-permute-start(bf16[128,640]{1,0:T(8,128)(2,1)S(1)} %get-tuple-element.97), channel_id=1, source_target_pairs={{0,8},{1,9},{2,10},{3,11},{4,12},{5,13},{6,14},{7,15},{8,0},{9,1},... | collective-permute-start | bytes 491528 | tf_op jit(solution)/shard_map/ppermute | solution.py:26
  132.1 9.5 %collective-permute-start.30 = (bf16[16,128]{1,0:T(8,128)(2,1)S(1)}, bf16[16,128]{1,0:T(8,128)(2,1)S(1)}, u32[]{:S(2)}, u32[]{:S(2)}) collective-permute-start(bf16[16,128]{1,0:T(8,128)(2,1)S(1)} %get-tuple-element.98), channel_id=1, source_target_pairs={{0,8},{1,9},{2,10},{3,11},{4,12},{5,13},{6,14},{7,15},{8,0},{9,1},... | collective-permute-start | bytes 12296 | tf_op jit(solution)/shard_map/ppermute | solution.py:26
  143.4 1.7 %collective-permute-start.31 = (bf16[4,320,128]{2,1,0:T(8,128)(2,1)S(1)}, bf16[4,320,128]{2,1,0:T(8,128)(2,1)S(1)}, u32[]{:S(2)}, u32[]{:S(2)}) collective-permute-start(bf16[4,320,128]{2,1,0:T(8,128)(2,1)S(1)} %get-tuple-element.100), channel_id=1, source_target_pairs={{0,1},{1,0},{2,3},{3,2},{4,5},{5,4},{6,7},{7,6},{8,9},{9,8},{10,11... | collective-permute-start | bytes 983048 | tf_op jit(solution)/shard_map/ppermute | solution.py:26
  145.2 5.4 %collective-permute-start.32 = (bf16[320,128]{1,0:T(8,128)(2,1)S(1)}, bf16[320,128]{1,0:T(8,128)(2,1)S(1)}, u32[]{:S(2)}, u32[]{:S(2)}) collective-permute-start(bf16[320,128]{1,0:T(8,128)(2,1)S(1)} %get-tuple-element.121), channel_id=1, source_target_pairs={{0,2},{1,3},{2,0},{3,1},{4,6},{5,7},{6,4},{7,5},{8,10},{9,11},{10,... | collective-permute-start | bytes 245768 | tf_op jit(solution)/shard_map/ppermute | solution.py:26
  146.3 6.0 %collective-permute-start.34 = (bf16[320,128]{1,0:T(8,128)(2,1)S(1)}, bf16[320,128]{1,0:T(8,128)(2,1)S(1)}, u32[]{:S(2)}, u32[]{:S(2)}) collective-permute-start(bf16[320,128]{1,0:T(8,128)(2,1)S(1)} %get-tuple-element.122), channel_id=1, source_target_pairs={{0,6},{1,7},{2,4},{3,5},{4,2},{5,3},{6,0},{7,1},{8,14},{9,15},{10,... | collective-permute-start | bytes 245768 | tf_op jit(solution)/shard_map/ppermute | solution.py:26
  146.4 6.3 %collective-permute-start.33 = (bf16[320,128]{1,0:T(8,128)(2,1)S(1)}, bf16[320,128]{1,0:T(8,128)(2,1)S(1)}, u32[]{:S(2)}, u32[]{:S(2)}) collective-permute-start(bf16[320,128]{1,0:T(8,128)(2,1)S(1)} %get-tuple-element.123), channel_id=1, source_target_pairs={{0,4},{1,5},{2,6},{3,7},{4,0},{5,1},{6,2},{7,3},{8,12},{9,13},{10,... | collective-permute-start | bytes 245768 | tf_op jit(solution)/shard_map/ppermute | solution.py:26

commit v6 on v5

--- a/solution.py
+++ b/solution.py
@@ -50,10 +50,11 @@
 
 
 def prepare_kernel(
-    pair, counts, width, heads_ref, starts_ref, weight_any, hidden_any, gain_any, extra_any, *refs
+    pair, heads, blocks, width, place_ref, weight_any, hidden_any, gain_any, extra_any, *refs
 ):
     weight_ref, hidden_ref, gain_ref, extra_ref, normed, sems = refs[-6:]
-    head_refs, out_refs = refs[: len(counts)], refs[len(counts) : -6]
+    head_refs, out_refs = refs[: len(heads)], refs[len(heads) : -6]
+    place_now = [place_ref[number] for number in range(4)]
     rows = hidden_ref.shape[0]
     lanes = extra_ref.shape[1]
     more = out_refs[0].shape[0] - rows
@@ -71,23 +72,19 @@
     for copy in copies:
         copy.start()
     copies[0].wait()
-    number = 0
-    for head_ref in head_refs:
-        for place in range(head_ref.shape[0]):
-            column = pl.multiple_of(heads_ref[number] * pair, pair)
-            head_ref[place] = weight_ref[:, pl.ds(column, pair)]
-            number += 1
+    for head_ref, group in zip(head_refs, heads):
+        for number, head in enumerate(group):
+            column = pl.multiple_of(head(*place_now) * pair, pair)
+            head_ref[number] = weight_ref[:, pl.ds(column, pair)]
     for copy in copies[1:]:
         copy.wait()
     hidden = hidden_ref[...].astype(F32)
     inverse = lax.rsqrt(jnp.mean(hidden * hidden, axis=1, keepdims=True) + EPSILON)
     normed[...] = (hidden * inverse * gain_ref[...]).astype(BF16)
-    number = 0
-    for out_ref in out_refs:
-        for place in range(out_ref.shape[1] // width):
-            start = pl.multiple_of(starts_ref[number] * width, 128)
-            out_ref[:rows, place * width : (place + 1) * width] = normed[:, pl.ds(start, width)]
-            number += 1
+    for out_ref, group in zip(out_refs, blocks):
+        for number, block in enumerate(group):
+            start = pl.multiple_of(block(*place_now) * width, 128)
+            out_ref[:rows, number * width : (number + 1) * width] = normed[:, pl.ds(start, width)]
         for block in range(out_ref.shape[1] // lanes):
             out_ref[rows:, block * lanes : (block + 1) * lanes] = extra_ref[
                 block * more : (block + 1) * more, :
@@ -98,13 +95,16 @@
     return unit % 64 == 0 and rows % 16 == 0
 
 
-def prepared(weight, head_groups, pair, hidden, gain, groups, width, extra, kernels):
+def prepared(weight, head_groups, pair, hidden, gain, groups, width, extra, place_now, kernels):
     rows, depth = hidden.shape
     total_width = len(groups[0]) * width
     more = extra.size // total_width
     if not kernels:
+        now = [place_now[number] for number in range(4)]
         columns = [
-            jnp.stack([lax.dynamic_slice_in_dim(weight, head * pair, pair, 1) for head in group])
+            jnp.stack(
+                [lax.dynamic_slice_in_dim(weight, head(*now) * pair, pair, 1) for head in group]
+            )
             for group in head_groups
         ]
         hidden_float = hidden.astype(F32)
@@ -112,7 +112,9 @@
         normed = (hidden_float * inverse * gain[None, :]).astype(BF16)
         results = []
         for group in groups:
-            blocks = [lax.dynamic_slice_in_dim(normed, block * width, width, 1) for block in group]
+            blocks = [
+                lax.dynamic_slice_in_dim(normed, block(*now) * width, width, 1) for block in group
+            ]
             rest = extra.reshape(more, total_width)
             results.append(jnp.concatenate([jnp.concatenate(blocks, axis=1), rest], axis=0))
         return columns, results
@@ -120,10 +122,10 @@
     vmem = pl.BlockSpec(memory_space=pltpu.VMEM)
     smem = pl.BlockSpec(memory_space=pltpu.SMEM)
     results = pl.pallas_call(
-        functools.partial(prepare_kernel, pair, counts, width),
+        functools.partial(prepare_kernel, pair, head_groups, groups, width),
         out_shape=[jax.ShapeDtypeStruct((count, weight.shape[0], pair), BF16) for count in counts]
         + [jax.ShapeDtypeStruct((rows + more, total_width), BF16) for group in groups],
-        in_specs=[smem, smem] + [pl.BlockSpec(memory_space=pltpu.HBM)] * 4,
+        in_specs=[smem] + [pl.BlockSpec(memory_space=pltpu.HBM)] * 4,
         out_specs=[vmem] * (len(counts) + len(groups)),
         scratch_shapes=[
             pltpu.VMEM(weight.shape, BF16),
@@ -136,8 +138,7 @@
         compiler_params=pltpu.CompilerParams(vmem_limit_bytes=60 * 1024 * 1024),
         name="prepare",
     )(
-        jnp.stack([head for group in head_groups for head in group]).astype(jnp.int32),
-        jnp.stack([block for group in groups for block in group]).astype(jnp.int32),
+        place_now,
         weight,
         hidden,
         gain[None, :],
@@ -146,14 +147,38 @@
     return results[: len(counts)], results[len(counts) :]
 
 
-def project_kernel(rows, heads, pair, start, first_ref, heads_ref, weight_any, traded_ref, *refs):
+def stage_kernel(pair, heads, place_ref, weight_ref, tokens_ref, kept_ref, own_ref):
+    place_now = [place_ref[number] for number in range(4)]
+    for number, head in enumerate(heads):
+        column = pl.multiple_of(head(*place_now) * pair, pair)
+        kept_ref[number] = weight_ref[:, pl.ds(column, pair)]
+    own_ref[...] = tokens_ref[: own_ref.shape[0], :]
+
+
+def staged(weight, heads, pair, tokens, place_now, kernels):
+    if not kernels:
+        now = [place_now[number] for number in range(4)]
+        columns = [lax.dynamic_slice_in_dim(weight, head(*now) * pair, pair, 1) for head in heads]
+        return jnp.stack(columns), tokens
+    shapes = [
+        jax.ShapeDtypeStruct((len(heads), weight.shape[0], pair), BF16),
+        jax.ShapeDtypeStruct(tokens.shape, BF16),
+    ]
+    return call(
+        functools.partial(stage_kernel, pair, heads),
+        "stage",
+        shapes,
+        [place_now],
+        [weight, tokens],
+    )
+
+
+def project_kernel(rows, heads, start, first_ref, kept_ref, traded_ref, *refs):
     token_refs, refs = refs[: 2 * CHIPS], refs[2 * CHIPS :]
-    own, weight, sem = refs[-3:]
-    out_refs = refs[-3 - heads : -3]
-    blocks = refs[: -3 - heads]
-    unit = own.shape[0]
-    get_own = pltpu.make_async_copy(weight_any, own, sem)
-    get_own.start()
+    weight = refs[-1]
+    out_refs = refs[-1 - heads : -1]
+    blocks = refs[: -1 - heads]
+    unit, pair = kept_ref.shape[1:]
 
     def put(head, tile, second, value):
         which = 1 - first_ref[tile] if second else first_ref[tile]
@@ -161,13 +186,10 @@
         weight[pl.ds(base, unit), head * pair : (head + 1) * pair] = value
 
     for head in range(heads):
+        put(head, 0, 0, kept_ref[start + head])
         put(head, 0, 1, traded_ref[start + head])
         for number, block_ref in enumerate(blocks):
             put(head, 1 + number // 2, number % 2, block_ref[head])
-    get_own.wait()
-    for head in range(heads):
-        column = pl.multiple_of(heads_ref[head] * pair, pair)
-        put(head, 0, 0, own[:, pl.ds(column, pair)])
     for number, token_ref in enumerate(token_refs):
         span = slice(number * rows, (number + 1) * rows)
         result = jnp.dot(token_ref[:rows, :], weight[...], preferred_element_type=F32).astype(BF16)
@@ -175,13 +197,13 @@
             out_ref[span, :] = result[:, head * pair : (head + 1) * pair]
 
 
-def projected(tokens, heads, pair, kv_weight, traded, start, firsts, blocks, rows, kernels):
-    unit, depth = kv_weight.shape[0], tokens[0].shape[1]
+def projected(tokens, heads, kept, traded, start, firsts, blocks, rows, kernels):
+    unit, pair = kept.shape[1:]
+    depth = tokens[0].shape[1]
     count = len(tokens) * rows
     firsts = jnp.stack(firsts).astype(jnp.int32)
     if not kernels:
-        kept = jnp.stack([lax.dynamic_slice_in_dim(kv_weight, h * pair, pair, 1) for h in heads])
-        pieces = [kept, traded[start : start + len(heads)]] + blocks
+        pieces = [kept[start : start + heads], traded[start : start + heads]] + blocks
         ordered = []
         for tile in range(len(pieces) // 2):
             one, two = pieces[2 * tile : 2 * tile + 2]
@@ -195,24 +217,19 @@
     smem = pl.BlockSpec(memory_space=pltpu.SMEM)
     return list(
         pl.pallas_call(
-            functools.partial(project_kernel, rows, len(heads), pair, start),
-            out_shape=[jax.ShapeDtypeStruct((count, pair), BF16)] * len(heads),
-            in_specs=[smem, smem, pl.BlockSpec(memory_space=pltpu.HBM), vmem]
-            + [vmem] * (len(tokens) + len(blocks)),
-            out_specs=[vmem] * len(heads),
-            scratch_shapes=[
-                pltpu.VMEM(kv_weight.shape, BF16),
-                pltpu.VMEM((depth, len(heads) * pair), BF16),
-                pltpu.SemaphoreType.DMA,
-            ],
+            functools.partial(project_kernel, rows, heads, start),
+            out_shape=[jax.ShapeDtypeStruct((count, pair), BF16)] * heads,
+            in_specs=[smem] + [vmem] * (2 + len(tokens) + len(blocks)),
+            out_specs=[vmem] * heads,
+            scratch_shapes=[pltpu.VMEM((depth, heads * pair), BF16)],
             compiler_params=pltpu.CompilerParams(vmem_limit_bytes=20 * 1024 * 1024),
             cost_estimate=pl.CostEstimate(
-                flops=PROJECT_COST * 2 * len(heads) * count * depth * pair,
+                flops=PROJECT_COST * 2 * heads * count * depth * pair,
                 bytes_accessed=2 * count * depth,
                 transcendentals=0,
             ),
             name="project",
-        )(firsts, jnp.stack(heads).astype(jnp.int32), kv_weight, traded, *tokens, *blocks)
+        )(firsts, kept, traded, *tokens, *blocks)
     )
 
 
@@ -351,7 +368,7 @@
     return jnp.stack([low, high], axis=1).reshape(-1, ours.shape[-1])
 
 
-def key_values_of(hidden, kv_gain, kv_weight, query_states, meanwhile):
+def key_values_of(hidden, kv_gain, kv_weight, query_states, place_now, meanwhile):
     lane_count = lax.axis_size("row")
     tile_count = lane_count // KVH
     me = lax.axis_index("row")
@@ -363,23 +380,32 @@
     part = lax.axis_index("groups") if share else 0
 
     order = [place for round_ in ROUNDS for place in round_]
-    heads = {place: (chip ^ place) * 2 + core for place in order}
-    others = {place: (chip ^ place) * 2 + 1 - core for place in order}
-    sent = [[heads[place] ^ part for place in round_] for round_ in ROUNDS]
+
+    def kept_head(place):
+        return lambda chip, core, tile, part: (chip ^ place) * 2 + core
+
+    def sent_head(place):
+        return lambda chip, core, tile, part: ((chip ^ place) * 2 + core) ^ part
+
+    def other_head(place):
+        return lambda chip, core, tile, part: (chip ^ place) * 2 + 1 - core
+
+    def block(place, j):
+        return lambda chip, core, tile, part: (tile ^ j) * CHIPS + (chip ^ place)
+
     kernels = in_kernels(unit, rows)
     width = 2 * unit
     pieces, features = prepared(
         kv_weight,
-        sent + [[others[p] for p in order]],
+        [[sent_head(place) for place in round_] for round_ in ROUNDS]
+        + [[other_head(place) for place in order]],
         pair,
         hidden,
         kv_gain,
-        [
-            [(tile ^ j) * CHIPS + (chip ^ place) for j in range(tile_count)]
-            for place in range(CHIPS)
-        ],
+        [[block(place, j) for j in range(tile_count)] for place in range(CHIPS)],
         width,
         query_states,
+        place_now,
         kernels,
     )
     sent, traded = pieces[:-1], pieces[-1]
@@ -401,24 +427,30 @@
     traded = swapped(traded, 1)
 
     def shared(number):
-        blocks = []
-        for j, value in enumerate(far[number], 1):
-            other = swapped(value, 1, "groups") if share else to_tile(traded[number], j, False)
-            blocks += [value, other]
-        return blocks
+        start = sum(len(round_) for round_ in ROUNDS[:number])
+        return [
+            swapped(value, 1, "groups")
+            if share
+            else to_tile(traded[start : start + len(ROUNDS[number])], j, False)
+            for j, value in enumerate(far[number], 1)
+        ]
 
     firsts = [core] + [core ^ part] * (tile_count - 1)
-    blocks = shared(0)
-    held[2], held[3], blocks, far = lax.optimization_barrier((held[2], held[3], blocks, far))
+    kv_weight, own, _ = lax.optimization_barrier((kv_weight, held[0], far[0]))
+    kept, own = staged(
+        kv_weight, [kept_head(place) for place in order], pair, own, place_now, kernels
+    )
+    held[1], kept, own = lax.optimization_barrier((held[1], kept, own))
+    halves = [shared(number) for number in range(len(ROUNDS))]
+    held[2], held[3], halves[0], far = lax.optimization_barrier((held[2], held[3], halves[0], far))
     tokens = held + [swapped(piece, 1) for piece in held]
+    tokens[0] = own
     total = None
     done = 0
     for number, round_ in enumerate(ROUNDS):
-        if number:
-            blocks = shared(number)
-        here = [heads[place] for place in round_]
+        blocks = [piece for pair_ in zip(far[number], halves[number]) for piece in pair_]
         partials = projected(
-            tokens, here, pair, kv_weight, traded, done, firsts, blocks, rows, kernels
+            tokens, len(round_), kept, traded, done, firsts, blocks, rows, kernels
         )
         done += len(round_)
         if number == 0:
@@ -483,7 +515,8 @@
 
     me = lax.axis_index("row")
     chip, core = me // 2 % CHIPS, me % 2
-    place_now = jnp.stack([chip, core]).astype(jnp.int32)
+    part = lax.axis_index("groups") if lax.axis_size("groups") == 2 else 0
+    place_now = jnp.stack([chip, core, tile, part]).astype(jnp.int32)
     unit, rows = query_states.shape[0], hidden.shape[0]
     kernels = in_kernels(unit, rows)
     width = query_weight.shape[3]
@@ -528,7 +561,7 @@
         )
 
     key_values, key_pos, parts = key_values_of(
-        hidden, kv_gain, kv_weight, query_states, functools.partial(query_parts, 0)
+        hidden, kv_gain, kv_weight, query_states, place_now, functools.partial(query_parts, 0)
     )
     positions = [query_pos[:, None], query_floor[:, None], key_pos[None, :]]
     for section in range(query_gain.shape[0]):

time: 154 us -> 150 us (0.974)
  local copies, waits for them, and re-layouts: 11.9 us -> 9.95 us
  waiting for transfers between devices: 75.9 us -> 74.1 us
    ppermute x2, waiting for transfers between devices: 16.4 us -> 14.4 us  [to_tile(): return lax.ppermute(value, ('groups', 'row'), pairs)]
    pallas_call x6 -> x7, Pallas kernels: 12.7 us -> 13.1 us  [call(): pl.pallas_call(kernel, out_shape=out_shape, in_specs=[smem] * len(scalars...]
  transfers between devices with their start and end apart: 35 -> 35, of which waited for: 22 -> 21; matrix products, arithmetic and copies ran while one was open for 6% -> 5% of each run, Pallas kernels for 6% -> 6%
where the time goes in v6:
time: 150 us
  waiting for transfers between devices  74.1 us (49%)
  starting transfers between devices  39.7 us (26%)
  Pallas kernels  23.9 us (16%)
  local copies, waits for them, and re-layouts  9.95 us (7%)
  other arithmetic  2.01 us (1%)
    ppermute x33, waiting for transfers between devices, swapped(): return lax.ppermute(value, axis, pairs)  59.7 us
    ppermute x33, starting transfers between devices, swapped(): return lax.ppermute(value, axis, pairs)  35.5 us
    ppermute x2, waiting for transfers between devices, to_tile(): return lax.ppermute(value, ('groups', 'row'), pairs)  14.4 us
    pallas_call x7, Pallas kernels, call(): pl.pallas_call(kernel, out_shape=out_shape, in_specs=[smem] * len(scalars...  13.1 us
    pallas_call x2, Pallas kernels, projected(): pl.pallas_call(functools.partial(project_kernel, rows, heads, start), out...  6.08 us
    squeeze x1, local copies, waits for them, and re-layouts, query_parts(): query_weight[section, 0]  5.15 us
    pallas_call x1, Pallas kernels, prepared(): pl.pallas_call(functools.partial(prepare_kernel, pair, head_groups, group...  4.77 us
    ppermute x2, starting transfers between devices, to_tile(): return lax.ppermute(value, ('groups', 'row'), pairs)  4.18 us
  transfers between devices with their start and end apart: 35, of which 21 were waited for; matrix products, arithmetic and copies ran while one was open for 5% of the time, Pallas kernels for 6%

profile of v6, /device:TPU:0, one launch (start us, length us, event | category | flops | bytes accessed | tf_op | source)
XLA Modules:
  0.0 150.0 jit_solution(13806606526993181774)
XLA Ops:
  0.6 4.8 %prepare.1 = (bf16[2,320,256]{2,1,0:T(8,128)(2,1)}, bf16[2,320,256]{2,1,0:T(8,128)(2,1)}, bf16[4,320,256]{2,1,0:T(8,128)(2,1)}, bf16[160,1280]{1,0:T(8,128)(2,1)...) custom-call(s32[4]{0:T(128)} %pad_add_fusion.place_ref, ...), custom_call_target="tpu_custom_call" | custom-call | tf_op jit(solution)/shard_map/prepare/pallas_call | solution.py:124
  5.3 4.1 %collective-permute-start.1 = (bf16[2,320,256]{2,1,0:T(8,128)(2,1)}, bf16[2,320,256]{2,1,0:T(8,128)(2,1)}, u32[]{:S(2)}, u32[]{:S(2)}) collective-permute-start(bf16[2,320,256]{2,1,0:T(8,128)(2,1)} %get-tuple-element.64), channel_id=1, source_target_pairs={{0,8},{1,9},{2,10},{3,11},{4,12},{5,13},{6,14},{7,15},{8,0},{9,1},... | collective-permute-start | bytes 983048 | tf_op jit(solution)/shard_map/ppermute | solution.py:421
  9.5 1.7 %collective-permute-start = (bf16[160,1280]{1,0:T(8,128)(2,1)}, bf16[160,1280]{1,0:T(8,128)(2,1)}, u32[]{:S(2)}, u32[]{:S(2)}) collective-permute-start(bf16[160,1280]{1,0:T(8,128)(2,1)} %get-tuple-element.61), channel_id=1, source_target_pairs={{0,2},{1,3},{2,0},{3,1},{4,6},{5,7},{6,4},{7,5},{8,10},{9,11},{10,... | collective-permute-start | bytes 1228808 | tf_op jit(solution)/shard_map/ppermute | solution.py:26
  11.3 1.6 %collective-permute-start.3 = (bf16[160,1280]{1,0:T(8,128)(2,1)}, bf16[160,1280]{1,0:T(8,128)(2,1)}, u32[]{:S(2)}, u32[]{:S(2)}) collective-permute-start(bf16[160,1280]{1,0:T(8,128)(2,1)} %get-tuple-element.73), channel_id=1, source_target_pairs={{0,4},{1,5},{2,6},{3,7},{4,0},{5,1},{6,2},{7,3},{8,12},{9,13},{10,... | collective-permute-start | bytes 1228808 | tf_op jit(solution)/shard_map/ppermute | solution.py:26
  13.0 0.9 fusion.21
  13.9 5.1 %slice_bitcast_fusion.2 = (bf16[2560,640]{1,0:T(8,128)(2,1)S(1)}, bf16[2560,640]{1,0:T(8,128)(2,1)}) fusion(bf16[2,1,2560,640]{3,2,1,0:T(8,128)(2,1)} %param.13), kind=kLoop, calls=%fused_computation.2 | loop fusion | bytes 13107200 | tf_op jit(solution)/shard_map/squeeze | solution.py:553
  19.6 12.9 %collective-permute-done.1.refs_8_ = bf16[2,320,256]{2,1,0:T(8,128)(2,1)} collective-permute-done((bf16[2,320,256]{2,1,0:T(8,128)(2,1)}, bf16[2,320,256]{2,1,0:T(8,128)(2,1)}, u32[]{:S(2)}, u32[]{:S(2)}) %collective-permute-start.1) | collective-permute-done | bytes 327712 | tf_op jit(solution)/shard_map/ppermute | solution.py:421
  32.4 1.1 collective-permute-start.5
  34.1 1.3 copy-done.1
  35.5 1.0 copy-done.2
  37.1 1.5 %collective-permute-done.6.refs_8_ = bf16[2,320,256]{2,1,0:T(8,128)(2,1)} collective-permute-done((bf16[2,320,256]{2,1,0:T(8,128)(2,1)}, bf16[2,320,256]{2,1,0:T(8,128)(2,1)}, u32[]{:S(2)}, u32[]{:S(2)}) %collective-permute-start.6) | collective-permute-done | bytes 327712 | tf_op jit(solution)/shard_map/ppermute | solution.py:421
  39.1 4.5 %collective-permute-done.4.refs_3_ = bf16[160,1280]{1,0:T(8,128)(2,1)} collective-permute-done((bf16[160,1280]{1,0:T(8,128)(2,1)}, bf16[160,1280]{1,0:T(8,128)(2,1)}, u32[]{:S(2)}, u32[]{:S(2)}) %collective-permute-start.4) | collective-permute-done | bytes 409632 | tf_op jit(solution)/shard_map/ppermute | solution.py:26
  44.2 2.1 %collective-permute-start.13 = (bf16[2,320,256]{2,1,0:T(8,128)(2,1)}, bf16[2,320,256]{2,1,0:T(8,128)(2,1)S(1)}, u32[]{:S(2)}, u32[]{:S(2)}) collective-permute-start(bf16[2,320,256]{2,1,0:T(8,128)(2,1)} %collective-permute-done.6.refs_8_), channel_id=1, source_target_pairs={{0,16},{16,0},{1,17},{17,1},{2,18},{18,2},{3,19},{19,3},{4,20},{20... | collective-permute-start | bytes 983048 | tf_op jit(solution)/shard_map/ppermute | solution.py:26
  46.4 3.1 %project.2 = (bf16[1024,256]{1,0:T(8,128)(2,1)S(1)}, bf16[1024,256]{1,0:T(8,128)(2,1)S(1)}) custom-call(s32[2]{0:T(128)S(1)} %pad_add_fusion.1.first_ref, bf16[4,320,256]{2,1,0:T(8,128)(2,1)S(1)} %get-tuple-element.69.kept_ref, bf16[4,320,256]{2,1,0:T(8,128)(2,1)S(1)} %collective-permute-done.2.traded_ref, bf16[160,1280]{1,0:T(8,128)(2,1)S(1)} %get-tuple-element.84.refs_0_, ...), custom_call_target="tpu_custom_call" | custom-call | flops 10737418240 | bytes 2621440 | tf_op jit(solution)/shard_map/project/pallas_call | solution.py:219
  49.5 1.6 %collective-permute-start.11 = (bf16[1024,256]{1,0:T(8,128)(2,1)S(1)}, bf16[1024,256]{1,0:T(8,128)(2,1)S(1)}, u32[]{:S(2)}, u32[]{:S(2)}) collective-permute-start(bf16[1024,256]{1,0:T(8,128)(2,1)S(1)} %get-tuple-element.82), channel_id=1, source_target_pairs={{0,2},{1,3},{2,0},{3,1},{4,6},{5,7},{6,4},{7,5},{8,10},{9,11},{10,... | collective-permute-start | bytes 1572872 | tf_op jit(solution)/shard_map/ppermute | solution.py:26
  51.2 3.3 %collective-permute-done.13.refs_9_ = bf16[2,320,256]{2,1,0:T(8,128)(2,1)S(1)} collective-permute-done((bf16[2,320,256]{2,1,0:T(8,128)(2,1)}, bf16[2,320,256]{2,1,0:T(8,128)(2,1)S(1)}, u32[]{:S(2)}, u32[]{:S(2)}) %collective-permute-start.13) | collective-permute-done | bytes 327712 | tf_op jit(solution)/shard_map/ppermute | solution.py:26
  54.5 3.0 %project.3 = (bf16[1024,256]{1,0:T(8,128)(2,1)S(1)}, bf16[1024,256]{1,0:T(8,128)(2,1)S(1)}) custom-call(s32[2]{0:T(128)S(1)} %pad_add_fusion.1.first_ref, bf16[4,320,256]{2,1,0:T(8,128)(2,1)S(1)} %get-tuple-element.69.kept_ref, bf16[4,320,256]{2,1,0:T(8,128)(2,1)S(1)} %collective-permute-done.2.traded_ref, bf16[160,1280]{1,0:T(8,128)(2,1)S(1)} %get-tuple-element.84.refs_0_, ...), custom_call_target="tpu_custom_call" | custom-call | flops 10737418240 | bytes 2621440 | tf_op jit(solution)/shard_map/project/pallas_call | solution.py:219
  57.4 1.2 collective-permute-start.14
  58.7 2.8 %query.2 = (bf16[128,640]{1,0:T(8,128)(2,1)S(1)}, f32[128,640]{1,0:T(8,128)S(1)}, bf16[16,128]{1,0:T(8,128)(2,1)S(1)}, f32[128,128]{1,0:T(8,128)S(1)}) custom-call(s32[4]{0:T(128)S(1)} %copy-done.3, f32[1,2560]{1,0:T(1,128)S(1)} %constant_dynamic-slice_fusion.1.gain_ref, bf16[2560,640]{1,0:T(8,128)(2,1)S(1)} %get-tuple-element.121.weight_ref, ...), custom_call_target="tpu_custom_call" | custom-call | flops 419430400 | bytes 3281920 | tf_op jit(solution)/shard_map/query/pallas_call | solution.py:350
  61.4 4.7 %collective-permute-start.16 = (bf16[16,128]{1,0:T(8,128)(2,1)S(1)}, bf16[16,128]{1,0:T(8,128)(2,1)S(1)}, u32[]{:S(2)}, u32[]{:S(2)}) collective-permute-start(bf16[16,128]{1,0:T(8,128)(2,1)S(1)} %get-tuple-element.98), channel_id=1, source_target_pairs={{0,8},{1,9},{2,10},{3,11},{4,12},{5,13},{6,14},{7,15},{8,0},{9,1},... | collective-permute-start | bytes 12296 | tf_op jit(solution)/shard_map/ppermute | solution.py:26
  66.4 12.9 %collective-permute-done.14 = bf16[1024,256]{1,0:T(8,128)(2,1)S(1)} collective-permute-done((bf16[1024,256]{1,0:T(8,128)(2,1)S(1)}, bf16[1024,256]{1,0:T(8,128)(2,1)S(1)}, u32[]{:S(2)}, u32[]{:S(2)}) %collective-permute-start.14) | collective-permute-done | bytes 524320 | tf_op jit(solution)/shard_map/ppermute | solution.py:26
  79.8 1.9 %attend.2 = (bf16[128,640]{1,0:T(8,128)(2,1)S(1)}, f32[128,640]{1,0:T(8,128)S(1)}, bf16[16,128]{1,0:T(8,128)(2,1)S(1)}, f32[128,128]{1,0:T(8,128)S(1)}) custom-call(s32[128,1]{1,0:T(8,128)S(1)} %fusion.12.query_pos_ref, s32[128,1]{1,0:T(8,128)S(1)} %broadcast_in_dim_reshape.5.query_floor_ref, s32[1,1024]{1,0:T(1,128)S(1)} %bitcast.77, ...), custom_call_target="tpu_custom_call" | custom-call | flops 209715200 | bytes 891392 | tf_op jit(solution)/shard_map/attend/pallas_call | solution.py:350
  81.7 2.8 %collective-permute-start.18 = (bf16[16,128]{1,0:T(8,128)(2,1)S(1)}, bf16[16,128]{1,0:T(8,128)(2,1)S(1)}, u32[]{:S(2)}, u32[]{:S(2)}) collective-permute-start(bf16[16,128]{1,0:T(8,128)(2,1)S(1)} %get-tuple-element.102), channel_id=1, source_target_pairs={{0,8},{1,9},{2,10},{3,11},{4,12},{5,13},{6,14},{7,15},{8,0},{9,1},... | collective-permute-start | bytes 12296 | tf_op jit(solution)/shard_map/ppermute | solution.py:26
  85.3 1.0 collective-permute-done.18.refs_1_
  86.3 7.6 %collective-permute-done.17.refs_0_ = bf16[128,640]{1,0:T(8,128)(2,1)S(1)} collective-permute-done((bf16[128,640]{1,0:T(8,128)(2,1)S(1)}, bf16[128,640]{1,0:T(8,128)(2,1)S(1)}, u32[]{:S(2)}, u32[]{:S(2)}) %collective-permute-start.17) | collective-permute-done | bytes 163872 | tf_op jit(solution)/shard_map/ppermute | solution.py:26
  93.9 1.8 %update.2 = (f32[4,320,128]{2,1,0:T(8,128)S(1)}, bf16[4,320,128]{2,1,0:T(8,128)(2,1)S(1)}) custom-call(s32[4]{0:T(128)S(1)} %copy-done.3, bf16[2560,640]{1,0:T(8,128)(2,1)S(1)} %get-tuple-element.123.weight_ref, f32[128,640]{1,0:T(8,128)S(1)} %get-tuple-element.99.kept_ref, f32[128,128]{1,0:T(8,128)S(1)} %get-tuple-element.100.totals_ref, ...), custom_call_target="tpu_custom_call" | custom-call | flops 419430400 | bytes 3641344 | tf_op jit(solution)/shard_map/update/pallas_call | solution.py:350
  95.7 1.6 %collective-permute-done.19 = bf16[4,320,128]{2,1,0:T(8,128)(2,1)S(1)} collective-permute-done((bf16[4,320,128]{2,1,0:T(8,128)(2,1)S(1)}, bf16[4,320,128]{2,1,0:T(8,128)(2,1)S(1)}, u32[]{:S(2)}, u32[]{:S(2)}) %collective-permute-start.19) | collective-permute-done | bytes 327712 | tf_op jit(solution)/shard_map/ppermute | solution.py:26
  97.5 0.9 collective-permute-start.20
  98.4 2.6 %collective-permute-start.21 = (bf16[320,128]{1,0:T(8,128)(2,1)S(1)}, bf16[320,128]{1,0:T(8,128)(2,1)S(1)}, u32[]{:S(2)}, u32[]{:S(2)}) collective-permute-start(bf16[320,128]{1,0:T(8,128)(2,1)S(1)} %get-tuple-element.140), channel_id=1, source_target_pairs={{0,4},{1,5},{2,6},{3,7},{4,0},{5,1},{6,2},{7,3},{8,12},{9,13},{10,... | collective-permute-start | bytes 245768 | tf_op jit(solution)/shard_map/ppermute | solution.py:26
  101.0 1.9 %collective-permute-done.20 = bf16[320,128]{1,0:T(8,128)(2,1)S(1)} collective-permute-done((bf16[320,128]{1,0:T(8,128)(2,1)S(1)}, bf16[320,128]{1,0:T(8,128)(2,1)S(1)}, u32[]{:S(2)}, u32[]{:S(2)}) %collective-permute-start.20) | collective-permute-done | bytes 81952 | tf_op jit(solution)/shard_map/ppermute | solution.py:26
  102.9 1.4 collective-permute-done.22
  105.9 1.5 %collective-permute-start.24 = (bf16[320,128]{1,0:T(8,128)(2,1)S(1)}, bf16[320,128]{1,0:T(8,128)(2,1)S(1)}, u32[]{:S(2)}, u32[]{:S(2)}) collective-permute-start(bf16[320,128]{1,0:T(8,128)(2,1)S(1)} %fusion.11.refs_0_), channel_id=1, source_target_pairs={{0,4},{1,5},{2,6},{3,7},{4,0},{5,1},{6,2},{7,3},{8,12},{9,13},{10,... | collective-permute-start | bytes 245768 | tf_op jit(solution)/shard_map/ppermute | solution.py:26
  107.4 1.2 collective-permute-start.23
  108.6 1.9 %collective-permute-done.25.refs_3_ = bf16[320,128]{1,0:T(8,128)(2,1)S(1)} collective-permute-done((bf16[320,128]{1,0:T(8,128)(2,1)S(1)}, bf16[320,128]{1,0:T(8,128)(2,1)S(1)}, u32[]{:S(2)}, u32[]{:S(2)}) %collective-permute-start.25) | collective-permute-done | bytes 81952 | tf_op jit(solution)/shard_map/ppermute | solution.py:26
  110.7 1.1 collective-permute-done.23.refs_1_
  112.0 1.6 %collective-permute-done.26.refs_4_ = bf16[4,320,128]{2,1,0:T(8,128)(2,1)S(1)} collective-permute-done((bf16[4,320,128]{2,1,0:T(8,128)(2,1)S(1)}, bf16[4,320,128]{2,1,0:T(8,128)(2,1)S(1)}, u32[]{:S(2)}, u32[]{:S(2)}) %collective-permute-start.26) | collective-permute-done | bytes 327712 | tf_op jit(solution)/shard_map/ppermute | solution.py:26
  113.6 2.3 %query.3 = (bf16[128,640]{1,0:T(8,128)(2,1)S(1)}, f32[128,640]{1,0:T(8,128)S(1)}, bf16[16,128]{1,0:T(8,128)(2,1)S(1)}, f32[128,128]{1,0:T(8,128)S(1)}) custom-call(s32[4]{0:T(128)S(1)} %copy-done.3, f32[1,2560]{1,0:T(1,128)S(1)} %constant_dynamic-slice_fusion.gain_ref, bf16[2560,640]{1,0:T(8,128)(2,1)S(1)} %copy-done, bf16[320,128]{1,0:T(8,128)(2,1)S(1)} %fusion.11.refs_0_, ...), custom_call_target="tpu_custom_call" | custom-call | flops 419430400 | bytes 3281920 | tf_op jit(solution)/shard_map/query/pallas_call | solution.py:350
  116.4 2.5 %collective-permute-start.28 = (bf16[16,128]{1,0:T(8,128)(2,1)S(1)}, bf16[16,128]{1,0:T(8,128)(2,1)S(1)}, u32[]{:S(2)}, u32[]{:S(2)}) collective-permute-start(bf16[16,128]{1,0:T(8,128)(2,1)S(1)} %get-tuple-element.108), channel_id=1, source_target_pairs={{0,8},{1,9},{2,10},{3,11},{4,12},{5,13},{6,14},{7,15},{8,0},{9,1},... | collective-permute-start | bytes 12296 | tf_op jit(solution)/shard_map/ppermute | solution.py:26
  118.9 7.8 %collective-permute-done.28.refs_3_ = bf16[16,128]{1,0:T(8,128)(2,1)S(1)} collective-permute-done((bf16[16,128]{1,0:T(8,128)(2,1)S(1)}, bf16[16,128]{1,0:T(8,128)(2,1)S(1)}, u32[]{:S(2)}, u32[]{:S(2)}) %collective-permute-start.28) | collective-permute-done | bytes 4128 | tf_op jit(solution)/shard_map/ppermute | solution.py:26
  126.8 1.9 %attend.3 = (bf16[128,640]{1,0:T(8,128)(2,1)S(1)}, f32[128,640]{1,0:T(8,128)S(1)}, bf16[16,128]{1,0:T(8,128)(2,1)S(1)}, f32[128,128]{1,0:T(8,128)S(1)}) custom-call(s32[128,1]{1,0:T(8,128)S(1)} %fusion.12.query_pos_ref, s32[128,1]{1,0:T(8,128)S(1)} %broadcast_in_dim_reshape.5.query_floor_ref, s32[1,1024]{1,0:T(1,128)S(1)} %bitcast.78, ...), custom_call_target="tpu_custom_call" | custom-call | flops 209715200 | bytes 891392 | tf_op jit(solution)/shard_map/attend/pallas_call | solution.py:350
  128.8 2.9 %collective-permute-start.30 = (bf16[16,128]{1,0:T(8,128)(2,1)S(1)}, bf16[16,128]{1,0:T(8,128)(2,1)S(1)}, u32[]{:S(2)}, u32[]{:S(2)}) collective-permute-start(bf16[16,128]{1,0:T(8,128)(2,1)S(1)} %get-tuple-element.112), channel_id=1, source_target_pairs={{0,8},{1,9},{2,10},{3,11},{4,12},{5,13},{6,14},{7,15},{8,0},{9,1},... | collective-permute-start | bytes 12296 | tf_op jit(solution)/shard_map/ppermute | solution.py:26
  131.7 6.6 %collective-permute-done.30.refs_1_ = bf16[16,128]{1,0:T(8,128)(2,1)S(1)} collective-permute-done((bf16[16,128]{1,0:T(8,128)(2,1)S(1)}, bf16[16,128]{1,0:T(8,128)(2,1)S(1)}, u32[]{:S(2)}, u32[]{:S(2)}) %collective-permute-start.30) | collective-permute-done | bytes 4128 | tf_op jit(solution)/shard_map/ppermute | solution.py:26
  138.2 1.8 %update.3 = (f32[4,320,128]{2,1,0:T(8,128)S(1)}, bf16[4,320,128]{2,1,0:T(8,128)(2,1)S(1)}) custom-call(s32[4]{0:T(128)S(1)} %copy-done.3, bf16[2560,640]{1,0:T(8,128)(2,1)S(1)} %get-tuple-element.124.weight_ref, f32[128,640]{1,0:T(8,128)S(1)} %get-tuple-element.109.kept_ref, f32[128,128]{1,0:T(8,128)S(1)} %get-tuple-element.110.totals_ref, ...), custom_call_target="tpu_custom_call" | custom-call | flops 419430400 | bytes 3641344 | tf_op jit(solution)/shard_map/update/pallas_call | solution.py:350
  140.1 1.6 %collective-permute-done.31 = bf16[4,320,128]{2,1,0:T(8,128)(2,1)S(1)} collective-permute-done((bf16[4,320,128]{2,1,0:T(8,128)(2,1)S(1)}, bf16[4,320,128]{2,1,0:T(8,128)(2,1)S(1)}, u32[]{:S(2)}, u32[]{:S(2)}) %collective-permute-start.31) | collective-permute-done | bytes 327712 | tf_op jit(solution)/shard_map/ppermute | solution.py:26
  141.8 1.0 collective-permute-start.32
  143.0 2.4 %collective-permute-start.33 = (bf16[320,128]{1,0:T(8,128)(2,1)S(1)}, bf16[320,128]{1,0:T(8,128)(2,1)S(1)}, u32[]{:S(2)}, u32[]{:S(2)}) collective-permute-start(bf16[320,128]{1,0:T(8,128)(2,1)S(1)} %get-tuple-element.137), channel_id=1, source_target_pairs={{0,4},{1,5},{2,6},{3,7},{4,0},{5,1},{6,2},{7,3},{8,12},{9,13},{10,... | collective-permute-start | bytes 245768 | tf_op jit(solution)/shard_map/ppermute | solution.py:26
  145.4 1.9 %collective-permute-done.32 = bf16[320,128]{1,0:T(8,128)(2,1)S(1)} collective-permute-done((bf16[320,128]{1,0:T(8,128)(2,1)S(1)}, bf16[320,128]{1,0:T(8,128)(2,1)S(1)}, u32[]{:S(2)}, u32[]{:S(2)}) %collective-permute-start.32) | collective-permute-done | bytes 81952 | tf_op jit(solution)/shard_map/ppermute | solution.py:26
  147.3 1.6 %collective-permute-done.34 = bf16[320,128]{1,0:T(8,128)(2,1)S(1)} collective-permute-done((bf16[320,128]{1,0:T(8,128)(2,1)S(1)}, bf16[320,128]{1,0:T(8,128)(2,1)S(1)}, u32[]{:S(2)}, u32[]{:S(2)}) %collective-permute-start.34) | collective-permute-done | bytes 81952 | tf_op jit(solution)/shard_map/ppermute | solution.py:26
  (77 shorter events, 9.4 us)
Async XLA Ops:
  5.3 27.1 %collective-permute-start.1 = (bf16[2,320,256]{2,1,0:T(8,128)(2,1)}, bf16[2,320,256]{2,1,0:T(8,128)(2,1)}, u32[]{:S(2)}, u32[]{:S(2)}) collective-permute-start(bf16[2,320,256]{2,1,0:T(8,128)(2,1)} %get-tuple-element.64), channel_id=1, source_target_pairs={{0,8},{1,9},{2,10},{3,11},{4,12},{5,13},{6,14},{7,15},{8,0},{9,1},... | collective-permute-start | bytes 983048 | tf_op jit(solution)/shard_map/ppermute | solution.py:421
  9.4 29.2 %collective-permute-start.6 = (bf16[2,320,256]{2,1,0:T(8,128)(2,1)}, bf16[2,320,256]{2,1,0:T(8,128)(2,1)}, u32[]{:S(2)}, u32[]{:S(2)}) collective-permute-start(bf16[2,320,256]{2,1,0:T(8,128)(2,1)} %get-tuple-element.75), channel_id=1, source_target_pairs={{0,8},{1,9},{2,10},{3,11},{4,12},{5,13},{6,14},{7,15},{8,0},{9,1},... | collective-permute-start | bytes 983048 | tf_op jit(solution)/shard_map/ppermute | solution.py:421
  9.5 24.2 %collective-permute-start = (bf16[160,1280]{1,0:T(8,128)(2,1)}, bf16[160,1280]{1,0:T(8,128)(2,1)}, u32[]{:S(2)}, u32[]{:S(2)}) collective-permute-start(bf16[160,1280]{1,0:T(8,128)(2,1)} %get-tuple-element.61), channel_id=1, source_target_pairs={{0,2},{1,3},{2,0},{3,1},{4,6},{5,7},{6,4},{7,5},{8,10},{9,11},{10,... | collective-permute-start | bytes 1228808 | tf_op jit(solution)/shard_map/ppermute | solution.py:26
  11.3 27.4 %collective-permute-start.3 = (bf16[160,1280]{1,0:T(8,128)(2,1)}, bf16[160,1280]{1,0:T(8,128)(2,1)}, u32[]{:S(2)}, u32[]{:S(2)}) collective-permute-start(bf16[160,1280]{1,0:T(8,128)(2,1)} %get-tuple-element.73), channel_id=1, source_target_pairs={{0,4},{1,5},{2,6},{3,7},{4,0},{5,1},{6,2},{7,3},{8,12},{9,13},{10,... | collective-permute-start | bytes 1228808 | tf_op jit(solution)/shard_map/ppermute | solution.py:26
  12.8 30.8 %collective-permute-start.4 = (bf16[160,1280]{1,0:T(8,128)(2,1)}, bf16[160,1280]{1,0:T(8,128)(2,1)}, u32[]{:S(2)}, u32[]{:S(2)}) collective-permute-start(bf16[160,1280]{1,0:T(8,128)(2,1)} %get-tuple-element.74), channel_id=1, source_target_pairs={{0,6},{1,7},{2,4},{3,5},{4,2},{5,3},{6,0},{7,1},{8,14},{9,15},{10,... | collective-permute-start | bytes 1228808 | tf_op jit(solution)/shard_map/ppermute | solution.py:26
  13.9 5.2 %copy-start.5 = (s32[2,2]{1,0:T(2,128)S(1)}, s32[2,2]{1,0:T(2,128)}, u32[]{:S(2)}) copy-start(s32[2,2]{1,0:T(2,128)} %param.15) | copy-start | bytes 52
  13.9 20.2 %copy-start.3 = (s32[4]{0:T(128)S(1)}, s32[4]{0:T(128)}, u32[]{:S(2)}) copy-start(s32[4]{0:T(128)} %pad_add_fusion.place_ref) | copy-start | bytes 52
  32.4 11.2 %collective-permute-start.5 = (bf16[2,320,256]{2,1,0:T(8,128)(2,1)}, bf16[2,320,256]{2,1,0:T(8,128)(2,1)}, u32[]{:S(2)}, u32[]{:S(2)}) collective-permute-start(bf16[2,320,256]{2,1,0:T(8,128)(2,1)} %collective-permute-done.1.refs_8_), channel_id=1, source_target_pairs={{0,16},{16,0},{1,17},{17,1},{2,18},{18,2},{3,19},{19,3},{4,20},{20... | collective-permute-start | bytes 983048 | tf_op jit(solution)/shard_map/ppermute | solution.py:26
  33.7 12.6 %collective-permute-start.2 = (bf16[4,320,256]{2,1,0:T(8,128)(2,1)}, bf16[4,320,256]{2,1,0:T(8,128)(2,1)S(1)}, u32[]{:S(2)}, u32[]{:S(2)}) collective-permute-start(bf16[4,320,256]{2,1,0:T(8,128)(2,1)} %get-tuple-element.70), channel_id=1, source_target_pairs={{0,1},{1,0},{2,3},{3,2},{4,5},{5,4},{6,7},{7,6},{8,9},{9,8},{10,11... | collective-permute-start | bytes 1966088 | tf_op jit(solution)/shard_map/ppermute | solution.py:26
  34.1 1.3 copy-start.1
  35.4 1.0 copy-start.2
  38.6 5.6 %collective-permute-start.7 = (bf16[160,1280]{1,0:T(8,128)(2,1)S(1)}, bf16[160,1280]{1,0:T(8,128)(2,1)S(1)}, u32[]{:S(2)}, u32[]{:S(2)}) collective-permute-start(bf16[160,1280]{1,0:T(8,128)(2,1)S(1)} %copy-done.2), channel_id=1, source_target_pairs={{0,1},{1,0},{2,3},{3,2},{4,5},{5,4},{6,7},{7,6},{8,9},{9,8},{10,11... | collective-permute-start | bytes 1228808 | tf_op jit(solution)/shard_map/ppermute | solution.py:26
  38.6 7.7 %collective-permute-start.8 = (bf16[160,1280]{1,0:T(8,128)(2,1)}, bf16[160,1280]{1,0:T(8,128)(2,1)S(1)}, u32[]{:S(2)}, u32[]{:S(2)}) collective-permute-start(bf16[160,1280]{1,0:T(8,128)(2,1)} %collective-permute-done.refs_1_), channel_id=1, source_target_pairs={{0,1},{1,0},{2,3},{3,2},{4,5},{5,4},{6,7},{7,6},{8,9},{9,8},{10,11... | collective-permute-start | bytes 1228808 | tf_op jit(solution)/shard_map/ppermute | solution.py:26
  43.7 2.7 %collective-permute-start.9 = (bf16[160,1280]{1,0:T(8,128)(2,1)}, bf16[160,1280]{1,0:T(8,128)(2,1)S(1)}, u32[]{:S(2)}, u32[]{:S(2)}) collective-permute-start(bf16[160,1280]{1,0:T(8,128)(2,1)} %collective-permute-done.3.refs_2_), channel_id=1, source_target_pairs={{0,1},{1,0},{2,3},{3,2},{4,5},{5,4},{6,7},{7,6},{8,9},{9,8},{10,11... | collective-permute-start | bytes 1228808 | tf_op jit(solution)/shard_map/ppermute | solution.py:26
  43.7 2.7 %collective-permute-start.10 = (bf16[160,1280]{1,0:T(8,128)(2,1)}, bf16[160,1280]{1,0:T(8,128)(2,1)S(1)}, u32[]{:S(2)}, u32[]{:S(2)}) collective-permute-start(bf16[160,1280]{1,0:T(8,128)(2,1)} %collective-permute-done.4.refs_3_), channel_id=1, source_target_pairs={{0,1},{1,0},{2,3},{3,2},{4,5},{5,4},{6,7},{7,6},{8,9},{9,8},{10,11... | collective-permute-start | bytes 1228808 | tf_op jit(solution)/shard_map/ppermute | solution.py:26
  44.2 10.2 %collective-permute-start.13 = (bf16[2,320,256]{2,1,0:T(8,128)(2,1)}, bf16[2,320,256]{2,1,0:T(8,128)(2,1)S(1)}, u32[]{:S(2)}, u32[]{:S(2)}) collective-permute-start(bf16[2,320,256]{2,1,0:T(8,128)(2,1)} %collective-permute-done.6.refs_8_), channel_id=1, source_target_pairs={{0,16},{16,0},{1,17},{17,1},{2,18},{18,2},{3,19},{19,3},{4,20},{20... | collective-permute-start | bytes 983048 | tf_op jit(solution)/shard_map/ppermute | solution.py:26
  49.5 16.7 %collective-permute-start.11 = (bf16[1024,256]{1,0:T(8,128)(2,1)S(1)}, bf16[1024,256]{1,0:T(8,128)(2,1)S(1)}, u32[]{:S(2)}, u32[]{:S(2)}) collective-permute-start(bf16[1024,256]{1,0:T(8,128)(2,1)S(1)} %get-tuple-element.82), channel_id=1, source_target_pairs={{0,2},{1,3},{2,0},{3,1},{4,6},{5,7},{6,4},{7,5},{8,10},{9,11},{10,... | collective-permute-start | bytes 1572872 | tf_op jit(solution)/shard_map/ppermute | solution.py:26
  51.0 15.3 %collective-permute-start.12 = (bf16[1024,256]{1,0:T(8,128)(2,1)S(1)}, bf16[1024,256]{1,0:T(8,128)(2,1)S(1)}, u32[]{:S(2)}, u32[]{:S(2)}) collective-permute-start(bf16[1024,256]{1,0:T(8,128)(2,1)S(1)} %get-tuple-element.83), channel_id=1, source_target_pairs={{0,4},{1,5},{2,6},{3,7},{4,0},{5,1},{6,2},{7,3},{8,12},{9,13},{10,... | collective-permute-start | bytes 1572872 | tf_op jit(solution)/shard_map/ppermute | solution.py:26
  57.4 21.9 %collective-permute-start.14 = (bf16[1024,256]{1,0:T(8,128)(2,1)S(1)}, bf16[1024,256]{1,0:T(8,128)(2,1)S(1)}, u32[]{:S(2)}, u32[]{:S(2)}) collective-permute-start(bf16[1024,256]{1,0:T(8,128)(2,1)S(1)} %get-tuple-element.93), channel_id=1, source_target_pairs={{0,6},{1,7},{2,4},{3,5},{4,2},{5,3},{6,0},{7,1},{8,14},{9,15},{10,... | collective-permute-start | bytes 1572872 | tf_op jit(solution)/shard_map/ppermute | solution.py:26
  58.7 26.0 %slice-start = ((s8[6553600]{0:T(1024)(128)(4,1)}), s8[2359296]{0:T(1024)(128)(4,1)S(1)}, s32[]{:S(2)}) async-start(s8[6553600]{0:T(1024)(128)(4,1)} %bitcast.79), calls=%async_computation | async-start | bytes 4718592
  61.4 18.4 %collective-permute-start.16 = (bf16[16,128]{1,0:T(8,128)(2,1)S(1)}, bf16[16,128]{1,0:T(8,128)(2,1)S(1)}, u32[]{:S(2)}, u32[]{:S(2)}) collective-permute-start(bf16[16,128]{1,0:T(8,128)(2,1)S(1)} %get-tuple-element.98), channel_id=1, source_target_pairs={{0,8},{1,9},{2,10},{3,11},{4,12},{5,13},{6,14},{7,15},{8,0},{9,1},... | collective-permute-start | bytes 12296 | tf_op jit(solution)/shard_map/ppermute | solution.py:26
  66.1 13.7 %collective-permute-start.15 = (bf16[128,640]{1,0:T(8,128)(2,1)S(1)}, bf16[128,640]{1,0:T(8,128)(2,1)S(1)}, u32[]{:S(2)}, u32[]{:S(2)}) collective-permute-start(bf16[128,640]{1,0:T(8,128)(2,1)S(1)} %get-tuple-element.97), channel_id=1, source_target_pairs={{0,8},{1,9},{2,10},{3,11},{4,12},{5,13},{6,14},{7,15},{8,0},{9,1},... | collective-permute-start | bytes 491528 | tf_op jit(solution)/shard_map/ppermute | solution.py:26
  66.3 18.4 %slice-start.1 = ((s8[6553600]{0:T(1024)(128)(4,1)}), s8[4194304]{0:T(1024)(128)(4,1)S(1)}, s32[]{:S(2)}) async-start(s8[6553600]{0:T(1024)(128)(4,1)} %bitcast.79), calls=%async_computation.1 | async-start | bytes 8388608
  81.7 4.6 %collective-permute-start.18 = (bf16[16,128]{1,0:T(8,128)(2,1)S(1)}, bf16[16,128]{1,0:T(8,128)(2,1)S(1)}, u32[]{:S(2)}, u32[]{:S(2)}) collective-permute-start(bf16[16,128]{1,0:T(8,128)(2,1)S(1)} %get-tuple-element.102), channel_id=1, source_target_pairs={{0,8},{1,9},{2,10},{3,11},{4,12},{5,13},{6,14},{7,15},{8,0},{9,1},... | collective-permute-start | bytes 12296 | tf_op jit(solution)/shard_map/ppermute | solution.py:26
  84.5 9.4 %collective-permute-start.17 = (bf16[128,640]{1,0:T(8,128)(2,1)S(1)}, bf16[128,640]{1,0:T(8,128)(2,1)S(1)}, u32[]{:S(2)}, u32[]{:S(2)}) collective-permute-start(bf16[128,640]{1,0:T(8,128)(2,1)S(1)} %get-tuple-element.101), channel_id=1, source_target_pairs={{0,8},{1,9},{2,10},{3,11},{4,12},{5,13},{6,14},{7,15},{8,0},{9,1},... | collective-permute-start | bytes 491528 | tf_op jit(solution)/shard_map/ppermute | solution.py:26
  85.3 19.7 %copy-start.4 = (bf16[320,128]{1,0:T(8,128)(2,1)S(1)}, bf16[320,128]{1,0:T(8,128)(2,1)}, u32[]{:S(2)}) copy-start(bf16[320,128]{1,0:T(8,128)(2,1)} %extra_any.1) | copy-start | bytes 245764
  93.9 19.7 %copy-start = (bf16[2560,640]{1,0:T(8,128)(2,1)S(1)}, bf16[2560,640]{1,0:T(8,128)(2,1)}, u32[]{:S(2)}) copy-start(bf16[2560,640]{1,0:T(8,128)(2,1)} %get-tuple-element.122.weight_ref) | copy-start | bytes 9830404
  95.7 1.7 %collective-permute-start.19 = (bf16[4,320,128]{2,1,0:T(8,128)(2,1)S(1)}, bf16[4,320,128]{2,1,0:T(8,128)(2,1)S(1)}, u32[]{:S(2)}, u32[]{:S(2)}) collective-permute-start(bf16[4,320,128]{2,1,0:T(8,128)(2,1)S(1)} %get-tuple-element.104), channel_id=1, source_target_pairs={{0,1},{1,0},{2,3},{3,2},{4,5},{5,4},{6,7},{7,6},{8,9},{9,8},{10,11... | collective-permute-start | bytes 983048 | tf_op jit(solution)/shard_map/ppermute | solution.py:26
  97.5 5.5 %collective-permute-start.20 = (bf16[320,128]{1,0:T(8,128)(2,1)S(1)}, bf16[320,128]{1,0:T(8,128)(2,1)S(1)}, u32[]{:S(2)}, u32[]{:S(2)}) collective-permute-start(bf16[320,128]{1,0:T(8,128)(2,1)S(1)} %get-tuple-element.138), channel_id=1, source_target_pairs={{0,2},{1,3},{2,0},{3,1},{4,6},{5,7},{6,4},{7,5},{8,10},{9,11},{10,... | collective-permute-start | bytes 245768 | tf_op jit(solution)/shard_map/ppermute | solution.py:26
  98.4 6.0 %collective-permute-start.22 = (bf16[320,128]{1,0:T(8,128)(2,1)S(1)}, bf16[320,128]{1,0:T(8,128)(2,1)S(1)}, u32[]{:S(2)}, u32[]{:S(2)}) collective-permute-start(bf16[320,128]{1,0:T(8,128)(2,1)S(1)} %get-tuple-element.139), channel_id=1, source_target_pairs={{0,6},{1,7},{2,4},{3,5},{4,2},{5,3},{6,0},{7,1},{8,14},{9,15},{10,... | collective-permute-start | bytes 245768 | tf_op jit(solution)/shard_map/ppermute | solution.py:26
  98.4 6.6 %collective-permute-start.21 = (bf16[320,128]{1,0:T(8,128)(2,1)S(1)}, bf16[320,128]{1,0:T(8,128)(2,1)S(1)}, u32[]{:S(2)}, u32[]{:S(2)}) collective-permute-start(bf16[320,128]{1,0:T(8,128)(2,1)S(1)} %get-tuple-element.140), channel_id=1, source_target_pairs={{0,4},{1,5},{2,6},{3,7},{4,0},{5,1},{6,2},{7,3},{8,12},{9,13},{10,... | collective-permute-start | bytes 245768 | tf_op jit(solution)/shard_map/ppermute | solution.py:26
  105.0 5.4 %collective-permute-start.25 = (bf16[320,128]{1,0:T(8,128)(2,1)S(1)}, bf16[320,128]{1,0:T(8,128)(2,1)S(1)}, u32[]{:S(2)}, u32[]{:S(2)}) collective-permute-start(bf16[320,128]{1,0:T(8,128)(2,1)S(1)} %fusion.11.refs_0_), channel_id=1, source_target_pairs={{0,6},{1,7},{2,4},{3,5},{4,2},{5,3},{6,0},{7,1},{8,14},{9,15},{10,... | collective-permute-start | bytes 245768 | tf_op jit(solution)/shard_map/ppermute | solution.py:26
  105.9 4.8 %collective-permute-start.24 = (bf16[320,128]{1,0:T(8,128)(2,1)S(1)}, bf16[320,128]{1,0:T(8,128)(2,1)S(1)}, u32[]{:S(2)}, u32[]{:S(2)}) collective-permute-start(bf16[320,128]{1,0:T(8,128)(2,1)S(1)} %fusion.11.refs_0_), channel_id=1, source_target_pairs={{0,4},{1,5},{2,6},{3,7},{4,0},{5,1},{6,2},{7,3},{8,12},{9,13},{10,... | collective-permute-start | bytes 245768 | tf_op jit(solution)/shard_map/ppermute | solution.py:26
  107.4 4.4 %collective-permute-start.23 = (bf16[320,128]{1,0:T(8,128)(2,1)S(1)}, bf16[320,128]{1,0:T(8,128)(2,1)S(1)}, u32[]{:S(2)}, u32[]{:S(2)}) collective-permute-start(bf16[320,128]{1,0:T(8,128)(2,1)S(1)} %fusion.11.refs_0_), channel_id=1, source_target_pairs={{0,2},{1,3},{2,0},{3,1},{4,6},{5,7},{6,4},{7,5},{8,10},{9,11},{10,... | collective-permute-start | bytes 245768 | tf_op jit(solution)/shard_map/ppermute | solution.py:26
  111.9 1.7 %collective-permute-start.26 = (bf16[4,320,128]{2,1,0:T(8,128)(2,1)S(1)}, bf16[4,320,128]{2,1,0:T(8,128)(2,1)S(1)}, u32[]{:S(2)}, u32[]{:S(2)}) collective-permute-start(bf16[4,320,128]{2,1,0:T(8,128)(2,1)S(1)} %pad_maximum_fusion), channel_id=1, source_target_pairs={{0,1},{1,0},{2,3},{3,2},{4,5},{5,4},{6,7},{7,6},{8,9},{9,8},{10,11... | collective-permute-start | bytes 983048 | tf_op jit(solution)/shard_map/ppermute | solution.py:26
  115.9 10.8 %collective-permute-start.27 = (bf16[128,640]{1,0:T(8,128)(2,1)S(1)}, bf16[128,640]{1,0:T(8,128)(2,1)S(1)}, u32[]{:S(2)}, u32[]{:S(2)}) collective-permute-start(bf16[128,640]{1,0:T(8,128)(2,1)S(1)} %get-tuple-element.107), channel_id=1, source_target_pairs={{0,8},{1,9},{2,10},{3,11},{4,12},{5,13},{6,14},{7,15},{8,0},{9,1},... | collective-permute-start | bytes 491528 | tf_op jit(solution)/shard_map/ppermute | solution.py:26
  116.4 10.3 %collective-permute-start.28 = (bf16[16,128]{1,0:T(8,128)(2,1)S(1)}, bf16[16,128]{1,0:T(8,128)(2,1)S(1)}, u32[]{:S(2)}, u32[]{:S(2)}) collective-permute-start(bf16[16,128]{1,0:T(8,128)(2,1)S(1)} %get-tuple-element.108), channel_id=1, source_target_pairs={{0,8},{1,9},{2,10},{3,11},{4,12},{5,13},{6,14},{7,15},{8,0},{9,1},... | collective-permute-start | bytes 12296 | tf_op jit(solution)/shard_map/ppermute | solution.py:26
  128.7 9.6 %collective-permute-start.29 = (bf16[128,640]{1,0:T(8,128)(2,1)S(1)}, bf16[128,640]{1,0:T(8,128)(2,1)S(1)}, u32[]{:S(2)}, u32[]{:S(2)}) collective-permute-start(bf16[128,640]{1,0:T(8,128)(2,1)S(1)} %get-tuple-element.111), channel_id=1, source_target_pairs={{0,8},{1,9},{2,10},{3,11},{4,12},{5,13},{6,14},{7,15},{8,0},{9,1},... | collective-permute-start | bytes 491528 | tf_op jit(solution)/shard_map/ppermute | solution.py:26
  128.8 9.5 %collective-permute-start.30 = (bf16[16,128]{1,0:T(8,128)(2,1)S(1)}, bf16[16,128]{1,0:T(8,128)(2,1)S(1)}, u32[]{:S(2)}, u32[]{:S(2)}) collective-permute-start(bf16[16,128]{1,0:T(8,128)(2,1)S(1)} %get-tuple-element.112), channel_id=1, source_target_pairs={{0,8},{1,9},{2,10},{3,11},{4,12},{5,13},{6,14},{7,15},{8,0},{9,1},... | collective-permute-start | bytes 12296 | tf_op jit(solution)/shard_map/ppermute | solution.py:26
  140.0 1.7 %collective-permute-start.31 = (bf16[4,320,128]{2,1,0:T(8,128)(2,1)S(1)}, bf16[4,320,128]{2,1,0:T(8,128)(2,1)S(1)}, u32[]{:S(2)}, u32[]{:S(2)}) collective-permute-start(bf16[4,320,128]{2,1,0:T(8,128)(2,1)S(1)} %get-tuple-element.114), channel_id=1, source_target_pairs={{0,1},{1,0},{2,3},{3,2},{4,5},{5,4},{6,7},{7,6},{8,9},{9,8},{10,11... | collective-permute-start | bytes 983048 | tf_op jit(solution)/shard_map/ppermute | solution.py:26
  141.8 5.4 %collective-permute-start.32 = (bf16[320,128]{1,0:T(8,128)(2,1)S(1)}, bf16[320,128]{1,0:T(8,128)(2,1)S(1)}, u32[]{:S(2)}, u32[]{:S(2)}) collective-permute-start(bf16[320,128]{1,0:T(8,128)(2,1)S(1)} %get-tuple-element.135), channel_id=1, source_target_pairs={{0,2},{1,3},{2,0},{3,1},{4,6},{5,7},{6,4},{7,5},{8,10},{9,11},{10,... | collective-permute-start | bytes 245768 | tf_op jit(solution)/shard_map/ppermute | solution.py:26
  142.9 6.0 %collective-permute-start.34 = (bf16[320,128]{1,0:T(8,128)(2,1)S(1)}, bf16[320,128]{1,0:T(8,128)(2,1)S(1)}, u32[]{:S(2)}, u32[]{:S(2)}) collective-permute-start(bf16[320,128]{1,0:T(8,128)(2,1)S(1)} %get-tuple-element.136), channel_id=1, source_target_pairs={{0,6},{1,7},{2,4},{3,5},{4,2},{5,3},{6,0},{7,1},{8,14},{9,15},{10,... | collective-permute-start | bytes 245768 | tf_op jit(solution)/shard_map/ppermute | solution.py:26
  143.0 6.3 %collective-permute-start.33 = (bf16[320,128]{1,0:T(8,128)(2,1)S(1)}, bf16[320,128]{1,0:T(8,128)(2,1)S(1)}, u32[]{:S(2)}, u32[]{:S(2)}) collective-permute-start(bf16[320,128]{1,0:T(8,128)(2,1)S(1)} %get-tuple-element.137), channel_id=1, source_target_pairs={{0,4},{1,5},{2,6},{3,7},{4,0},{5,1},{6,2},{7,3},{8,12},{9,13},{10,... | collective-permute-start | bytes 245768 | tf_op jit(solution)/shard_map/ppermute | solution.py:26

commit v7 on v6

--- a/solution.py
+++ b/solution.py
@@ -234,8 +234,8 @@
 
 
 def query_kernel(lanes, place_ref, gain_ref, weight_ref, *refs):
-    piece_refs, refs = refs[:-7], refs[-7:]
-    sent_ref, kept_ref, squares_sent_ref, squares_ref, stream, parts, sems = refs
+    piece_refs, refs = refs[:-9], refs[-9:]
+    results, own_ref, (stream, turned, parts, sems) = refs[:4], refs[4], refs[5:]
     unit = stream.shape[0] // KVH
     more = parts.shape[1]
     blocks = parts.shape[2] // lanes
@@ -265,18 +265,44 @@
             stream[pl.ds(pl.multiple_of(bases[number] + block * more, more), more), :] = parts[
                 number, :, block * lanes : (block + 1) * lanes
             ]
-    rows = stream[...].astype(F32).T
+    turned[...] = stream[...].astype(F32).T
+    query_step(turned[...], gain_ref, weight_ref, *results)
+    half = own_ref.shape[0]
+    own_ref[...] = turned[pl.ds(pl.multiple_of(place_ref[1] * half, half), half), :].astype(BF16)
+
+
+def query_step(rows, gain_ref, weight_ref, sent_ref, kept_ref, squares_sent_ref, squares_ref):
     squares = jnp.sum(rows * rows, axis=1, keepdims=True)
     scaled = (rows * gain_ref[...]).astype(BF16)
     partial = jnp.dot(scaled, weight_ref[...], preferred_element_type=F32)
     kept_ref[...] = partial
     sent_ref[...] = partial.astype(BF16)
-    spread = jnp.broadcast_to(squares, (lanes, lanes))
+    spread = jnp.broadcast_to(squares, squares_ref.shape)
     squares_ref[...] = spread
     across = spread.T[:8]
     high = across.astype(BF16)
     squares_sent_ref[:8] = high
     squares_sent_ref[8:] = (across - high.astype(F32)).astype(BF16)
+
+
+def both_cores(place_ref, ours_ref, theirs_ref, rows):
+    half = ours_ref.shape[0]
+    for which, ref in ((place_ref[1], ours_ref), (1 - place_ref[1], theirs_ref)):
+        rows[pl.ds(pl.multiple_of(which * half, half), half), :] = ref[...]
+
+
+def later_query_kernel(place_ref, gain_ref, weight_ref, ours_ref, theirs_ref, *refs):
+    results, rows = refs[:-1], refs[-1]
+    both_cores(place_ref, ours_ref, theirs_ref, rows)
+    query_step(rows[...].astype(F32), gain_ref, weight_ref, *results)
+
+
+def own_rows_kernel(place_ref, ours_ref, theirs_ref, out_ref, rows, turned):
+    both_cores(place_ref, ours_ref, theirs_ref, rows)
+    unit = out_ref.shape[0]
+    column = pl.multiple_of(place_ref[0] * 2 * unit, 2 * unit)
+    turned[...] = rows[:, pl.ds(column, 2 * unit)].astype(F32).T
+    out_ref[...] = turned[pl.ds(pl.multiple_of(place_ref[1] * unit, unit), unit), :].astype(BF16)
 
 
 def spread_back(pair_ref, lanes):
@@ -316,22 +342,38 @@
     totals_sent_ref[8:] = (across - high.astype(F32)).astype(BF16)
 
 
-def update_kernel(others, place_ref, weight_ref, kept_ref, totals_ref, *refs):
-    far, (own_ref, sent_ref) = refs[: 2 * others], refs[2 * others :]
+def attended_of(others, kept_ref, totals_ref, far):
     lanes = kept_ref.shape[0]
-    unit = own_ref.shape[1]
     weighted = kept_ref[...]
     totals = totals_ref[...]
     for other in range(others):
         weighted = weighted + far[2 * other][...].astype(F32)
         totals = totals + spread_back(far[2 * other + 1], lanes)
-    attended = jnp.concatenate(
+    return jnp.concatenate(
         [
             (weighted[:, head * HD : (head + 1) * HD] / totals[:, head : head + 1]).astype(BF16)
             for head in range(weighted.shape[1] // HD)
         ],
         axis=1,
     )
+
+
+def update_rows_kernel(others, place_ref, weight_ref, kept_ref, totals_ref, *refs):
+    far, (own_ref, sent_ref, update) = refs[: 2 * others], refs[2 * others :]
+    attended = attended_of(others, kept_ref, totals_ref, far)
+    update[...] = lax.dot_general(
+        attended, weight_ref[...], (((1,), (1,)), ((), ())), preferred_element_type=F32
+    )
+    half = own_ref.shape[0]
+    for which, out_ref in ((place_ref[1], own_ref), (1 - place_ref[1], sent_ref)):
+        rows = update[pl.ds(pl.multiple_of(which * half, half), half), :]
+        out_ref[...] = rows.astype(out_ref.dtype)
+
+
+def update_kernel(others, place_ref, weight_ref, kept_ref, totals_ref, *refs):
+    far, (own_ref, sent_ref) = refs[: 2 * others], refs[2 * others :]
+    unit = own_ref.shape[1]
+    attended = attended_of(others, kept_ref, totals_ref, far)
     for core, out_ref in enumerate((own_ref, sent_ref)):
         for chip in range(CHIPS):
             base = ((place_ref[0] ^ chip) * 2 + (place_ref[1] ^ core)) * unit
@@ -484,6 +526,17 @@
     return total
 
 
+def reduce_rows(kept, sent):
+    both = (kept + swapped(sent, 1).astype(F32)).astype(BF16)
+    halves = jnp.split(both, 2, axis=1)
+    for masks in ((2, 4), (4, 2)):
+        halves = [
+            (half.astype(F32) + swapped(half, mask).astype(F32)).astype(BF16)
+            for half, mask in zip(halves, masks)
+        ]
+    return jnp.concatenate(halves, axis=1)
+
+
 def attend_rows(queries, query_pos, query_floor, key_values, key_pos):
     row_count = queries.shape[0]
     head_count = queries.shape[1] // HD
@@ -525,6 +578,7 @@
     spread = jax.ShapeDtypeStruct((query_count, query_count), F32)
     wide = [jax.ShapeDtypeStruct((query_count, width), kind) for kind in (BF16, F32)]
     flops = 2 * query_count * slice_depth * width
+    halved = jax.ShapeDtypeStruct((query_count // 2, slice_depth), BF16)
 
     def query_parts(section, pieces):
         gain = lax.dynamic_slice_in_dim(query_gain[section], tile * slice_depth, slice_depth)
@@ -548,11 +602,12 @@
         return call(
             functools.partial(query_kernel, query_count),
             "query",
-            wide + [small, spread],
+            wide + [small, spread, halved],
             [place_now],
             [gain[None, :], query_weight[section, 0]],
             [
                 pltpu.VMEM((slice_depth, query_count), BF16),
+                pltpu.VMEM((query_count, slice_depth), F32),
                 pltpu.VMEM((KVH, own_rows.size // (2 * unit * tile_count), 2 * unit * tile_count), BF16),
                 pltpu.SemaphoreType.DMA((KVH,)),
             ],
@@ -564,8 +619,11 @@
         hidden, kv_gain, kv_weight, query_states, place_now, functools.partial(query_parts, 0)
     )
     positions = [query_pos[:, None], query_floor[:, None], key_pos[None, :]]
-    for section in range(query_gain.shape[0]):
-        if section:
+    if kernels:
+        stream, parts = parts[4], parts[:4]
+    sections = query_gain.shape[0]
+    for section in range(sections):
+        if section and not kernels:
             parts = query_parts(section, gather_rows(own_rows))
         sent, partial, squares_sent, squares = parts
         if kernels:
@@ -580,14 +638,51 @@
                 flops // 2,
             )
             far = zip(over_tiles(sent, tile_count)[1:], over_tiles(totals_sent, tile_count)[1:])
+            arrays = [output_weight[section, 0], weighted, totals]
+            arrays += [value for pair in far for value in pair]
+            if section + 1 < sections:
+                kept, sent = call(
+                    functools.partial(update_rows_kernel, tile_count - 1),
+                    "update",
+                    [jax.ShapeDtypeStruct(halved.shape, F32), halved],
+                    [place_now],
+                    arrays,
+                    [pltpu.VMEM((query_count, slice_depth), F32)],
+                    flops,
+                )
+                stream = (stream.astype(F32) + reduce_rows(kept, sent).astype(F32)).astype(BF16)
+                theirs = swapped(stream, 1)
+                gain = lax.dynamic_slice_in_dim(
+                    query_gain[section + 1], tile * slice_depth, slice_depth
+                )
+                parts = call(
+                    later_query_kernel,
+                    "query",
+                    wide + [small, spread],
+                    [place_now],
+                    [gain[None, :], query_weight[section + 1, 0], stream, theirs],
+                    [pltpu.VMEM((query_count, slice_depth), BF16)],
+                    flops,
+                )
+                own_rows = call(
+                    own_rows_kernel,
+                    "own_rows",
+                    [jax.ShapeDtypeStruct(own_rows.shape, BF16)],
+                    [place_now],
+                    [stream, theirs],
+                    [
+                        pltpu.VMEM((query_count, slice_depth), BF16),
+                        pltpu.VMEM((2 * unit, query_count), F32),
+                    ],
+                )[0]
+                continue
             shape = (CHIPS, unit, query_count)
             kept, sent = call(
                 functools.partial(update_kernel, tile_count - 1),
                 "update",
                 [jax.ShapeDtypeStruct(shape, F32), jax.ShapeDtypeStruct(shape, BF16)],
                 [place_now],
-                [output_weight[section, 0], weighted, totals]
-                + [value for pair in far for value in pair],
+                arrays,
                 (),
                 flops,
             )

time: 150 us -> 147 us (0.980)
  starting transfers between devices: 39.7 us -> 35 us
  waiting for transfers between devices: 74.1 us -> 75.7 us
    ppermute x33 -> x31, starting transfers between devices: 35.5 us -> 30.9 us  [swapped(): return lax.ppermute(value, axis, pairs)]
    ppermute x33 -> x31, waiting for transfers between devices: 59.7 us -> 61.3 us  [swapped(): return lax.ppermute(value, axis, pairs)]
    pallas_call x7 -> x8, Pallas kernels: 13.1 us -> 12.9 us  [call(): pl.pallas_call(kernel, out_shape=out_shape, in_specs=[smem] * len(scalars...]
  transfers between devices with their start and end apart: 35 -> 33, of which waited for: 21 -> 19; matrix products, arithmetic and copies ran while one was open for 5% -> 6% of each run, Pallas kernels for 6% -> 7%
where the time goes in v7:
time: 147 us
  waiting for transfers between devices  75.7 us (51%)
  starting transfers between devices  35 us (24%)
  Pallas kernels  23.7 us (16%)
  local copies, waits for them, and re-layouts  9.95 us (7%)
  other arithmetic  2.22 us (2%)
    ppermute x31, waiting for transfers between devices, swapped(): return lax.ppermute(value, axis, pairs)  61.3 us
    ppermute x31, starting transfers between devices, swapped(): return lax.ppermute(value, axis, pairs)  30.9 us
    ppermute x2, waiting for transfers between devices, to_tile(): return lax.ppermute(value, ('groups', 'row'), pairs)  14.4 us
    pallas_call x8, Pallas kernels, call(): pl.pallas_call(kernel, out_shape=out_shape, in_specs=[smem] * len(scalars...  12.9 us
    pallas_call x2, Pallas kernels, projected(): pl.pallas_call(functools.partial(project_kernel, rows, heads, start), out...  6.08 us
    squeeze x1, local copies, waits for them, and re-layouts, query_parts(): query_weight[section, 0]  5.15 us
    pallas_call x1, Pallas kernels, prepared(): pl.pallas_call(functools.partial(prepare_kernel, pair, head_groups, group...  4.79 us
    ppermute x2, starting transfers between devices, to_tile(): return lax.ppermute(value, ('groups', 'row'), pairs)  4.18 us
  transfers between devices with their start and end apart: 33, of which 19 were waited for; matrix products, arithmetic and copies ran while one was open for 6% of the time, Pallas kernels for 7%

profile of v7, /device:TPU:0, one launch (start us, length us, event | category | flops | bytes accessed | tf_op | source)
XLA Modules:
  0.0 147.0 jit_solution(4467913854290620651)
XLA Ops:
  0.0 0.7 pad_add_fusion.place_ref
  0.7 4.8 %prepare.1 = (bf16[2,320,256]{2,1,0:T(8,128)(2,1)}, bf16[2,320,256]{2,1,0:T(8,128)(2,1)}, bf16[4,320,256]{2,1,0:T(8,128)(2,1)}, bf16[160,1280]{1,0:T(8,128)(2,1)...) custom-call(s32[4]{0:T(128)} %pad_add_fusion.place_ref, ...), custom_call_target="tpu_custom_call" | custom-call | tf_op jit(solution)/shard_map/prepare/pallas_call | solution.py:124
  5.4 4.1 %collective-permute-start.1 = (bf16[2,320,256]{2,1,0:T(8,128)(2,1)}, bf16[2,320,256]{2,1,0:T(8,128)(2,1)}, u32[]{:S(2)}, u32[]{:S(2)}) collective-permute-start(bf16[2,320,256]{2,1,0:T(8,128)(2,1)} %get-tuple-element.65), channel_id=1, source_target_pairs={{0,8},{1,9},{2,10},{3,11},{4,12},{5,13},{6,14},{7,15},{8,0},{9,1},... | collective-permute-start | bytes 983048 | tf_op jit(solution)/shard_map/ppermute | solution.py:463
  9.6 1.7 %collective-permute-start = (bf16[160,1280]{1,0:T(8,128)(2,1)}, bf16[160,1280]{1,0:T(8,128)(2,1)}, u32[]{:S(2)}, u32[]{:S(2)}) collective-permute-start(bf16[160,1280]{1,0:T(8,128)(2,1)} %get-tuple-element.62), channel_id=1, source_target_pairs={{0,2},{1,3},{2,0},{3,1},{4,6},{5,7},{6,4},{7,5},{8,10},{9,11},{10,... | collective-permute-start | bytes 1228808 | tf_op jit(solution)/shard_map/ppermute | solution.py:26
  11.4 1.6 %collective-permute-start.3 = (bf16[160,1280]{1,0:T(8,128)(2,1)}, bf16[160,1280]{1,0:T(8,128)(2,1)}, u32[]{:S(2)}, u32[]{:S(2)}) collective-permute-start(bf16[160,1280]{1,0:T(8,128)(2,1)} %get-tuple-element.74), channel_id=1, source_target_pairs={{0,4},{1,5},{2,6},{3,7},{4,0},{5,1},{6,2},{7,3},{8,12},{9,13},{10,... | collective-permute-start | bytes 1228808 | tf_op jit(solution)/shard_map/ppermute | solution.py:26
  13.1 0.9 fusion.16
  14.0 5.1 %slice_bitcast_fusion.3 = (bf16[2560,640]{1,0:T(8,128)(2,1)S(1)}, bf16[2560,640]{1,0:T(8,128)(2,1)}) fusion(bf16[2,1,2560,640]{3,2,1,0:T(8,128)(2,1)} %param.13), kind=kLoop, calls=%fused_computation.3 | loop fusion | bytes 13107200 | tf_op jit(solution)/shard_map/squeeze | solution.py:607
  19.7 12.9 %collective-permute-done.1.refs_8_ = bf16[2,320,256]{2,1,0:T(8,128)(2,1)} collective-permute-done((bf16[2,320,256]{2,1,0:T(8,128)(2,1)}, bf16[2,320,256]{2,1,0:T(8,128)(2,1)}, u32[]{:S(2)}, u32[]{:S(2)}) %collective-permute-start.1) | collective-permute-done | bytes 327712 | tf_op jit(solution)/shard_map/ppermute | solution.py:463
  32.5 1.1 collective-permute-start.5
  34.2 1.3 copy-done.1
  35.6 1.0 copy-done.2
  36.6 0.6 stage.1
  37.2 1.5 %collective-permute-done.6.refs_8_ = bf16[2,320,256]{2,1,0:T(8,128)(2,1)} collective-permute-done((bf16[2,320,256]{2,1,0:T(8,128)(2,1)}, bf16[2,320,256]{2,1,0:T(8,128)(2,1)}, u32[]{:S(2)}, u32[]{:S(2)}) %collective-permute-start.6) | collective-permute-done | bytes 327712 | tf_op jit(solution)/shard_map/ppermute | solution.py:463
  39.3 4.5 %collective-permute-done.4.refs_3_ = bf16[160,1280]{1,0:T(8,128)(2,1)} collective-permute-done((bf16[160,1280]{1,0:T(8,128)(2,1)}, bf16[160,1280]{1,0:T(8,128)(2,1)}, u32[]{:S(2)}, u32[]{:S(2)}) %collective-permute-start.4) | collective-permute-done | bytes 409632 | tf_op jit(solution)/shard_map/ppermute | solution.py:26
  44.4 2.1 %collective-permute-start.13 = (bf16[2,320,256]{2,1,0:T(8,128)(2,1)}, bf16[2,320,256]{2,1,0:T(8,128)(2,1)S(1)}, u32[]{:S(2)}, u32[]{:S(2)}) collective-permute-start(bf16[2,320,256]{2,1,0:T(8,128)(2,1)} %collective-permute-done.6.refs_8_), channel_id=1, source_target_pairs={{0,16},{16,0},{1,17},{17,1},{2,18},{18,2},{3,19},{19,3},{4,20},{20... | collective-permute-start | bytes 983048 | tf_op jit(solution)/shard_map/ppermute | solution.py:26
  46.5 3.1 %project.2 = (bf16[1024,256]{1,0:T(8,128)(2,1)S(1)}, bf16[1024,256]{1,0:T(8,128)(2,1)S(1)}) custom-call(s32[2]{0:T(128)S(1)} %pad_add_fusion.1.first_ref, bf16[4,320,256]{2,1,0:T(8,128)(2,1)S(1)} %get-tuple-element.70.kept_ref, bf16[4,320,256]{2,1,0:T(8,128)(2,1)S(1)} %collective-permute-done.2.traded_ref, bf16[160,1280]{1,0:T(8,128)(2,1)S(1)} %get-tuple-element.83.refs_0_, ...), custom_call_target="tpu_custom_call" | custom-call | flops 10737418240 | bytes 2621440 | tf_op jit(solution)/shard_map/project/pallas_call | solution.py:219
  49.6 1.6 %collective-permute-start.11 = (bf16[1024,256]{1,0:T(8,128)(2,1)S(1)}, bf16[1024,256]{1,0:T(8,128)(2,1)S(1)}, u32[]{:S(2)}, u32[]{:S(2)}) collective-permute-start(bf16[1024,256]{1,0:T(8,128)(2,1)S(1)} %get-tuple-element.92), channel_id=1, source_target_pairs={{0,2},{1,3},{2,0},{3,1},{4,6},{5,7},{6,4},{7,5},{8,10},{9,11},{10,... | collective-permute-start | bytes 1572872 | tf_op jit(solution)/shard_map/ppermute | solution.py:26
  51.3 3.3 %collective-permute-done.13.refs_9_ = bf16[2,320,256]{2,1,0:T(8,128)(2,1)S(1)} collective-permute-done((bf16[2,320,256]{2,1,0:T(8,128)(2,1)}, bf16[2,320,256]{2,1,0:T(8,128)(2,1)S(1)}, u32[]{:S(2)}, u32[]{:S(2)}) %collective-permute-start.13) | collective-permute-done | bytes 327712 | tf_op jit(solution)/shard_map/ppermute | solution.py:26
  54.6 3.0 %project.3 = (bf16[1024,256]{1,0:T(8,128)(2,1)S(1)}, bf16[1024,256]{1,0:T(8,128)(2,1)S(1)}) custom-call(s32[2]{0:T(128)S(1)} %pad_add_fusion.1.first_ref, bf16[4,320,256]{2,1,0:T(8,128)(2,1)S(1)} %get-tuple-element.70.kept_ref, bf16[4,320,256]{2,1,0:T(8,128)(2,1)S(1)} %collective-permute-done.2.traded_ref, bf16[160,1280]{1,0:T(8,128)(2,1)S(1)} %get-tuple-element.83.refs_0_, ...), custom_call_target="tpu_custom_call" | custom-call | flops 10737418240 | bytes 2621440 | tf_op jit(solution)/shard_map/project/pallas_call | solution.py:219
  57.6 1.2 collective-permute-start.14
  58.8 2.8 %query.2 = (bf16[128,640]{1,0:T(8,128)(2,1)S(1)}, f32[128,640]{1,0:T(8,128)S(1)}, bf16[16,128]{1,0:T(8,128)(2,1)S(1)}, f32[128,128]{1,0:T(8,128)S(1)}, bf16[64,2560]{1,0:T(8,128)(2,1)S(1)}) custom-call(s32[4]{0:T(128)S(1)} %copy-done.3, f32[1,2560]{1,0:T(1,128)S(1)} %constant_dynamic-slice_fusion.1.gain_ref, ...), custom_call_target="tpu_custom_call" | custom-call | flops 419430400 | bytes 3281920 | tf_op jit(solution)/shard_map/query/pallas_call | solution.py:392
  61.6 4.7 %collective-permute-start.16 = (bf16[16,128]{1,0:T(8,128)(2,1)S(1)}, bf16[16,128]{1,0:T(8,128)(2,1)S(1)}, u32[]{:S(2)}, u32[]{:S(2)}) collective-permute-start(bf16[16,128]{1,0:T(8,128)(2,1)S(1)} %get-tuple-element.100), channel_id=1, source_target_pairs={{0,8},{1,9},{2,10},{3,11},{4,12},{5,13},{6,14},{7,15},{8,0},{9,1},... | collective-permute-start | bytes 12296 | tf_op jit(solution)/shard_map/ppermute | solution.py:26
  66.6 12.8 %collective-permute-done.14 = bf16[1024,256]{1,0:T(8,128)(2,1)S(1)} collective-permute-done((bf16[1024,256]{1,0:T(8,128)(2,1)S(1)}, bf16[1024,256]{1,0:T(8,128)(2,1)S(1)}, u32[]{:S(2)}, u32[]{:S(2)}) %collective-permute-start.14) | collective-permute-done | bytes 524320 | tf_op jit(solution)/shard_map/ppermute | solution.py:26
  79.9 1.9 %attend.2 = (bf16[128,640]{1,0:T(8,128)(2,1)S(1)}, f32[128,640]{1,0:T(8,128)S(1)}, bf16[16,128]{1,0:T(8,128)(2,1)S(1)}, f32[128,128]{1,0:T(8,128)S(1)}) custom-call(s32[128,1]{1,0:T(8,128)S(1)} %fusion.7.query_pos_ref, s32[128,1]{1,0:T(8,128)S(1)} %broadcast_in_dim_reshape.5.query_floor_ref, s32[1,1024]{1,0:T(1,128)S(1)} %bitcast.51, ...), custom_call_target="tpu_custom_call" | custom-call | flops 209715200 | bytes 891392 | tf_op jit(solution)/shard_map/attend/pallas_call | solution.py:392
  81.8 2.8 %collective-permute-start.18 = (bf16[16,128]{1,0:T(8,128)(2,1)S(1)}, bf16[16,128]{1,0:T(8,128)(2,1)S(1)}, u32[]{:S(2)}, u32[]{:S(2)}) collective-permute-start(bf16[16,128]{1,0:T(8,128)(2,1)S(1)} %get-tuple-element.104), channel_id=1, source_target_pairs={{0,8},{1,9},{2,10},{3,11},{4,12},{5,13},{6,14},{7,15},{8,0},{9,1},... | collective-permute-start | bytes 12296 | tf_op jit(solution)/shard_map/ppermute | solution.py:26
  85.4 1.0 collective-permute-done.18.refs_1_
  86.4 7.6 %collective-permute-done.17.refs_0_ = bf16[128,640]{1,0:T(8,128)(2,1)S(1)} collective-permute-done((bf16[128,640]{1,0:T(8,128)(2,1)S(1)}, bf16[128,640]{1,0:T(8,128)(2,1)S(1)}, u32[]{:S(2)}, u32[]{:S(2)}) %collective-permute-start.17) | collective-permute-done | bytes 163872 | tf_op jit(solution)/shard_map/ppermute | solution.py:26
  94.0 1.9 %update.2 = (f32[64,2560]{1,0:T(8,128)S(1)}, bf16[64,2560]{1,0:T(8,128)(2,1)S(1)}) custom-call(s32[4]{0:T(128)S(1)} %copy-done.3, bf16[2560,640]{1,0:T(8,128)(2,1)S(1)} %get-tuple-element.121.weight_ref, f32[128,640]{1,0:T(8,128)S(1)} %get-tuple-element.101.kept_ref, f32[128,128]{1,0:T(8,128)S(1)} %get-tuple-element.102.totals_ref, ...), custom_call_target="tpu_custom_call" | custom-call | flops 419430400 | bytes 3641344 | tf_op jit(solution)/shard_map/update/pallas_call | solution.py:392
  96.0 1.6 %collective-permute-done.19 = bf16[64,2560]{1,0:T(8,128)(2,1)S(1)} collective-permute-done((bf16[64,2560]{1,0:T(8,128)(2,1)S(1)}, bf16[64,2560]{1,0:T(8,128)(2,1)S(1)}, u32[]{:S(2)}, u32[]{:S(2)}) %collective-permute-start.19) | collective-permute-done | bytes 327712 | tf_op jit(solution)/shard_map/ppermute | solution.py:26
  97.7 0.9 collective-permute-start.20
  98.6 5.4 %collective-permute-done.20 = bf16[64,1280]{1,0:T(8,128)(2,1)S(1)} collective-permute-done((bf16[64,1280]{1,0:T(8,128)(2,1)S(1)}, bf16[64,1280]{1,0:T(8,128)(2,1)S(1)}, u32[]{:S(2)}, u32[]{:S(2)}) %collective-permute-start.20) | collective-permute-done | bytes 163872 | tf_op jit(solution)/shard_map/ppermute | solution.py:26
  105.0 1.2 collective-permute-start.23
  106.1 3.9 %collective-permute-done.21 = bf16[64,1280]{1,0:T(8,128)(2,1)S(1)} collective-permute-done((bf16[64,1280]{1,0:T(8,128)(2,1)S(1)}, bf16[64,1280]{1,0:T(8,128)(2,1)S(1)}, u32[]{:S(2)}, u32[]{:S(2)}) %collective-permute-start.21) | collective-permute-done | bytes 163872 | tf_op jit(solution)/shard_map/ppermute | solution.py:26
  110.5 1.6 %collective-permute-done.24.theirs_ref = bf16[64,2560]{1,0:T(8,128)(2,1)S(1)} collective-permute-done((bf16[64,2560]{1,0:T(8,128)(2,1)S(1)}, bf16[64,2560]{1,0:T(8,128)(2,1)S(1)}, u32[]{:S(2)}, u32[]{:S(2)}) %collective-permute-start.24) | collective-permute-done | bytes 327712 | tf_op jit(solution)/shard_map/ppermute | solution.py:26
  112.1 1.3 query.3
  113.4 1.7 %collective-permute-start.25 = (bf16[128,640]{1,0:T(8,128)(2,1)S(1)}, bf16[128,640]{1,0:T(8,128)(2,1)S(1)}, u32[]{:S(2)}, u32[]{:S(2)}) collective-permute-start(bf16[128,640]{1,0:T(8,128)(2,1)S(1)} %get-tuple-element.109), channel_id=1, source_target_pairs={{0,8},{1,9},{2,10},{3,11},{4,12},{5,13},{6,14},{7,15},{8,0},{9,1},... | collective-permute-start | bytes 491528 | tf_op jit(solution)/shard_map/ppermute | solution.py:26
  115.1 1.3 collective-permute-start.26
  116.4 7.9 %collective-permute-done.26.refs_3_ = bf16[16,128]{1,0:T(8,128)(2,1)S(1)} collective-permute-done((bf16[16,128]{1,0:T(8,128)(2,1)S(1)}, bf16[16,128]{1,0:T(8,128)(2,1)S(1)}, u32[]{:S(2)}, u32[]{:S(2)}) %collective-permute-start.26) | collective-permute-done | bytes 4128 | tf_op jit(solution)/shard_map/ppermute | solution.py:26
  124.3 1.9 %attend.3 = (bf16[128,640]{1,0:T(8,128)(2,1)S(1)}, f32[128,640]{1,0:T(8,128)S(1)}, bf16[16,128]{1,0:T(8,128)(2,1)S(1)}, f32[128,128]{1,0:T(8,128)S(1)}) custom-call(s32[128,1]{1,0:T(8,128)S(1)} %fusion.7.query_pos_ref, s32[128,1]{1,0:T(8,128)S(1)} %broadcast_in_dim_reshape.5.query_floor_ref, s32[1,1024]{1,0:T(1,128)S(1)} %bitcast.52, ...), custom_call_target="tpu_custom_call" | custom-call | flops 209715200 | bytes 891392 | tf_op jit(solution)/shard_map/attend/pallas_call | solution.py:392
  126.3 2.9 %collective-permute-start.28 = (bf16[16,128]{1,0:T(8,128)(2,1)S(1)}, bf16[16,128]{1,0:T(8,128)(2,1)S(1)}, u32[]{:S(2)}, u32[]{:S(2)}) collective-permute-start(bf16[16,128]{1,0:T(8,128)(2,1)S(1)} %get-tuple-element.114), channel_id=1, source_target_pairs={{0,8},{1,9},{2,10},{3,11},{4,12},{5,13},{6,14},{7,15},{8,0},{9,1},... | collective-permute-start | bytes 12296 | tf_op jit(solution)/shard_map/ppermute | solution.py:26
  129.2 6.0 %collective-permute-done.28.refs_1_ = bf16[16,128]{1,0:T(8,128)(2,1)S(1)} collective-permute-done((bf16[16,128]{1,0:T(8,128)(2,1)S(1)}, bf16[16,128]{1,0:T(8,128)(2,1)S(1)}, u32[]{:S(2)}, u32[]{:S(2)}) %collective-permute-start.28) | collective-permute-done | bytes 4128 | tf_op jit(solution)/shard_map/ppermute | solution.py:26
  135.2 1.8 %update.3 = (f32[4,320,128]{2,1,0:T(8,128)S(1)}, bf16[4,320,128]{2,1,0:T(8,128)(2,1)S(1)}) custom-call(s32[4]{0:T(128)S(1)} %copy-done.3, bf16[2560,640]{1,0:T(8,128)(2,1)S(1)} %get-tuple-element.122.weight_ref, f32[128,640]{1,0:T(8,128)S(1)} %get-tuple-element.111.kept_ref, f32[128,128]{1,0:T(8,128)S(1)} %get-tuple-element.112.totals_ref, ...), custom_call_target="tpu_custom_call" | custom-call | flops 419430400 | bytes 3641344 | tf_op jit(solution)/shard_map/update/pallas_call | solution.py:392
  137.0 1.6 %collective-permute-done.29 = bf16[4,320,128]{2,1,0:T(8,128)(2,1)S(1)} collective-permute-done((bf16[4,320,128]{2,1,0:T(8,128)(2,1)S(1)}, bf16[4,320,128]{2,1,0:T(8,128)(2,1)S(1)}, u32[]{:S(2)}, u32[]{:S(2)}) %collective-permute-start.29) | collective-permute-done | bytes 327712 | tf_op jit(solution)/shard_map/ppermute | solution.py:26
  138.8 1.4 collective-permute-start.30
  140.2 2.2 %collective-permute-start.31 = (bf16[320,128]{1,0:T(8,128)(2,1)S(1)}, bf16[320,128]{1,0:T(8,128)(2,1)S(1)}, u32[]{:S(2)}, u32[]{:S(2)}) collective-permute-start(bf16[320,128]{1,0:T(8,128)(2,1)S(1)} %get-tuple-element.137), channel_id=1, source_target_pairs={{0,4},{1,5},{2,6},{3,7},{4,0},{5,1},{6,2},{7,3},{8,12},{9,13},{10,... | collective-permute-start | bytes 245768 | tf_op jit(solution)/shard_map/ppermute | solution.py:26
  142.3 0.7 own_rows.1
  143.3 2.8 %collective-permute-done.32 = bf16[320,128]{1,0:T(8,128)(2,1)S(1)} collective-permute-done((bf16[320,128]{1,0:T(8,128)(2,1)S(1)}, bf16[320,128]{1,0:T(8,128)(2,1)S(1)}, u32[]{:S(2)}, u32[]{:S(2)}) %collective-permute-start.32) | collective-permute-done | bytes 81952 | tf_op jit(solution)/shard_map/ppermute | solution.py:26
  146.3 0.7 fusion.6
  (74 shorter events, 6.4 us)
Async XLA Ops:
  5.4 27.1 %collective-permute-start.1 = (bf16[2,320,256]{2,1,0:T(8,128)(2,1)}, bf16[2,320,256]{2,1,0:T(8,128)(2,1)}, u32[]{:S(2)}, u32[]{:S(2)}) collective-permute-start(bf16[2,320,256]{2,1,0:T(8,128)(2,1)} %get-tuple-element.65), channel_id=1, source_target_pairs={{0,8},{1,9},{2,10},{3,11},{4,12},{5,13},{6,14},{7,15},{8,0},{9,1},... | collective-permute-start | bytes 983048 | tf_op jit(solution)/shard_map/ppermute | solution.py:463
  9.5 29.2 %collective-permute-start.6 = (bf16[2,320,256]{2,1,0:T(8,128)(2,1)}, bf16[2,320,256]{2,1,0:T(8,128)(2,1)}, u32[]{:S(2)}, u32[]{:S(2)}) collective-permute-start(bf16[2,320,256]{2,1,0:T(8,128)(2,1)} %get-tuple-element.76), channel_id=1, source_target_pairs={{0,8},{1,9},{2,10},{3,11},{4,12},{5,13},{6,14},{7,15},{8,0},{9,1},... | collective-permute-start | bytes 983048 | tf_op jit(solution)/shard_map/ppermute | solution.py:463
  9.6 24.2 %collective-permute-start = (bf16[160,1280]{1,0:T(8,128)(2,1)}, bf16[160,1280]{1,0:T(8,128)(2,1)}, u32[]{:S(2)}, u32[]{:S(2)}) collective-permute-start(bf16[160,1280]{1,0:T(8,128)(2,1)} %get-tuple-element.62), channel_id=1, source_target_pairs={{0,2},{1,3},{2,0},{3,1},{4,6},{5,7},{6,4},{7,5},{8,10},{9,11},{10,... | collective-permute-start | bytes 1228808 | tf_op jit(solution)/shard_map/ppermute | solution.py:26
  11.4 27.4 %collective-permute-start.3 = (bf16[160,1280]{1,0:T(8,128)(2,1)}, bf16[160,1280]{1,0:T(8,128)(2,1)}, u32[]{:S(2)}, u32[]{:S(2)}) collective-permute-start(bf16[160,1280]{1,0:T(8,128)(2,1)} %get-tuple-element.74), channel_id=1, source_target_pairs={{0,4},{1,5},{2,6},{3,7},{4,0},{5,1},{6,2},{7,3},{8,12},{9,13},{10,... | collective-permute-start | bytes 1228808 | tf_op jit(solution)/shard_map/ppermute | solution.py:26
  13.0 30.8 %collective-permute-start.4 = (bf16[160,1280]{1,0:T(8,128)(2,1)}, bf16[160,1280]{1,0:T(8,128)(2,1)}, u32[]{:S(2)}, u32[]{:S(2)}) collective-permute-start(bf16[160,1280]{1,0:T(8,128)(2,1)} %get-tuple-element.75), channel_id=1, source_target_pairs={{0,6},{1,7},{2,4},{3,5},{4,2},{5,3},{6,0},{7,1},{8,14},{9,15},{10,... | collective-permute-start | bytes 1228808 | tf_op jit(solution)/shard_map/ppermute | solution.py:26
  14.0 5.2 %copy-start.4 = (s32[2,2]{1,0:T(2,128)S(1)}, s32[2,2]{1,0:T(2,128)}, u32[]{:S(2)}) copy-start(s32[2,2]{1,0:T(2,128)} %param.15) | copy-start | bytes 52
  14.0 20.2 %copy-start.3 = (s32[4]{0:T(128)S(1)}, s32[4]{0:T(128)}, u32[]{:S(2)}) copy-start(s32[4]{0:T(128)} %pad_add_fusion.place_ref) | copy-start | bytes 52
  32.5 11.2 %collective-permute-start.5 = (bf16[2,320,256]{2,1,0:T(8,128)(2,1)}, bf16[2,320,256]{2,1,0:T(8,128)(2,1)}, u32[]{:S(2)}, u32[]{:S(2)}) collective-permute-start(bf16[2,320,256]{2,1,0:T(8,128)(2,1)} %collective-permute-done.1.refs_8_), channel_id=1, source_target_pairs={{0,16},{16,0},{1,17},{17,1},{2,18},{18,2},{3,19},{19,3},{4,20},{20... | collective-permute-start | bytes 983048 | tf_op jit(solution)/shard_map/ppermute | solution.py:26
  33.8 12.6 %collective-permute-start.2 = (bf16[4,320,256]{2,1,0:T(8,128)(2,1)}, bf16[4,320,256]{2,1,0:T(8,128)(2,1)S(1)}, u32[]{:S(2)}, u32[]{:S(2)}) collective-permute-start(bf16[4,320,256]{2,1,0:T(8,128)(2,1)} %get-tuple-element.71), channel_id=1, source_target_pairs={{0,1},{1,0},{2,3},{3,2},{4,5},{5,4},{6,7},{7,6},{8,9},{9,8},{10,11... | collective-permute-start | bytes 1966088 | tf_op jit(solution)/shard_map/ppermute | solution.py:26
  34.2 1.3 copy-start.1
  35.6 1.0 copy-start.2
  38.7 5.6 %collective-permute-start.7 = (bf16[160,1280]{1,0:T(8,128)(2,1)S(1)}, bf16[160,1280]{1,0:T(8,128)(2,1)S(1)}, u32[]{:S(2)}, u32[]{:S(2)}) collective-permute-start(bf16[160,1280]{1,0:T(8,128)(2,1)S(1)} %copy-done.2), channel_id=1, source_target_pairs={{0,1},{1,0},{2,3},{3,2},{4,5},{5,4},{6,7},{7,6},{8,9},{9,8},{10,11... | collective-permute-start | bytes 1228808 | tf_op jit(solution)/shard_map/ppermute | solution.py:26
  38.7 7.7 %collective-permute-start.8 = (bf16[160,1280]{1,0:T(8,128)(2,1)}, bf16[160,1280]{1,0:T(8,128)(2,1)S(1)}, u32[]{:S(2)}, u32[]{:S(2)}) collective-permute-start(bf16[160,1280]{1,0:T(8,128)(2,1)} %collective-permute-done.refs_1_), channel_id=1, source_target_pairs={{0,1},{1,0},{2,3},{3,2},{4,5},{5,4},{6,7},{7,6},{8,9},{9,8},{10,11... | collective-permute-start | bytes 1228808 | tf_op jit(solution)/shard_map/ppermute | solution.py:26
  43.8 2.7 %collective-permute-start.9 = (bf16[160,1280]{1,0:T(8,128)(2,1)}, bf16[160,1280]{1,0:T(8,128)(2,1)S(1)}, u32[]{:S(2)}, u32[]{:S(2)}) collective-permute-start(bf16[160,1280]{1,0:T(8,128)(2,1)} %collective-permute-done.3.refs_2_), channel_id=1, source_target_pairs={{0,1},{1,0},{2,3},{3,2},{4,5},{5,4},{6,7},{7,6},{8,9},{9,8},{10,11... | collective-permute-start | bytes 1228808 | tf_op jit(solution)/shard_map/ppermute | solution.py:26
  43.8 2.7 %collective-permute-start.10 = (bf16[160,1280]{1,0:T(8,128)(2,1)}, bf16[160,1280]{1,0:T(8,128)(2,1)S(1)}, u32[]{:S(2)}, u32[]{:S(2)}) collective-permute-start(bf16[160,1280]{1,0:T(8,128)(2,1)} %collective-permute-done.4.refs_3_), channel_id=1, source_target_pairs={{0,1},{1,0},{2,3},{3,2},{4,5},{5,4},{6,7},{7,6},{8,9},{9,8},{10,11... | collective-permute-start | bytes 1228808 | tf_op jit(solution)/shard_map/ppermute | solution.py:26
  44.4 10.2 %collective-permute-start.13 = (bf16[2,320,256]{2,1,0:T(8,128)(2,1)}, bf16[2,320,256]{2,1,0:T(8,128)(2,1)S(1)}, u32[]{:S(2)}, u32[]{:S(2)}) collective-permute-start(bf16[2,320,256]{2,1,0:T(8,128)(2,1)} %collective-permute-done.6.refs_8_), channel_id=1, source_target_pairs={{0,16},{16,0},{1,17},{17,1},{2,18},{18,2},{3,19},{19,3},{4,20},{20... | collective-permute-start | bytes 983048 | tf_op jit(solution)/shard_map/ppermute | solution.py:26
  49.6 16.8 %collective-permute-start.11 = (bf16[1024,256]{1,0:T(8,128)(2,1)S(1)}, bf16[1024,256]{1,0:T(8,128)(2,1)S(1)}, u32[]{:S(2)}, u32[]{:S(2)}) collective-permute-start(bf16[1024,256]{1,0:T(8,128)(2,1)S(1)} %get-tuple-element.92), channel_id=1, source_target_pairs={{0,2},{1,3},{2,0},{3,1},{4,6},{5,7},{6,4},{7,5},{8,10},{9,11},{10,... | collective-permute-start | bytes 1572872 | tf_op jit(solution)/shard_map/ppermute | solution.py:26
  51.2 15.3 %collective-permute-start.12 = (bf16[1024,256]{1,0:T(8,128)(2,1)S(1)}, bf16[1024,256]{1,0:T(8,128)(2,1)S(1)}, u32[]{:S(2)}, u32[]{:S(2)}) collective-permute-start(bf16[1024,256]{1,0:T(8,128)(2,1)S(1)} %get-tuple-element.93), channel_id=1, source_target_pairs={{0,4},{1,5},{2,6},{3,7},{4,0},{5,1},{6,2},{7,3},{8,12},{9,13},{10,... | collective-permute-start | bytes 1572872 | tf_op jit(solution)/shard_map/ppermute | solution.py:26
  57.6 21.9 %collective-permute-start.14 = (bf16[1024,256]{1,0:T(8,128)(2,1)S(1)}, bf16[1024,256]{1,0:T(8,128)(2,1)S(1)}, u32[]{:S(2)}, u32[]{:S(2)}) collective-permute-start(bf16[1024,256]{1,0:T(8,128)(2,1)S(1)} %get-tuple-element.95), channel_id=1, source_target_pairs={{0,6},{1,7},{2,4},{3,5},{4,2},{5,3},{6,0},{7,1},{8,14},{9,15},{10,... | collective-permute-start | bytes 1572872 | tf_op jit(solution)/shard_map/ppermute | solution.py:26
  58.8 26.0 %slice-start = ((s8[6553600]{0:T(1024)(128)(4,1)}), s8[2359296]{0:T(1024)(128)(4,1)S(1)}, s32[]{:S(2)}) async-start(s8[6553600]{0:T(1024)(128)(4,1)} %bitcast.53), calls=%async_computation | async-start | bytes 4718592
  61.6 18.3 %collective-permute-start.16 = (bf16[16,128]{1,0:T(8,128)(2,1)S(1)}, bf16[16,128]{1,0:T(8,128)(2,1)S(1)}, u32[]{:S(2)}, u32[]{:S(2)}) collective-permute-start(bf16[16,128]{1,0:T(8,128)(2,1)S(1)} %get-tuple-element.100), channel_id=1, source_target_pairs={{0,8},{1,9},{2,10},{3,11},{4,12},{5,13},{6,14},{7,15},{8,0},{9,1},... | collective-permute-start | bytes 12296 | tf_op jit(solution)/shard_map/ppermute | solution.py:26
  66.3 13.6 %collective-permute-start.15 = (bf16[128,640]{1,0:T(8,128)(2,1)S(1)}, bf16[128,640]{1,0:T(8,128)(2,1)S(1)}, u32[]{:S(2)}, u32[]{:S(2)}) collective-permute-start(bf16[128,640]{1,0:T(8,128)(2,1)S(1)} %get-tuple-element.99), channel_id=1, source_target_pairs={{0,8},{1,9},{2,10},{3,11},{4,12},{5,13},{6,14},{7,15},{8,0},{9,1},... | collective-permute-start | bytes 491528 | tf_op jit(solution)/shard_map/ppermute | solution.py:26
  66.5 18.3 %slice-start.1 = ((s8[6553600]{0:T(1024)(128)(4,1)}), s8[4194304]{0:T(1024)(128)(4,1)S(1)}, s32[]{:S(2)}) async-start(s8[6553600]{0:T(1024)(128)(4,1)} %bitcast.53), calls=%async_computation.1 | async-start | bytes 8388608
  81.8 4.6 %collective-permute-start.18 = (bf16[16,128]{1,0:T(8,128)(2,1)S(1)}, bf16[16,128]{1,0:T(8,128)(2,1)S(1)}, u32[]{:S(2)}, u32[]{:S(2)}) collective-permute-start(bf16[16,128]{1,0:T(8,128)(2,1)S(1)} %get-tuple-element.104), channel_id=1, source_target_pairs={{0,8},{1,9},{2,10},{3,11},{4,12},{5,13},{6,14},{7,15},{8,0},{9,1},... | collective-permute-start | bytes 12296 | tf_op jit(solution)/shard_map/ppermute | solution.py:26
  84.6 9.4 %collective-permute-start.17 = (bf16[128,640]{1,0:T(8,128)(2,1)S(1)}, bf16[128,640]{1,0:T(8,128)(2,1)S(1)}, u32[]{:S(2)}, u32[]{:S(2)}) collective-permute-start(bf16[128,640]{1,0:T(8,128)(2,1)S(1)} %get-tuple-element.103), channel_id=1, source_target_pairs={{0,8},{1,9},{2,10},{3,11},{4,12},{5,13},{6,14},{7,15},{8,0},{9,1},... | collective-permute-start | bytes 491528 | tf_op jit(solution)/shard_map/ppermute | solution.py:26
  95.9 16.3 %copy-start = (bf16[2560,640]{1,0:T(8,128)(2,1)S(1)}, bf16[2560,640]{1,0:T(8,128)(2,1)}, u32[]{:S(2)}) copy-start(bf16[2560,640]{1,0:T(8,128)(2,1)} %get-tuple-element.124.weight_ref) | copy-start | bytes 9830404
  95.9 1.7 %collective-permute-start.19 = (bf16[64,2560]{1,0:T(8,128)(2,1)S(1)}, bf16[64,2560]{1,0:T(8,128)(2,1)S(1)}, u32[]{:S(2)}, u32[]{:S(2)}) collective-permute-start(bf16[64,2560]{1,0:T(8,128)(2,1)S(1)} %get-tuple-element.106), channel_id=1, source_target_pairs={{0,1},{1,0},{2,3},{3,2},{4,5},{5,4},{6,7},{7,6},{8,9},{9,8},{10,11... | collective-permute-start | bytes 983048 | tf_op jit(solution)/shard_map/ppermute | solution.py:26
  97.7 6.3 %collective-permute-start.20 = (bf16[64,1280]{1,0:T(8,128)(2,1)S(1)}, bf16[64,1280]{1,0:T(8,128)(2,1)S(1)}, u32[]{:S(2)}, u32[]{:S(2)}) collective-permute-start(bf16[64,1280]{1,0:T(8,128)(2,1)S(1)} %get-tuple-element.140), channel_id=1, source_target_pairs={{0,2},{1,3},{2,0},{3,1},{4,6},{5,7},{6,4},{7,5},{8,10},{9,11},{10,... | collective-permute-start | bytes 491528 | tf_op jit(solution)/shard_map/ppermute | solution.py:26
  98.6 6.0 %collective-permute-start.22 = (bf16[64,1280]{1,0:T(8,128)(2,1)S(1)}, bf16[64,1280]{1,0:T(8,128)(2,1)S(1)}, u32[]{:S(2)}, u32[]{:S(2)}) collective-permute-start(bf16[64,1280]{1,0:T(8,128)(2,1)S(1)} %get-tuple-element.141), channel_id=1, source_target_pairs={{0,4},{1,5},{2,6},{3,7},{4,0},{5,1},{6,2},{7,3},{8,12},{9,13},{10,... | collective-permute-start | bytes 491528 | tf_op jit(solution)/shard_map/ppermute | solution.py:26
  104.6 5.4 %collective-permute-start.21 = (bf16[64,1280]{1,0:T(8,128)(2,1)S(1)}, bf16[64,1280]{1,0:T(8,128)(2,1)S(1)}, u32[]{:S(2)}, u32[]{:S(2)}) collective-permute-start(bf16[64,1280]{1,0:T(8,128)(2,1)S(1)} %get-tuple-element.138), channel_id=1, source_target_pairs={{0,4},{1,5},{2,6},{3,7},{4,0},{5,1},{6,2},{7,3},{8,12},{9,13},{10,... | collective-permute-start | bytes 491528 | tf_op jit(solution)/shard_map/ppermute | solution.py:26
  105.0 5.3 %collective-permute-start.23 = (bf16[64,1280]{1,0:T(8,128)(2,1)S(1)}, bf16[64,1280]{1,0:T(8,128)(2,1)S(1)}, u32[]{:S(2)}, u32[]{:S(2)}) collective-permute-start(bf16[64,1280]{1,0:T(8,128)(2,1)S(1)} %get-tuple-element.139), channel_id=1, source_target_pairs={{0,2},{1,3},{2,0},{3,1},{4,6},{5,7},{6,4},{7,5},{8,10},{9,11},{10,... | collective-permute-start | bytes 491528 | tf_op jit(solution)/shard_map/ppermute | solution.py:26
  110.4 1.7 %collective-permute-start.24 = (bf16[64,2560]{1,0:T(8,128)(2,1)S(1)}, bf16[64,2560]{1,0:T(8,128)(2,1)S(1)}, u32[]{:S(2)}, u32[]{:S(2)}) collective-permute-start(bf16[64,2560]{1,0:T(8,128)(2,1)S(1)} %add_convert_fusion.ours_ref), channel_id=1, source_target_pairs={{0,1},{1,0},{2,3},{3,2},{4,5},{5,4},{6,7},{7,6},{8,9},{9,8},{10,11... | collective-permute-start | bytes 983048 | tf_op jit(solution)/shard_map/ppermute | solution.py:26
  113.4 10.9 %collective-permute-start.25 = (bf16[128,640]{1,0:T(8,128)(2,1)S(1)}, bf16[128,640]{1,0:T(8,128)(2,1)S(1)}, u32[]{:S(2)}, u32[]{:S(2)}) collective-permute-start(bf16[128,640]{1,0:T(8,128)(2,1)S(1)} %get-tuple-element.109), channel_id=1, source_target_pairs={{0,8},{1,9},{2,10},{3,11},{4,12},{5,13},{6,14},{7,15},{8,0},{9,1},... | collective-permute-start | bytes 491528 | tf_op jit(solution)/shard_map/ppermute | solution.py:26
  115.1 9.2 %collective-permute-start.26 = (bf16[16,128]{1,0:T(8,128)(2,1)S(1)}, bf16[16,128]{1,0:T(8,128)(2,1)S(1)}, u32[]{:S(2)}, u32[]{:S(2)}) collective-permute-start(bf16[16,128]{1,0:T(8,128)(2,1)S(1)} %get-tuple-element.110), channel_id=1, source_target_pairs={{0,8},{1,9},{2,10},{3,11},{4,12},{5,13},{6,14},{7,15},{8,0},{9,1},... | collective-permute-start | bytes 12296 | tf_op jit(solution)/shard_map/ppermute | solution.py:26
  126.2 9.0 %collective-permute-start.27 = (bf16[128,640]{1,0:T(8,128)(2,1)S(1)}, bf16[128,640]{1,0:T(8,128)(2,1)S(1)}, u32[]{:S(2)}, u32[]{:S(2)}) collective-permute-start(bf16[128,640]{1,0:T(8,128)(2,1)S(1)} %get-tuple-element.113), channel_id=1, source_target_pairs={{0,8},{1,9},{2,10},{3,11},{4,12},{5,13},{6,14},{7,15},{8,0},{9,1},... | collective-permute-start | bytes 491528 | tf_op jit(solution)/shard_map/ppermute | solution.py:26
  126.3 8.9 %collective-permute-start.28 = (bf16[16,128]{1,0:T(8,128)(2,1)S(1)}, bf16[16,128]{1,0:T(8,128)(2,1)S(1)}, u32[]{:S(2)}, u32[]{:S(2)}) collective-permute-start(bf16[16,128]{1,0:T(8,128)(2,1)S(1)} %get-tuple-element.114), channel_id=1, source_target_pairs={{0,8},{1,9},{2,10},{3,11},{4,12},{5,13},{6,14},{7,15},{8,0},{9,1},... | collective-permute-start | bytes 12296 | tf_op jit(solution)/shard_map/ppermute | solution.py:26
  137.0 1.7 %collective-permute-start.29 = (bf16[4,320,128]{2,1,0:T(8,128)(2,1)S(1)}, bf16[4,320,128]{2,1,0:T(8,128)(2,1)S(1)}, u32[]{:S(2)}, u32[]{:S(2)}) collective-permute-start(bf16[4,320,128]{2,1,0:T(8,128)(2,1)S(1)} %get-tuple-element.116), channel_id=1, source_target_pairs={{0,1},{1,0},{2,3},{3,2},{4,5},{5,4},{6,7},{7,6},{8,9},{9,8},{10,11... | collective-permute-start | bytes 983048 | tf_op jit(solution)/shard_map/ppermute | solution.py:26
  138.8 4.6 %collective-permute-start.30 = (bf16[320,128]{1,0:T(8,128)(2,1)S(1)}, bf16[320,128]{1,0:T(8,128)(2,1)S(1)}, u32[]{:S(2)}, u32[]{:S(2)}) collective-permute-start(bf16[320,128]{1,0:T(8,128)(2,1)S(1)} %get-tuple-element.135), channel_id=1, source_target_pairs={{0,2},{1,3},{2,0},{3,1},{4,6},{5,7},{6,4},{7,5},{8,10},{9,11},{10,... | collective-permute-start | bytes 245768 | tf_op jit(solution)/shard_map/ppermute | solution.py:26
  140.2 6.0 %collective-permute-start.32 = (bf16[320,128]{1,0:T(8,128)(2,1)S(1)}, bf16[320,128]{1,0:T(8,128)(2,1)S(1)}, u32[]{:S(2)}, u32[]{:S(2)}) collective-permute-start(bf16[320,128]{1,0:T(8,128)(2,1)S(1)} %get-tuple-element.136), channel_id=1, source_target_pairs={{0,6},{1,7},{2,4},{3,5},{4,2},{5,3},{6,0},{7,1},{8,14},{9,15},{10,... | collective-permute-start | bytes 245768 | tf_op jit(solution)/shard_map/ppermute | solution.py:26
  140.2 6.1 %collective-permute-start.31 = (bf16[320,128]{1,0:T(8,128)(2,1)S(1)}, bf16[320,128]{1,0:T(8,128)(2,1)S(1)}, u32[]{:S(2)}, u32[]{:S(2)}) collective-permute-start(bf16[320,128]{1,0:T(8,128)(2,1)S(1)} %get-tuple-element.137), channel_id=1, source_target_pairs={{0,4},{1,5},{2,6},{3,7},{4,0},{5,1},{6,2},{7,3},{8,12},{9,13},{10,... | collective-permute-start | bytes 245768 | tf_op jit(solution)/shard_map/ppermute | solution.py:26

commit v8 on v7

--- a/solution.py
+++ b/solution.py
@@ -13,12 +13,15 @@
 QBLK = 64
 CAP = 30.0
 EPSILON = 1e-05
+LOG2_E = 1.4426950408889634
 BF16 = jnp.bfloat16
 F32 = jnp.float32
 
 CHIPS = KVH // 2
-ROUNDS = ((1, 2), (3, 0))
+ROUNDS = ((2, 1), (3, 0))
 PROJECT_COST = 8
+BAND = 32
+HEADS_AT_ONCE = (2, 2)
 
 
 def swapped(value, mask, axis="row"):
@@ -53,46 +56,53 @@
     pair, heads, blocks, width, place_ref, weight_any, hidden_any, gain_any, extra_any, *refs
 ):
     weight_ref, hidden_ref, gain_ref, extra_ref, normed, sems = refs[-6:]
-    head_refs, out_refs = refs[: len(heads)], refs[len(heads) : -6]
+    results = len(heads) + len(blocks)
+    targets, refs = refs[:results], refs[results:-6]
     place_now = [place_ref[number] for number in range(4)]
     rows = hidden_ref.shape[0]
     lanes = extra_ref.shape[1]
-    more = out_refs[0].shape[0] - rows
+    bands = [slice(band, band + BAND) for band in range(0, rows, BAND)]
+    pairs = [(weight_any, weight_ref), (gain_any, gain_ref), (extra_any, extra_ref)]
+    pairs += [(hidden_any.at[band], hidden_ref.at[band]) for band in bands]
     copies = [
         pltpu.make_async_copy(source, target, sems.at[number])
-        for number, (source, target) in enumerate(
-            (
-                (weight_any, weight_ref),
-                (hidden_any, hidden_ref),
-                (gain_any, gain_ref),
-                (extra_any, extra_ref),
-            )
-        )
+        for number, (source, target) in enumerate(pairs)
+    ]
+    outs = [
+        pltpu.make_async_copy(source, target, sems.at[len(copies) + number])
+        for number, (source, target) in enumerate(zip(refs, targets))
     ]
     for copy in copies:
         copy.start()
     copies[0].wait()
-    for head_ref, group in zip(head_refs, heads):
+    for head_ref, group, out in zip(refs, heads, outs):
         for number, head in enumerate(group):
             column = pl.multiple_of(head(*place_now) * pair, pair)
             head_ref[number] = weight_ref[:, pl.ds(column, pair)]
-    for copy in copies[1:]:
+        out.start()
+    copies[1].wait()
+    copies[2].wait()
+    for band, copy in zip(bands, copies[3:]):
         copy.wait()
-    hidden = hidden_ref[...].astype(F32)
-    inverse = lax.rsqrt(jnp.mean(hidden * hidden, axis=1, keepdims=True) + EPSILON)
-    normed[...] = (hidden * inverse * gain_ref[...]).astype(BF16)
-    for out_ref, group in zip(out_refs, blocks):
+        hidden = hidden_ref[band, :].astype(F32)
+        inverse = lax.rsqrt(jnp.mean(hidden * hidden, axis=1, keepdims=True) + EPSILON)
+        normed[band, :] = (hidden * inverse * gain_ref[...]).astype(BF16)
+    for out_ref, group, out in zip(refs[len(heads) :], blocks, outs[len(heads) :]):
         for number, block in enumerate(group):
             start = pl.multiple_of(block(*place_now) * width, 128)
             out_ref[:rows, number * width : (number + 1) * width] = normed[:, pl.ds(start, width)]
-        for block in range(out_ref.shape[1] // lanes):
+        more = out_ref.shape[0] - rows
+        for block in range(out_ref.shape[1] // lanes if more else 0):
             out_ref[rows:, block * lanes : (block + 1) * lanes] = extra_ref[
                 block * more : (block + 1) * more, :
             ]
+        out.start()
+    for out in outs:
+        out.wait()
 
 
 def in_kernels(unit, rows):
-    return unit % 64 == 0 and rows % 16 == 0
+    return unit % 64 == 0 and rows % BAND == 0
 
 
 def prepared(weight, head_groups, pair, hidden, gain, groups, width, extra, place_now, kernels):
@@ -117,55 +127,55 @@
             ]
             rest = extra.reshape(more, total_width)
             results.append(jnp.concatenate([jnp.concatenate(blocks, axis=1), rest], axis=0))
+        results[-1] = results[-1][:rows]
         return columns, results
     counts = [len(group) for group in head_groups]
-    vmem = pl.BlockSpec(memory_space=pltpu.VMEM)
-    smem = pl.BlockSpec(memory_space=pltpu.SMEM)
+    shapes = [(count, weight.shape[0], pair) for count in counts]
+    shapes += [(rows + more, total_width)] * (len(groups) - 1) + [(rows, total_width)]
     results = pl.pallas_call(
         functools.partial(prepare_kernel, pair, head_groups, groups, width),
-        out_shape=[jax.ShapeDtypeStruct((count, weight.shape[0], pair), BF16) for count in counts]
-        + [jax.ShapeDtypeStruct((rows + more, total_width), BF16) for group in groups],
-        in_specs=[smem] + [pl.BlockSpec(memory_space=pltpu.HBM)] * 4,
-        out_specs=[vmem] * (len(counts) + len(groups)),
-        scratch_shapes=[
+        out_shape=[jax.ShapeDtypeStruct(shape, BF16) for shape in shapes],
+        in_specs=[pl.BlockSpec(memory_space=pltpu.SMEM)]
+        + [pl.BlockSpec(memory_space=pltpu.HBM)] * 4,
+        out_specs=[pl.BlockSpec(memory_space=pl.ANY)] * len(shapes),
+        scratch_shapes=[pltpu.VMEM(shape, BF16) for shape in shapes]
+        + [
             pltpu.VMEM(weight.shape, BF16),
             pltpu.VMEM((rows, depth), BF16),
             pltpu.VMEM((1, depth), F32),
             pltpu.VMEM(extra.shape, BF16),
             pltpu.VMEM((rows, depth), BF16),
-            pltpu.SemaphoreType.DMA((4,)),
+            pltpu.SemaphoreType.DMA((3 + rows // BAND + len(shapes),)),
         ],
         compiler_params=pltpu.CompilerParams(vmem_limit_bytes=60 * 1024 * 1024),
         name="prepare",
-    )(
-        place_now,
-        weight,
-        hidden,
-        gain[None, :],
-        extra,
-    )
+    )(place_now, weight, hidden, gain[None, :], extra)
     return results[: len(counts)], results[len(counts) :]
 
 
-def stage_kernel(pair, heads, place_ref, weight_ref, tokens_ref, kept_ref, own_ref):
+def stage_kernel(pair, groups, place_ref, weight_ref, tokens_ref, *refs):
     place_now = [place_ref[number] for number in range(4)]
-    for number, head in enumerate(heads):
-        column = pl.multiple_of(head(*place_now) * pair, pair)
-        kept_ref[number] = weight_ref[:, pl.ds(column, pair)]
-    own_ref[...] = tokens_ref[: own_ref.shape[0], :]
-
-
-def staged(weight, heads, pair, tokens, place_now, kernels):
+    for out_ref, heads in zip(refs, groups):
+        for number, head in enumerate(heads):
+            column = pl.multiple_of(head(*place_now) * pair, pair)
+            out_ref[number] = weight_ref[:, pl.ds(column, pair)]
+    refs[-1][...] = tokens_ref[...]
+
+
+def staged(weight, groups, pair, tokens, place_now, kernels):
     if not kernels:
         now = [place_now[number] for number in range(4)]
-        columns = [lax.dynamic_slice_in_dim(weight, head(*now) * pair, pair, 1) for head in heads]
-        return jnp.stack(columns), tokens
+        return [
+            jnp.stack(
+                [lax.dynamic_slice_in_dim(weight, head(*now) * pair, pair, 1) for head in heads]
+            )
+            for heads in groups
+        ] + [tokens]
     shapes = [
-        jax.ShapeDtypeStruct((len(heads), weight.shape[0], pair), BF16),
-        jax.ShapeDtypeStruct(tokens.shape, BF16),
-    ]
+        jax.ShapeDtypeStruct((len(heads), weight.shape[0], pair), BF16) for heads in groups
+    ] + [jax.ShapeDtypeStruct(tokens.shape, BF16)]
     return call(
-        functools.partial(stage_kernel, pair, heads),
+        functools.partial(stage_kernel, pair, groups),
         "stage",
         shapes,
         [place_now],
@@ -173,7 +183,7 @@
     )
 
 
-def project_kernel(rows, heads, start, first_ref, kept_ref, traded_ref, *refs):
+def project_kernel(rows, heads, start, place, first_ref, kept_ref, traded_ref, *refs):
     token_refs, refs = refs[: 2 * CHIPS], refs[2 * CHIPS :]
     weight = refs[-1]
     out_refs = refs[-1 - heads : -1]
@@ -189,7 +199,7 @@
         put(head, 0, 0, kept_ref[start + head])
         put(head, 0, 1, traded_ref[start + head])
         for number, block_ref in enumerate(blocks):
-            put(head, 1 + number // 2, number % 2, block_ref[head])
+            put(head, 1 + number // 2, number % 2, block_ref[place + head])
     for number, token_ref in enumerate(token_refs):
         span = slice(number * rows, (number + 1) * rows)
         result = jnp.dot(token_ref[:rows, :], weight[...], preferred_element_type=F32).astype(BF16)
@@ -197,13 +207,14 @@
             out_ref[span, :] = result[:, head * pair : (head + 1) * pair]
 
 
-def projected(tokens, heads, kept, traded, start, firsts, blocks, rows, kernels):
+def projected(tokens, heads, kept, traded, start, place, firsts, blocks, rows, kernels):
     unit, pair = kept.shape[1:]
     depth = tokens[0].shape[1]
     count = len(tokens) * rows
     firsts = jnp.stack(firsts).astype(jnp.int32)
     if not kernels:
-        pieces = [kept[start : start + heads], traded[start : start + heads]] + blocks
+        pieces = [kept[start : start + heads], traded[start : start + heads]]
+        pieces += [block[place : place + heads] for block in blocks]
         ordered = []
         for tile in range(len(pieces) // 2):
             one, two = pieces[2 * tile : 2 * tile + 2]
@@ -217,7 +228,7 @@
     smem = pl.BlockSpec(memory_space=pltpu.SMEM)
     return list(
         pl.pallas_call(
-            functools.partial(project_kernel, rows, heads, start),
+            functools.partial(project_kernel, rows, heads, start, place),
             out_shape=[jax.ShapeDtypeStruct((count, pair), BF16)] * heads,
             in_specs=[smem] + [vmem] * (2 + len(tokens) + len(blocks)),
             out_specs=[vmem] * heads,
@@ -329,8 +340,9 @@
         span = slice(head * HD, (head + 1) * HD)
         scores = lax.dot_general(
             queries[:, span], keys, (((1,), (1,)), ((), ())), preferred_element_type=F32
-        ) * HD ** (-0.5)
-        weights = jnp.where(visible, jnp.exp(CAP * jnp.tanh(scores / CAP)), 0.0)
+        )
+        capped = jnp.tanh(scores * (HD ** (-0.5) / CAP))
+        weights = jnp.where(visible, jnp.exp2(capped * (CAP * LOG2_E)), 0.0)
         totals = jnp.where(lane == head, jnp.sum(weights, axis=1, keepdims=True), totals)
         weighted = jnp.dot(weights.astype(BF16), values, preferred_element_type=F32)
         out_ref[:, span] = weighted
@@ -437,10 +449,9 @@
 
     kernels = in_kernels(unit, rows)
     width = 2 * unit
-    pieces, features = prepared(
+    sent, features = prepared(
         kv_weight,
-        [[sent_head(place) for place in round_] for round_ in ROUNDS]
-        + [[other_head(place) for place in order]],
+        [[sent_head(place) for place in round_] for round_ in ROUNDS],
         pair,
         hidden,
         kv_gain,
@@ -450,8 +461,6 @@
         place_now,
         kernels,
     )
-    sent, traded = pieces[:-1], pieces[-1]
-
     def to_tile(value, j, flip):
         if not share:
             return swapped(value, j * KVH)
@@ -465,8 +474,17 @@
     far = [[to_tile(value, j, True) for j in range(1, tile_count)] for value in sent]
     held = [features[0]] + [swapped(features[p], 2 * p) for p in range(1, CHIPS)]
 
-    traded, held[1] = lax.optimization_barrier((traded, held[1]))
+    kv_weight, own, _ = lax.optimization_barrier((kv_weight, held[0], far[0]))
+    kept, traded, own = staged(
+        kv_weight,
+        [[kept_head(place) for place in order], [other_head(place) for place in order]],
+        pair,
+        own,
+        place_now,
+        kernels,
+    )
     traded = swapped(traded, 1)
+    held[1], kept, own = lax.optimization_barrier((held[1], kept, own))
 
     def shared(number):
         start = sum(len(round_) for round_ in ROUNDS[:number])
@@ -478,26 +496,34 @@
         ]
 
     firsts = [core] + [core ^ part] * (tile_count - 1)
-    kv_weight, own, _ = lax.optimization_barrier((kv_weight, held[0], far[0]))
-    kept, own = staged(
-        kv_weight, [kept_head(place) for place in order], pair, own, place_now, kernels
-    )
-    held[1], kept, own = lax.optimization_barrier((held[1], kept, own))
     halves = [shared(number) for number in range(len(ROUNDS))]
     held[2], held[3], halves[0], far = lax.optimization_barrier((held[2], held[3], halves[0], far))
     tokens = held + [swapped(piece, 1) for piece in held]
     tokens[0] = own
+    last_rows = swapped(held[2][rows:], 2)
     total = None
     done = 0
     for number, round_ in enumerate(ROUNDS):
         blocks = [piece for pair_ in zip(far[number], halves[number]) for piece in pair_]
-        partials = projected(
-            tokens, len(round_), kept, traded, done, firsts, blocks, rows, kernels
-        )
+        partials = []
+        for inner in range(0, len(round_), HEADS_AT_ONCE[number]):
+            partials += projected(
+                tokens,
+                HEADS_AT_ONCE[number],
+                kept,
+                traded,
+                done + inner,
+                inner,
+                firsts,
+                blocks,
+                rows,
+                kernels,
+            )
         done += len(round_)
         if number == 0:
-            partials, tokens = lax.optimization_barrier((partials, tokens))
-            results = meanwhile(tokens)
+            partials, tokens, last_rows = lax.optimization_barrier((partials, tokens, last_rows))
+            query_rows = tokens[: CHIPS - 1] + [last_rows] + tokens[CHIPS:-1] + [swapped(last_rows, 1)]
+            results = meanwhile(query_rows)
         for partial, place in zip(partials, round_):
             if place:
                 partial = swapped(partial, 2 * place)

time: 147 us -> 146 us (level)
    ppermute x31 -> x33, starting transfers between devices: 30.9 us -> 29.2 us  [swapped(): return lax.ppermute(value, axis, pairs)]
    ppermute x31 -> x33, waiting for transfers between devices: 61.3 us -> 60.6 us  [swapped(): return lax.ppermute(value, axis, pairs)]
  transfers between devices with their start and end apart: 33 -> 35, of which waited for: 19 -> 21; matrix products, arithmetic and copies ran while one was open for 6% -> 6% of each run, Pallas kernels for 7% -> 7%
where the time goes in v8:
time: 146 us; the launch traced here: 145 us
  waiting for transfers between devices  75.4 us (52%)
  starting transfers between devices  33.7 us (23%)
  Pallas kernels  22.9 us (16%)
  local copies, waits for them, and re-layouts  10.8 us (7%)
  other arithmetic  2.27 us (2%)
    ppermute x33, waiting for transfers between devices, swapped(): return lax.ppermute(value, axis, pairs)  60.6 us
    ppermute x33, starting transfers between devices, swapped(): return lax.ppermute(value, axis, pairs)  29.2 us
    ppermute x2, waiting for transfers between devices, to_tile(): return lax.ppermute(value, ('groups', 'row'), pairs)  14.8 us
    pallas_call x8, Pallas kernels, call(): pl.pallas_call(kernel, out_shape=out_shape, in_specs=[smem] * len(scalars...  12.7 us
    pallas_call x2, Pallas kernels, projected(): pl.pallas_call(functools.partial(project_kernel, rows, heads, start, plac...  6.02 us
    squeeze x1, local copies, waits for them, and re-layouts, query_parts(): query_weight[section, 0]  5.16 us
    ppermute x2, starting transfers between devices, to_tile(): return lax.ppermute(value, ('groups', 'row'), pairs)  4.44 us
    pallas_call x1, Pallas kernels, prepared(): pl.pallas_call(functools.partial(prepare_kernel, pair, head_groups, group...  4.19 us
  transfers between devices with their start and end apart: 35, of which 21 were waited for; matrix products, arithmetic and copies ran while one was open for 6% of the time, Pallas kernels for 7%

profile of v8, /device:TPU:0, one launch (start us, length us, event | category | flops | bytes accessed | tf_op | source)
XLA Modules:
  0.0 145.4 jit_solution(14352673394708900758)
XLA Ops:
  0.6 4.2 %prepare.1 = (bf16[2,320,256]{2,1,0:T(8,128)(2,1)}, bf16[2,320,256]{2,1,0:T(8,128)(2,1)}, bf16[160,1280]{1,0:T(8,128)(2,1)}, bf16[160,1280]{1,0:T(8,128)(2,1)}, ...) custom-call(s32[4]{0:T(128)} %pad_add_fusion.place_ref, bf16[320,2048]{1,0:T(8,128)(2,1)} %weight_ref, ...), custom_call_target="tpu_custom_call" | custom-call | tf_op jit(solution)/shard_map/prepare/pallas_call | solution.py:135
  4.8 4.1 %collective-permute-start.1 = (bf16[2,320,256]{2,1,0:T(8,128)(2,1)}, bf16[2,320,256]{2,1,0:T(8,128)(2,1)}, u32[]{:S(2)}, u32[]{:S(2)}) collective-permute-start(bf16[2,320,256]{2,1,0:T(8,128)(2,1)} %get-tuple-element.62), channel_id=1, source_target_pairs={{0,8},{1,9},{2,10},{3,11},{4,12},{5,13},{6,14},{7,15},{8,0},{9,1},... | collective-permute-start | bytes 983048 | tf_op jit(solution)/shard_map/ppermute | solution.py:472
  8.9 2.5 %collective-permute-start.4 = (bf16[128,1280]{1,0:T(8,128)(2,1)}, bf16[128,1280]{1,0:T(8,128)(2,1)}, u32[]{:S(2)}, u32[]{:S(2)}) collective-permute-start(bf16[128,1280]{1,0:T(8,128)(2,1)} %get-tuple-element.72), channel_id=1, source_target_pairs={{0,6},{1,7},{2,4},{3,5},{4,2},{5,3},{6,0},{7,1},{8,14},{9,15},{10,... | collective-permute-start | bytes 983048 | tf_op jit(solution)/shard_map/ppermute | solution.py:29
  12.5 0.9 fusion.16
  13.4 5.2 %slice_bitcast_fusion.3 = (bf16[2560,640]{1,0:T(8,128)(2,1)}, bf16[2560,640]{1,0:T(8,128)(2,1)S(1)}) fusion(bf16[2,1,2560,640]{3,2,1,0:T(8,128)(2,1)} %param.13), kind=kLoop, calls=%fused_computation.3 | loop fusion | bytes 13107200 | tf_op jit(solution)/shard_map/squeeze | solution.py:633
  19.1 6.6 %collective-permute-done.1.refs_8_ = bf16[2,320,256]{2,1,0:T(8,128)(2,1)} collective-permute-done((bf16[2,320,256]{2,1,0:T(8,128)(2,1)}, bf16[2,320,256]{2,1,0:T(8,128)(2,1)}, u32[]{:S(2)}, u32[]{:S(2)}) %collective-permute-start.1) | collective-permute-done | bytes 327712 | tf_op jit(solution)/shard_map/ppermute | solution.py:472
  26.2 1.3 copy-done.1
  27.5 1.0 copy-done.2
  29.9 8.3 %collective-permute-done.6.refs_8_ = bf16[2,320,256]{2,1,0:T(8,128)(2,1)} collective-permute-done((bf16[2,320,256]{2,1,0:T(8,128)(2,1)}, bf16[2,320,256]{2,1,0:T(8,128)(2,1)}, u32[]{:S(2)}, u32[]{:S(2)}) %collective-permute-start.6) | collective-permute-done | bytes 327712 | tf_op jit(solution)/shard_map/ppermute | solution.py:472
  38.2 2.9 %collective-permute-done.3.refs_2_ = bf16[160,1280]{1,0:T(8,128)(2,1)} collective-permute-done((bf16[160,1280]{1,0:T(8,128)(2,1)}, bf16[160,1280]{1,0:T(8,128)(2,1)}, u32[]{:S(2)}, u32[]{:S(2)}) %collective-permute-start.3) | collective-permute-done | bytes 409632 | tf_op jit(solution)/shard_map/ppermute | solution.py:29
  41.6 0.9 slice.83
  42.5 2.2 %collective-permute-start.15 = (bf16[2,320,256]{2,1,0:T(8,128)(2,1)}, bf16[2,320,256]{2,1,0:T(8,128)(2,1)S(1)}, u32[]{:S(2)}, u32[]{:S(2)}) collective-permute-start(bf16[2,320,256]{2,1,0:T(8,128)(2,1)} %collective-permute-done.6.refs_8_), channel_id=1, source_target_pairs={{0,16},{16,0},{1,17},{17,1},{2,18},{18,2},{3,19},{19,3},{4,20},{20... | collective-permute-start | bytes 983048 | tf_op jit(solution)/shard_map/ppermute | solution.py:29
  45.3 3.1 %project.2 = (bf16[1024,256]{1,0:T(8,128)(2,1)S(1)}, bf16[1024,256]{1,0:T(8,128)(2,1)S(1)}) custom-call(s32[2]{0:T(128)S(1)} %pad_add_fusion.1.first_ref, bf16[4,320,256]{2,1,0:T(8,128)(2,1)S(1)} %get-tuple-element.67.kept_ref, bf16[4,320,256]{2,1,0:T(8,128)(2,1)S(1)} %collective-permute-done.2.traded_ref, bf16[160,1280]{1,0:T(8,128)(2,1)S(1)} %get-tuple-element.80.refs_0_, ...), custom_call_target="tpu_custom_call" | custom-call | flops 10737418240 | bytes 2621440 | tf_op jit(solution)/shard_map/project/pallas_call | solution.py:230
  48.3 0.8 collective-permute-done.11.refs_3_
  49.2 0.8 collective-permute-start.13
  50.0 1.2 collective-permute-start.14
  51.2 1.6 %collective-permute-done.15.refs_9_ = bf16[2,320,256]{2,1,0:T(8,128)(2,1)S(1)} collective-permute-done((bf16[2,320,256]{2,1,0:T(8,128)(2,1)}, bf16[2,320,256]{2,1,0:T(8,128)(2,1)S(1)}, u32[]{:S(2)}, u32[]{:S(2)}) %collective-permute-start.15) | collective-permute-done | bytes 327712 | tf_op jit(solution)/shard_map/ppermute | solution.py:29
  52.8 3.0 %project.3 = (bf16[1024,256]{1,0:T(8,128)(2,1)S(1)}, bf16[1024,256]{1,0:T(8,128)(2,1)S(1)}) custom-call(s32[2]{0:T(128)S(1)} %pad_add_fusion.1.first_ref, bf16[4,320,256]{2,1,0:T(8,128)(2,1)S(1)} %get-tuple-element.67.kept_ref, bf16[4,320,256]{2,1,0:T(8,128)(2,1)S(1)} %collective-permute-done.2.traded_ref, bf16[160,1280]{1,0:T(8,128)(2,1)S(1)} %get-tuple-element.80.refs_0_, ...), custom_call_target="tpu_custom_call" | custom-call | flops 10737418240 | bytes 2621440 | tf_op jit(solution)/shard_map/project/pallas_call | solution.py:230
  55.8 1.6 %collective-permute-start.16 = (bf16[1024,256]{1,0:T(8,128)(2,1)S(1)}, bf16[1024,256]{1,0:T(8,128)(2,1)S(1)}, u32[]{:S(2)}, u32[]{:S(2)}) collective-permute-start(bf16[1024,256]{1,0:T(8,128)(2,1)S(1)} %get-tuple-element.93), channel_id=1, source_target_pairs={{0,6},{1,7},{2,4},{3,5},{4,2},{5,3},{6,0},{7,1},{8,14},{9,15},{10,... | collective-permute-start | bytes 1572872 | tf_op jit(solution)/shard_map/ppermute | solution.py:29
  57.4 2.9 %query.2 = (bf16[128,640]{1,0:T(8,128)(2,1)S(1)}, f32[128,640]{1,0:T(8,128)S(1)}, bf16[16,128]{1,0:T(8,128)(2,1)S(1)}, f32[128,128]{1,0:T(8,128)S(1)}, bf16[64,2560]{1,0:T(8,128)(2,1)S(1)}) custom-call(s32[4]{0:T(128)S(1)} %copy-done.3, f32[1,2560]{1,0:T(1,128)S(1)} %constant_dynamic-slice_fusion.1.gain_ref, bf16[2560,640]{1,0:T(8,128)(2,1)S(1)} %copy-done, ...), custom_call_target="tpu_custom_call" | custom-call | flops 419430400 | bytes 3281920 | tf_op jit(solution)/shard_map/query/pallas_call | solution.py:404
  60.3 1.5 %collective-permute-start.18 = (bf16[16,128]{1,0:T(8,128)(2,1)S(1)}, bf16[16,128]{1,0:T(8,128)(2,1)S(1)}, u32[]{:S(2)}, u32[]{:S(2)}) collective-permute-start(bf16[16,128]{1,0:T(8,128)(2,1)S(1)} %get-tuple-element.98), channel_id=1, source_target_pairs={{0,8},{1,9},{2,10},{3,11},{4,12},{5,13},{6,14},{7,15},{8,0},{9,1},... | collective-permute-start | bytes 12296 | tf_op jit(solution)/shard_map/ppermute | solution.py:29
  61.8 1.5 %collective-permute-start.17 = (bf16[128,640]{1,0:T(8,128)(2,1)S(1)}, bf16[128,640]{1,0:T(8,128)(2,1)S(1)}, u32[]{:S(2)}, u32[]{:S(2)}) collective-permute-start(bf16[128,640]{1,0:T(8,128)(2,1)S(1)} %get-tuple-element.97), channel_id=1, source_target_pairs={{0,8},{1,9},{2,10},{3,11},{4,12},{5,13},{6,14},{7,15},{8,0},{9,1},... | collective-permute-start | bytes 491528 | tf_op jit(solution)/shard_map/ppermute | solution.py:29
  63.3 2.1 %collective-permute-done.14 = bf16[1024,256]{1,0:T(8,128)(2,1)S(1)} collective-permute-done((bf16[1024,256]{1,0:T(8,128)(2,1)S(1)}, bf16[1024,256]{1,0:T(8,128)(2,1)S(1)}, u32[]{:S(2)}, u32[]{:S(2)}) %collective-permute-start.14) | collective-permute-done | bytes 524320 | tf_op jit(solution)/shard_map/ppermute | solution.py:29
  65.6 13.0 %collective-permute-done.16 = bf16[1024,256]{1,0:T(8,128)(2,1)S(1)} collective-permute-done((bf16[1024,256]{1,0:T(8,128)(2,1)S(1)}, bf16[1024,256]{1,0:T(8,128)(2,1)S(1)}, u32[]{:S(2)}, u32[]{:S(2)}) %collective-permute-start.16) | collective-permute-done | bytes 524320 | tf_op jit(solution)/shard_map/ppermute | solution.py:29
  79.1 1.7 %attend.2 = (bf16[128,640]{1,0:T(8,128)(2,1)S(1)}, f32[128,640]{1,0:T(8,128)S(1)}, bf16[16,128]{1,0:T(8,128)(2,1)S(1)}, f32[128,128]{1,0:T(8,128)S(1)}) custom-call(s32[128,1]{1,0:T(8,128)S(1)} %fusion.7.query_pos_ref, s32[128,1]{1,0:T(8,128)S(1)} %broadcast_in_dim_reshape.5.query_floor_ref, s32[1,1024]{1,0:T(1,128)S(1)} %bitcast.51, ...), custom_call_target="tpu_custom_call" | custom-call | flops 209715200 | bytes 891392 | tf_op jit(solution)/shard_map/attend/pallas_call | solution.py:404
  80.8 1.1 collective-permute-start.20
  81.9 1.9 %collective-permute-start.19 = (bf16[128,640]{1,0:T(8,128)(2,1)S(1)}, bf16[128,640]{1,0:T(8,128)(2,1)S(1)}, u32[]{:S(2)}, u32[]{:S(2)}) collective-permute-start(bf16[128,640]{1,0:T(8,128)(2,1)S(1)} %get-tuple-element.101), channel_id=1, source_target_pairs={{0,8},{1,9},{2,10},{3,11},{4,12},{5,13},{6,14},{7,15},{8,0},{9,1},... | collective-permute-start | bytes 491528 | tf_op jit(solution)/shard_map/ppermute | solution.py:29
  84.4 1.0 collective-permute-done.20.refs_1_
  85.4 6.4 %collective-permute-done.19.refs_0_ = bf16[128,640]{1,0:T(8,128)(2,1)S(1)} collective-permute-done((bf16[128,640]{1,0:T(8,128)(2,1)S(1)}, bf16[128,640]{1,0:T(8,128)(2,1)S(1)}, u32[]{:S(2)}, u32[]{:S(2)}) %collective-permute-start.19) | collective-permute-done | bytes 163872 | tf_op jit(solution)/shard_map/ppermute | solution.py:29
  91.9 1.9 %update.2 = (f32[64,2560]{1,0:T(8,128)S(1)}, bf16[64,2560]{1,0:T(8,128)(2,1)S(1)}) custom-call(s32[4]{0:T(128)S(1)} %copy-done.3, bf16[2560,640]{1,0:T(8,128)(2,1)S(1)} %get-tuple-element.119.weight_ref, f32[128,640]{1,0:T(8,128)S(1)} %get-tuple-element.99.kept_ref, f32[128,128]{1,0:T(8,128)S(1)} %get-tuple-element.100.totals_ref, ...), custom_call_target="tpu_custom_call" | custom-call | flops 419430400 | bytes 3641344 | tf_op jit(solution)/shard_map/update/pallas_call | solution.py:404
  93.8 1.6 %collective-permute-done.21 = bf16[64,2560]{1,0:T(8,128)(2,1)S(1)} collective-permute-done((bf16[64,2560]{1,0:T(8,128)(2,1)S(1)}, bf16[64,2560]{1,0:T(8,128)(2,1)S(1)}, u32[]{:S(2)}, u32[]{:S(2)}) %collective-permute-start.21) | collective-permute-done | bytes 327712 | tf_op jit(solution)/shard_map/ppermute | solution.py:29
  95.5 1.4 collective-permute-start.22
  96.9 4.9 %collective-permute-done.22 = bf16[64,1280]{1,0:T(8,128)(2,1)S(1)} collective-permute-done((bf16[64,1280]{1,0:T(8,128)(2,1)S(1)}, bf16[64,1280]{1,0:T(8,128)(2,1)S(1)}, u32[]{:S(2)}, u32[]{:S(2)}) %collective-permute-start.22) | collective-permute-done | bytes 163872 | tf_op jit(solution)/shard_map/ppermute | solution.py:29
  101.8 1.0 collective-permute-done.24
  104.0 4.3 %collective-permute-done.23 = bf16[64,1280]{1,0:T(8,128)(2,1)S(1)} collective-permute-done((bf16[64,1280]{1,0:T(8,128)(2,1)S(1)}, bf16[64,1280]{1,0:T(8,128)(2,1)S(1)}, u32[]{:S(2)}, u32[]{:S(2)}) %collective-permute-start.23) | collective-permute-done | bytes 163872 | tf_op jit(solution)/shard_map/ppermute | solution.py:29
  108.9 1.6 %collective-permute-done.26.theirs_ref = bf16[64,2560]{1,0:T(8,128)(2,1)S(1)} collective-permute-done((bf16[64,2560]{1,0:T(8,128)(2,1)S(1)}, bf16[64,2560]{1,0:T(8,128)(2,1)S(1)}, u32[]{:S(2)}, u32[]{:S(2)}) %collective-permute-start.26) | collective-permute-done | bytes 327712 | tf_op jit(solution)/shard_map/ppermute | solution.py:29
  110.5 1.3 query.3
  111.7 2.2 %collective-permute-start.27 = (bf16[128,640]{1,0:T(8,128)(2,1)S(1)}, bf16[128,640]{1,0:T(8,128)(2,1)S(1)}, u32[]{:S(2)}, u32[]{:S(2)}) collective-permute-start(bf16[128,640]{1,0:T(8,128)(2,1)S(1)} %get-tuple-element.107), channel_id=1, source_target_pairs={{0,8},{1,9},{2,10},{3,11},{4,12},{5,13},{6,14},{7,15},{8,0},{9,1},... | collective-permute-start | bytes 491528 | tf_op jit(solution)/shard_map/ppermute | solution.py:29
  113.9 0.8 collective-permute-start.28
  114.7 7.9 %collective-permute-done.28.refs_3_ = bf16[16,128]{1,0:T(8,128)(2,1)S(1)} collective-permute-done((bf16[16,128]{1,0:T(8,128)(2,1)S(1)}, bf16[16,128]{1,0:T(8,128)(2,1)S(1)}, u32[]{:S(2)}, u32[]{:S(2)}) %collective-permute-start.28) | collective-permute-done | bytes 4128 | tf_op jit(solution)/shard_map/ppermute | solution.py:29
  122.6 1.7 %attend.3 = (bf16[128,640]{1,0:T(8,128)(2,1)S(1)}, f32[128,640]{1,0:T(8,128)S(1)}, bf16[16,128]{1,0:T(8,128)(2,1)S(1)}, f32[128,128]{1,0:T(8,128)S(1)}) custom-call(s32[128,1]{1,0:T(8,128)S(1)} %fusion.7.query_pos_ref, s32[128,1]{1,0:T(8,128)S(1)} %broadcast_in_dim_reshape.5.query_floor_ref, s32[1,1024]{1,0:T(1,128)S(1)} %bitcast.52, ...), custom_call_target="tpu_custom_call" | custom-call | flops 209715200 | bytes 891392 | tf_op jit(solution)/shard_map/attend/pallas_call | solution.py:404
  124.4 2.9 %collective-permute-start.30 = (bf16[16,128]{1,0:T(8,128)(2,1)S(1)}, bf16[16,128]{1,0:T(8,128)(2,1)S(1)}, u32[]{:S(2)}, u32[]{:S(2)}) collective-permute-start(bf16[16,128]{1,0:T(8,128)(2,1)S(1)} %get-tuple-element.112), channel_id=1, source_target_pairs={{0,8},{1,9},{2,10},{3,11},{4,12},{5,13},{6,14},{7,15},{8,0},{9,1},... | collective-permute-start | bytes 12296 | tf_op jit(solution)/shard_map/ppermute | solution.py:29
  127.3 6.3 %collective-permute-done.30.refs_1_ = bf16[16,128]{1,0:T(8,128)(2,1)S(1)} collective-permute-done((bf16[16,128]{1,0:T(8,128)(2,1)S(1)}, bf16[16,128]{1,0:T(8,128)(2,1)S(1)}, u32[]{:S(2)}, u32[]{:S(2)}) %collective-permute-start.30) | collective-permute-done | bytes 4128 | tf_op jit(solution)/shard_map/ppermute | solution.py:29
  133.6 1.8 %update.3 = (f32[4,320,128]{2,1,0:T(8,128)S(1)}, bf16[4,320,128]{2,1,0:T(8,128)(2,1)S(1)}) custom-call(s32[4]{0:T(128)S(1)} %copy-done.3, bf16[2560,640]{1,0:T(8,128)(2,1)S(1)} %get-tuple-element.120.weight_ref, f32[128,640]{1,0:T(8,128)S(1)} %get-tuple-element.109.kept_ref, f32[128,128]{1,0:T(8,128)S(1)} %get-tuple-element.110.totals_ref, ...), custom_call_target="tpu_custom_call" | custom-call | flops 419430400 | bytes 3641344 | tf_op jit(solution)/shard_map/update/pallas_call | solution.py:404
  135.5 1.6 %collective-permute-done.31 = bf16[4,320,128]{2,1,0:T(8,128)(2,1)S(1)} collective-permute-done((bf16[4,320,128]{2,1,0:T(8,128)(2,1)S(1)}, bf16[4,320,128]{2,1,0:T(8,128)(2,1)S(1)}, u32[]{:S(2)}, u32[]{:S(2)}) %collective-permute-start.31) | collective-permute-done | bytes 327712 | tf_op jit(solution)/shard_map/ppermute | solution.py:29
  137.2 1.2 collective-permute-start.32
  138.4 2.4 %collective-permute-start.33 = (bf16[320,128]{1,0:T(8,128)(2,1)S(1)}, bf16[320,128]{1,0:T(8,128)(2,1)S(1)}, u32[]{:S(2)}, u32[]{:S(2)}) collective-permute-start(bf16[320,128]{1,0:T(8,128)(2,1)S(1)} %get-tuple-element.135), channel_id=1, source_target_pairs={{0,4},{1,5},{2,6},{3,7},{4,0},{5,1},{6,2},{7,3},{8,12},{9,13},{10,... | collective-permute-start | bytes 245768 | tf_op jit(solution)/shard_map/ppermute | solution.py:29
  141.8 2.6 %collective-permute-done.34 = bf16[320,128]{1,0:T(8,128)(2,1)S(1)} collective-permute-done((bf16[320,128]{1,0:T(8,128)(2,1)S(1)}, bf16[320,128]{1,0:T(8,128)(2,1)S(1)}, u32[]{:S(2)}, u32[]{:S(2)}) %collective-permute-start.34) | collective-permute-done | bytes 81952 | tf_op jit(solution)/shard_map/ppermute | solution.py:29
  (79 shorter events, 10.5 us)
Async XLA Ops:
  4.8 20.9 %collective-permute-start.1 = (bf16[2,320,256]{2,1,0:T(8,128)(2,1)}, bf16[2,320,256]{2,1,0:T(8,128)(2,1)}, u32[]{:S(2)}, u32[]{:S(2)}) collective-permute-start(bf16[2,320,256]{2,1,0:T(8,128)(2,1)} %get-tuple-element.62), channel_id=1, source_target_pairs={{0,8},{1,9},{2,10},{3,11},{4,12},{5,13},{6,14},{7,15},{8,0},{9,1},... | collective-permute-start | bytes 983048 | tf_op jit(solution)/shard_map/ppermute | solution.py:472
  8.9 20.7 %collective-permute-start.4 = (bf16[128,1280]{1,0:T(8,128)(2,1)}, bf16[128,1280]{1,0:T(8,128)(2,1)}, u32[]{:S(2)}, u32[]{:S(2)}) collective-permute-start(bf16[128,1280]{1,0:T(8,128)(2,1)} %get-tuple-element.72), channel_id=1, source_target_pairs={{0,6},{1,7},{2,4},{3,5},{4,2},{5,3},{6,0},{7,1},{8,14},{9,15},{10,... | collective-permute-start | bytes 983048 | tf_op jit(solution)/shard_map/ppermute | solution.py:29
  11.4 26.7 %collective-permute-start.6 = (bf16[2,320,256]{2,1,0:T(8,128)(2,1)}, bf16[2,320,256]{2,1,0:T(8,128)(2,1)}, u32[]{:S(2)}, u32[]{:S(2)}) collective-permute-start(bf16[2,320,256]{2,1,0:T(8,128)(2,1)} %get-tuple-element.73), channel_id=1, source_target_pairs={{0,8},{1,9},{2,10},{3,11},{4,12},{5,13},{6,14},{7,15},{8,0},{9,1},... | collective-permute-start | bytes 983048 | tf_op jit(solution)/shard_map/ppermute | solution.py:472
  11.7 17.5 %collective-permute-start = (bf16[160,1280]{1,0:T(8,128)(2,1)}, bf16[160,1280]{1,0:T(8,128)(2,1)}, u32[]{:S(2)}, u32[]{:S(2)}) collective-permute-start(bf16[160,1280]{1,0:T(8,128)(2,1)} %get-tuple-element.60), channel_id=1, source_target_pairs={{0,2},{1,3},{2,0},{3,1},{4,6},{5,7},{6,4},{7,5},{8,10},{9,11},{10,... | collective-permute-start | bytes 1228808 | tf_op jit(solution)/shard_map/ppermute | solution.py:29
  12.3 28.7 %collective-permute-start.3 = (bf16[160,1280]{1,0:T(8,128)(2,1)}, bf16[160,1280]{1,0:T(8,128)(2,1)}, u32[]{:S(2)}, u32[]{:S(2)}) collective-permute-start(bf16[160,1280]{1,0:T(8,128)(2,1)} %get-tuple-element.71), channel_id=1, source_target_pairs={{0,4},{1,5},{2,6},{3,7},{4,0},{5,1},{6,2},{7,3},{8,12},{9,13},{10,... | collective-permute-start | bytes 1228808 | tf_op jit(solution)/shard_map/ppermute | solution.py:29
  13.4 5.2 %copy-start.4 = (s32[2,2]{1,0:T(2,128)S(1)}, s32[2,2]{1,0:T(2,128)}, u32[]{:S(2)}) copy-start(s32[2,2]{1,0:T(2,128)} %param.15) | copy-start | bytes 52
  13.4 12.8 %copy-start.3 = (s32[4]{0:T(128)S(1)}, s32[4]{0:T(128)}, u32[]{:S(2)}) copy-start(s32[4]{0:T(128)} %pad_add_fusion.place_ref) | copy-start | bytes 52
  25.7 15.4 %collective-permute-start.5 = (bf16[2,320,256]{2,1,0:T(8,128)(2,1)}, bf16[2,320,256]{2,1,0:T(8,128)(2,1)}, u32[]{:S(2)}, u32[]{:S(2)}) collective-permute-start(bf16[2,320,256]{2,1,0:T(8,128)(2,1)} %collective-permute-done.1.refs_8_), channel_id=1, source_target_pairs={{0,16},{16,0},{1,17},{17,1},{2,18},{18,2},{3,19},{19,3},{4,20},{20... | collective-permute-start | bytes 983048 | tf_op jit(solution)/shard_map/ppermute | solution.py:29
  26.2 1.3 copy-start.1
  27.5 1.0 copy-start.2
  29.3 16.0 %collective-permute-start.2 = (bf16[4,320,256]{2,1,0:T(8,128)(2,1)S(1)}, bf16[4,320,256]{2,1,0:T(8,128)(2,1)S(1)}, u32[]{:S(2)}, u32[]{:S(2)}) collective-permute-start(bf16[4,320,256]{2,1,0:T(8,128)(2,1)S(1)} %get-tuple-element.68), channel_id=1, source_target_pairs={{0,1},{1,0},{2,3},{3,2},{4,5},{5,4},{6,7},{7,6},{8,9},{9,8},{10,11... | collective-permute-start | bytes 1966088 | tf_op jit(solution)/shard_map/ppermute | solution.py:29
  29.7 12.9 %collective-permute-start.7 = (bf16[160,1280]{1,0:T(8,128)(2,1)S(1)}, bf16[160,1280]{1,0:T(8,128)(2,1)S(1)}, u32[]{:S(2)}, u32[]{:S(2)}) collective-permute-start(bf16[160,1280]{1,0:T(8,128)(2,1)S(1)} %copy-done.2), channel_id=1, source_target_pairs={{0,1},{1,0},{2,3},{3,2},{4,5},{5,4},{6,7},{7,6},{8,9},{9,8},{10,11... | collective-permute-start | bytes 1228808 | tf_op jit(solution)/shard_map/ppermute | solution.py:29
  38.2 6.6 %collective-permute-start.8 = (bf16[160,1280]{1,0:T(8,128)(2,1)}, bf16[160,1280]{1,0:T(8,128)(2,1)S(1)}, u32[]{:S(2)}, u32[]{:S(2)}) collective-permute-start(bf16[160,1280]{1,0:T(8,128)(2,1)} %collective-permute-done.refs_1_), channel_id=1, source_target_pairs={{0,1},{1,0},{2,3},{3,2},{4,5},{5,4},{6,7},{7,6},{8,9},{9,8},{10,11... | collective-permute-start | bytes 1228808 | tf_op jit(solution)/shard_map/ppermute | solution.py:29
  41.0 4.2 %collective-permute-start.9 = (bf16[160,1280]{1,0:T(8,128)(2,1)}, bf16[160,1280]{1,0:T(8,128)(2,1)S(1)}, u32[]{:S(2)}, u32[]{:S(2)}) collective-permute-start(bf16[160,1280]{1,0:T(8,128)(2,1)} %collective-permute-done.3.refs_2_), channel_id=1, source_target_pairs={{0,1},{1,0},{2,3},{3,2},{4,5},{5,4},{6,7},{7,6},{8,9},{9,8},{10,11... | collective-permute-start | bytes 1228808 | tf_op jit(solution)/shard_map/ppermute | solution.py:29
  41.1 4.1 %collective-permute-start.10 = (bf16[128,1280]{1,0:T(8,128)(2,1)}, bf16[128,1280]{1,0:T(8,128)(2,1)S(1)}, u32[]{:S(2)}, u32[]{:S(2)}) collective-permute-start(bf16[128,1280]{1,0:T(8,128)(2,1)} %collective-permute-done.4.refs_3_), channel_id=1, source_target_pairs={{0,1},{1,0},{2,3},{3,2},{4,5},{5,4},{6,7},{7,6},{8,9},{9,8},{10,11... | collective-permute-start | bytes 983048 | tf_op jit(solution)/shard_map/ppermute | solution.py:29
  42.5 10.3 %collective-permute-start.15 = (bf16[2,320,256]{2,1,0:T(8,128)(2,1)}, bf16[2,320,256]{2,1,0:T(8,128)(2,1)S(1)}, u32[]{:S(2)}, u32[]{:S(2)}) collective-permute-start(bf16[2,320,256]{2,1,0:T(8,128)(2,1)} %collective-permute-done.6.refs_8_), channel_id=1, source_target_pairs={{0,16},{16,0},{1,17},{17,1},{2,18},{18,2},{3,19},{19,3},{4,20},{20... | collective-permute-start | bytes 983048 | tf_op jit(solution)/shard_map/ppermute | solution.py:29
  44.7 4.4 %collective-permute-start.11 = (bf16[32,1280]{1,0:T(8,128)(2,1)S(1)}, bf16[32,1280]{1,0:T(8,128)(2,1)S(1)}, u32[]{:S(2)}, u32[]{:S(2)}) collective-permute-start(bf16[32,1280]{1,0:T(8,128)(2,1)S(1)} %slice.83), channel_id=1, source_target_pairs={{0,2},{1,3},{2,0},{3,1},{4,6},{5,7},{6,4},{7,5},{8,10},{9,11},{10,... | collective-permute-start | bytes 245768 | tf_op jit(solution)/shard_map/ppermute | solution.py:29
  49.2 8.3 %copy-start = (bf16[2560,640]{1,0:T(8,128)(2,1)S(1)}, bf16[2560,640]{1,0:T(8,128)(2,1)}, u32[]{:S(2)}) copy-start(bf16[2560,640]{1,0:T(8,128)(2,1)} %get-tuple-element.121.weight_ref) | copy-start | bytes 9830404
  49.2 8.3 %collective-permute-start.12 = (bf16[32,1280]{1,0:T(8,128)(2,1)S(1)}, bf16[32,1280]{1,0:T(8,128)(2,1)S(1)}, u32[]{:S(2)}, u32[]{:S(2)}) collective-permute-start(bf16[32,1280]{1,0:T(8,128)(2,1)S(1)} %collective-permute-done.11.refs_3_), channel_id=1, source_target_pairs={{0,1},{1,0},{2,3},{3,2},{4,5},{5,4},{6,7},{7,6},{8,9},{9,8},{10,11... | collective-permute-start | bytes 245768 | tf_op jit(solution)/shard_map/ppermute | solution.py:29
  49.2 16.3 %collective-permute-start.13 = (bf16[1024,256]{1,0:T(8,128)(2,1)S(1)}, bf16[1024,256]{1,0:T(8,128)(2,1)S(1)}, u32[]{:S(2)}, u32[]{:S(2)}) collective-permute-start(bf16[1024,256]{1,0:T(8,128)(2,1)S(1)} %get-tuple-element.88), channel_id=1, source_target_pairs={{0,4},{1,5},{2,6},{3,7},{4,0},{5,1},{6,2},{7,3},{8,12},{9,13},{10,... | collective-permute-start | bytes 1572872 | tf_op jit(solution)/shard_map/ppermute | solution.py:29
  50.0 15.4 %collective-permute-start.14 = (bf16[1024,256]{1,0:T(8,128)(2,1)S(1)}, bf16[1024,256]{1,0:T(8,128)(2,1)S(1)}, u32[]{:S(2)}, u32[]{:S(2)}) collective-permute-start(bf16[1024,256]{1,0:T(8,128)(2,1)S(1)} %get-tuple-element.89), channel_id=1, source_target_pairs={{0,2},{1,3},{2,0},{3,1},{4,6},{5,7},{6,4},{7,5},{8,10},{9,11},{10,... | collective-permute-start | bytes 1572872 | tf_op jit(solution)/shard_map/ppermute | solution.py:29
  55.8 22.7 %collective-permute-start.16 = (bf16[1024,256]{1,0:T(8,128)(2,1)S(1)}, bf16[1024,256]{1,0:T(8,128)(2,1)S(1)}, u32[]{:S(2)}, u32[]{:S(2)}) collective-permute-start(bf16[1024,256]{1,0:T(8,128)(2,1)S(1)} %get-tuple-element.93), channel_id=1, source_target_pairs={{0,6},{1,7},{2,4},{3,5},{4,2},{5,3},{6,0},{7,1},{8,14},{9,15},{10,... | collective-permute-start | bytes 1572872 | tf_op jit(solution)/shard_map/ppermute | solution.py:29
  57.4 26.4 %slice-start = ((s8[6553600]{0:T(1024)(128)(4,1)}), s8[2359296]{0:T(1024)(128)(4,1)S(1)}, s32[]{:S(2)}) async-start(s8[6553600]{0:T(1024)(128)(4,1)} %bitcast.53), calls=%async_computation | async-start | bytes 4718592
  60.3 18.8 %collective-permute-start.18 = (bf16[16,128]{1,0:T(8,128)(2,1)S(1)}, bf16[16,128]{1,0:T(8,128)(2,1)S(1)}, u32[]{:S(2)}, u32[]{:S(2)}) collective-permute-start(bf16[16,128]{1,0:T(8,128)(2,1)S(1)} %get-tuple-element.98), channel_id=1, source_target_pairs={{0,8},{1,9},{2,10},{3,11},{4,12},{5,13},{6,14},{7,15},{8,0},{9,1},... | collective-permute-start | bytes 12296 | tf_op jit(solution)/shard_map/ppermute | solution.py:29
  61.8 17.3 %collective-permute-start.17 = (bf16[128,640]{1,0:T(8,128)(2,1)S(1)}, bf16[128,640]{1,0:T(8,128)(2,1)S(1)}, u32[]{:S(2)}, u32[]{:S(2)}) collective-permute-start(bf16[128,640]{1,0:T(8,128)(2,1)S(1)} %get-tuple-element.97), channel_id=1, source_target_pairs={{0,8},{1,9},{2,10},{3,11},{4,12},{5,13},{6,14},{7,15},{8,0},{9,1},... | collective-permute-start | bytes 491528 | tf_op jit(solution)/shard_map/ppermute | solution.py:29
  65.5 18.4 %slice-start.1 = ((s8[6553600]{0:T(1024)(128)(4,1)}), s8[4194304]{0:T(1024)(128)(4,1)S(1)}, s32[]{:S(2)}) async-start(s8[6553600]{0:T(1024)(128)(4,1)} %bitcast.53), calls=%async_computation.1 | async-start | bytes 8388608
  80.8 4.6 %collective-permute-start.20 = (bf16[16,128]{1,0:T(8,128)(2,1)S(1)}, bf16[16,128]{1,0:T(8,128)(2,1)S(1)}, u32[]{:S(2)}, u32[]{:S(2)}) collective-permute-start(bf16[16,128]{1,0:T(8,128)(2,1)S(1)} %get-tuple-element.102), channel_id=1, source_target_pairs={{0,8},{1,9},{2,10},{3,11},{4,12},{5,13},{6,14},{7,15},{8,0},{9,1},... | collective-permute-start | bytes 12296 | tf_op jit(solution)/shard_map/ppermute | solution.py:29
  81.9 10.0 %collective-permute-start.19 = (bf16[128,640]{1,0:T(8,128)(2,1)S(1)}, bf16[128,640]{1,0:T(8,128)(2,1)S(1)}, u32[]{:S(2)}, u32[]{:S(2)}) collective-permute-start(bf16[128,640]{1,0:T(8,128)(2,1)S(1)} %get-tuple-element.101), channel_id=1, source_target_pairs={{0,8},{1,9},{2,10},{3,11},{4,12},{5,13},{6,14},{7,15},{8,0},{9,1},... | collective-permute-start | bytes 491528 | tf_op jit(solution)/shard_map/ppermute | solution.py:29
  93.7 1.7 %collective-permute-start.21 = (bf16[64,2560]{1,0:T(8,128)(2,1)S(1)}, bf16[64,2560]{1,0:T(8,128)(2,1)S(1)}, u32[]{:S(2)}, u32[]{:S(2)}) collective-permute-start(bf16[64,2560]{1,0:T(8,128)(2,1)S(1)} %get-tuple-element.104), channel_id=1, source_target_pairs={{0,1},{1,0},{2,3},{3,2},{4,5},{5,4},{6,7},{7,6},{8,9},{9,8},{10,11... | collective-permute-start | bytes 983048 | tf_op jit(solution)/shard_map/ppermute | solution.py:29
  95.5 6.3 %collective-permute-start.22 = (bf16[64,1280]{1,0:T(8,128)(2,1)S(1)}, bf16[64,1280]{1,0:T(8,128)(2,1)S(1)}, u32[]{:S(2)}, u32[]{:S(2)}) collective-permute-start(bf16[64,1280]{1,0:T(8,128)(2,1)S(1)} %get-tuple-element.138), channel_id=1, source_target_pairs={{0,2},{1,3},{2,0},{3,1},{4,6},{5,7},{6,4},{7,5},{8,10},{9,11},{10,... | collective-permute-start | bytes 491528 | tf_op jit(solution)/shard_map/ppermute | solution.py:29
  96.9 6.0 %collective-permute-start.24 = (bf16[64,1280]{1,0:T(8,128)(2,1)S(1)}, bf16[64,1280]{1,0:T(8,128)(2,1)S(1)}, u32[]{:S(2)}, u32[]{:S(2)}) collective-permute-start(bf16[64,1280]{1,0:T(8,128)(2,1)S(1)} %get-tuple-element.139), channel_id=1, source_target_pairs={{0,4},{1,5},{2,6},{3,7},{4,0},{5,1},{6,2},{7,3},{8,12},{9,13},{10,... | collective-permute-start | bytes 491528 | tf_op jit(solution)/shard_map/ppermute | solution.py:29
  103.0 5.4 %collective-permute-start.23 = (bf16[64,1280]{1,0:T(8,128)(2,1)S(1)}, bf16[64,1280]{1,0:T(8,128)(2,1)S(1)}, u32[]{:S(2)}, u32[]{:S(2)}) collective-permute-start(bf16[64,1280]{1,0:T(8,128)(2,1)S(1)} %get-tuple-element.136), channel_id=1, source_target_pairs={{0,4},{1,5},{2,6},{3,7},{4,0},{5,1},{6,2},{7,3},{8,12},{9,13},{10,... | collective-permute-start | bytes 491528 | tf_op jit(solution)/shard_map/ppermute | solution.py:29
  103.3 5.3 %collective-permute-start.25 = (bf16[64,1280]{1,0:T(8,128)(2,1)S(1)}, bf16[64,1280]{1,0:T(8,128)(2,1)S(1)}, u32[]{:S(2)}, u32[]{:S(2)}) collective-permute-start(bf16[64,1280]{1,0:T(8,128)(2,1)S(1)} %get-tuple-element.137), channel_id=1, source_target_pairs={{0,2},{1,3},{2,0},{3,1},{4,6},{5,7},{6,4},{7,5},{8,10},{9,11},{10,... | collective-permute-start | bytes 491528 | tf_op jit(solution)/shard_map/ppermute | solution.py:29
  108.8 1.7 %collective-permute-start.26 = (bf16[64,2560]{1,0:T(8,128)(2,1)S(1)}, bf16[64,2560]{1,0:T(8,128)(2,1)S(1)}, u32[]{:S(2)}, u32[]{:S(2)}) collective-permute-start(bf16[64,2560]{1,0:T(8,128)(2,1)S(1)} %add_convert_fusion.ours_ref), channel_id=1, source_target_pairs={{0,1},{1,0},{2,3},{3,2},{4,5},{5,4},{6,7},{7,6},{8,9},{9,8},{10,11... | collective-permute-start | bytes 983048 | tf_op jit(solution)/shard_map/ppermute | solution.py:29
  111.7 10.9 %collective-permute-start.27 = (bf16[128,640]{1,0:T(8,128)(2,1)S(1)}, bf16[128,640]{1,0:T(8,128)(2,1)S(1)}, u32[]{:S(2)}, u32[]{:S(2)}) collective-permute-start(bf16[128,640]{1,0:T(8,128)(2,1)S(1)} %get-tuple-element.107), channel_id=1, source_target_pairs={{0,8},{1,9},{2,10},{3,11},{4,12},{5,13},{6,14},{7,15},{8,0},{9,1},... | collective-permute-start | bytes 491528 | tf_op jit(solution)/shard_map/ppermute | solution.py:29
  113.9 8.7 %collective-permute-start.28 = (bf16[16,128]{1,0:T(8,128)(2,1)S(1)}, bf16[16,128]{1,0:T(8,128)(2,1)S(1)}, u32[]{:S(2)}, u32[]{:S(2)}) collective-permute-start(bf16[16,128]{1,0:T(8,128)(2,1)S(1)} %get-tuple-element.108), channel_id=1, source_target_pairs={{0,8},{1,9},{2,10},{3,11},{4,12},{5,13},{6,14},{7,15},{8,0},{9,1},... | collective-permute-start | bytes 12296 | tf_op jit(solution)/shard_map/ppermute | solution.py:29
  124.4 9.3 %collective-permute-start.29 = (bf16[128,640]{1,0:T(8,128)(2,1)S(1)}, bf16[128,640]{1,0:T(8,128)(2,1)S(1)}, u32[]{:S(2)}, u32[]{:S(2)}) collective-permute-start(bf16[128,640]{1,0:T(8,128)(2,1)S(1)} %get-tuple-element.111), channel_id=1, source_target_pairs={{0,8},{1,9},{2,10},{3,11},{4,12},{5,13},{6,14},{7,15},{8,0},{9,1},... | collective-permute-start | bytes 491528 | tf_op jit(solution)/shard_map/ppermute | solution.py:29
  124.4 9.2 %collective-permute-start.30 = (bf16[16,128]{1,0:T(8,128)(2,1)S(1)}, bf16[16,128]{1,0:T(8,128)(2,1)S(1)}, u32[]{:S(2)}, u32[]{:S(2)}) collective-permute-start(bf16[16,128]{1,0:T(8,128)(2,1)S(1)} %get-tuple-element.112), channel_id=1, source_target_pairs={{0,8},{1,9},{2,10},{3,11},{4,12},{5,13},{6,14},{7,15},{8,0},{9,1},... | collective-permute-start | bytes 12296 | tf_op jit(solution)/shard_map/ppermute | solution.py:29
  135.4 1.7 %collective-permute-start.31 = (bf16[4,320,128]{2,1,0:T(8,128)(2,1)S(1)}, bf16[4,320,128]{2,1,0:T(8,128)(2,1)S(1)}, u32[]{:S(2)}, u32[]{:S(2)}) collective-permute-start(bf16[4,320,128]{2,1,0:T(8,128)(2,1)S(1)} %get-tuple-element.114), channel_id=1, source_target_pairs={{0,1},{1,0},{2,3},{3,2},{4,5},{5,4},{6,7},{7,6},{8,9},{9,8},{10,11... | collective-permute-start | bytes 983048 | tf_op jit(solution)/shard_map/ppermute | solution.py:29
  137.2 4.6 %collective-permute-start.32 = (bf16[320,128]{1,0:T(8,128)(2,1)S(1)}, bf16[320,128]{1,0:T(8,128)(2,1)S(1)}, u32[]{:S(2)}, u32[]{:S(2)}) collective-permute-start(bf16[320,128]{1,0:T(8,128)(2,1)S(1)} %get-tuple-element.133), channel_id=1, source_target_pairs={{0,2},{1,3},{2,0},{3,1},{4,6},{5,7},{6,4},{7,5},{8,10},{9,11},{10,... | collective-permute-start | bytes 245768 | tf_op jit(solution)/shard_map/ppermute | solution.py:29
  138.4 6.0 %collective-permute-start.34 = (bf16[320,128]{1,0:T(8,128)(2,1)S(1)}, bf16[320,128]{1,0:T(8,128)(2,1)S(1)}, u32[]{:S(2)}, u32[]{:S(2)}) collective-permute-start(bf16[320,128]{1,0:T(8,128)(2,1)S(1)} %get-tuple-element.134), channel_id=1, source_target_pairs={{0,6},{1,7},{2,4},{3,5},{4,2},{5,3},{6,0},{7,1},{8,14},{9,15},{10,... | collective-permute-start | bytes 245768 | tf_op jit(solution)/shard_map/ppermute | solution.py:29
  138.4 6.3 %collective-permute-start.33 = (bf16[320,128]{1,0:T(8,128)(2,1)S(1)}, bf16[320,128]{1,0:T(8,128)(2,1)S(1)}, u32[]{:S(2)}, u32[]{:S(2)}) collective-permute-start(bf16[320,128]{1,0:T(8,128)(2,1)S(1)} %get-tuple-element.135), channel_id=1, source_target_pairs={{0,4},{1,5},{2,6},{3,7},{4,0},{5,1},{6,2},{7,3},{8,12},{9,13},{10,... | collective-permute-start | bytes 245768 | tf_op jit(solution)/shard_map/ppermute | solution.py:29

commit v9 on v8

--- a/solution.py
+++ b/solution.py
@@ -52,13 +52,19 @@
     return pieces
 
 
+def here():
+    me = lax.axis_index("row")
+    part = lax.axis_index("groups") if lax.axis_size("groups") == 2 else 0
+    return [me // 2 % CHIPS, me % 2, me // KVH, part]
+
+
 def prepare_kernel(
-    pair, heads, blocks, width, place_ref, weight_any, hidden_any, gain_any, extra_any, *refs
+    pair, heads, blocks, width, weight_any, hidden_any, gain_any, extra_any, *refs
 ):
     weight_ref, hidden_ref, gain_ref, extra_ref, normed, sems = refs[-6:]
     results = len(heads) + len(blocks)
     targets, refs = refs[:results], refs[results:-6]
-    place_now = [place_ref[number] for number in range(4)]
+    place_now = here()
     rows = hidden_ref.shape[0]
     lanes = extra_ref.shape[1]
     bands = [slice(band, band + BAND) for band in range(0, rows, BAND)]
@@ -135,8 +141,7 @@
     results = pl.pallas_call(
         functools.partial(prepare_kernel, pair, head_groups, groups, width),
         out_shape=[jax.ShapeDtypeStruct(shape, BF16) for shape in shapes],
-        in_specs=[pl.BlockSpec(memory_space=pltpu.SMEM)]
-        + [pl.BlockSpec(memory_space=pltpu.HBM)] * 4,
+        in_specs=[pl.BlockSpec(memory_space=pltpu.HBM)] * 4,
         out_specs=[pl.BlockSpec(memory_space=pl.ANY)] * len(shapes),
         scratch_shapes=[pltpu.VMEM(shape, BF16) for shape in shapes]
         + [
@@ -149,7 +154,7 @@
         ],
         compiler_params=pltpu.CompilerParams(vmem_limit_bytes=60 * 1024 * 1024),
         name="prepare",
-    )(place_now, weight, hidden, gain[None, :], extra)
+    )(weight, hidden, gain[None, :], extra)
     return results[: len(counts)], results[len(counts) :]
 
 
@@ -336,17 +341,24 @@
     keys, values = kv_ref[:, :HD], kv_ref[:, HD:]
     lane = lax.broadcasted_iota(jnp.int32, (lanes, lanes), 1)
     totals = jnp.zeros((lanes, lanes), F32)
-    for head in range(queries.shape[1] // HD):
+    heads = queries.shape[1] // HD
+    stacked = jnp.concatenate([queries[:, h * HD : (h + 1) * HD] for h in range(heads)], axis=0)
+    scores = lax.dot_general(
+        stacked, keys, (((1,), (1,)), ((), ())), preferred_element_type=F32
+    )
+    capped = jnp.tanh(scores * (HD ** (-0.5) / CAP))
+    weights = jnp.exp2(capped * (CAP * LOG2_E)).reshape(heads, lanes, -1)
+    weights = jnp.where(visible[None], weights, 0.0)
+    sums = jnp.sum(weights, axis=2, keepdims=True)
+    weighted = jnp.dot(
+        weights.astype(BF16).reshape(heads * lanes, -1), values, preferred_element_type=F32
+    )
+    for head in range(heads):
         span = slice(head * HD, (head + 1) * HD)
-        scores = lax.dot_general(
-            queries[:, span], keys, (((1,), (1,)), ((), ())), preferred_element_type=F32
-        )
-        capped = jnp.tanh(scores * (HD ** (-0.5) / CAP))
-        weights = jnp.where(visible, jnp.exp2(capped * (CAP * LOG2_E)), 0.0)
-        totals = jnp.where(lane == head, jnp.sum(weights, axis=1, keepdims=True), totals)
-        weighted = jnp.dot(weights.astype(BF16), values, preferred_element_type=F32)
-        out_ref[:, span] = weighted
-        sent_ref[:, span] = weighted.astype(BF16)
+        totals = jnp.where(lane == head, sums[head], totals)
+        part = weighted[head * lanes : (head + 1) * lanes]
+        out_ref[:, span] = part
+        sent_ref[:, span] = part.astype(BF16)
     totals_ref[...] = totals
     across = totals.T[:8]
     high = across.astype(BF16)

time: 146 us -> 143 us (0.979)
  Pallas kernels: 22.9 us -> 21 us
  transfers between devices with their start and end apart: 35 -> 35, of which waited for: 21 -> 21; matrix products, arithmetic and copies ran while one was open for 6% -> 7% of each run, Pallas kernels for 7% -> 7%
where the time goes in v9:
time: 143 us
  waiting for transfers between devices  74.6 us (52%)
  starting transfers between devices  33.6 us (23%)
  Pallas kernels  21 us (15%)
  local copies, waits for them, and re-layouts  11.6 us (8%)
  other arithmetic  1.71 us (1%)
    ppermute x33, waiting for transfers between devices, swapped(): return lax.ppermute(value, axis, pairs)  60.6 us
    ppermute x33, starting transfers between devices, swapped(): return lax.ppermute(value, axis, pairs)  29.2 us
    ppermute x2, waiting for transfers between devices, to_tile(): return lax.ppermute(value, ('groups', 'row'), pairs)  14 us
    pallas_call x8, Pallas kernels, call(): pl.pallas_call(kernel, out_shape=out_shape, in_specs=[smem] * len(scalars...  11.5 us
    pallas_call x2, Pallas kernels, projected(): pl.pallas_call(functools.partial(project_kernel, rows, heads, start, plac...  5.92 us
    squeeze x1, local copies, waits for them, and re-layouts, query_parts(): query_weight[section, 0]  5.15 us
    ppermute x2, starting transfers between devices, to_tile(): return lax.ppermute(value, ('groups', 'row'), pairs)  4.44 us
    pallas_call x1, Pallas kernels, prepared(): pl.pallas_call(functools.partial(prepare_kernel, pair, head_groups, group...  3.54 us
  transfers between devices with their start and end apart: 35, of which 21 were waited for; matrix products, arithmetic and copies ran while one was open for 7% of the time, Pallas kernels for 7%

profile of v9, /device:TPU:0, one launch (start us, length us, event | category | flops | bytes accessed | tf_op | source)
XLA Modules:
  0.0 142.9 jit_solution(5657394180202052320)
XLA Ops:
  0.0 3.5 %prepare.1 = (bf16[2,320,256]{2,1,0:T(8,128)(2,1)}, bf16[2,320,256]{2,1,0:T(8,128)(2,1)}, bf16[160,1280]{1,0:T(8,128)(2,1)}, bf16[160,1280]{1,0:T(8,128)(2,1)}, ...) custom-call(bf16[320,2048]{1,0:T(8,128)(2,1)} %weight_ref, bf16[128,5120]{1,0:T(8,128)(2,1)} %hidden_any.1, ...), custom_call_target="tpu_custom_call" | custom-call | tf_op jit(solution)/shard_map/prepare/pallas_call | solution.py:141
  3.5 4.1 %collective-permute-start.1 = (bf16[2,320,256]{2,1,0:T(8,128)(2,1)}, bf16[2,320,256]{2,1,0:T(8,128)(2,1)}, u32[]{:S(2)}, u32[]{:S(2)}) collective-permute-start(bf16[2,320,256]{2,1,0:T(8,128)(2,1)} %get-tuple-element.62), channel_id=1, source_target_pairs={{0,8},{1,9},{2,10},{3,11},{4,12},{5,13},{6,14},{7,15},{8,0},{9,1},... | collective-permute-start | bytes 983048 | tf_op jit(solution)/shard_map/ppermute | solution.py:484
  7.6 2.5 %collective-permute-start.4 = (bf16[128,1280]{1,0:T(8,128)(2,1)}, bf16[128,1280]{1,0:T(8,128)(2,1)}, u32[]{:S(2)}, u32[]{:S(2)}) collective-permute-start(bf16[128,1280]{1,0:T(8,128)(2,1)} %get-tuple-element.72), channel_id=1, source_target_pairs={{0,6},{1,7},{2,4},{3,5},{4,2},{5,3},{6,0},{7,1},{8,14},{9,15},{10,... | collective-permute-start | bytes 983048 | tf_op jit(solution)/shard_map/ppermute | solution.py:29
  11.2 1.0 slice_reduce_fusion
  12.2 0.9 fusion.16
  13.3 5.1 %slice_bitcast_fusion.3 = (bf16[2560,640]{1,0:T(8,128)(2,1)}, bf16[2560,640]{1,0:T(8,128)(2,1)S(1)}) fusion(bf16[2,1,2560,640]{3,2,1,0:T(8,128)(2,1)} %param.13), kind=kLoop, calls=%fused_computation.3 | loop fusion | bytes 13107200 | tf_op jit(solution)/shard_map/squeeze | solution.py:645
  18.8 5.6 %collective-permute-done.1.refs_8_ = bf16[2,320,256]{2,1,0:T(8,128)(2,1)} collective-permute-done((bf16[2,320,256]{2,1,0:T(8,128)(2,1)}, bf16[2,320,256]{2,1,0:T(8,128)(2,1)}, u32[]{:S(2)}, u32[]{:S(2)}) %collective-permute-start.1) | collective-permute-done | bytes 327712 | tf_op jit(solution)/shard_map/ppermute | solution.py:484
  24.8 1.3 copy-done.1
  26.1 1.0 copy-done.2
  28.5 8.4 %collective-permute-done.6.refs_8_ = bf16[2,320,256]{2,1,0:T(8,128)(2,1)} collective-permute-done((bf16[2,320,256]{2,1,0:T(8,128)(2,1)}, bf16[2,320,256]{2,1,0:T(8,128)(2,1)}, u32[]{:S(2)}, u32[]{:S(2)}) %collective-permute-start.6) | collective-permute-done | bytes 327712 | tf_op jit(solution)/shard_map/ppermute | solution.py:484
  36.9 2.9 %collective-permute-done.3.refs_2_ = bf16[160,1280]{1,0:T(8,128)(2,1)} collective-permute-done((bf16[160,1280]{1,0:T(8,128)(2,1)}, bf16[160,1280]{1,0:T(8,128)(2,1)}, u32[]{:S(2)}, u32[]{:S(2)}) %collective-permute-start.3) | collective-permute-done | bytes 409632 | tf_op jit(solution)/shard_map/ppermute | solution.py:29
  40.4 0.9 slice.83
  41.3 2.2 %collective-permute-start.15 = (bf16[2,320,256]{2,1,0:T(8,128)(2,1)}, bf16[2,320,256]{2,1,0:T(8,128)(2,1)S(1)}, u32[]{:S(2)}, u32[]{:S(2)}) collective-permute-start(bf16[2,320,256]{2,1,0:T(8,128)(2,1)} %collective-permute-done.6.refs_8_), channel_id=1, source_target_pairs={{0,16},{16,0},{1,17},{17,1},{2,18},{18,2},{3,19},{19,3},{4,20},{20... | collective-permute-start | bytes 983048 | tf_op jit(solution)/shard_map/ppermute | solution.py:29
  44.0 3.0 %project.2 = (bf16[1024,256]{1,0:T(8,128)(2,1)S(1)}, bf16[1024,256]{1,0:T(8,128)(2,1)S(1)}) custom-call(s32[2]{0:T(128)S(1)} %pad_add_fusion.1.first_ref, bf16[4,320,256]{2,1,0:T(8,128)(2,1)S(1)} %get-tuple-element.67.kept_ref, bf16[4,320,256]{2,1,0:T(8,128)(2,1)S(1)} %collective-permute-done.2.traded_ref, bf16[160,1280]{1,0:T(8,128)(2,1)S(1)} %get-tuple-element.80.refs_0_, ...), custom_call_target="tpu_custom_call" | custom-call | flops 10737418240 | bytes 2621440 | tf_op jit(solution)/shard_map/project/pallas_call | solution.py:235
  47.0 0.9 collective-permute-done.11.refs_3_
  48.7 1.3 collective-permute-start.14
  50.0 1.6 %collective-permute-done.15.refs_9_ = bf16[2,320,256]{2,1,0:T(8,128)(2,1)S(1)} collective-permute-done((bf16[2,320,256]{2,1,0:T(8,128)(2,1)}, bf16[2,320,256]{2,1,0:T(8,128)(2,1)S(1)}, u32[]{:S(2)}, u32[]{:S(2)}) %collective-permute-start.15) | collective-permute-done | bytes 327712 | tf_op jit(solution)/shard_map/ppermute | solution.py:29
  51.6 3.0 %project.3 = (bf16[1024,256]{1,0:T(8,128)(2,1)S(1)}, bf16[1024,256]{1,0:T(8,128)(2,1)S(1)}) custom-call(s32[2]{0:T(128)S(1)} %pad_add_fusion.1.first_ref, bf16[4,320,256]{2,1,0:T(8,128)(2,1)S(1)} %get-tuple-element.67.kept_ref, bf16[4,320,256]{2,1,0:T(8,128)(2,1)S(1)} %collective-permute-done.2.traded_ref, bf16[160,1280]{1,0:T(8,128)(2,1)S(1)} %get-tuple-element.80.refs_0_, ...), custom_call_target="tpu_custom_call" | custom-call | flops 10737418240 | bytes 2621440 | tf_op jit(solution)/shard_map/project/pallas_call | solution.py:235
  54.5 1.6 %collective-permute-start.16 = (bf16[1024,256]{1,0:T(8,128)(2,1)S(1)}, bf16[1024,256]{1,0:T(8,128)(2,1)S(1)}, u32[]{:S(2)}, u32[]{:S(2)}) collective-permute-start(bf16[1024,256]{1,0:T(8,128)(2,1)S(1)} %get-tuple-element.93), channel_id=1, source_target_pairs={{0,6},{1,7},{2,4},{3,5},{4,2},{5,3},{6,0},{7,1},{8,14},{9,15},{10,... | collective-permute-start | bytes 1572872 | tf_op jit(solution)/shard_map/ppermute | solution.py:29
  56.2 2.9 %query.2 = (bf16[128,640]{1,0:T(8,128)(2,1)S(1)}, f32[128,640]{1,0:T(8,128)S(1)}, bf16[16,128]{1,0:T(8,128)(2,1)S(1)}, f32[128,128]{1,0:T(8,128)S(1)}, bf16[64,2560]{1,0:T(8,128)(2,1)S(1)}) custom-call(s32[4]{0:T(128)S(1)} %pad_add_fusion.place_ref, f32[1,2560]{1,0:T(1,128)S(1)} %constant_dynamic-slice_fusion.1.gain_ref, bf16[2560,640]{1,0:T(8,128)(2,1)S(1)} %copy-done, ...), custom_call_target="tpu_custom_call" | custom-call | flops 419430400 | bytes 3281920 | tf_op jit(solution)/shard_map/query/pallas_call | solution.py:416
  59.0 1.5 %collective-permute-start.18 = (bf16[16,128]{1,0:T(8,128)(2,1)S(1)}, bf16[16,128]{1,0:T(8,128)(2,1)S(1)}, u32[]{:S(2)}, u32[]{:S(2)}) collective-permute-start(bf16[16,128]{1,0:T(8,128)(2,1)S(1)} %get-tuple-element.98), channel_id=1, source_target_pairs={{0,8},{1,9},{2,10},{3,11},{4,12},{5,13},{6,14},{7,15},{8,0},{9,1},... | collective-permute-start | bytes 12296 | tf_op jit(solution)/shard_map/ppermute | solution.py:29
  60.5 1.5 %collective-permute-start.17 = (bf16[128,640]{1,0:T(8,128)(2,1)S(1)}, bf16[128,640]{1,0:T(8,128)(2,1)S(1)}, u32[]{:S(2)}, u32[]{:S(2)}) collective-permute-start(bf16[128,640]{1,0:T(8,128)(2,1)S(1)} %get-tuple-element.97), channel_id=1, source_target_pairs={{0,8},{1,9},{2,10},{3,11},{4,12},{5,13},{6,14},{7,15},{8,0},{9,1},... | collective-permute-start | bytes 491528 | tf_op jit(solution)/shard_map/ppermute | solution.py:29
  62.1 2.1 %collective-permute-done.14 = bf16[1024,256]{1,0:T(8,128)(2,1)S(1)} collective-permute-done((bf16[1024,256]{1,0:T(8,128)(2,1)S(1)}, bf16[1024,256]{1,0:T(8,128)(2,1)S(1)}, u32[]{:S(2)}, u32[]{:S(2)}) %collective-permute-start.14) | collective-permute-done | bytes 524320 | tf_op jit(solution)/shard_map/ppermute | solution.py:29
  64.3 12.8 %collective-permute-done.16 = bf16[1024,256]{1,0:T(8,128)(2,1)S(1)} collective-permute-done((bf16[1024,256]{1,0:T(8,128)(2,1)S(1)}, bf16[1024,256]{1,0:T(8,128)(2,1)S(1)}, u32[]{:S(2)}, u32[]{:S(2)}) %collective-permute-start.16) | collective-permute-done | bytes 524320 | tf_op jit(solution)/shard_map/ppermute | solution.py:29
  77.7 1.1 attend.2
  78.8 1.1 collective-permute-start.20
  79.9 1.9 %collective-permute-start.19 = (bf16[128,640]{1,0:T(8,128)(2,1)S(1)}, bf16[128,640]{1,0:T(8,128)(2,1)S(1)}, u32[]{:S(2)}, u32[]{:S(2)}) collective-permute-start(bf16[128,640]{1,0:T(8,128)(2,1)S(1)} %get-tuple-element.101), channel_id=1, source_target_pairs={{0,8},{1,9},{2,10},{3,11},{4,12},{5,13},{6,14},{7,15},{8,0},{9,1},... | collective-permute-start | bytes 491528 | tf_op jit(solution)/shard_map/ppermute | solution.py:29
  82.4 1.0 collective-permute-done.20.refs_1_
  83.4 6.5 %collective-permute-done.19.refs_0_ = bf16[128,640]{1,0:T(8,128)(2,1)S(1)} collective-permute-done((bf16[128,640]{1,0:T(8,128)(2,1)S(1)}, bf16[128,640]{1,0:T(8,128)(2,1)S(1)}, u32[]{:S(2)}, u32[]{:S(2)}) %collective-permute-start.19) | collective-permute-done | bytes 163872 | tf_op jit(solution)/shard_map/ppermute | solution.py:29
  89.9 1.9 %update.2 = (f32[64,2560]{1,0:T(8,128)S(1)}, bf16[64,2560]{1,0:T(8,128)(2,1)S(1)}) custom-call(s32[4]{0:T(128)S(1)} %pad_add_fusion.place_ref, bf16[2560,640]{1,0:T(8,128)(2,1)S(1)} %get-tuple-element.119.weight_ref, f32[128,640]{1,0:T(8,128)S(1)} %get-tuple-element.99.kept_ref, f32[128,128]{1,0:T(8,128)S(1)} %get-tuple-element.100.totals_ref, ...), custom_call_target="tpu_custom_call" | custom-call | flops 419430400 | bytes 3641344 | tf_op jit(solution)/shard_map/update/pallas_call | solution.py:416
  91.9 1.6 %collective-permute-done.21 = bf16[64,2560]{1,0:T(8,128)(2,1)S(1)} collective-permute-done((bf16[64,2560]{1,0:T(8,128)(2,1)S(1)}, bf16[64,2560]{1,0:T(8,128)(2,1)S(1)}, u32[]{:S(2)}, u32[]{:S(2)}) %collective-permute-start.21) | collective-permute-done | bytes 327712 | tf_op jit(solution)/shard_map/ppermute | solution.py:29
  93.6 1.5 %collective-permute-start.22 = (bf16[64,1280]{1,0:T(8,128)(2,1)S(1)}, bf16[64,1280]{1,0:T(8,128)(2,1)S(1)}, u32[]{:S(2)}, u32[]{:S(2)}) collective-permute-start(bf16[64,1280]{1,0:T(8,128)(2,1)S(1)} %get-tuple-element.138), channel_id=1, source_target_pairs={{0,2},{1,3},{2,0},{3,1},{4,6},{5,7},{6,4},{7,5},{8,10},{9,11},{10,... | collective-permute-start | bytes 491528 | tf_op jit(solution)/shard_map/ppermute | solution.py:29
  95.1 4.8 %collective-permute-done.22 = bf16[64,1280]{1,0:T(8,128)(2,1)S(1)} collective-permute-done((bf16[64,1280]{1,0:T(8,128)(2,1)S(1)}, bf16[64,1280]{1,0:T(8,128)(2,1)S(1)}, u32[]{:S(2)}, u32[]{:S(2)}) %collective-permute-start.22) | collective-permute-done | bytes 163872 | tf_op jit(solution)/shard_map/ppermute | solution.py:29
  99.9 1.1 collective-permute-done.24
  102.1 4.4 %collective-permute-done.23 = bf16[64,1280]{1,0:T(8,128)(2,1)S(1)} collective-permute-done((bf16[64,1280]{1,0:T(8,128)(2,1)S(1)}, bf16[64,1280]{1,0:T(8,128)(2,1)S(1)}, u32[]{:S(2)}, u32[]{:S(2)}) %collective-permute-start.23) | collective-permute-done | bytes 163872 | tf_op jit(solution)/shard_map/ppermute | solution.py:29
  107.0 1.6 %collective-permute-done.26.theirs_ref = bf16[64,2560]{1,0:T(8,128)(2,1)S(1)} collective-permute-done((bf16[64,2560]{1,0:T(8,128)(2,1)S(1)}, bf16[64,2560]{1,0:T(8,128)(2,1)S(1)}, u32[]{:S(2)}, u32[]{:S(2)}) %collective-permute-start.26) | collective-permute-done | bytes 327712 | tf_op jit(solution)/shard_map/ppermute | solution.py:29
  108.6 1.3 query.3
  109.9 2.1 %collective-permute-start.27 = (bf16[128,640]{1,0:T(8,128)(2,1)S(1)}, bf16[128,640]{1,0:T(8,128)(2,1)S(1)}, u32[]{:S(2)}, u32[]{:S(2)}) collective-permute-start(bf16[128,640]{1,0:T(8,128)(2,1)S(1)} %get-tuple-element.107), channel_id=1, source_target_pairs={{0,8},{1,9},{2,10},{3,11},{4,12},{5,13},{6,14},{7,15},{8,0},{9,1},... | collective-permute-start | bytes 491528 | tf_op jit(solution)/shard_map/ppermute | solution.py:29
  112.0 0.9 collective-permute-start.28
  112.9 7.9 %collective-permute-done.28.refs_3_ = bf16[16,128]{1,0:T(8,128)(2,1)S(1)} collective-permute-done((bf16[16,128]{1,0:T(8,128)(2,1)S(1)}, bf16[16,128]{1,0:T(8,128)(2,1)S(1)}, u32[]{:S(2)}, u32[]{:S(2)}) %collective-permute-start.28) | collective-permute-done | bytes 4128 | tf_op jit(solution)/shard_map/ppermute | solution.py:29
  120.8 1.1 attend.3
  122.0 2.9 %collective-permute-start.30 = (bf16[16,128]{1,0:T(8,128)(2,1)S(1)}, bf16[16,128]{1,0:T(8,128)(2,1)S(1)}, u32[]{:S(2)}, u32[]{:S(2)}) collective-permute-start(bf16[16,128]{1,0:T(8,128)(2,1)S(1)} %get-tuple-element.112), channel_id=1, source_target_pairs={{0,8},{1,9},{2,10},{3,11},{4,12},{5,13},{6,14},{7,15},{8,0},{9,1},... | collective-permute-start | bytes 12296 | tf_op jit(solution)/shard_map/ppermute | solution.py:29
  124.9 6.2 %collective-permute-done.30.refs_1_ = bf16[16,128]{1,0:T(8,128)(2,1)S(1)} collective-permute-done((bf16[16,128]{1,0:T(8,128)(2,1)S(1)}, bf16[16,128]{1,0:T(8,128)(2,1)S(1)}, u32[]{:S(2)}, u32[]{:S(2)}) %collective-permute-start.30) | collective-permute-done | bytes 4128 | tf_op jit(solution)/shard_map/ppermute | solution.py:29
  131.1 1.8 %update.3 = (f32[4,320,128]{2,1,0:T(8,128)S(1)}, bf16[4,320,128]{2,1,0:T(8,128)(2,1)S(1)}) custom-call(s32[4]{0:T(128)S(1)} %pad_add_fusion.place_ref, bf16[2560,640]{1,0:T(8,128)(2,1)S(1)} %get-tuple-element.120.weight_ref, f32[128,640]{1,0:T(8,128)S(1)} %get-tuple-element.109.kept_ref, f32[128,128]{1,0:T(8,128)S(1)} %get-tuple-element.110.totals_ref, ...), custom_call_target="tpu_custom_call" | custom-call | flops 419430400 | bytes 3641344 | tf_op jit(solution)/shard_map/update/pallas_call | solution.py:416
  133.0 1.6 %collective-permute-done.31 = bf16[4,320,128]{2,1,0:T(8,128)(2,1)S(1)} collective-permute-done((bf16[4,320,128]{2,1,0:T(8,128)(2,1)S(1)}, bf16[4,320,128]{2,1,0:T(8,128)(2,1)S(1)}, u32[]{:S(2)}, u32[]{:S(2)}) %collective-permute-start.31) | collective-permute-done | bytes 327712 | tf_op jit(solution)/shard_map/ppermute | solution.py:29
  134.7 1.2 collective-permute-start.32
  135.9 2.3 %collective-permute-start.33 = (bf16[320,128]{1,0:T(8,128)(2,1)S(1)}, bf16[320,128]{1,0:T(8,128)(2,1)S(1)}, u32[]{:S(2)}, u32[]{:S(2)}) collective-permute-start(bf16[320,128]{1,0:T(8,128)(2,1)S(1)} %get-tuple-element.135), channel_id=1, source_target_pairs={{0,4},{1,5},{2,6},{3,7},{4,0},{5,1},{6,2},{7,3},{8,12},{9,13},{10,... | collective-permute-start | bytes 245768 | tf_op jit(solution)/shard_map/ppermute | solution.py:29
  139.3 2.6 %collective-permute-done.34 = bf16[320,128]{1,0:T(8,128)(2,1)S(1)} collective-permute-done((bf16[320,128]{1,0:T(8,128)(2,1)S(1)}, bf16[320,128]{1,0:T(8,128)(2,1)S(1)}, u32[]{:S(2)}, u32[]{:S(2)}) %collective-permute-start.34) | collective-permute-done | bytes 81952 | tf_op jit(solution)/shard_map/ppermute | solution.py:29
  (75 shorter events, 10.4 us)
Async XLA Ops:
  3.5 20.9 %collective-permute-start.1 = (bf16[2,320,256]{2,1,0:T(8,128)(2,1)}, bf16[2,320,256]{2,1,0:T(8,128)(2,1)}, u32[]{:S(2)}, u32[]{:S(2)}) collective-permute-start(bf16[2,320,256]{2,1,0:T(8,128)(2,1)} %get-tuple-element.62), channel_id=1, source_target_pairs={{0,8},{1,9},{2,10},{3,11},{4,12},{5,13},{6,14},{7,15},{8,0},{9,1},... | collective-permute-start | bytes 983048 | tf_op jit(solution)/shard_map/ppermute | solution.py:484
  7.6 20.6 %collective-permute-start.4 = (bf16[128,1280]{1,0:T(8,128)(2,1)}, bf16[128,1280]{1,0:T(8,128)(2,1)}, u32[]{:S(2)}, u32[]{:S(2)}) collective-permute-start(bf16[128,1280]{1,0:T(8,128)(2,1)} %get-tuple-element.72), channel_id=1, source_target_pairs={{0,6},{1,7},{2,4},{3,5},{4,2},{5,3},{6,0},{7,1},{8,14},{9,15},{10,... | collective-permute-start | bytes 983048 | tf_op jit(solution)/shard_map/ppermute | solution.py:29
  10.2 26.7 %collective-permute-start.6 = (bf16[2,320,256]{2,1,0:T(8,128)(2,1)}, bf16[2,320,256]{2,1,0:T(8,128)(2,1)}, u32[]{:S(2)}, u32[]{:S(2)}) collective-permute-start(bf16[2,320,256]{2,1,0:T(8,128)(2,1)} %get-tuple-element.73), channel_id=1, source_target_pairs={{0,8},{1,9},{2,10},{3,11},{4,12},{5,13},{6,14},{7,15},{8,0},{9,1},... | collective-permute-start | bytes 983048 | tf_op jit(solution)/shard_map/ppermute | solution.py:484
  10.5 17.3 %collective-permute-start = (bf16[160,1280]{1,0:T(8,128)(2,1)}, bf16[160,1280]{1,0:T(8,128)(2,1)}, u32[]{:S(2)}, u32[]{:S(2)}) collective-permute-start(bf16[160,1280]{1,0:T(8,128)(2,1)} %get-tuple-element.60), channel_id=1, source_target_pairs={{0,2},{1,3},{2,0},{3,1},{4,6},{5,7},{6,4},{7,5},{8,10},{9,11},{10,... | collective-permute-start | bytes 1228808 | tf_op jit(solution)/shard_map/ppermute | solution.py:29
  11.0 28.7 %collective-permute-start.3 = (bf16[160,1280]{1,0:T(8,128)(2,1)}, bf16[160,1280]{1,0:T(8,128)(2,1)}, u32[]{:S(2)}, u32[]{:S(2)}) collective-permute-start(bf16[160,1280]{1,0:T(8,128)(2,1)} %get-tuple-element.71), channel_id=1, source_target_pairs={{0,4},{1,5},{2,6},{3,7},{4,0},{5,1},{6,2},{7,3},{8,12},{9,13},{10,... | collective-permute-start | bytes 1228808 | tf_op jit(solution)/shard_map/ppermute | solution.py:29
  24.4 15.4 %collective-permute-start.5 = (bf16[2,320,256]{2,1,0:T(8,128)(2,1)}, bf16[2,320,256]{2,1,0:T(8,128)(2,1)S(1)}, u32[]{:S(2)}, u32[]{:S(2)}) collective-permute-start(bf16[2,320,256]{2,1,0:T(8,128)(2,1)} %collective-permute-done.1.refs_8_), channel_id=1, source_target_pairs={{0,16},{16,0},{1,17},{17,1},{2,18},{18,2},{3,19},{19,3},{4,20},{20... | collective-permute-start | bytes 983048 | tf_op jit(solution)/shard_map/ppermute | solution.py:29
  24.8 1.3 copy-start.1
  26.1 1.0 copy-start.2
  27.8 16.2 %collective-permute-start.2 = (bf16[4,320,256]{2,1,0:T(8,128)(2,1)S(1)}, bf16[4,320,256]{2,1,0:T(8,128)(2,1)S(1)}, u32[]{:S(2)}, u32[]{:S(2)}) collective-permute-start(bf16[4,320,256]{2,1,0:T(8,128)(2,1)S(1)} %get-tuple-element.68), channel_id=1, source_target_pairs={{0,1},{1,0},{2,3},{3,2},{4,5},{5,4},{6,7},{7,6},{8,9},{9,8},{10,11... | collective-permute-start | bytes 1966088 | tf_op jit(solution)/shard_map/ppermute | solution.py:29
  28.2 13.0 %collective-permute-start.7 = (bf16[160,1280]{1,0:T(8,128)(2,1)S(1)}, bf16[160,1280]{1,0:T(8,128)(2,1)S(1)}, u32[]{:S(2)}, u32[]{:S(2)}) collective-permute-start(bf16[160,1280]{1,0:T(8,128)(2,1)S(1)} %copy-done.2), channel_id=1, source_target_pairs={{0,1},{1,0},{2,3},{3,2},{4,5},{5,4},{6,7},{7,6},{8,9},{9,8},{10,11... | collective-permute-start | bytes 1228808 | tf_op jit(solution)/shard_map/ppermute | solution.py:29
  36.9 6.6 %collective-permute-start.8 = (bf16[160,1280]{1,0:T(8,128)(2,1)}, bf16[160,1280]{1,0:T(8,128)(2,1)S(1)}, u32[]{:S(2)}, u32[]{:S(2)}) collective-permute-start(bf16[160,1280]{1,0:T(8,128)(2,1)} %collective-permute-done.refs_1_), channel_id=1, source_target_pairs={{0,1},{1,0},{2,3},{3,2},{4,5},{5,4},{6,7},{7,6},{8,9},{9,8},{10,11... | collective-permute-start | bytes 1228808 | tf_op jit(solution)/shard_map/ppermute | solution.py:29
  39.8 4.2 %collective-permute-start.9 = (bf16[160,1280]{1,0:T(8,128)(2,1)}, bf16[160,1280]{1,0:T(8,128)(2,1)S(1)}, u32[]{:S(2)}, u32[]{:S(2)}) collective-permute-start(bf16[160,1280]{1,0:T(8,128)(2,1)} %collective-permute-done.3.refs_2_), channel_id=1, source_target_pairs={{0,1},{1,0},{2,3},{3,2},{4,5},{5,4},{6,7},{7,6},{8,9},{9,8},{10,11... | collective-permute-start | bytes 1228808 | tf_op jit(solution)/shard_map/ppermute | solution.py:29
  39.8 4.1 %collective-permute-start.10 = (bf16[128,1280]{1,0:T(8,128)(2,1)}, bf16[128,1280]{1,0:T(8,128)(2,1)S(1)}, u32[]{:S(2)}, u32[]{:S(2)}) collective-permute-start(bf16[128,1280]{1,0:T(8,128)(2,1)} %collective-permute-done.4.refs_3_), channel_id=1, source_target_pairs={{0,1},{1,0},{2,3},{3,2},{4,5},{5,4},{6,7},{7,6},{8,9},{9,8},{10,11... | collective-permute-start | bytes 983048 | tf_op jit(solution)/shard_map/ppermute | solution.py:29
  41.3 10.3 %collective-permute-start.15 = (bf16[2,320,256]{2,1,0:T(8,128)(2,1)}, bf16[2,320,256]{2,1,0:T(8,128)(2,1)S(1)}, u32[]{:S(2)}, u32[]{:S(2)}) collective-permute-start(bf16[2,320,256]{2,1,0:T(8,128)(2,1)} %collective-permute-done.6.refs_8_), channel_id=1, source_target_pairs={{0,16},{16,0},{1,17},{17,1},{2,18},{18,2},{3,19},{19,3},{4,20},{20... | collective-permute-start | bytes 983048 | tf_op jit(solution)/shard_map/ppermute | solution.py:29
  43.5 4.4 %collective-permute-start.11 = (bf16[32,1280]{1,0:T(8,128)(2,1)S(1)}, bf16[32,1280]{1,0:T(8,128)(2,1)S(1)}, u32[]{:S(2)}, u32[]{:S(2)}) collective-permute-start(bf16[32,1280]{1,0:T(8,128)(2,1)S(1)} %slice.83), channel_id=1, source_target_pairs={{0,2},{1,3},{2,0},{3,1},{4,6},{5,7},{6,4},{7,5},{8,10},{9,11},{10,... | collective-permute-start | bytes 245768 | tf_op jit(solution)/shard_map/ppermute | solution.py:29
  47.9 8.3 %copy-start = (bf16[2560,640]{1,0:T(8,128)(2,1)S(1)}, bf16[2560,640]{1,0:T(8,128)(2,1)}, u32[]{:S(2)}) copy-start(bf16[2560,640]{1,0:T(8,128)(2,1)} %get-tuple-element.121.weight_ref) | copy-start | bytes 9830404
  47.9 8.3 %collective-permute-start.12 = (bf16[32,1280]{1,0:T(8,128)(2,1)S(1)}, bf16[32,1280]{1,0:T(8,128)(2,1)S(1)}, u32[]{:S(2)}, u32[]{:S(2)}) collective-permute-start(bf16[32,1280]{1,0:T(8,128)(2,1)S(1)} %collective-permute-done.11.refs_3_), channel_id=1, source_target_pairs={{0,1},{1,0},{2,3},{3,2},{4,5},{5,4},{6,7},{7,6},{8,9},{9,8},{10,11... | collective-permute-start | bytes 245768 | tf_op jit(solution)/shard_map/ppermute | solution.py:29
  47.9 16.3 %collective-permute-start.13 = (bf16[1024,256]{1,0:T(8,128)(2,1)S(1)}, bf16[1024,256]{1,0:T(8,128)(2,1)S(1)}, u32[]{:S(2)}, u32[]{:S(2)}) collective-permute-start(bf16[1024,256]{1,0:T(8,128)(2,1)S(1)} %get-tuple-element.88), channel_id=1, source_target_pairs={{0,4},{1,5},{2,6},{3,7},{4,0},{5,1},{6,2},{7,3},{8,12},{9,13},{10,... | collective-permute-start | bytes 1572872 | tf_op jit(solution)/shard_map/ppermute | solution.py:29
  48.7 15.5 %collective-permute-start.14 = (bf16[1024,256]{1,0:T(8,128)(2,1)S(1)}, bf16[1024,256]{1,0:T(8,128)(2,1)S(1)}, u32[]{:S(2)}, u32[]{:S(2)}) collective-permute-start(bf16[1024,256]{1,0:T(8,128)(2,1)S(1)} %get-tuple-element.89), channel_id=1, source_target_pairs={{0,2},{1,3},{2,0},{3,1},{4,6},{5,7},{6,4},{7,5},{8,10},{9,11},{10,... | collective-permute-start | bytes 1572872 | tf_op jit(solution)/shard_map/ppermute | solution.py:29
  54.5 22.6 %collective-permute-start.16 = (bf16[1024,256]{1,0:T(8,128)(2,1)S(1)}, bf16[1024,256]{1,0:T(8,128)(2,1)S(1)}, u32[]{:S(2)}, u32[]{:S(2)}) collective-permute-start(bf16[1024,256]{1,0:T(8,128)(2,1)S(1)} %get-tuple-element.93), channel_id=1, source_target_pairs={{0,6},{1,7},{2,4},{3,5},{4,2},{5,3},{6,0},{7,1},{8,14},{9,15},{10,... | collective-permute-start | bytes 1572872 | tf_op jit(solution)/shard_map/ppermute | solution.py:29
  56.2 25.6 %slice-start = ((s8[6553600]{0:T(1024)(128)(4,1)}), s8[2359296]{0:T(1024)(128)(4,1)S(1)}, s32[]{:S(2)}) async-start(s8[6553600]{0:T(1024)(128)(4,1)} %bitcast.53), calls=%async_computation | async-start | bytes 4718592
  59.0 18.6 %collective-permute-start.18 = (bf16[16,128]{1,0:T(8,128)(2,1)S(1)}, bf16[16,128]{1,0:T(8,128)(2,1)S(1)}, u32[]{:S(2)}, u32[]{:S(2)}) collective-permute-start(bf16[16,128]{1,0:T(8,128)(2,1)S(1)} %get-tuple-element.98), channel_id=1, source_target_pairs={{0,8},{1,9},{2,10},{3,11},{4,12},{5,13},{6,14},{7,15},{8,0},{9,1},... | collective-permute-start | bytes 12296 | tf_op jit(solution)/shard_map/ppermute | solution.py:29
  60.5 17.1 %collective-permute-start.17 = (bf16[128,640]{1,0:T(8,128)(2,1)S(1)}, bf16[128,640]{1,0:T(8,128)(2,1)S(1)}, u32[]{:S(2)}, u32[]{:S(2)}) collective-permute-start(bf16[128,640]{1,0:T(8,128)(2,1)S(1)} %get-tuple-element.97), channel_id=1, source_target_pairs={{0,8},{1,9},{2,10},{3,11},{4,12},{5,13},{6,14},{7,15},{8,0},{9,1},... | collective-permute-start | bytes 491528 | tf_op jit(solution)/shard_map/ppermute | solution.py:29
  64.2 17.6 %slice-start.1 = ((s8[6553600]{0:T(1024)(128)(4,1)}), s8[4194304]{0:T(1024)(128)(4,1)S(1)}, s32[]{:S(2)}) async-start(s8[6553600]{0:T(1024)(128)(4,1)} %bitcast.53), calls=%async_computation.1 | async-start | bytes 8388608
  78.8 4.6 %collective-permute-start.20 = (bf16[16,128]{1,0:T(8,128)(2,1)S(1)}, bf16[16,128]{1,0:T(8,128)(2,1)S(1)}, u32[]{:S(2)}, u32[]{:S(2)}) collective-permute-start(bf16[16,128]{1,0:T(8,128)(2,1)S(1)} %get-tuple-element.102), channel_id=1, source_target_pairs={{0,8},{1,9},{2,10},{3,11},{4,12},{5,13},{6,14},{7,15},{8,0},{9,1},... | collective-permute-start | bytes 12296 | tf_op jit(solution)/shard_map/ppermute | solution.py:29
  79.9 10.0 %collective-permute-start.19 = (bf16[128,640]{1,0:T(8,128)(2,1)S(1)}, bf16[128,640]{1,0:T(8,128)(2,1)S(1)}, u32[]{:S(2)}, u32[]{:S(2)}) collective-permute-start(bf16[128,640]{1,0:T(8,128)(2,1)S(1)} %get-tuple-element.101), channel_id=1, source_target_pairs={{0,8},{1,9},{2,10},{3,11},{4,12},{5,13},{6,14},{7,15},{8,0},{9,1},... | collective-permute-start | bytes 491528 | tf_op jit(solution)/shard_map/ppermute | solution.py:29
  91.8 1.7 %collective-permute-start.21 = (bf16[64,2560]{1,0:T(8,128)(2,1)S(1)}, bf16[64,2560]{1,0:T(8,128)(2,1)S(1)}, u32[]{:S(2)}, u32[]{:S(2)}) collective-permute-start(bf16[64,2560]{1,0:T(8,128)(2,1)S(1)} %get-tuple-element.104), channel_id=1, source_target_pairs={{0,1},{1,0},{2,3},{3,2},{4,5},{5,4},{6,7},{7,6},{8,9},{9,8},{10,11... | collective-permute-start | bytes 983048 | tf_op jit(solution)/shard_map/ppermute | solution.py:29
  93.6 6.3 %collective-permute-start.22 = (bf16[64,1280]{1,0:T(8,128)(2,1)S(1)}, bf16[64,1280]{1,0:T(8,128)(2,1)S(1)}, u32[]{:S(2)}, u32[]{:S(2)}) collective-permute-start(bf16[64,1280]{1,0:T(8,128)(2,1)S(1)} %get-tuple-element.138), channel_id=1, source_target_pairs={{0,2},{1,3},{2,0},{3,1},{4,6},{5,7},{6,4},{7,5},{8,10},{9,11},{10,... | collective-permute-start | bytes 491528 | tf_op jit(solution)/shard_map/ppermute | solution.py:29
  95.1 6.0 %collective-permute-start.24 = (bf16[64,1280]{1,0:T(8,128)(2,1)S(1)}, bf16[64,1280]{1,0:T(8,128)(2,1)S(1)}, u32[]{:S(2)}, u32[]{:S(2)}) collective-permute-start(bf16[64,1280]{1,0:T(8,128)(2,1)S(1)} %get-tuple-element.139), channel_id=1, source_target_pairs={{0,4},{1,5},{2,6},{3,7},{4,0},{5,1},{6,2},{7,3},{8,12},{9,13},{10,... | collective-permute-start | bytes 491528 | tf_op jit(solution)/shard_map/ppermute | solution.py:29
  101.1 5.4 %collective-permute-start.23 = (bf16[64,1280]{1,0:T(8,128)(2,1)S(1)}, bf16[64,1280]{1,0:T(8,128)(2,1)S(1)}, u32[]{:S(2)}, u32[]{:S(2)}) collective-permute-start(bf16[64,1280]{1,0:T(8,128)(2,1)S(1)} %get-tuple-element.136), channel_id=1, source_target_pairs={{0,4},{1,5},{2,6},{3,7},{4,0},{5,1},{6,2},{7,3},{8,12},{9,13},{10,... | collective-permute-start | bytes 491528 | tf_op jit(solution)/shard_map/ppermute | solution.py:29
  101.5 5.3 %collective-permute-start.25 = (bf16[64,1280]{1,0:T(8,128)(2,1)S(1)}, bf16[64,1280]{1,0:T(8,128)(2,1)S(1)}, u32[]{:S(2)}, u32[]{:S(2)}) collective-permute-start(bf16[64,1280]{1,0:T(8,128)(2,1)S(1)} %get-tuple-element.137), channel_id=1, source_target_pairs={{0,2},{1,3},{2,0},{3,1},{4,6},{5,7},{6,4},{7,5},{8,10},{9,11},{10,... | collective-permute-start | bytes 491528 | tf_op jit(solution)/shard_map/ppermute | solution.py:29
  106.9 1.7 %collective-permute-start.26 = (bf16[64,2560]{1,0:T(8,128)(2,1)S(1)}, bf16[64,2560]{1,0:T(8,128)(2,1)S(1)}, u32[]{:S(2)}, u32[]{:S(2)}) collective-permute-start(bf16[64,2560]{1,0:T(8,128)(2,1)S(1)} %add_convert_fusion.ours_ref), channel_id=1, source_target_pairs={{0,1},{1,0},{2,3},{3,2},{4,5},{5,4},{6,7},{7,6},{8,9},{9,8},{10,11... | collective-permute-start | bytes 983048 | tf_op jit(solution)/shard_map/ppermute | solution.py:29
  109.9 10.9 %collective-permute-start.27 = (bf16[128,640]{1,0:T(8,128)(2,1)S(1)}, bf16[128,640]{1,0:T(8,128)(2,1)S(1)}, u32[]{:S(2)}, u32[]{:S(2)}) collective-permute-start(bf16[128,640]{1,0:T(8,128)(2,1)S(1)} %get-tuple-element.107), channel_id=1, source_target_pairs={{0,8},{1,9},{2,10},{3,11},{4,12},{5,13},{6,14},{7,15},{8,0},{9,1},... | collective-permute-start | bytes 491528 | tf_op jit(solution)/shard_map/ppermute | solution.py:29
  112.0 8.8 %collective-permute-start.28 = (bf16[16,128]{1,0:T(8,128)(2,1)S(1)}, bf16[16,128]{1,0:T(8,128)(2,1)S(1)}, u32[]{:S(2)}, u32[]{:S(2)}) collective-permute-start(bf16[16,128]{1,0:T(8,128)(2,1)S(1)} %get-tuple-element.108), channel_id=1, source_target_pairs={{0,8},{1,9},{2,10},{3,11},{4,12},{5,13},{6,14},{7,15},{8,0},{9,1},... | collective-permute-start | bytes 12296 | tf_op jit(solution)/shard_map/ppermute | solution.py:29
  121.9 9.2 %collective-permute-start.29 = (bf16[128,640]{1,0:T(8,128)(2,1)S(1)}, bf16[128,640]{1,0:T(8,128)(2,1)S(1)}, u32[]{:S(2)}, u32[]{:S(2)}) collective-permute-start(bf16[128,640]{1,0:T(8,128)(2,1)S(1)} %get-tuple-element.111), channel_id=1, source_target_pairs={{0,8},{1,9},{2,10},{3,11},{4,12},{5,13},{6,14},{7,15},{8,0},{9,1},... | collective-permute-start | bytes 491528 | tf_op jit(solution)/shard_map/ppermute | solution.py:29
  122.0 9.1 %collective-permute-start.30 = (bf16[16,128]{1,0:T(8,128)(2,1)S(1)}, bf16[16,128]{1,0:T(8,128)(2,1)S(1)}, u32[]{:S(2)}, u32[]{:S(2)}) collective-permute-start(bf16[16,128]{1,0:T(8,128)(2,1)S(1)} %get-tuple-element.112), channel_id=1, source_target_pairs={{0,8},{1,9},{2,10},{3,11},{4,12},{5,13},{6,14},{7,15},{8,0},{9,1},... | collective-permute-start | bytes 12296 | tf_op jit(solution)/shard_map/ppermute | solution.py:29
  132.9 1.7 %collective-permute-start.31 = (bf16[4,320,128]{2,1,0:T(8,128)(2,1)S(1)}, bf16[4,320,128]{2,1,0:T(8,128)(2,1)S(1)}, u32[]{:S(2)}, u32[]{:S(2)}) collective-permute-start(bf16[4,320,128]{2,1,0:T(8,128)(2,1)S(1)} %get-tuple-element.114), channel_id=1, source_target_pairs={{0,1},{1,0},{2,3},{3,2},{4,5},{5,4},{6,7},{7,6},{8,9},{9,8},{10,11... | collective-permute-start | bytes 983048 | tf_op jit(solution)/shard_map/ppermute | solution.py:29
  134.7 4.6 %collective-permute-start.32 = (bf16[320,128]{1,0:T(8,128)(2,1)S(1)}, bf16[320,128]{1,0:T(8,128)(2,1)S(1)}, u32[]{:S(2)}, u32[]{:S(2)}) collective-permute-start(bf16[320,128]{1,0:T(8,128)(2,1)S(1)} %get-tuple-element.133), channel_id=1, source_target_pairs={{0,2},{1,3},{2,0},{3,1},{4,6},{5,7},{6,4},{7,5},{8,10},{9,11},{10,... | collective-permute-start | bytes 245768 | tf_op jit(solution)/shard_map/ppermute | solution.py:29
  135.9 6.0 %collective-permute-start.34 = (bf16[320,128]{1,0:T(8,128)(2,1)S(1)}, bf16[320,128]{1,0:T(8,128)(2,1)S(1)}, u32[]{:S(2)}, u32[]{:S(2)}) collective-permute-start(bf16[320,128]{1,0:T(8,128)(2,1)S(1)} %get-tuple-element.134), channel_id=1, source_target_pairs={{0,6},{1,7},{2,4},{3,5},{4,2},{5,3},{6,0},{7,1},{8,14},{9,15},{10,... | collective-permute-start | bytes 245768 | tf_op jit(solution)/shard_map/ppermute | solution.py:29
  135.9 6.3 %collective-permute-start.33 = (bf16[320,128]{1,0:T(8,128)(2,1)S(1)}, bf16[320,128]{1,0:T(8,128)(2,1)S(1)}, u32[]{:S(2)}, u32[]{:S(2)}) collective-permute-start(bf16[320,128]{1,0:T(8,128)(2,1)S(1)} %get-tuple-element.135), channel_id=1, source_target_pairs={{0,4},{1,5},{2,6},{3,7},{4,0},{5,1},{6,2},{7,3},{8,12},{9,13},{10,... | collective-permute-start | bytes 245768 | tf_op jit(solution)/shard_map/ppermute | solution.py:29

commit v10 on v9

--- a/solution.py
+++ b/solution.py
@@ -249,7 +249,8 @@
     )
 
 
-def query_kernel(lanes, place_ref, gain_ref, weight_ref, *refs):
+def query_kernel(lanes, gain_ref, weight_ref, *refs):
+    place_ref = here()
     piece_refs, refs = refs[:-9], refs[-9:]
     results, own_ref, (stream, turned, parts, sems) = refs[:4], refs[4], refs[5:]
     unit = stream.shape[0] // KVH
@@ -296,9 +297,7 @@
     spread = jnp.broadcast_to(squares, squares_ref.shape)
     squares_ref[...] = spread
     across = spread.T[:8]
-    high = across.astype(BF16)
-    squares_sent_ref[:8] = high
-    squares_sent_ref[8:] = (across - high.astype(F32)).astype(BF16)
+    squares_sent_ref[...] = parted(across)
 
 
 def both_cores(place_ref, ours_ref, theirs_ref, rows):
@@ -307,13 +306,14 @@
         rows[pl.ds(pl.multiple_of(which * half, half), half), :] = ref[...]
 
 
-def later_query_kernel(place_ref, gain_ref, weight_ref, ours_ref, theirs_ref, *refs):
+def later_query_kernel(gain_ref, weight_ref, ours_ref, theirs_ref, *refs):
     results, rows = refs[:-1], refs[-1]
-    both_cores(place_ref, ours_ref, theirs_ref, rows)
+    both_cores(here(), ours_ref, theirs_ref, rows)
     query_step(rows[...].astype(F32), gain_ref, weight_ref, *results)
 
 
-def own_rows_kernel(place_ref, ours_ref, theirs_ref, out_ref, rows, turned):
+def own_rows_kernel(ours_ref, theirs_ref, out_ref, rows, turned):
+    place_ref = here()
     both_cores(place_ref, ours_ref, theirs_ref, rows)
     unit = out_ref.shape[0]
     column = pl.multiple_of(place_ref[0] * 2 * unit, 2 * unit)
@@ -321,8 +321,14 @@
     out_ref[...] = turned[pl.ds(pl.multiple_of(place_ref[1] * unit, unit), unit), :].astype(BF16)
 
 
+def parted(across):
+    high = across.astype(BF16).astype(F32)
+    return jnp.concatenate([high, across - high], axis=0).astype(BF16)
+
+
 def spread_back(pair_ref, lanes):
-    across = pair_ref[:8].astype(F32) + pair_ref[8:].astype(F32)
+    pair = pair_ref[...].astype(F32)
+    across = pair[:8] + pair[8:]
     return jnp.concatenate([across, jnp.zeros((lanes - 8, lanes), F32)], axis=0).T
 
 
@@ -360,10 +366,7 @@
         out_ref[:, span] = part
         sent_ref[:, span] = part.astype(BF16)
     totals_ref[...] = totals
-    across = totals.T[:8]
-    high = across.astype(BF16)
-    totals_sent_ref[:8] = high
-    totals_sent_ref[8:] = (across - high.astype(F32)).astype(BF16)
+    totals_sent_ref[...] = parted(totals.T[:8])
 
 
 def attended_of(others, kept_ref, totals_ref, far):
@@ -382,7 +385,8 @@
     )
 
 
-def update_rows_kernel(others, place_ref, weight_ref, kept_ref, totals_ref, *refs):
+def update_rows_kernel(others, weight_ref, kept_ref, totals_ref, *refs):
+    place_ref = here()
     far, (own_ref, sent_ref, update) = refs[: 2 * others], refs[2 * others :]
     attended = attended_of(others, kept_ref, totals_ref, far)
     update[...] = lax.dot_general(
@@ -394,7 +398,8 @@
         out_ref[...] = rows.astype(out_ref.dtype)
 
 
-def update_kernel(others, place_ref, weight_ref, kept_ref, totals_ref, *refs):
+def update_kernel(others, weight_ref, kept_ref, totals_ref, *refs):
+    place_ref = here()
     far, (own_ref, sent_ref) = refs[: 2 * others], refs[2 * others :]
     unit = own_ref.shape[1]
     attended = attended_of(others, kept_ref, totals_ref, far)
@@ -641,7 +646,7 @@
             functools.partial(query_kernel, query_count),
             "query",
             wide + [small, spread, halved],
-            [place_now],
+            [],
             [gain[None, :], query_weight[section, 0]],
             [
                 pltpu.VMEM((slice_depth, query_count), BF16),
@@ -683,7 +688,7 @@
                     functools.partial(update_rows_kernel, tile_count - 1),
                     "update",
                     [jax.ShapeDtypeStruct(halved.shape, F32), halved],
-                    [place_now],
+                    [],
                     arrays,
                     [pltpu.VMEM((query_count, slice_depth), F32)],
                     flops,
@@ -697,7 +702,7 @@
                     later_query_kernel,
                     "query",
                     wide + [small, spread],
-                    [place_now],
+                    [],
                     [gain[None, :], query_weight[section + 1, 0], stream, theirs],
                     [pltpu.VMEM((query_count, slice_depth), BF16)],
                     flops,
@@ -706,7 +711,7 @@
                     own_rows_kernel,
                     "own_rows",
                     [jax.ShapeDtypeStruct(own_rows.shape, BF16)],
-                    [place_now],
+                    [],
                     [stream, theirs],
                     [
                         pltpu.VMEM((query_count, slice_depth), BF16),
@@ -719,7 +724,7 @@
                 functools.partial(update_kernel, tile_count - 1),
                 "update",
                 [jax.ShapeDtypeStruct(shape, F32), jax.ShapeDtypeStruct(shape, BF16)],
-                [place_now],
+                [],
                 arrays,
                 (),
                 flops,

time: 143 us -> 142 us (level)
  Pallas kernels: 21 us -> 18.6 us
    pallas_call x8, Pallas kernels: 11.5 us -> 9.17 us  [call(): pl.pallas_call(kernel, out_shape=out_shape, in_specs=[smem] * len(scalars...]
where the time goes in v10:
time: 142 us; the launch traced here: 141 us
  waiting for transfers between devices  75.6 us (53%)
  starting transfers between devices  33.6 us (24%)
  Pallas kernels  18.6 us (13%)
  local copies, waits for them, and re-layouts  11.6 us (8%)
  other arithmetic  1.7 us (1%)
    ppermute x33, waiting for transfers between devices, swapped(): return lax.ppermute(value, axis, pairs)  61.6 us
    ppermute x33, starting transfers between devices, swapped(): return lax.ppermute(value, axis, pairs)  29.2 us
    ppermute x2, waiting for transfers between devices, to_tile(): return lax.ppermute(value, ('groups', 'row'), pairs)  14 us
    pallas_call x8, Pallas kernels, call(): pl.pallas_call(kernel, out_shape=out_shape, in_specs=[smem] * len(scalars...  9.17 us
    pallas_call x2, Pallas kernels, projected(): pl.pallas_call(functools.partial(project_kernel, rows, heads, start, plac...  5.92 us
    squeeze x1, local copies, waits for them, and re-layouts, query_parts(): query_weight[section, 0]  5.15 us
    ppermute x2, starting transfers between devices, to_tile(): return lax.ppermute(value, ('groups', 'row'), pairs)  4.44 us
    pallas_call x1, Pallas kernels, prepared(): pl.pallas_call(functools.partial(prepare_kernel, pair, head_groups, group...  3.54 us
  transfers between devices with their start and end apart: 35, of which 21 were waited for; matrix products, arithmetic and copies ran while one was open for 7% of the time, Pallas kernels for 7%

profile of v10, /device:TPU:0, one launch (start us, length us, event | category | flops | bytes accessed | tf_op | source)
XLA Modules:
  0.0 141.5 jit_solution(17631544607766365898)
XLA Ops:
  0.0 3.5 %prepare.1 = (bf16[2,320,256]{2,1,0:T(8,128)(2,1)}, bf16[2,320,256]{2,1,0:T(8,128)(2,1)}, bf16[160,1280]{1,0:T(8,128)(2,1)}, bf16[160,1280]{1,0:T(8,128)(2,1)}, ...) custom-call(bf16[320,2048]{1,0:T(8,128)(2,1)} %weight_ref, bf16[128,5120]{1,0:T(8,128)(2,1)} %hidden_any.1, ...), custom_call_target="tpu_custom_call" | custom-call | tf_op jit(solution)/shard_map/prepare/pallas_call | solution.py:141
  3.5 4.1 %collective-permute-start.1 = (bf16[2,320,256]{2,1,0:T(8,128)(2,1)}, bf16[2,320,256]{2,1,0:T(8,128)(2,1)}, u32[]{:S(2)}, u32[]{:S(2)}) collective-permute-start(bf16[2,320,256]{2,1,0:T(8,128)(2,1)} %get-tuple-element.62), channel_id=1, source_target_pairs={{0,8},{1,9},{2,10},{3,11},{4,12},{5,13},{6,14},{7,15},{8,0},{9,1},... | collective-permute-start | bytes 983048 | tf_op jit(solution)/shard_map/ppermute | solution.py:489
  7.6 2.5 %collective-permute-start.4 = (bf16[128,1280]{1,0:T(8,128)(2,1)}, bf16[128,1280]{1,0:T(8,128)(2,1)}, u32[]{:S(2)}, u32[]{:S(2)}) collective-permute-start(bf16[128,1280]{1,0:T(8,128)(2,1)} %get-tuple-element.72), channel_id=1, source_target_pairs={{0,6},{1,7},{2,4},{3,5},{4,2},{5,3},{6,0},{7,1},{8,14},{9,15},{10,... | collective-permute-start | bytes 983048 | tf_op jit(solution)/shard_map/ppermute | solution.py:29
  11.2 1.0 slice_reduce_fusion
  12.2 0.9 fusion.16
  13.3 5.1 %slice_bitcast_fusion.3 = (bf16[2560,640]{1,0:T(8,128)(2,1)}, bf16[2560,640]{1,0:T(8,128)(2,1)S(1)}) fusion(bf16[2,1,2560,640]{3,2,1,0:T(8,128)(2,1)} %param.13), kind=kLoop, calls=%fused_computation.3 | loop fusion | bytes 13107200 | tf_op jit(solution)/shard_map/squeeze | solution.py:650
  18.8 5.6 %collective-permute-done.1.refs_8_ = bf16[2,320,256]{2,1,0:T(8,128)(2,1)} collective-permute-done((bf16[2,320,256]{2,1,0:T(8,128)(2,1)}, bf16[2,320,256]{2,1,0:T(8,128)(2,1)}, u32[]{:S(2)}, u32[]{:S(2)}) %collective-permute-start.1) | collective-permute-done | bytes 327712 | tf_op jit(solution)/shard_map/ppermute | solution.py:489
  24.8 1.3 copy-done.1
  26.1 1.0 copy-done.2
  28.5 8.4 %collective-permute-done.6.refs_8_ = bf16[2,320,256]{2,1,0:T(8,128)(2,1)} collective-permute-done((bf16[2,320,256]{2,1,0:T(8,128)(2,1)}, bf16[2,320,256]{2,1,0:T(8,128)(2,1)}, u32[]{:S(2)}, u32[]{:S(2)}) %collective-permute-start.6) | collective-permute-done | bytes 327712 | tf_op jit(solution)/shard_map/ppermute | solution.py:489
  36.9 2.9 %collective-permute-done.3.refs_2_ = bf16[160,1280]{1,0:T(8,128)(2,1)} collective-permute-done((bf16[160,1280]{1,0:T(8,128)(2,1)}, bf16[160,1280]{1,0:T(8,128)(2,1)}, u32[]{:S(2)}, u32[]{:S(2)}) %collective-permute-start.3) | collective-permute-done | bytes 409632 | tf_op jit(solution)/shard_map/ppermute | solution.py:29
  40.4 0.9 slice.83
  41.3 2.2 %collective-permute-start.15 = (bf16[2,320,256]{2,1,0:T(8,128)(2,1)}, bf16[2,320,256]{2,1,0:T(8,128)(2,1)S(1)}, u32[]{:S(2)}, u32[]{:S(2)}) collective-permute-start(bf16[2,320,256]{2,1,0:T(8,128)(2,1)} %collective-permute-done.6.refs_8_), channel_id=1, source_target_pairs={{0,16},{16,0},{1,17},{17,1},{2,18},{18,2},{3,19},{19,3},{4,20},{20... | collective-permute-start | bytes 983048 | tf_op jit(solution)/shard_map/ppermute | solution.py:29
  44.0 3.0 %project.2 = (bf16[1024,256]{1,0:T(8,128)(2,1)S(1)}, bf16[1024,256]{1,0:T(8,128)(2,1)S(1)}) custom-call(s32[2]{0:T(128)S(1)} %pad_add_fusion.first_ref, bf16[4,320,256]{2,1,0:T(8,128)(2,1)S(1)} %get-tuple-element.67.kept_ref, bf16[4,320,256]{2,1,0:T(8,128)(2,1)S(1)} %collective-permute-done.2.traded_ref, bf16[160,1280]{1,0:T(8,128)(2,1)S(1)} %get-tuple-element.80.refs_0_, ...), custom_call_target="tpu_custom_call" | custom-call | flops 10737418240 | bytes 2621440 | tf_op jit(solution)/shard_map/project/pallas_call | solution.py:235
  47.0 0.9 collective-permute-done.11.refs_3_
  48.7 1.3 collective-permute-start.14
  50.0 1.6 %collective-permute-done.15.refs_9_ = bf16[2,320,256]{2,1,0:T(8,128)(2,1)S(1)} collective-permute-done((bf16[2,320,256]{2,1,0:T(8,128)(2,1)}, bf16[2,320,256]{2,1,0:T(8,128)(2,1)S(1)}, u32[]{:S(2)}, u32[]{:S(2)}) %collective-permute-start.15) | collective-permute-done | bytes 327712 | tf_op jit(solution)/shard_map/ppermute | solution.py:29
  51.6 3.0 %project.3 = (bf16[1024,256]{1,0:T(8,128)(2,1)S(1)}, bf16[1024,256]{1,0:T(8,128)(2,1)S(1)}) custom-call(s32[2]{0:T(128)S(1)} %pad_add_fusion.first_ref, bf16[4,320,256]{2,1,0:T(8,128)(2,1)S(1)} %get-tuple-element.67.kept_ref, bf16[4,320,256]{2,1,0:T(8,128)(2,1)S(1)} %collective-permute-done.2.traded_ref, bf16[160,1280]{1,0:T(8,128)(2,1)S(1)} %get-tuple-element.80.refs_0_, ...), custom_call_target="tpu_custom_call" | custom-call | flops 10737418240 | bytes 2621440 | tf_op jit(solution)/shard_map/project/pallas_call | solution.py:235
  54.5 1.6 %collective-permute-start.16 = (bf16[1024,256]{1,0:T(8,128)(2,1)S(1)}, bf16[1024,256]{1,0:T(8,128)(2,1)S(1)}, u32[]{:S(2)}, u32[]{:S(2)}) collective-permute-start(bf16[1024,256]{1,0:T(8,128)(2,1)S(1)} %get-tuple-element.93), channel_id=1, source_target_pairs={{0,6},{1,7},{2,4},{3,5},{4,2},{5,3},{6,0},{7,1},{8,14},{9,15},{10,... | collective-permute-start | bytes 1572872 | tf_op jit(solution)/shard_map/ppermute | solution.py:29
  56.2 2.5 %query.2 = (bf16[128,640]{1,0:T(8,128)(2,1)S(1)}, f32[128,640]{1,0:T(8,128)S(1)}, bf16[16,128]{1,0:T(8,128)(2,1)S(1)}, f32[128,128]{1,0:T(8,128)S(1)}, bf16[64,2560]{1,0:T(8,128)(2,1)S(1)}) custom-call(f32[1,2560]{1,0:T(1,128)S(1)} %constant_dynamic-slice_fusion.1.gain_ref, bf16[2560,640]{1,0:T(8,128)(2,1)S(1)} %copy-done, ...), custom_call_target="tpu_custom_call" | custom-call | flops 419430400 | bytes 3281920 | tf_op jit(solution)/shard_map/query/pallas_call | solution.py:421
  58.7 1.5 %collective-permute-start.18 = (bf16[16,128]{1,0:T(8,128)(2,1)S(1)}, bf16[16,128]{1,0:T(8,128)(2,1)S(1)}, u32[]{:S(2)}, u32[]{:S(2)}) collective-permute-start(bf16[16,128]{1,0:T(8,128)(2,1)S(1)} %get-tuple-element.98), channel_id=1, source_target_pairs={{0,8},{1,9},{2,10},{3,11},{4,12},{5,13},{6,14},{7,15},{8,0},{9,1},... | collective-permute-start | bytes 12296 | tf_op jit(solution)/shard_map/ppermute | solution.py:29
  60.2 1.5 %collective-permute-start.17 = (bf16[128,640]{1,0:T(8,128)(2,1)S(1)}, bf16[128,640]{1,0:T(8,128)(2,1)S(1)}, u32[]{:S(2)}, u32[]{:S(2)}) collective-permute-start(bf16[128,640]{1,0:T(8,128)(2,1)S(1)} %get-tuple-element.97), channel_id=1, source_target_pairs={{0,8},{1,9},{2,10},{3,11},{4,12},{5,13},{6,14},{7,15},{8,0},{9,1},... | collective-permute-start | bytes 491528 | tf_op jit(solution)/shard_map/ppermute | solution.py:29
  61.6 2.1 %collective-permute-done.14 = bf16[1024,256]{1,0:T(8,128)(2,1)S(1)} collective-permute-done((bf16[1024,256]{1,0:T(8,128)(2,1)S(1)}, bf16[1024,256]{1,0:T(8,128)(2,1)S(1)}, u32[]{:S(2)}, u32[]{:S(2)}) %collective-permute-start.14) | collective-permute-done | bytes 524320 | tf_op jit(solution)/shard_map/ppermute | solution.py:29
  64.0 13.2 %collective-permute-done.16 = bf16[1024,256]{1,0:T(8,128)(2,1)S(1)} collective-permute-done((bf16[1024,256]{1,0:T(8,128)(2,1)S(1)}, bf16[1024,256]{1,0:T(8,128)(2,1)S(1)}, u32[]{:S(2)}, u32[]{:S(2)}) %collective-permute-start.16) | collective-permute-done | bytes 524320 | tf_op jit(solution)/shard_map/ppermute | solution.py:29
  77.7 1.1 attend.2
  78.8 1.1 collective-permute-start.20
  79.9 1.9 %collective-permute-start.19 = (bf16[128,640]{1,0:T(8,128)(2,1)S(1)}, bf16[128,640]{1,0:T(8,128)(2,1)S(1)}, u32[]{:S(2)}, u32[]{:S(2)}) collective-permute-start(bf16[128,640]{1,0:T(8,128)(2,1)S(1)} %get-tuple-element.101), channel_id=1, source_target_pairs={{0,8},{1,9},{2,10},{3,11},{4,12},{5,13},{6,14},{7,15},{8,0},{9,1},... | collective-permute-start | bytes 491528 | tf_op jit(solution)/shard_map/ppermute | solution.py:29
  82.4 1.0 collective-permute-done.20.refs_1_
  83.4 6.5 %collective-permute-done.19.refs_0_ = bf16[128,640]{1,0:T(8,128)(2,1)S(1)} collective-permute-done((bf16[128,640]{1,0:T(8,128)(2,1)S(1)}, bf16[128,640]{1,0:T(8,128)(2,1)S(1)}, u32[]{:S(2)}, u32[]{:S(2)}) %collective-permute-start.19) | collective-permute-done | bytes 163872 | tf_op jit(solution)/shard_map/ppermute | solution.py:29
  89.9 1.5 %update.2 = (f32[64,2560]{1,0:T(8,128)S(1)}, bf16[64,2560]{1,0:T(8,128)(2,1)S(1)}) custom-call(bf16[2560,640]{1,0:T(8,128)(2,1)S(1)} %get-tuple-element.119.weight_ref, f32[128,640]{1,0:T(8,128)S(1)} %get-tuple-element.99.kept_ref, f32[128,128]{1,0:T(8,128)S(1)} %get-tuple-element.100.totals_ref, bf16[128,640]{1,0:T(8,128)(2,1)S(1)} %collective-permute-done.19.refs_0_, ...), custom_call_target="tpu_custom_call" | custom-call | flops 419430400 | bytes 3641344 | tf_op jit(solution)/shard_map/update/pallas_call | solution.py:421
  91.5 1.6 %collective-permute-done.21 = bf16[64,2560]{1,0:T(8,128)(2,1)S(1)} collective-permute-done((bf16[64,2560]{1,0:T(8,128)(2,1)S(1)}, bf16[64,2560]{1,0:T(8,128)(2,1)S(1)}, u32[]{:S(2)}, u32[]{:S(2)}) %collective-permute-start.21) | collective-permute-done | bytes 327712 | tf_op jit(solution)/shard_map/ppermute | solution.py:29
  93.2 1.5 %collective-permute-start.22 = (bf16[64,1280]{1,0:T(8,128)(2,1)S(1)}, bf16[64,1280]{1,0:T(8,128)(2,1)S(1)}, u32[]{:S(2)}, u32[]{:S(2)}) collective-permute-start(bf16[64,1280]{1,0:T(8,128)(2,1)S(1)} %get-tuple-element.138), channel_id=1, source_target_pairs={{0,2},{1,3},{2,0},{3,1},{4,6},{5,7},{6,4},{7,5},{8,10},{9,11},{10,... | collective-permute-start | bytes 491528 | tf_op jit(solution)/shard_map/ppermute | solution.py:29
  94.7 4.8 %collective-permute-done.22 = bf16[64,1280]{1,0:T(8,128)(2,1)S(1)} collective-permute-done((bf16[64,1280]{1,0:T(8,128)(2,1)S(1)}, bf16[64,1280]{1,0:T(8,128)(2,1)S(1)}, u32[]{:S(2)}, u32[]{:S(2)}) %collective-permute-start.22) | collective-permute-done | bytes 163872 | tf_op jit(solution)/shard_map/ppermute | solution.py:29
  99.5 1.1 collective-permute-done.24
  101.7 4.4 %collective-permute-done.23 = bf16[64,1280]{1,0:T(8,128)(2,1)S(1)} collective-permute-done((bf16[64,1280]{1,0:T(8,128)(2,1)S(1)}, bf16[64,1280]{1,0:T(8,128)(2,1)S(1)}, u32[]{:S(2)}, u32[]{:S(2)}) %collective-permute-start.23) | collective-permute-done | bytes 163872 | tf_op jit(solution)/shard_map/ppermute | solution.py:29
  106.6 1.6 %collective-permute-done.26.theirs_ref = bf16[64,2560]{1,0:T(8,128)(2,1)S(1)} collective-permute-done((bf16[64,2560]{1,0:T(8,128)(2,1)S(1)}, bf16[64,2560]{1,0:T(8,128)(2,1)S(1)}, u32[]{:S(2)}, u32[]{:S(2)}) %collective-permute-start.26) | collective-permute-done | bytes 327712 | tf_op jit(solution)/shard_map/ppermute | solution.py:29
  109.0 2.1 %collective-permute-start.27 = (bf16[128,640]{1,0:T(8,128)(2,1)S(1)}, bf16[128,640]{1,0:T(8,128)(2,1)S(1)}, u32[]{:S(2)}, u32[]{:S(2)}) collective-permute-start(bf16[128,640]{1,0:T(8,128)(2,1)S(1)} %get-tuple-element.107), channel_id=1, source_target_pairs={{0,8},{1,9},{2,10},{3,11},{4,12},{5,13},{6,14},{7,15},{8,0},{9,1},... | collective-permute-start | bytes 491528 | tf_op jit(solution)/shard_map/ppermute | solution.py:29
  111.1 0.9 collective-permute-start.28
  111.9 7.9 %collective-permute-done.28.refs_3_ = bf16[16,128]{1,0:T(8,128)(2,1)S(1)} collective-permute-done((bf16[16,128]{1,0:T(8,128)(2,1)S(1)}, bf16[16,128]{1,0:T(8,128)(2,1)S(1)}, u32[]{:S(2)}, u32[]{:S(2)}) %collective-permute-start.28) | collective-permute-done | bytes 4128 | tf_op jit(solution)/shard_map/ppermute | solution.py:29
  119.9 1.1 attend.3
  121.1 2.9 %collective-permute-start.30 = (bf16[16,128]{1,0:T(8,128)(2,1)S(1)}, bf16[16,128]{1,0:T(8,128)(2,1)S(1)}, u32[]{:S(2)}, u32[]{:S(2)}) collective-permute-start(bf16[16,128]{1,0:T(8,128)(2,1)S(1)} %get-tuple-element.112), channel_id=1, source_target_pairs={{0,8},{1,9},{2,10},{3,11},{4,12},{5,13},{6,14},{7,15},{8,0},{9,1},... | collective-permute-start | bytes 12296 | tf_op jit(solution)/shard_map/ppermute | solution.py:29
  124.0 6.2 %collective-permute-done.30.refs_1_ = bf16[16,128]{1,0:T(8,128)(2,1)S(1)} collective-permute-done((bf16[16,128]{1,0:T(8,128)(2,1)S(1)}, bf16[16,128]{1,0:T(8,128)(2,1)S(1)}, u32[]{:S(2)}, u32[]{:S(2)}) %collective-permute-start.30) | collective-permute-done | bytes 4128 | tf_op jit(solution)/shard_map/ppermute | solution.py:29
  130.2 1.2 update.3
  131.6 1.6 %collective-permute-done.31 = bf16[4,320,128]{2,1,0:T(8,128)(2,1)S(1)} collective-permute-done((bf16[4,320,128]{2,1,0:T(8,128)(2,1)S(1)}, bf16[4,320,128]{2,1,0:T(8,128)(2,1)S(1)}, u32[]{:S(2)}, u32[]{:S(2)}) %collective-permute-start.31) | collective-permute-done | bytes 327712 | tf_op jit(solution)/shard_map/ppermute | solution.py:29
  133.3 1.2 collective-permute-start.32
  134.5 2.3 %collective-permute-start.33 = (bf16[320,128]{1,0:T(8,128)(2,1)S(1)}, bf16[320,128]{1,0:T(8,128)(2,1)S(1)}, u32[]{:S(2)}, u32[]{:S(2)}) collective-permute-start(bf16[320,128]{1,0:T(8,128)(2,1)S(1)} %get-tuple-element.135), channel_id=1, source_target_pairs={{0,4},{1,5},{2,6},{3,7},{4,0},{5,1},{6,2},{7,3},{8,12},{9,13},{10,... | collective-permute-start | bytes 245768 | tf_op jit(solution)/shard_map/ppermute | solution.py:29
  137.1 0.8 collective-permute-done.32
  137.8 2.6 %collective-permute-done.34 = bf16[320,128]{1,0:T(8,128)(2,1)S(1)} collective-permute-done((bf16[320,128]{1,0:T(8,128)(2,1)S(1)}, bf16[320,128]{1,0:T(8,128)(2,1)S(1)}, u32[]{:S(2)}, u32[]{:S(2)}) %collective-permute-start.34) | collective-permute-done | bytes 81952 | tf_op jit(solution)/shard_map/ppermute | solution.py:29
  (75 shorter events, 10.3 us)
Async XLA Ops:
  3.5 20.9 %collective-permute-start.1 = (bf16[2,320,256]{2,1,0:T(8,128)(2,1)}, bf16[2,320,256]{2,1,0:T(8,128)(2,1)}, u32[]{:S(2)}, u32[]{:S(2)}) collective-permute-start(bf16[2,320,256]{2,1,0:T(8,128)(2,1)} %get-tuple-element.62), channel_id=1, source_target_pairs={{0,8},{1,9},{2,10},{3,11},{4,12},{5,13},{6,14},{7,15},{8,0},{9,1},... | collective-permute-start | bytes 983048 | tf_op jit(solution)/shard_map/ppermute | solution.py:489
  7.6 20.6 %collective-permute-start.4 = (bf16[128,1280]{1,0:T(8,128)(2,1)}, bf16[128,1280]{1,0:T(8,128)(2,1)}, u32[]{:S(2)}, u32[]{:S(2)}) collective-permute-start(bf16[128,1280]{1,0:T(8,128)(2,1)} %get-tuple-element.72), channel_id=1, source_target_pairs={{0,6},{1,7},{2,4},{3,5},{4,2},{5,3},{6,0},{7,1},{8,14},{9,15},{10,... | collective-permute-start | bytes 983048 | tf_op jit(solution)/shard_map/ppermute | solution.py:29
  10.2 26.7 %collective-permute-start.6 = (bf16[2,320,256]{2,1,0:T(8,128)(2,1)}, bf16[2,320,256]{2,1,0:T(8,128)(2,1)}, u32[]{:S(2)}, u32[]{:S(2)}) collective-permute-start(bf16[2,320,256]{2,1,0:T(8,128)(2,1)} %get-tuple-element.73), channel_id=1, source_target_pairs={{0,8},{1,9},{2,10},{3,11},{4,12},{5,13},{6,14},{7,15},{8,0},{9,1},... | collective-permute-start | bytes 983048 | tf_op jit(solution)/shard_map/ppermute | solution.py:489
  10.5 17.3 %collective-permute-start = (bf16[160,1280]{1,0:T(8,128)(2,1)}, bf16[160,1280]{1,0:T(8,128)(2,1)}, u32[]{:S(2)}, u32[]{:S(2)}) collective-permute-start(bf16[160,1280]{1,0:T(8,128)(2,1)} %get-tuple-element.60), channel_id=1, source_target_pairs={{0,2},{1,3},{2,0},{3,1},{4,6},{5,7},{6,4},{7,5},{8,10},{9,11},{10,... | collective-permute-start | bytes 1228808 | tf_op jit(solution)/shard_map/ppermute | solution.py:29
  11.0 28.7 %collective-permute-start.3 = (bf16[160,1280]{1,0:T(8,128)(2,1)}, bf16[160,1280]{1,0:T(8,128)(2,1)}, u32[]{:S(2)}, u32[]{:S(2)}) collective-permute-start(bf16[160,1280]{1,0:T(8,128)(2,1)} %get-tuple-element.71), channel_id=1, source_target_pairs={{0,4},{1,5},{2,6},{3,7},{4,0},{5,1},{6,2},{7,3},{8,12},{9,13},{10,... | collective-permute-start | bytes 1228808 | tf_op jit(solution)/shard_map/ppermute | solution.py:29
  24.4 15.4 %collective-permute-start.5 = (bf16[2,320,256]{2,1,0:T(8,128)(2,1)}, bf16[2,320,256]{2,1,0:T(8,128)(2,1)S(1)}, u32[]{:S(2)}, u32[]{:S(2)}) collective-permute-start(bf16[2,320,256]{2,1,0:T(8,128)(2,1)} %collective-permute-done.1.refs_8_), channel_id=1, source_target_pairs={{0,16},{16,0},{1,17},{17,1},{2,18},{18,2},{3,19},{19,3},{4,20},{20... | collective-permute-start | bytes 983048 | tf_op jit(solution)/shard_map/ppermute | solution.py:29
  24.8 1.3 copy-start.1
  26.1 1.0 copy-start.2
  27.8 16.2 %collective-permute-start.2 = (bf16[4,320,256]{2,1,0:T(8,128)(2,1)S(1)}, bf16[4,320,256]{2,1,0:T(8,128)(2,1)S(1)}, u32[]{:S(2)}, u32[]{:S(2)}) collective-permute-start(bf16[4,320,256]{2,1,0:T(8,128)(2,1)S(1)} %get-tuple-element.68), channel_id=1, source_target_pairs={{0,1},{1,0},{2,3},{3,2},{4,5},{5,4},{6,7},{7,6},{8,9},{9,8},{10,11... | collective-permute-start | bytes 1966088 | tf_op jit(solution)/shard_map/ppermute | solution.py:29
  28.2 13.0 %collective-permute-start.7 = (bf16[160,1280]{1,0:T(8,128)(2,1)S(1)}, bf16[160,1280]{1,0:T(8,128)(2,1)S(1)}, u32[]{:S(2)}, u32[]{:S(2)}) collective-permute-start(bf16[160,1280]{1,0:T(8,128)(2,1)S(1)} %copy-done.2), channel_id=1, source_target_pairs={{0,1},{1,0},{2,3},{3,2},{4,5},{5,4},{6,7},{7,6},{8,9},{9,8},{10,11... | collective-permute-start | bytes 1228808 | tf_op jit(solution)/shard_map/ppermute | solution.py:29
  36.9 6.6 %collective-permute-start.8 = (bf16[160,1280]{1,0:T(8,128)(2,1)}, bf16[160,1280]{1,0:T(8,128)(2,1)S(1)}, u32[]{:S(2)}, u32[]{:S(2)}) collective-permute-start(bf16[160,1280]{1,0:T(8,128)(2,1)} %collective-permute-done.refs_1_), channel_id=1, source_target_pairs={{0,1},{1,0},{2,3},{3,2},{4,5},{5,4},{6,7},{7,6},{8,9},{9,8},{10,11... | collective-permute-start | bytes 1228808 | tf_op jit(solution)/shard_map/ppermute | solution.py:29
  39.8 4.2 %collective-permute-start.9 = (bf16[160,1280]{1,0:T(8,128)(2,1)}, bf16[160,1280]{1,0:T(8,128)(2,1)S(1)}, u32[]{:S(2)}, u32[]{:S(2)}) collective-permute-start(bf16[160,1280]{1,0:T(8,128)(2,1)} %collective-permute-done.3.refs_2_), channel_id=1, source_target_pairs={{0,1},{1,0},{2,3},{3,2},{4,5},{5,4},{6,7},{7,6},{8,9},{9,8},{10,11... | collective-permute-start | bytes 1228808 | tf_op jit(solution)/shard_map/ppermute | solution.py:29
  39.8 4.1 %collective-permute-start.10 = (bf16[128,1280]{1,0:T(8,128)(2,1)}, bf16[128,1280]{1,0:T(8,128)(2,1)S(1)}, u32[]{:S(2)}, u32[]{:S(2)}) collective-permute-start(bf16[128,1280]{1,0:T(8,128)(2,1)} %collective-permute-done.4.refs_3_), channel_id=1, source_target_pairs={{0,1},{1,0},{2,3},{3,2},{4,5},{5,4},{6,7},{7,6},{8,9},{9,8},{10,11... | collective-permute-start | bytes 983048 | tf_op jit(solution)/shard_map/ppermute | solution.py:29
  41.3 10.3 %collective-permute-start.15 = (bf16[2,320,256]{2,1,0:T(8,128)(2,1)}, bf16[2,320,256]{2,1,0:T(8,128)(2,1)S(1)}, u32[]{:S(2)}, u32[]{:S(2)}) collective-permute-start(bf16[2,320,256]{2,1,0:T(8,128)(2,1)} %collective-permute-done.6.refs_8_), channel_id=1, source_target_pairs={{0,16},{16,0},{1,17},{17,1},{2,18},{18,2},{3,19},{19,3},{4,20},{20... | collective-permute-start | bytes 983048 | tf_op jit(solution)/shard_map/ppermute | solution.py:29
  43.5 4.4 %collective-permute-start.11 = (bf16[32,1280]{1,0:T(8,128)(2,1)S(1)}, bf16[32,1280]{1,0:T(8,128)(2,1)S(1)}, u32[]{:S(2)}, u32[]{:S(2)}) collective-permute-start(bf16[32,1280]{1,0:T(8,128)(2,1)S(1)} %slice.83), channel_id=1, source_target_pairs={{0,2},{1,3},{2,0},{3,1},{4,6},{5,7},{6,4},{7,5},{8,10},{9,11},{10,... | collective-permute-start | bytes 245768 | tf_op jit(solution)/shard_map/ppermute | solution.py:29
  47.9 8.3 %copy-start = (bf16[2560,640]{1,0:T(8,128)(2,1)S(1)}, bf16[2560,640]{1,0:T(8,128)(2,1)}, u32[]{:S(2)}) copy-start(bf16[2560,640]{1,0:T(8,128)(2,1)} %get-tuple-element.121.weight_ref) | copy-start | bytes 9830404
  47.9 8.3 %collective-permute-start.12 = (bf16[32,1280]{1,0:T(8,128)(2,1)S(1)}, bf16[32,1280]{1,0:T(8,128)(2,1)S(1)}, u32[]{:S(2)}, u32[]{:S(2)}) collective-permute-start(bf16[32,1280]{1,0:T(8,128)(2,1)S(1)} %collective-permute-done.11.refs_3_), channel_id=1, source_target_pairs={{0,1},{1,0},{2,3},{3,2},{4,5},{5,4},{6,7},{7,6},{8,9},{9,8},{10,11... | collective-permute-start | bytes 245768 | tf_op jit(solution)/shard_map/ppermute | solution.py:29
  47.9 16.0 %collective-permute-start.13 = (bf16[1024,256]{1,0:T(8,128)(2,1)S(1)}, bf16[1024,256]{1,0:T(8,128)(2,1)S(1)}, u32[]{:S(2)}, u32[]{:S(2)}) collective-permute-start(bf16[1024,256]{1,0:T(8,128)(2,1)S(1)} %get-tuple-element.88), channel_id=1, source_target_pairs={{0,4},{1,5},{2,6},{3,7},{4,0},{5,1},{6,2},{7,3},{8,12},{9,13},{10,... | collective-permute-start | bytes 1572872 | tf_op jit(solution)/shard_map/ppermute | solution.py:29
  48.7 15.1 %collective-permute-start.14 = (bf16[1024,256]{1,0:T(8,128)(2,1)S(1)}, bf16[1024,256]{1,0:T(8,128)(2,1)S(1)}, u32[]{:S(2)}, u32[]{:S(2)}) collective-permute-start(bf16[1024,256]{1,0:T(8,128)(2,1)S(1)} %get-tuple-element.89), channel_id=1, source_target_pairs={{0,2},{1,3},{2,0},{3,1},{4,6},{5,7},{6,4},{7,5},{8,10},{9,11},{10,... | collective-permute-start | bytes 1572872 | tf_op jit(solution)/shard_map/ppermute | solution.py:29
  54.5 22.6 %collective-permute-start.16 = (bf16[1024,256]{1,0:T(8,128)(2,1)S(1)}, bf16[1024,256]{1,0:T(8,128)(2,1)S(1)}, u32[]{:S(2)}, u32[]{:S(2)}) collective-permute-start(bf16[1024,256]{1,0:T(8,128)(2,1)S(1)} %get-tuple-element.93), channel_id=1, source_target_pairs={{0,6},{1,7},{2,4},{3,5},{4,2},{5,3},{6,0},{7,1},{8,14},{9,15},{10,... | collective-permute-start | bytes 1572872 | tf_op jit(solution)/shard_map/ppermute | solution.py:29
  56.2 25.6 %slice-start = ((s8[6553600]{0:T(1024)(128)(4,1)}), s8[2359296]{0:T(1024)(128)(4,1)S(1)}, s32[]{:S(2)}) async-start(s8[6553600]{0:T(1024)(128)(4,1)} %bitcast.53), calls=%async_computation | async-start | bytes 4718592
  58.7 19.0 %collective-permute-start.18 = (bf16[16,128]{1,0:T(8,128)(2,1)S(1)}, bf16[16,128]{1,0:T(8,128)(2,1)S(1)}, u32[]{:S(2)}, u32[]{:S(2)}) collective-permute-start(bf16[16,128]{1,0:T(8,128)(2,1)S(1)} %get-tuple-element.98), channel_id=1, source_target_pairs={{0,8},{1,9},{2,10},{3,11},{4,12},{5,13},{6,14},{7,15},{8,0},{9,1},... | collective-permute-start | bytes 12296 | tf_op jit(solution)/shard_map/ppermute | solution.py:29
  60.2 17.5 %collective-permute-start.17 = (bf16[128,640]{1,0:T(8,128)(2,1)S(1)}, bf16[128,640]{1,0:T(8,128)(2,1)S(1)}, u32[]{:S(2)}, u32[]{:S(2)}) collective-permute-start(bf16[128,640]{1,0:T(8,128)(2,1)S(1)} %get-tuple-element.97), channel_id=1, source_target_pairs={{0,8},{1,9},{2,10},{3,11},{4,12},{5,13},{6,14},{7,15},{8,0},{9,1},... | collective-permute-start | bytes 491528 | tf_op jit(solution)/shard_map/ppermute | solution.py:29
  63.9 17.9 %slice-start.1 = ((s8[6553600]{0:T(1024)(128)(4,1)}), s8[4194304]{0:T(1024)(128)(4,1)S(1)}, s32[]{:S(2)}) async-start(s8[6553600]{0:T(1024)(128)(4,1)} %bitcast.53), calls=%async_computation.1 | async-start | bytes 8388608
  78.8 4.6 %collective-permute-start.20 = (bf16[16,128]{1,0:T(8,128)(2,1)S(1)}, bf16[16,128]{1,0:T(8,128)(2,1)S(1)}, u32[]{:S(2)}, u32[]{:S(2)}) collective-permute-start(bf16[16,128]{1,0:T(8,128)(2,1)S(1)} %get-tuple-element.102), channel_id=1, source_target_pairs={{0,8},{1,9},{2,10},{3,11},{4,12},{5,13},{6,14},{7,15},{8,0},{9,1},... | collective-permute-start | bytes 12296 | tf_op jit(solution)/shard_map/ppermute | solution.py:29
  79.9 10.0 %collective-permute-start.19 = (bf16[128,640]{1,0:T(8,128)(2,1)S(1)}, bf16[128,640]{1,0:T(8,128)(2,1)S(1)}, u32[]{:S(2)}, u32[]{:S(2)}) collective-permute-start(bf16[128,640]{1,0:T(8,128)(2,1)S(1)} %get-tuple-element.101), channel_id=1, source_target_pairs={{0,8},{1,9},{2,10},{3,11},{4,12},{5,13},{6,14},{7,15},{8,0},{9,1},... | collective-permute-start | bytes 491528 | tf_op jit(solution)/shard_map/ppermute | solution.py:29
  91.4 1.7 %collective-permute-start.21 = (bf16[64,2560]{1,0:T(8,128)(2,1)S(1)}, bf16[64,2560]{1,0:T(8,128)(2,1)S(1)}, u32[]{:S(2)}, u32[]{:S(2)}) collective-permute-start(bf16[64,2560]{1,0:T(8,128)(2,1)S(1)} %get-tuple-element.104), channel_id=1, source_target_pairs={{0,1},{1,0},{2,3},{3,2},{4,5},{5,4},{6,7},{7,6},{8,9},{9,8},{10,11... | collective-permute-start | bytes 983048 | tf_op jit(solution)/shard_map/ppermute | solution.py:29
  93.2 6.3 %collective-permute-start.22 = (bf16[64,1280]{1,0:T(8,128)(2,1)S(1)}, bf16[64,1280]{1,0:T(8,128)(2,1)S(1)}, u32[]{:S(2)}, u32[]{:S(2)}) collective-permute-start(bf16[64,1280]{1,0:T(8,128)(2,1)S(1)} %get-tuple-element.138), channel_id=1, source_target_pairs={{0,2},{1,3},{2,0},{3,1},{4,6},{5,7},{6,4},{7,5},{8,10},{9,11},{10,... | collective-permute-start | bytes 491528 | tf_op jit(solution)/shard_map/ppermute | solution.py:29
  94.7 6.0 %collective-permute-start.24 = (bf16[64,1280]{1,0:T(8,128)(2,1)S(1)}, bf16[64,1280]{1,0:T(8,128)(2,1)S(1)}, u32[]{:S(2)}, u32[]{:S(2)}) collective-permute-start(bf16[64,1280]{1,0:T(8,128)(2,1)S(1)} %get-tuple-element.139), channel_id=1, source_target_pairs={{0,4},{1,5},{2,6},{3,7},{4,0},{5,1},{6,2},{7,3},{8,12},{9,13},{10,... | collective-permute-start | bytes 491528 | tf_op jit(solution)/shard_map/ppermute | solution.py:29
  100.7 5.4 %collective-permute-start.23 = (bf16[64,1280]{1,0:T(8,128)(2,1)S(1)}, bf16[64,1280]{1,0:T(8,128)(2,1)S(1)}, u32[]{:S(2)}, u32[]{:S(2)}) collective-permute-start(bf16[64,1280]{1,0:T(8,128)(2,1)S(1)} %get-tuple-element.136), channel_id=1, source_target_pairs={{0,4},{1,5},{2,6},{3,7},{4,0},{5,1},{6,2},{7,3},{8,12},{9,13},{10,... | collective-permute-start | bytes 491528 | tf_op jit(solution)/shard_map/ppermute | solution.py:29
  101.1 5.3 %collective-permute-start.25 = (bf16[64,1280]{1,0:T(8,128)(2,1)S(1)}, bf16[64,1280]{1,0:T(8,128)(2,1)S(1)}, u32[]{:S(2)}, u32[]{:S(2)}) collective-permute-start(bf16[64,1280]{1,0:T(8,128)(2,1)S(1)} %get-tuple-element.137), channel_id=1, source_target_pairs={{0,2},{1,3},{2,0},{3,1},{4,6},{5,7},{6,4},{7,5},{8,10},{9,11},{10,... | collective-permute-start | bytes 491528 | tf_op jit(solution)/shard_map/ppermute | solution.py:29
  106.5 1.7 %collective-permute-start.26 = (bf16[64,2560]{1,0:T(8,128)(2,1)S(1)}, bf16[64,2560]{1,0:T(8,128)(2,1)S(1)}, u32[]{:S(2)}, u32[]{:S(2)}) collective-permute-start(bf16[64,2560]{1,0:T(8,128)(2,1)S(1)} %add_convert_fusion.ours_ref), channel_id=1, source_target_pairs={{0,1},{1,0},{2,3},{3,2},{4,5},{5,4},{6,7},{7,6},{8,9},{9,8},{10,11... | collective-permute-start | bytes 983048 | tf_op jit(solution)/shard_map/ppermute | solution.py:29
  109.0 10.9 %collective-permute-start.27 = (bf16[128,640]{1,0:T(8,128)(2,1)S(1)}, bf16[128,640]{1,0:T(8,128)(2,1)S(1)}, u32[]{:S(2)}, u32[]{:S(2)}) collective-permute-start(bf16[128,640]{1,0:T(8,128)(2,1)S(1)} %get-tuple-element.107), channel_id=1, source_target_pairs={{0,8},{1,9},{2,10},{3,11},{4,12},{5,13},{6,14},{7,15},{8,0},{9,1},... | collective-permute-start | bytes 491528 | tf_op jit(solution)/shard_map/ppermute | solution.py:29
  111.1 8.8 %collective-permute-start.28 = (bf16[16,128]{1,0:T(8,128)(2,1)S(1)}, bf16[16,128]{1,0:T(8,128)(2,1)S(1)}, u32[]{:S(2)}, u32[]{:S(2)}) collective-permute-start(bf16[16,128]{1,0:T(8,128)(2,1)S(1)} %get-tuple-element.108), channel_id=1, source_target_pairs={{0,8},{1,9},{2,10},{3,11},{4,12},{5,13},{6,14},{7,15},{8,0},{9,1},... | collective-permute-start | bytes 12296 | tf_op jit(solution)/shard_map/ppermute | solution.py:29
  121.0 9.2 %collective-permute-start.29 = (bf16[128,640]{1,0:T(8,128)(2,1)S(1)}, bf16[128,640]{1,0:T(8,128)(2,1)S(1)}, u32[]{:S(2)}, u32[]{:S(2)}) collective-permute-start(bf16[128,640]{1,0:T(8,128)(2,1)S(1)} %get-tuple-element.111), channel_id=1, source_target_pairs={{0,8},{1,9},{2,10},{3,11},{4,12},{5,13},{6,14},{7,15},{8,0},{9,1},... | collective-permute-start | bytes 491528 | tf_op jit(solution)/shard_map/ppermute | solution.py:29
  121.1 9.1 %collective-permute-start.30 = (bf16[16,128]{1,0:T(8,128)(2,1)S(1)}, bf16[16,128]{1,0:T(8,128)(2,1)S(1)}, u32[]{:S(2)}, u32[]{:S(2)}) collective-permute-start(bf16[16,128]{1,0:T(8,128)(2,1)S(1)} %get-tuple-element.112), channel_id=1, source_target_pairs={{0,8},{1,9},{2,10},{3,11},{4,12},{5,13},{6,14},{7,15},{8,0},{9,1},... | collective-permute-start | bytes 12296 | tf_op jit(solution)/shard_map/ppermute | solution.py:29
  131.5 1.7 %collective-permute-start.31 = (bf16[4,320,128]{2,1,0:T(8,128)(2,1)S(1)}, bf16[4,320,128]{2,1,0:T(8,128)(2,1)S(1)}, u32[]{:S(2)}, u32[]{:S(2)}) collective-permute-start(bf16[4,320,128]{2,1,0:T(8,128)(2,1)S(1)} %get-tuple-element.114), channel_id=1, source_target_pairs={{0,1},{1,0},{2,3},{3,2},{4,5},{5,4},{6,7},{7,6},{8,9},{9,8},{10,11... | collective-permute-start | bytes 983048 | tf_op jit(solution)/shard_map/ppermute | solution.py:29
  133.3 4.6 %collective-permute-start.32 = (bf16[320,128]{1,0:T(8,128)(2,1)S(1)}, bf16[320,128]{1,0:T(8,128)(2,1)S(1)}, u32[]{:S(2)}, u32[]{:S(2)}) collective-permute-start(bf16[320,128]{1,0:T(8,128)(2,1)S(1)} %get-tuple-element.133), channel_id=1, source_target_pairs={{0,2},{1,3},{2,0},{3,1},{4,6},{5,7},{6,4},{7,5},{8,10},{9,11},{10,... | collective-permute-start | bytes 245768 | tf_op jit(solution)/shard_map/ppermute | solution.py:29
  134.5 6.0 %collective-permute-start.34 = (bf16[320,128]{1,0:T(8,128)(2,1)S(1)}, bf16[320,128]{1,0:T(8,128)(2,1)S(1)}, u32[]{:S(2)}, u32[]{:S(2)}) collective-permute-start(bf16[320,128]{1,0:T(8,128)(2,1)S(1)} %get-tuple-element.134), channel_id=1, source_target_pairs={{0,6},{1,7},{2,4},{3,5},{4,2},{5,3},{6,0},{7,1},{8,14},{9,15},{10,... | collective-permute-start | bytes 245768 | tf_op jit(solution)/shard_map/ppermute | solution.py:29
  134.5 6.3 %collective-permute-start.33 = (bf16[320,128]{1,0:T(8,128)(2,1)S(1)}, bf16[320,128]{1,0:T(8,128)(2,1)S(1)}, u32[]{:S(2)}, u32[]{:S(2)}) collective-permute-start(bf16[320,128]{1,0:T(8,128)(2,1)S(1)} %get-tuple-element.135), channel_id=1, source_target_pairs={{0,4},{1,5},{2,6},{3,7},{4,0},{5,1},{6,2},{7,3},{8,12},{9,13},{10,... | collective-permute-start | bytes 245768 | tf_op jit(solution)/shard_map/ppermute | solution.py:29
